TPU v7x, 32 devices: a whole 2x2x4 slice. The times are simulated.
32 devices in a mesh: wide: 8 (over z, x), narrow: 4 (over y, core).
Axes of the slice: x: 2, y: 2, z: 4, core: 2. Of those that a mesh axis runs over, the one named last changes fastest.
Arguments:
- tokens: bfloat16 [32768, 768], P(('wide', 'narrow')), may hold values from -6 to 6
- qkv_weight: float32 [768, 2304], P('narrow', 'wide'), may hold values from -0.21875 to 0.21875
- out_weight: float32 [768, 768], P('wide', 'narrow'), may hold values from -1.25 to 1.25
- up_weight: float32 [768, 3072], P('narrow', 'wide'), may hold values from -0.21875 to 0.21875
- down_weight: float32 [3072, 768], P('wide', 'narrow'), may hold values from -0.109375 to 0.109375
- vectors: float32 [9216], P(('wide', 'narrow')), may hold values from -1.2 to 1.5, as said below
- bucket_counts: int32 [32, 3], P(('wide', 'narrow')), may hold values from 0 to 16, as said below
- cotangent: bfloat16 [32768, 768], P(('wide', 'narrow')), may hold values from -6 to 6
Outputs:
- block_out: bfloat16 [32768, 768], P(('wide', 'narrow'))
- input_grad: bfloat16 [32768, 768], P(('wide', 'narrow'))
- qkv_grad: float32 [768, 2304], P('narrow', 'wide')
- out_grad: float32 [768, 768], P('wide', 'narrow')
- up_grad: float32 [768, 3072], P('narrow', 'wide')
- down_grad: float32 [3072, 768], P('wide', 'narrow')
- vector_grad: float32 [9216], P(('wide', 'narrow'))
Inputs may be any that keep to these rules, and one draw needn't show every extreme that they name: `bucket_counts`: row r gives how many images of 25, 49 and 64 patches device r holds, laid out in that order; together they fill its 1024 tokens exactly. No count exceeds 1024 // 64. `vectors`: gains lie in 0.5 to 1.5, all other entries in -1.2 to 1.2.
All inputs are finite; a program needn't handle non-finite values.
Results may differ from a plain program's by a relative error of at most 0.017.
Values may be sent and summed in bfloat16 or wider, within the bound.
No kernel may reach another device: no remote copies, remote signals or barrier semaphores. Data moves between devices by JAX's collectives and lax.ppermute only.
A program may use at most 256 MiB of HBM per device.

v0:
```python
import jax
import jax.numpy as jnp
from jax import lax
from jax.sharding import PartitionSpec as P

HEADS = 12
HEAD_DIM = 64
QROWS = 512
P_ONE = 25
P_TWO = 49
P_THREE = 64


EPS = 1e-06
NEG = -1e30


def layer_norm(values, gain, shift):
    center = values - jnp.mean(values, axis=-1, keepdims=True)
    spread = jnp.mean(center * center, axis=-1, keepdims=True)
    return center * lax.rsqrt(spread + EPS) * gain + shift


def image_ids(counts, rows):
    place = jnp.arange(rows, dtype=jnp.int32)
    first = counts[0] * P_ONE
    second = first + counts[1] * P_TWO
    bucket = (place >= first).astype(jnp.int32) + (place >= second).astype(jnp.int32)
    start = jnp.where(bucket == 0, 0, jnp.where(bucket == 1, first, second))
    length = jnp.where(bucket == 0, P_ONE, jnp.where(bucket == 1, P_TWO, P_THREE)).astype(jnp.int32)
    return bucket * rows + (place - start) // length


def gelu_exact(values):
    return jax.nn.gelu(values, approximate=False)


def contract_rows(left, right):
    return lax.dot_general(
        left, right, (((0,), (0,)), ((), ())), preferred_element_type=jnp.float32
    )


def contract_cols(left, right):
    return lax.dot_general(
        left, right, (((1,), (1,)), ((), ())), preferred_element_type=jnp.float32
    )


def windows_of(values, margin, blocks, fill):
    rows = values.shape[0]
    block_rows = rows // blocks
    rest = values.shape[1:]
    padded = jnp.pad(
        values, ((margin, margin),) + tuple(((0, 0) for unused in rest)), constant_values=fill
    )
    before = padded[:rows].reshape((blocks, block_rows) + rest)[:, :margin]
    middle = values.reshape((blocks, block_rows) + rest)
    after = padded[2 * margin : 2 * margin + rows].reshape((blocks, block_rows) + rest)[
        :, block_rows - margin :
    ]
    return jnp.concatenate([before, middle, after], axis=1)


def fold_windows(grads, margin, block_rows):
    blocks = grads.shape[0]
    width = grads.shape[2]
    middle = grads[:, margin : margin + block_rows]
    before = jnp.pad(grads[1:, :margin], ((0, 1), (block_rows - margin, 0), (0, 0)))
    after = jnp.pad(grads[:-1, margin + block_rows :], ((1, 0), (0, block_rows - margin), (0, 0)))
    return (middle + before + after).reshape(blocks * block_rows, width)


def per_device(
    tokens, qkv_weight, out_weight, up_weight, down_weight, vectors, bucket_counts, cotangent
):
    rows, width = tokens.shape
    halves = (
        lax.all_gather(qkv_weight.astype(jnp.bfloat16), "narrow", axis=0, tiled=True),
        lax.all_gather(out_weight.astype(jnp.bfloat16), "narrow", axis=1, tiled=True),
        lax.all_gather(up_weight.astype(jnp.bfloat16), "narrow", axis=0, tiled=True),
        lax.all_gather(down_weight.astype(jnp.bfloat16), "narrow", axis=1, tiled=True),
        lax.all_gather(vectors.astype(jnp.bfloat16), "narrow", axis=0, tiled=True),
    )
    wholes = (
        lax.all_gather(halves[0], "wide", axis=1, tiled=True),
        lax.all_gather(halves[1], "wide", axis=0, tiled=True),
        lax.all_gather(halves[2], "wide", axis=1, tiled=True),
        lax.all_gather(halves[3], "wide", axis=0, tiled=True),
        lax.all_gather(halves[4], "wide", axis=0, tiled=True),
    )
    qkv_full, out_full, up_full, down_full, packed = wholes
    params = packed.astype(jnp.float32)
    gain_one = params[0:width]
    shift_one = params[width : 2 * width]
    bias_query = params[2 * width : 3 * width]
    bias_value = params[3 * width : 4 * width]
    bias_out = params[4 * width : 5 * width]
    gain_two = params[5 * width : 6 * width]
    shift_two = params[6 * width : 7 * width]
    bias_down = params[7 * width : 8 * width]
    bias_up = params[8 * width :]
    inputs = tokens.astype(jnp.float32)
    hidden_one = layer_norm(inputs, gain_one, shift_one).astype(jnp.bfloat16)
    qkv_bias = jnp.concatenate([bias_query, jnp.zeros((width,), jnp.float32), bias_value])
    qkv_all = (jnp.dot(hidden_one, qkv_full, preferred_element_type=jnp.float32) + qkv_bias).astype(
        jnp.bfloat16
    )
    margin = P_THREE
    blocks = rows // QROWS
    span = QROWS + 2 * margin
    scale = HEAD_DIM ** (-0.5)
    query_blk = qkv_all[:, :width].reshape(blocks, QROWS, HEADS, HEAD_DIM)
    keys_win = windows_of(qkv_all[:, width : 2 * width], margin, blocks, 0).reshape(
        blocks, span, HEADS, HEAD_DIM
    )
    values_win = windows_of(qkv_all[:, 2 * width :], margin, blocks, 0).reshape(
        blocks, span, HEADS, HEAD_DIM
    )
    segment = image_ids(bucket_counts[0], rows)
    seg_rows = segment.reshape(blocks, QROWS)
    seg_cols = windows_of(segment, margin, blocks, -1)
    same = seg_rows[:, None, :, None] == seg_cols[:, None, None, :]
    raw = (
        jnp.einsum("bqhd,bkhd->bhqk", query_blk, keys_win, preferred_element_type=jnp.float32)
        * scale
    )
    masked = jnp.where(same, raw, NEG)
    top = jnp.max(masked, axis=3, keepdims=True)
    expo = jnp.exp(masked - top)
    total = jnp.sum(expo, axis=3, keepdims=True)
    probs_low = (expo / total).astype(jnp.bfloat16)
    log_total = top + jnp.log(total)
    attended = jnp.einsum(
        "bhqk,bkhd->bqhd", probs_low, values_win, preferred_element_type=jnp.float32
    )
    attn_low = attended.reshape(rows, width).astype(jnp.bfloat16)
    mid = inputs + jnp.dot(attn_low, out_full, preferred_element_type=jnp.float32) + bias_out
    hidden_two = layer_norm(mid, gain_two, shift_two).astype(jnp.bfloat16)
    pre_act = jnp.dot(hidden_two, up_full, preferred_element_type=jnp.float32) + bias_up
    activated = gelu_exact(pre_act).astype(jnp.bfloat16)
    output = mid + jnp.dot(activated, down_full, preferred_element_type=jnp.float32) + bias_down
    block_out = output.astype(jnp.bfloat16)
    grad_top = cotangent.astype(jnp.float32)
    d_down = contract_rows(activated, cotangent)
    d_bias_down = jnp.sum(grad_top, axis=0)
    grad_act = contract_cols(cotangent, down_full)
    unused_act, gelu_back = jax.vjp(gelu_exact, pre_act)
    grad_pre = gelu_back(grad_act)[0].astype(jnp.bfloat16)
    d_up = contract_rows(hidden_two, grad_pre)
    d_bias_up = jnp.sum(grad_pre.astype(jnp.float32), axis=0)
    grad_hidden_two = contract_cols(grad_pre, up_full)
    unused_two, norm_back_two = jax.vjp(layer_norm, mid, gain_two, shift_two)
    grad_mid_part, d_gain_two, d_shift_two = norm_back_two(grad_hidden_two)
    grad_mid = grad_top + grad_mid_part
    grad_mid_low = grad_mid.astype(jnp.bfloat16)
    d_out = contract_rows(attn_low, grad_mid_low)
    d_bias_out = jnp.sum(grad_mid_low.astype(jnp.float32), axis=0)
    grad_attn = contract_cols(grad_mid_low, out_full).astype(jnp.bfloat16)
    raw_again = (
        jnp.einsum("bqhd,bkhd->bhqk", query_blk, keys_win, preferred_element_type=jnp.float32)
        * scale
    )
    probs = jnp.exp(jnp.where(same, raw_again, NEG) - log_total)
    grad_blk = grad_attn.reshape(blocks, QROWS, HEADS, HEAD_DIM)
    grad_probs = jnp.einsum(
        "bqhd,bkhd->bhqk", grad_blk, values_win, preferred_element_type=jnp.float32
    )
    grad_scores = (
        probs * (grad_probs - jnp.sum(probs * grad_probs, axis=3, keepdims=True))
    ).astype(jnp.bfloat16)
    grad_query = (
        jnp.einsum("bhqk,bkhd->bqhd", grad_scores, keys_win, preferred_element_type=jnp.float32)
        * scale
    )
    grad_keys_win = (
        jnp.einsum("bhqk,bqhd->bkhd", grad_scores, query_blk, preferred_element_type=jnp.float32)
        * scale
    )
    grad_values_win = jnp.einsum(
        "bhqk,bqhd->bkhd", probs.astype(jnp.bfloat16), grad_blk, preferred_element_type=jnp.float32
    )
    grad_keys = fold_windows(grad_keys_win.reshape(blocks, span, width), margin, QROWS)
    grad_values = fold_windows(grad_values_win.reshape(blocks, span, width), margin, QROWS)
    grad_qkv = jnp.concatenate(
        [grad_query.reshape(rows, width), grad_keys, grad_values], axis=1
    ).astype(jnp.bfloat16)
    d_qkv = contract_rows(hidden_one, grad_qkv)
    column_sums = jnp.sum(grad_qkv.astype(jnp.float32), axis=0)
    grad_hidden_one = contract_cols(grad_qkv, qkv_full)
    unused_one, norm_back_one = jax.vjp(layer_norm, inputs, gain_one, shift_one)
    grad_in_part, d_gain_one, d_shift_one = norm_back_one(grad_hidden_one)
    input_grad = (grad_mid + grad_in_part).astype(jnp.bfloat16)
    d_vector = jnp.concatenate(
        [
            d_gain_one,
            d_shift_one,
            column_sums[:width],
            column_sums[2 * width :],
            d_bias_out,
            d_gain_two,
            d_shift_two,
            d_bias_down,
            d_bias_up,
        ]
    )
    partial_sums = (
        lax.psum_scatter(
            d_qkv.astype(jnp.bfloat16), "wide", scatter_dimension=1, tiled=True
        ).astype(jnp.float32),
        lax.psum_scatter(
            d_out.astype(jnp.bfloat16), "wide", scatter_dimension=0, tiled=True
        ).astype(jnp.float32),
        lax.psum_scatter(d_up.astype(jnp.bfloat16), "wide", scatter_dimension=1, tiled=True).astype(
            jnp.float32
        ),
        lax.psum_scatter(
            d_down.astype(jnp.bfloat16), "wide", scatter_dimension=0, tiled=True
        ).astype(jnp.float32),
        lax.psum_scatter(
            d_vector.astype(jnp.bfloat16), "wide", scatter_dimension=0, tiled=True
        ).astype(jnp.float32),
    )
    final = (
        lax.psum_scatter(
            partial_sums[0].astype(jnp.bfloat16), "narrow", scatter_dimension=0, tiled=True
        ).astype(jnp.float32),
        lax.psum_scatter(
            partial_sums[1].astype(jnp.bfloat16), "narrow", scatter_dimension=1, tiled=True
        ).astype(jnp.float32),
        lax.psum_scatter(
            partial_sums[2].astype(jnp.bfloat16), "narrow", scatter_dimension=0, tiled=True
        ).astype(jnp.float32),
        lax.psum_scatter(
            partial_sums[3].astype(jnp.bfloat16), "narrow", scatter_dimension=1, tiled=True
        ).astype(jnp.float32),
        lax.psum_scatter(
            partial_sums[4].astype(jnp.bfloat16), "narrow", scatter_dimension=0, tiled=True
        ).astype(jnp.float32),
    )
    return (block_out, input_grad, final[0], final[1], final[2], final[3], final[4])


def solution(mesh):
    return jax.shard_map(
        per_device,
        mesh=mesh,
        in_specs=(
            P(("wide", "narrow"), None),
            P("narrow", "wide"),
            P("wide", "narrow"),
            P("narrow", "wide"),
            P("wide", "narrow"),
            P(("wide", "narrow")),
            P(("wide", "narrow"), None),
            P(("wide", "narrow"), None),
        ),
        out_specs=(
            P(("wide", "narrow"), None),
            P(("wide", "narrow"), None),
            P("narrow", "wide"),
            P("wide", "narrow"),
            P("narrow", "wide"),
            P("wide", "narrow"),
            P(("wide", "narrow")),
        ),
        check_vma=False,
    )
```

profile of v0, /device:TPU:0, one launch (start us, length us, event | category | flops | bytes accessed | tf_op | source)
XLA Modules:
  0.0 831.3 jit_solution(9290434938617641362)
XLA Ops:
  8.3 9.0 %all_gather.32 = bf16[768,288]{1,0:T(8,128)(2,1)S(1)} all-gather(bf16[192,288]{1,0:T(8,128)(2,1)S(1)} %convert_element_type.150), channel_id=1, replica_groups=mesh['wide'=8,'narrow'=4] {'narrow'}, dimensions={0}, use_global_device_ids=true | all-gather | bytes 552960 | tf_op jit(solution)/shard_map/all_gather | solution.py:79
  25.9 8.1 all_gather.36
  34.1 8.1 all_gather.38
  46.1 6.7 all-reduce.7
  52.8 31.3 %all-gather = bf16[8,1,1152]{2,1,0:T(2,128)(2,1)S(1)} all-gather(bf16[1,1,1152]{2,1,0:T(2,128)(2,1)S(1)} %reshape.216), channel_id=1, replica_groups=mesh['wide'=8,'narrow'=4] {'wide'}, dimensions={0}, use_global_device_ids=true | all-gather | bytes 20736 | tf_op jit(solution)/shard_map/all_gather | solution.py:90
  91.9 6.7 add_convert_fusion.1
  138.6 16.6 %fusion.62 = (f32[2,12,512]{2,1,0:T(8,128)S(1)}, f32[2,12,512,640]{3,2,1,0:T(8,128)}) fusion(bf16[2,64,12,64]{1,3,2,0:T(8,128)(2,1)} %bitcast.94, bf16[2,512,12,64]{1,3,2,0:T(8,128)(2,1)} %copy.118, bf16[2,64,12,64]{1,3,2,0:T(8,128)(2,1)} %bitcast.96, bf16[2,512,12,64]{1,0,3,2:T(2,128)(2,1)S(1)} %reshape.204, pred[2,512,640]{2,1,0:T(8,128)(4,1)} %broadcast_compare_fusion), kind=kOutput, calls=%fused_computation.130 | convolution fusion | flops 1036111872 | bytes 35700736 | tf_op jit(solution)/shard_map/bqhd,bkhd->bhqk/dot_general | solution.py:125
  155.2 14.1 %fusion = f32[2,12,512]{2,1,0:T(8,128)S(1)} fusion(f32[2,12,512,640]{3,2,1,0:T(8,128)} %get-tuple-element.73, f32[2,12,512]{2,1,0:T(8,128)S(1)} %get-tuple-element.72), kind=kLoop, calls=%fused_computation.6 | loop fusion | flops 15716352 | bytes 31555584 | tf_op jit(solution)/shard_map/reduce_sum | solution.py:131
  169.9 13.2 %fusion.27 = bf16[2,512,12,64]{1,3,2,0:T(8,128)(2,1)S(1)} fusion(f32[2,12,512,640]{3,2,1,0:T(8,128)} %get-tuple-element.73, f32[2,12,512]{2,1,0:T(8,128)S(1)} %fusion, f32[2,12,512]{2,1,0:T(8,128)S(1)} %get-tuple-element.72, bf16[2,64,12,64]{1,3,2,0:T(8,128)(2,1)S(1)} %bitcast.88, bf16[2,512,12,64]{1,3,2,0:T(8,128)(2,1)S(1)} %copy-done.12, ...), kind=kOutput, calls=%fused_computation.72 | convolution fusion | flops 1036910592 | bytes 35094528 | tf_op jit(solution)/shard_map/bhqk,bkhd->bqhd/dot_general | solution.py:134
  190.7 18.6 %all-gather.10.cloned.1.call-done = bf16[768,3072]{1,0:T(8,128)(2,1)} async-done(((bf16[768,384]{1,0:T(8,128)(2,1)}), bf16[768,3072]{1,0:T(8,128)(2,1)}) %all-gather.10.cloned.1.call-update) | async-done | bytes 4718608 | tf_op jit(solution)/shard_map/all_gather | solution.py:88
  209.3 38.1 %multiply_convert_fusion.1 = (bf16[1024,3072]{1,0:T(8,128)(2,1)}, f32[1024,3072]{1,0:T(8,128)}, f32[1024,3072]{1,0:T(8,128)}) fusion(f32[3072]{0:T(1024)S(1)} %copy-done.45, bf16[768,3072]{1,0:T(8,128)(2,1)} %all-gather.10.cloned.1.call-done, f32[1024,768]{0,1:T(8,128)} %copy-done.3, f32[768]{0:T(1024)S(1)} %get-tuple-element.57, ...), kind=kOutput, calls=%fused_computation.14 | convolution fusion | flops 5043388416 | bytes 39348224 | tf_op jit(solution)/shard_map/dot_general | solution.py:140
  247.4 43.0 %all-gather.12.cloned.1.call-done = bf16[3072,768]{0,1:T(8,128)(2,1)} async-done(((bf16[384,768]{0,1:T(8,128)(2,1)}), bf16[3072,768]{0,1:T(8,128)(2,1)}) %all-gather.12.cloned.1.call-update) | async-done | bytes 4718608 | tf_op jit(solution)/shard_map/all_gather | solution.py:89
  290.5 17.5 %fusion.66 = (bf16[3072]{0:T(1024)(128)(2,1)}, bf16[1024,3072]{1,0:T(8,128)(2,1)}) fusion(f32[1024,3072]{1,0:T(8,128)} %get-tuple-element.44, bf16[1024,768]{1,0:T(8,128)(2,1)S(1)} %copy-done.15, bf16[3072,768]{0,1:T(8,128)(2,1)} %all-gather.12.cloned.1.call-done, f32[1024,3072]{1,0:T(8,128)} %get-tuple-element.76, f32[3072]{0:T(1024)S(1)} %copy-done.45), kind=kOutput, calls=%fused_computation.134 | convolution fusion | flops 4882166784 | bytes 37767168 | tf_op jit(solution)/shard_map/dot_general | solution.py:45
  307.9 9.4 %fusion.65 = (bf16[768]{0:T(1024)(128)(2,1)}, f32[1024,768]{1,0:T(8,128)}) fusion(bf16[1024,3072]{1,0:T(8,128)(2,1)} %get-tuple-element.84, bf16[768,3072]{1,0:T(8,128)(2,1)S(1)} %copy-done.58), kind=kOutput, calls=%fused_computation.133 | convolution fusion | flops 4832623616 | bytes 14157312 | tf_op jit(solution)/shard_map/dot_general | solution.py:45
  335.1 12.1 %fusion.2 = f32[2,12,64,640]{3,2,1,0:T(8,128)S(1)} fusion(f32[2,12,512,640]{3,2,1,0:T(8,128)} %get-tuple-element.73, f32[2,12,512]{2,1,0:T(8,128)S(1)} %copy-done.22, bf16[2,512,12,64]{1,0,3,2:T(2,128)(2,1)S(1)} %reshape.207), kind=kOutput, calls=%fused_computation.9 | convolution fusion | flops 1022361600 | bytes 37011456 | tf_op jit(solution)/shard_map/bhqk,bqhd->bkhd/dot_general | solution.py:180
  350.7 22.1 %multiply_reduce_fusion = (f32[2,12,512]{2,1,0:T(8,128)S(1)}, f32[2,12,512,640]{3,2,1,0:T(8,128)}) fusion(f32[2,12,512,640]{3,2,1,0:T(8,128)} %get-tuple-element.73, f32[2,12,512]{2,1,0:T(8,128)S(1)} %copy-done.22, bf16[2,64,12,64]{1,3,2,0:T(8,128)(2,1)S(1)} %bitcast.89, bf16[2,512,12,64]{1,3,2,0:T(8,128)(2,1)S(1)} %copy-done.13, ...), kind=kOutput, calls=%fused_computation.1 | convolution fusion | flops 1036111872 | bytes 66551808 | tf_op jit(solution)/shard_map/bqhd,bkhd->bhqk/dot_general | solution.py:166
  383.1 26.7 %multiply_convert_fusion = bf16[2,12,512,640]{3,2,1,0:T(8,128)(2,1)} fusion(f32[2,12,512,640]{3,2,1,0:T(8,128)} %get-tuple-element.78, f32[2,12,512,640]{3,2,1,0:T(8,128)} %get-tuple-element.73, f32[2,12,512]{2,1,0:T(8,128)S(1)} %get-tuple-element.77, f32[2,12,512]{2,1,0:T(8,128)S(1)} %copy-done.22), kind=kLoop, calls=%fused_computation | loop fusion | flops 31457280 | bytes 78741504 | tf_op jit(solution)/shard_map/convert_element_type | solution.py:171
  409.8 10.8 %fusion.26 = bf16[2,512,12,64]{1,3,2,0:T(8,128)(2,1)S(1)} fusion(bf16[2,12,512,640]{3,2,1,0:T(8,128)(2,1)} %multiply_convert_fusion, bf16[2,64,12,64]{1,3,2,0:T(8,128)(2,1)} %bitcast.95, bf16[2,512,12,64]{1,3,2,0:T(8,128)(2,1)S(1)} %copy-done.21, bf16[2,64,12,64]{1,3,2,0:T(8,128)(2,1)} %bitcast.97), kind=kOutput, calls=%fused_computation.71 | convolution fusion | flops 1014104064 | bytes 19267584 | tf_op jit(solution)/shard_map/bhqk,bkhd->bqhd/dot_general | solution.py:173
  423.7 6.8 convolution_multiply_fusion
  443.8 7.8 convolution_convert_fusion.2
  453.0 9.7 %convolution_convert_fusion = bf16[3072,768]{1,0:T(8,128)(2,1)} fusion(bf16[1024,3072]{1,0:T(8,128)(2,1)} %get-tuple-element.43, bf16[1024,768]{1,0:T(8,128)(2,1)S(1)} %copy-done.16), kind=kOutput, calls=%fused_computation.29 | convolution fusion | flops 4834197504 | bytes 12582912 | tf_op jit(solution)/shard_map/dot_general | solution.py:39
  463.4 9.9 %convolution_convert_fusion.1 = bf16[768,3072]{1,0:T(8,128)(2,1)} fusion(bf16[1024,3072]{1,0:T(8,128)(2,1)} %get-tuple-element.84, f32[1024,768]{0,1:T(8,128)} %copy-done.3, f32[768]{0:T(1024)S(1)} %copy-done.51, f32[768]{0:T(1024)S(1)} %copy-done.42, f32[1024]{0:T(1024)S(1)} %copy-done.44, f32[1024]{0:T(1024)S(1)} %broadcast_multiply_fusion), kind=kOutput, calls=%fused_computation.30 | convolution fusion | flops 4838129664 | bytes 14170112 | tf_op jit(solution)/shard_map/dot_general | solution.py:39
  473.3 6.7 copy.151
  484.4 10.1 %add_convert_fusion.5 = bf16[1024,768]{0,1:T(8,128)(2,1)} fusion(f32[1024,768]{0,1:T(8,128)} %copy-done.3, bf16[1024,3072]{1,0:T(8,128)(2,1)} %get-tuple-element.43, bf16[3072,768]{0,1:T(8,128)(2,1)} %all-gather.12.cloned.1.call-done, f32[768]{0:T(1024)S(1)} %copy-done.49), kind=kOutput, calls=%fused_computation.57 | convolution fusion | flops 4834197504 | bytes 15731712 | tf_op jit(solution)/shard_map/dot_general | solution.py:142
  497.2 32.0 %reduce-scatter.17.cloned.1.call-done = bf16[768,288]{0,1:T(8,128)(2,1)} async-done(((bf16[768,2304]{0,1:T(8,128)(2,1)}), bf16[768,288]{0,1:T(8,128)(2,1)}) %reduce-scatter.17.cloned.1.call-update) | async-done | bytes 442384 | tf_op jit(solution)/shard_map/reduce_scatter | solution.py:208
  531.6 8.5 %fusion.64 = (bf16[768]{0:T(1024)(128)(2,1)S(1)}, f32[1024,768]{1,0:T(8,128)}) fusion(bf16[768,2304]{0,1:T(8,128)(2,1)} %all-gather.6.cloned.1.call-done, bf16[1024,768]{0,1:T(8,128)(2,1)S(1)} %copy-done.18, bf16[1024,768]{0,1:T(8,128)(2,1)} %copy.137, bf16[1024,768]{0,1:T(8,128)(2,1)} %bitcast.77), kind=kOutput, calls=%fused_computation.132 | convolution fusion | flops 3638820096 | bytes 11404800 | tf_op jit(solution)/shard_map/dot_general | solution.py:45
  543.7 84.1 %reduce-scatter.23.cloned.1.call-done = bf16[384,768]{1,0:T(8,128)(2,1)} async-done(((bf16[3072,768]{1,0:T(8,128)(2,1)}), bf16[384,768]{1,0:T(8,128)(2,1)}) %reduce-scatter.23.cloned.1.call-update) | async-done | bytes 589840 | tf_op jit(solution)/shard_map/reduce_scatter | solution.py:217
  634.2 92.3 %reduce-scatter.29.cloned.1.call-done = bf16[384,768]{1,0:T(8,128)(2,1)} async-done(((bf16[3072,768]{1,0:T(8,128)(2,1)}), bf16[384,768]{1,0:T(8,128)(2,1)}) %reduce-scatter.29.cloned.1.call-update) | async-done | bytes 589840
  740.5 35.9 %all-reduce.8 = bf16[9216]{0:T(1024)(128)(2,1)S(1)} all-reduce(bf16[9216]{0:T(1024)(128)(2,1)S(1)} %constant_dynamic-update-slice_fusion), channel_id=10, replica_groups=mesh['wide'=8,'narrow'=4] {'wide'}, use_global_device_ids=true, to_apply=%region_27.28.clone | all-reduce | flops 9216 | bytes 36864
  776.5 5.6 all-reduce.9
  786.2 11.9 %reduce-scatter.31.cloned.1.call-done = bf16[192,384]{1,0:T(8,128)(2,1)} async-done(((bf16[768,384]{1,0:T(8,128)(2,1)}), bf16[192,384]{1,0:T(8,128)(2,1)}) %reduce-scatter.31.cloned.1.call-update) | async-done | bytes 147472
  800.0 22.6 %reduce-scatter.21.cloned.1.call-done = bf16[192,384]{1,0:T(8,128)(2,1)} async-done(((bf16[768,384]{1,0:T(8,128)(2,1)}), bf16[192,384]{1,0:T(8,128)(2,1)}) %reduce-scatter.21.cloned.1.call-update) | async-done | bytes 147472 | tf_op jit(solution)/shard_map/reduce_scatter | solution.py:231
  (268 shorter events, 156.8 us)
Async XLA Ops:
  7.2 18.7 %copy-start.29 = (f32[192,384]{1,0:T(8,128)S(1)}, f32[192,384]{1,0:T(8,128)}, u32[]{:S(2)}) copy-start(f32[192,384]{1,0:T(8,128)} %param.11) | copy-start | bytes 884740
  7.2 26.9 %copy-start.30 = (f32[384,192]{0,1:T(8,128)S(1)}, f32[384,192]{0,1:T(8,128)}, u32[]{:S(2)}) copy-start(f32[384,192]{0,1:T(8,128)} %param.12) | copy-start | bytes 884740
  7.2 84.6 %all-gather.6.cloned.1.call-start = ((), (), s32[]{:S(2)}) async-start(), calls=%async_computation.8 | async-start | bytes 3981312 | tf_op jit(solution)/shard_map/all_gather | solution.py:86
  17.3 25.0 %copy-start.56 = (s32[1,3]{1,0:T(1,128)S(1)}, s32[1,3]{1,0:T(1,128)}, u32[]{:S(2)}) copy-start(s32[1,3]{1,0:T(1,128)} %param.14) | copy-start | bytes 40
  17.3 27.3 %copy-start.55 = (f32[288]{0:T(512)S(1)}, f32[288]{0:T(512)}, u32[]{:S(2)}) copy-start(f32[288]{0:T(512)} %param.13) | copy-start | bytes 3460
  17.3 27.3 %copy-start.54 = (u32[32]{0:T(128)S(1)}, u32[32]{0:T(128)}, u32[]{:S(2)}) copy-start(u32[32]{0:T(128)} %constant.147) | copy-start | bytes 388
  18.3 166.9 %all-gather.8.cloned.1.call-start = ((), (), s32[]{:S(2)}) async-start(), calls=%async_computation.9 | async-start | bytes 1327104 | tf_op jit(solution)/shard_map/all_gather | solution.py:87
  25.8 183.5 %all-gather.10.cloned.1.call-start = ((), (), s32[]{:S(2)}) async-start(), calls=%async_computation.10 | async-start | bytes 5308416 | tf_op jit(solution)/shard_map/all_gather | solution.py:88
  34.0 256.5 %all-gather.12.cloned.1.call-start = ((), (), s32[]{:S(2)}) async-start(), calls=%async_computation.11 | async-start | bytes 5308416 | tf_op jit(solution)/shard_map/all_gather | solution.py:89
  42.2 440.4 %reduce-scatter.19.cloned.1.call-start = ((), (), s32[]{:S(2)}) async-start(), calls=%async_computation.13 | async-start | bytes 1327104 | tf_op jit(solution)/shard_map/reduce_scatter | solution.py:211
  85.4 123.9 %copy-start.50 = (f32[768]{0:T(1024)}, f32[768]{0:T(1024)S(1)}, u32[]{:S(2)}) copy-start(f32[768]{0:T(1024)S(1)} %get-tuple-element.57) | copy-start | bytes 9220
  85.4 239.1 %copy-start.41 = (f32[768]{0:T(1024)}, f32[768]{0:T(1024)S(1)}, u32[]{:S(2)}) copy-start(f32[768]{0:T(1024)S(1)} %get-tuple-element.58) | copy-start | bytes 9220
  88.8 96.4 %copy-start = (bf16[1024,768]{0,1:T(8,128)(2,1)}, bf16[1024,768]{0,1:T(8,128)(2,1)S(1)}, u32[]{:S(2)}) copy-start(bf16[1024,768]{0,1:T(8,128)(2,1)S(1)} %copy.108) | copy-start | bytes 4718596
  114.5 24.0 %copy-start.10 = (bf16[2,512,12,64]{1,0,3,2:T(2,128)(2,1)}, bf16[2,512,12,64]{1,0,3,2:T(2,128)(2,1)S(1)}, u32[]{:S(2)}) copy-start(bf16[2,512,12,64]{1,0,3,2:T(2,128)(2,1)S(1)} %reshape.204) | copy-start | bytes 4718596
  134.9 35.0 %copy-start.23 = (bf16[2,64,768]{1,2,0:T(8,128)(2,1)}, bf16[2,64,768]{1,2,0:T(8,128)(2,1)S(1)}, u32[]{:S(2)}) copy-start(bf16[2,64,768]{1,2,0:T(8,128)(2,1)S(1)} %copy.112) | copy-start | bytes 589828
  155.2 14.7 %copy-start.25 = (bf16[2,64,768]{1,2,0:T(8,128)(2,1)S(1)}, bf16[2,64,768]{1,2,0:T(8,128)(2,1)}, u32[]{:S(2)}) copy-start(bf16[2,64,768]{1,2,0:T(8,128)(2,1)} %copy.110) | copy-start | bytes 589828
  188.7 20.6 %copy-start.45 = (f32[3072]{0:T(1024)S(1)}, f32[3072]{0:T(1024)}, u32[]{:S(2)}) copy-start(f32[3072]{0:T(1024)} %slice.156) | copy-start | bytes 36868
  190.7 133.8 %copy-start.43 = (f32[1024]{0:T(1024)}, f32[1024]{0:T(1024)S(1)}, u32[]{:S(2)}) copy-start(f32[1024]{0:T(1024)S(1)} %fusion.41) | copy-start | bytes 12292
  209.3 81.1 %copy-start.15 = (bf16[1024,768]{1,0:T(8,128)(2,1)S(1)}, bf16[1024,768]{1,0:T(8,128)(2,1)}, u32[]{:S(2)}) copy-start(bf16[1024,768]{1,0:T(8,128)(2,1)} %param.15) | copy-start | bytes 4718596
  290.5 17.5 %copy-start.58 = (bf16[768,3072]{1,0:T(8,128)(2,1)S(1)}, bf16[768,3072]{1,0:T(8,128)(2,1)}, u32[]{:S(2)}) copy-start(bf16[768,3072]{1,0:T(8,128)(2,1)} %all-gather.10.cloned.1.call-done) | copy-start | bytes 14155780
  372.8 156.4 %reduce-scatter.17.cloned.1.call-start = ((), (), s32[]{:S(2)}) async-start(), calls=%async_computation.12 | async-start | bytes 3981312 | tf_op jit(solution)/shard_map/reduce_scatter | solution.py:208
  383.1 26.7 %copy-start.21 = (bf16[2,512,12,64]{1,3,2,0:T(8,128)(2,1)S(1)}, bf16[2,512,12,64]{1,3,2,0:T(8,128)(2,1)}, u32[]{:S(2)}) copy-start(bf16[2,512,12,64]{1,3,2,0:T(8,128)(2,1)} %copy.118) | copy-start | bytes 4718596
  451.6 176.2 %reduce-scatter.23.cloned.1.call-start = ((), (), s32[]{:S(2)}) async-start(), calls=%async_computation.15 | async-start | bytes 5308416 | tf_op jit(solution)/shard_map/reduce_scatter | solution.py:217
  462.8 263.7 %reduce-scatter.29.cloned.1.call-start = ((), (), s32[]{:S(2)}) async-start(), calls=%async_computation.18 | async-start | bytes 5308416
  480.1 302.7 %reduce-scatter.27.cloned.1.call-start = ((), (), s32[]{:S(2)}) async-start(), calls=%async_computation.17 | async-start | bytes 245760
  484.3 300.0 %reduce-scatter.25.cloned.1.call-start = ((), (), s32[]{:S(2)}) async-start(), calls=%async_computation.16 | async-start | bytes 737280
  494.5 37.1 %copy-start.18 = (bf16[1024,768]{0,1:T(8,128)(2,1)S(1)}, bf16[1024,768]{0,1:T(8,128)(2,1)}, u32[]{:S(2)}) copy-start(bf16[1024,768]{0,1:T(8,128)(2,1)} %copy.138) | copy-start | bytes 4718596
  531.3 266.8 %reduce-scatter.31.cloned.1.call-start = ((), (), s32[]{:S(2)}) async-start(), calls=%async_computation.19 | async-start | bytes 737280
  543.7 88.9 %copy-start.40 = (f32[1024]{0:T(1024)S(1)}, f32[1024]{0:T(1024)}, u32[]{:S(2)}) copy-start(f32[1024]{0:T(1024)} %copy-done.39) | copy-start | bytes 12292
  629.9 192.7 %reduce-scatter.21.cloned.1.call-start = ((), (), s32[]{:S(2)}) async-start(), calls=%async_computation.14 | async-start | bytes 737280 | tf_op jit(solution)/shard_map/reduce_scatter | solution.py:231
  632.8 95.8 %copy-start.9 = (bf16[1024,768]{0,1:T(8,128)(2,1)S(1)}, bf16[1024,768]{0,1:T(8,128)(2,1)}, u32[]{:S(2)}) copy-start(bf16[1024,768]{0,1:T(8,128)(2,1)} %copy.124) | copy-start | bytes 4718596
  632.8 95.8 %copy-start.38 = (f32[1024]{0:T(1024)S(1)}, f32[1024]{0:T(1024)}, u32[]{:S(2)}) copy-start(f32[1024]{0:T(1024)} %copy-done.37) | copy-start | bytes 12292
  (40 other events, 148.6 us)
Sparse Core Ops, SparseCore 0:
  18.4 66.5 all-gather.5
  87.8 39.5 all-gather.7
  129.5 79.7 all-gather.9
  211.2 79.1 all-gather.11
  373.0 62.2 reduce-scatter.18
  451.7 77.4 reduce-scatter.16
  532.8 94.8 reduce-scatter.22
  631.4 94.9 reduce-scatter.28
  729.5 19.5 reduce-scatter.26
  751.4 22.0 reduce-scatter.24
  776.0 22.0 reduce-scatter.30
  800.5 22.0 reduce-scatter.20
where the time goes:
time: 841 us; the launch traced here: 831 us
  waiting for transfers between devices  305 us (36%)
  matrix products  208 us (25%)
  local copies, waits for them, and re-layouts  118 us (14%)
  blocking collectives  110 us (13%)
  other arithmetic  71.1 us (8%)
  between operations  18.4 us (2%)
    unnamed x16, waiting for transfers between devices  104 us
    reduce_scatter x1, waiting for transfers between devices, per_device(): lax.psum_scatter(d_down.astype(jnp.bfloat16), 'wide', scatter_dimension=0...  84.1 us
    unnamed x157, local copies, waits for them, and re-layouts  50.7 us
    unnamed x3, blocking collectives  48.2 us
    all_gather x1, waiting for transfers between devices, per_device(): lax.all_gather(halves[3], 'wide', axis=0, tiled=True)  43 us
    dot_general x1, matrix products, per_device(): jnp.dot(hidden_two, up_full, preferred_element_type=jnp.float32) + bias_up  38.1 us
    dot_general x4, matrix products, contract_cols(): lax.dot_general(left, right, (((1,), (1,)), ((), ())), preferred_element_...  38.1 us
    reduce_scatter x1, waiting for transfers between devices, per_device(): lax.psum_scatter(d_qkv.astype(jnp.bfloat16), 'wide', scatter_dimension=1,...  32 us
  transfers between devices with their start and end apart: 12, of which 7 were waited for; matrix products, arithmetic and copies ran while one was open for 37% of the time, Pallas kernels for 0%

commit v1 on v0

--- a/solution.py
+++ b/solution.py
@@ -1,6 +1,8 @@
 import jax
 import jax.numpy as jnp
 from jax import lax
+from jax.experimental import pallas as pl
+from jax.experimental.pallas import tpu as pltpu
 from jax.sharding import PartitionSpec as P
 
 HEADS = 12
@@ -71,24 +73,249 @@
     return (middle + before + after).reshape(blocks * block_rows, width)
 
 
+BF = jnp.bfloat16
+F32 = jnp.float32
+AXES = ("wide", "narrow")
+
+
+class Topo:
+    def __init__(self, wide, narrow):
+        self.wide, self.narrow = wide, narrow
+        self.Y = narrow // 2
+        self.X = self.Y
+        self.Z = wide // self.X
+        side, deep = self.X, self.Z
+        self.zp = [self.perm(lambda z, x, y, c, k=k: ((z + k) % deep, x, y, c)) for k in range(deep)]
+        self.ap = [
+            self.perm(
+                lambda z, x, y, c, k=k: (z, (x + k) % side, y, c) if c == 0 else (z, x, (y + k) % side, c)
+            )
+            for k in range(side)
+        ]
+        self.bp = [
+            self.perm(
+                lambda z, x, y, c, k=k: (z, x, (y + k) % side, c) if c == 0 else (z, (x + k) % side, y, c)
+            )
+            for k in range(side)
+        ]
+        self.cp = self.perm(lambda z, x, y, c: (z, x, y, 1 - c))
+
+    def did(self, z, x, y, c):
+        return ((z * self.X + x) * self.Y + y) * 2 + c
+
+    def perm(self, target):
+        return [
+            (self.did(z, x, y, c), self.did(*target(z, x, y, c)))
+            for z in range(self.Z)
+            for x in range(self.X)
+            for y in range(self.Y)
+            for c in range(2)
+        ]
+
+    def here(self):
+        wide, narrow = lax.axis_index("wide"), lax.axis_index("narrow")
+        return wide // self.X, wide % self.X, narrow // 2, narrow % 2
+
+    def origins(self):
+        z0, x0, y0, c0 = self.here()
+        rows = []
+        for other in range(2):
+            c = (c0 + other) % 2
+            for kb in range(self.X):
+                for ka in range(self.X):
+                    x = (x0 + self.X - jnp.where(c == 0, ka, kb)) % self.X
+                    y = (y0 + self.Y - jnp.where(c == 0, kb, ka)) % self.Y
+                    for kz in range(self.Z):
+                        z = (z0 + self.Z - kz) % self.Z
+                        rows.append(jnp.stack([z * self.X + x, y, c]))
+        return jnp.stack(rows).astype(jnp.int32)
+
+
+def send(values, perm):
+    return lax.ppermute(values, AXES, perm)
+
+
+def pick_half(values, axis, index):
+    half = values.shape[axis] // 2
+    return lax.dynamic_slice_in_dim(values, index * half, half, axis)
+
+
+def pair_up(shard, topo, core):
+    mine = pick_half(shard, 0, core)
+    other = send(pick_half(shard, 0, 1 - core), topo.cp)
+    first = jnp.where(core == 0, mine, other)
+    second = jnp.where(core == 0, other, mine)
+    return jnp.concatenate([first, second], axis=1)
+
+
+def unpair(piece, topo, core):
+    mine = pick_half(piece, 1, core)
+    other = send(pick_half(piece, 1, 1 - core), topo.cp)
+    first = jnp.where(core == 0, mine, other)
+    second = jnp.where(core == 0, other, mine)
+    return jnp.concatenate([first, second], axis=0)
+
+
+def gather(piece, topo):
+    stack = jnp.stack([piece] + [send(piece, topo.zp[k]) for k in range(1, topo.Z)])
+    line = [stack] + [send(stack, topo.ap[k]) for k in range(1, topo.X)]
+    own = [p for k in range(topo.X) for p in (line if k == 0 else [send(q, topo.bp[k]) for q in line])]
+    return own + [send(p, topo.cp) for p in own]
+
+
+def total(first, *rest):
+    result = first.astype(F32)
+    for other in rest:
+        result = result + other.astype(F32)
+    return result
+
+
+def scatter(pieces, topo):
+    side, deep = topo.X, topo.Z
+    half = side * side
+    own = [total(pieces[i], send(pieces[half + i], topo.cp)).astype(BF) for i in range(half)]
+    line = [
+        total(own[a], *[send(own[k * side + a], topo.bp[side - k]) for k in range(1, side)]).astype(BF)
+        for a in range(side)
+    ]
+    stack = total(line[0], *[send(line[k], topo.ap[side - k]) for k in range(1, side)]).astype(BF)
+    return total(stack[0], *[send(stack[k], topo.zp[deep - k]) for k in range(1, deep)])
+
+
+def dma_call(kernel, out_shape, operands, n):
+    return pl.pallas_call(
+        kernel,
+        grid_spec=pltpu.PrefetchScalarGridSpec(
+            num_scalar_prefetch=1,
+            grid=(1,),
+            in_specs=[pl.BlockSpec(memory_space=pl.ANY)] * (len(operands) - 1),
+            out_specs=jax.tree.map(lambda _: pl.BlockSpec(memory_space=pl.ANY), out_shape),
+            scratch_shapes=[pltpu.SemaphoreType.DMA((n,))],
+        ),
+        out_shape=out_shape,
+    )(*operands)
+
+
+def assemble(pieces, places, low, rows, topo):
+    deep, lanes = topo.Z, pieces[0].shape[2]
+
+    def kernel(at, *refs):
+        out, sems = refs[-2], refs[-1]
+        copies = []
+        for i in range(len(pieces)):
+            for k in range(deep):
+                j = i * deep + k
+                row = pl.multiple_of((at[j, 0] * 2 + at[j, 2]) * rows, 16)
+                lane = pl.multiple_of(at[j, 1] * lanes, 128)
+                copy = pltpu.make_async_copy(
+                    refs[i].at[k, pl.ds(low, rows), :],
+                    out.at[pl.ds(row, rows), pl.ds(lane, lanes)],
+                    sems.at[j],
+                )
+                copy.start()
+                copies.append(copy)
+        for copy in copies:
+            copy.wait()
+
+    shape = jax.ShapeDtypeStruct((topo.wide * 2 * rows, topo.Y * lanes), pieces[0].dtype)
+    return dma_call(kernel, shape, (places, *pieces), len(pieces) * deep)
+
+
+def disassemble(whole, places, topo):
+    deep, rows, lanes = topo.Z, whole.shape[0] // (2 * topo.wide), whole.shape[1] // topo.Y
+    count = 2 * topo.X * topo.X
+
+    def kernel(at, src, *refs):
+        outs, sems = refs[:-1], refs[-1]
+        copies = []
+        for i in range(count):
+            for k in range(deep):
+                j = i * deep + k
+                row = pl.multiple_of((at[j, 0] * 2 + at[j, 2]) * rows, 16)
+                lane = pl.multiple_of(at[j, 1] * lanes, 128)
+                copy = pltpu.make_async_copy(
+                    src.at[pl.ds(row, rows), pl.ds(lane, lanes)], outs[i].at[k], sems.at[j]
+                )
+                copy.start()
+                copies.append(copy)
+        for copy in copies:
+            copy.wait()
+
+    shapes = [jax.ShapeDtypeStruct((deep, rows, lanes), whole.dtype)] * count
+    return dma_call(kernel, shapes, (places, whole), count * deep)
+
+
+def tail_rows(values, rows, lanes):
+    return jnp.pad(values[None], ((0, 15), (0, lanes - values.shape[0])))
+
+
+def vector_slots(places, topo):
+    slot = places[:, 0] * topo.narrow + places[:, 1] * 2 + places[:, 2]
+    return (slot[:, None] == jnp.arange(topo.wide * topo.narrow)[None]).astype(BF)
+
+
+def fits(topo, width, hidden):
+    lanes = 2 * width // topo.narrow
+    return lanes % 128 == 0 and (width // topo.wide) % 32 == 0 and (hidden // topo.wide) % 32 == 0
+
+
+def gather_weights(qkv_weight, out_weight, up_weight, down_weight, vectors, topo, places):
+    shards = [
+        qkv_weight.astype(BF).T,
+        out_weight.astype(BF),
+        up_weight.astype(BF).T,
+        down_weight.astype(BF),
+    ]
+    if places is None:
+        wholes = [
+            lax.all_gather(lax.all_gather(s, "narrow", axis=1, tiled=True), "wide", axis=0, tiled=True)
+            for s in shards
+        ]
+        return (*wholes, lax.all_gather(vectors.astype(BF), AXES, axis=0, tiled=True))
+    core = topo.here()[3]
+    first = pair_up(shards[0], topo, core)
+    rest = pair_up(
+        jnp.concatenate(
+            [pick_half(s, 0, h) for h in range(2) for s in shards[1:]], axis=0
+        ),
+        topo,
+        core,
+    )
+    rows = [s.shape[0] // 2 for s in shards]
+    lanes = first.shape[1]
+    one = gather(jnp.concatenate([first, tail_rows(vectors.astype(BF), 16, lanes)], axis=0), topo)
+    two = gather(rest[: rows[1] + rows[2]], topo)
+    three = gather(rest[rows[1] + rows[2] :], topo)
+    packed = jnp.concatenate([p[:, rows[0], : vectors.shape[0]] for p in one], axis=0)
+    ordered = lax.dot_general(
+        vector_slots(places, topo), packed, (((0,), (0,)), ((), ())), preferred_element_type=F32
+    )
+    return (
+        assemble(one, places, 0, rows[0], topo),
+        assemble(two, places, 0, rows[1], topo),
+        assemble(two, places, rows[1], rows[2], topo),
+        assemble(three, places, 0, rows[3], topo),
+        ordered.reshape(-1).astype(BF),
+    )
+
+
+def reduce_grad(whole, topo, places, extra=None):
+    if places is None:
+        part = lax.psum_scatter(whole.astype(BF), "wide", scatter_dimension=0, tiled=True)
+        return lax.psum_scatter(part, "narrow", scatter_dimension=1, tiled=True).astype(F32)
+    pieces = disassemble(whole.astype(BF), places, topo)
+    if extra is not None:
+        pieces = [jnp.concatenate([p, e], axis=1) for p, e in zip(pieces, extra)]
+    return scatter(pieces, topo)
+
 def per_device(
     tokens, qkv_weight, out_weight, up_weight, down_weight, vectors, bucket_counts, cotangent
 ):
     rows, width = tokens.shape
-    halves = (
-        lax.all_gather(qkv_weight.astype(jnp.bfloat16), "narrow", axis=0, tiled=True),
-        lax.all_gather(out_weight.astype(jnp.bfloat16), "narrow", axis=1, tiled=True),
-        lax.all_gather(up_weight.astype(jnp.bfloat16), "narrow", axis=0, tiled=True),
-        lax.all_gather(down_weight.astype(jnp.bfloat16), "narrow", axis=1, tiled=True),
-        lax.all_gather(vectors.astype(jnp.bfloat16), "narrow", axis=0, tiled=True),
-    )
-    wholes = (
-        lax.all_gather(halves[0], "wide", axis=1, tiled=True),
-        lax.all_gather(halves[1], "wide", axis=0, tiled=True),
-        lax.all_gather(halves[2], "wide", axis=1, tiled=True),
-        lax.all_gather(halves[3], "wide", axis=0, tiled=True),
-        lax.all_gather(halves[4], "wide", axis=0, tiled=True),
-    )
+    topo = Topo(lax.axis_size("wide"), lax.axis_size("narrow"))
+    places = topo.origins() if fits(topo, width, up_weight.shape[1] * topo.wide) else None
+    core = topo.here()[3]
+    wholes = gather_weights(qkv_weight, out_weight, up_weight, down_weight, vectors, topo, places)
     qkv_full, out_full, up_full, down_full, packed = wholes
     params = packed.astype(jnp.float32)
     gain_one = params[0:width]
@@ -103,7 +330,7 @@
     inputs = tokens.astype(jnp.float32)
     hidden_one = layer_norm(inputs, gain_one, shift_one).astype(jnp.bfloat16)
     qkv_bias = jnp.concatenate([bias_query, jnp.zeros((width,), jnp.float32), bias_value])
-    qkv_all = (jnp.dot(hidden_one, qkv_full, preferred_element_type=jnp.float32) + qkv_bias).astype(
+    qkv_all = (contract_cols(hidden_one, qkv_full) + qkv_bias).astype(
         jnp.bfloat16
     )
     margin = P_THREE
@@ -137,7 +364,7 @@
     attn_low = attended.reshape(rows, width).astype(jnp.bfloat16)
     mid = inputs + jnp.dot(attn_low, out_full, preferred_element_type=jnp.float32) + bias_out
     hidden_two = layer_norm(mid, gain_two, shift_two).astype(jnp.bfloat16)
-    pre_act = jnp.dot(hidden_two, up_full, preferred_element_type=jnp.float32) + bias_up
+    pre_act = contract_cols(hidden_two, up_full) + bias_up
     activated = gelu_exact(pre_act).astype(jnp.bfloat16)
     output = mid + jnp.dot(activated, down_full, preferred_element_type=jnp.float32) + bias_down
     block_out = output.astype(jnp.bfloat16)
@@ -147,9 +374,9 @@
     grad_act = contract_cols(cotangent, down_full)
     unused_act, gelu_back = jax.vjp(gelu_exact, pre_act)
     grad_pre = gelu_back(grad_act)[0].astype(jnp.bfloat16)
-    d_up = contract_rows(hidden_two, grad_pre)
+    d_up = contract_rows(grad_pre, hidden_two)
     d_bias_up = jnp.sum(grad_pre.astype(jnp.float32), axis=0)
-    grad_hidden_two = contract_cols(grad_pre, up_full)
+    grad_hidden_two = jnp.dot(grad_pre, up_full, preferred_element_type=F32)
     unused_two, norm_back_two = jax.vjp(layer_norm, mid, gain_two, shift_two)
     grad_mid_part, d_gain_two, d_shift_two = norm_back_two(grad_hidden_two)
     grad_mid = grad_top + grad_mid_part
@@ -185,9 +412,9 @@
     grad_qkv = jnp.concatenate(
         [grad_query.reshape(rows, width), grad_keys, grad_values], axis=1
     ).astype(jnp.bfloat16)
-    d_qkv = contract_rows(hidden_one, grad_qkv)
+    d_qkv = contract_rows(grad_qkv, hidden_one)
     column_sums = jnp.sum(grad_qkv.astype(jnp.float32), axis=0)
-    grad_hidden_one = contract_cols(grad_qkv, qkv_full)
+    grad_hidden_one = jnp.dot(grad_qkv, qkv_full, preferred_element_type=F32)
     unused_one, norm_back_one = jax.vjp(layer_norm, inputs, gain_one, shift_one)
     grad_in_part, d_gain_one, d_shift_one = norm_back_one(grad_hidden_one)
     input_grad = (grad_mid + grad_in_part).astype(jnp.bfloat16)
@@ -204,41 +431,25 @@
             d_bias_up,
         ]
     )
-    partial_sums = (
-        lax.psum_scatter(
-            d_qkv.astype(jnp.bfloat16), "wide", scatter_dimension=1, tiled=True
-        ).astype(jnp.float32),
-        lax.psum_scatter(
-            d_out.astype(jnp.bfloat16), "wide", scatter_dimension=0, tiled=True
-        ).astype(jnp.float32),
-        lax.psum_scatter(d_up.astype(jnp.bfloat16), "wide", scatter_dimension=1, tiled=True).astype(
-            jnp.float32
-        ),
-        lax.psum_scatter(
-            d_down.astype(jnp.bfloat16), "wide", scatter_dimension=0, tiled=True
-        ).astype(jnp.float32),
-        lax.psum_scatter(
-            d_vector.astype(jnp.bfloat16), "wide", scatter_dimension=0, tiled=True
-        ).astype(jnp.float32),
-    )
-    final = (
-        lax.psum_scatter(
-            partial_sums[0].astype(jnp.bfloat16), "narrow", scatter_dimension=0, tiled=True
-        ).astype(jnp.float32),
-        lax.psum_scatter(
-            partial_sums[1].astype(jnp.bfloat16), "narrow", scatter_dimension=1, tiled=True
-        ).astype(jnp.float32),
-        lax.psum_scatter(
-            partial_sums[2].astype(jnp.bfloat16), "narrow", scatter_dimension=0, tiled=True
-        ).astype(jnp.float32),
-        lax.psum_scatter(
-            partial_sums[3].astype(jnp.bfloat16), "narrow", scatter_dimension=1, tiled=True
-        ).astype(jnp.float32),
-        lax.psum_scatter(
-            partial_sums[4].astype(jnp.bfloat16), "narrow", scatter_dimension=0, tiled=True
-        ).astype(jnp.float32),
-    )
-    return (block_out, input_grad, final[0], final[1], final[2], final[3], final[4])
+    if places is None:
+        grads = [reduce_grad(g, topo, None) for g in (d_qkv, d_out, d_up, d_down)]
+        vector_grad = lax.psum_scatter(d_vector.astype(BF), AXES, scatter_dimension=0, tiled=True).astype(F32)
+    else:
+        lanes = topo.Y * 0 + 2 * width // topo.narrow
+        rel = jnp.dot(
+            vector_slots(places, topo),
+            d_vector.astype(BF).reshape(topo.wide * topo.narrow, -1),
+            preferred_element_type=F32,
+        ).astype(BF)
+        rel = jnp.pad(rel[:, None, :], ((0, 0), (0, 15), (0, lanes - rel.shape[1])))
+        extra = [rel[i : i + topo.Z] for i in range(0, rel.shape[0], topo.Z)]
+        down_sum = reduce_grad(d_down, topo, places)
+        up_sum = reduce_grad(d_up, topo, places)
+        out_sum = reduce_grad(d_out, topo, places)
+        qkv_sum = reduce_grad(d_qkv, topo, places, extra)
+        vector_grad = qkv_sum[-16, : vectors.shape[0]]
+        grads = [unpair(g, topo, core) for g in (qkv_sum[:-16], out_sum, up_sum, down_sum)]
+    return (block_out, input_grad, grads[0].T, grads[1], grads[2].T, grads[3], vector_grad)
 
 
 def solution(mesh):

time: 841 us -> 1450 us (1.72)
  Pallas kernels: 0 us -> 876 us
  waiting for transfers between devices: 305 us -> 75.1 us
  blocking collectives: 110 us -> 0 us
  starting transfers between devices: 0.67 us -> 70.9 us
  other arithmetic: 71.1 us -> 106 us
    pallas_call x0 -> x8, Pallas kernels: none -> 876 us  [dma_call(): pl.pallas_call(kernel, grid_spec=pltpu.PrefetchScalarGridSpec(num_scalar_...]
    reduce_scatter x4 -> x0, waiting for transfers between devices: 139 us -> none  [the longest x1 84.1 us: per_device(): lax.psum_scatter(d_down.astype(jnp.bfloat16), 'wide', scatter_dimension=0...]
    unnamed x16 -> x0, waiting for transfers between devices: 104 us -> none
    ppermute x0 -> x76, waiting for transfers between devices: none -> 75.1 us  [send(): return lax.ppermute(values, AXES, perm)]
    ppermute x0 -> x76, starting transfers between devices: none -> 70.9 us  [send(): return lax.ppermute(values, AXES, perm)]
    all_gather x5 -> x0, blocking collectives: 62.1 us -> none  [the longest x1 31.3 us: per_device(): lax.all_gather(halves[4], 'wide', axis=0, tiled=True)]
    all_gather x4 -> x0, waiting for transfers between devices: 61.6 us -> none  [the longest x1 43 us: per_device(): lax.all_gather(halves[3], 'wide', axis=0, tiled=True)]
    unnamed x3 -> x0, blocking collectives: 48.2 us -> none
  transfers between devices with their start and end apart: 12 -> 76, of which waited for: 7 -> 22; matrix products, arithmetic and copies ran while one was open for 37% -> 12% of each run, Pallas kernels for 0% -> 38%
where the time goes in v1:
time: 1450 us; the launch traced here: 1440 us
  Pallas kernels  876 us (60%)
  matrix products  198 us (14%)
  local copies, waits for them, and re-layouts  109 us (8%)
  other arithmetic  106 us (7%)
  waiting for transfers between devices  75.1 us (5%)
  starting transfers between devices  70.9 us (5%)
    pallas_call x8, Pallas kernels, dma_call(): pl.pallas_call(kernel, grid_spec=pltpu.PrefetchScalarGridSpec(num_scalar_...  876 us
    ppermute x76, waiting for transfers between devices, send(): return lax.ppermute(values, AXES, perm)  75.1 us
    ppermute x76, starting transfers between devices, send(): return lax.ppermute(values, AXES, perm)  70.9 us
    dot_general x4, matrix products, contract_cols(): lax.dot_general(left, right, (((1,), (1,)), ((), ())), preferred_element_...  63.6 us
    unnamed x236, local copies, waits for them, and re-layouts  30.9 us
  transfers between devices with their start and end apart: 76, of which 22 were waited for; matrix products, arithmetic and copies ran while one was open for 12% of the time, Pallas kernels for 38%

profile of v1, /device:TPU:0, one launch (start us, length us, event | category | flops | bytes accessed | tf_op | source)
XLA Modules:
  0.0 1439.0 jit_solution(6884084455525886259)
XLA Ops:
  64.2 7.6 collective-permute-start.13
  101.0 109.5 %shard_map.135 = bf16[2304,768]{1,0:T(8,128)(2,1)} custom-call(s32[32,3]{1,0:T(8,128)} %copy-done.27, bf16[4,160,384]{2,1,0:T(8,128)(2,1)} %pad_maximum_fusion.9.refs_0_, bf16[4,160,384]{2,1,0:T(8,128)(2,1)} %collective-permute-done.4.refs_1_, bf16[4,160,384]{2,1,0:T(8,128)(2,1)} %collective-permute-done.5.refs_2_, ...), custom_call_target="tpu_custom_call" | custom-call | tf_op jit(solution)/shard_map/pallas_call | solution.py:186
  210.6 6.7 add_convert_fusion
  245.2 17.1 %fusion.85 = (f32[2,12,512]{2,1,0:T(8,128)S(1)}, f32[2,12,512,640]{3,2,1,0:T(8,128)}) fusion(bf16[2,64,12,64]{1,3,2,0:T(8,128)(2,1)S(1)} %bitcast.293, bf16[2,512,12,64]{1,3,2,0:T(8,128)(2,1)} %copy.523, bf16[2,64,12,64]{1,3,2,0:T(8,128)(2,1)} %bitcast.295, bf16[2,512,12,64]{1,0,3,2:T(2,128)(2,1)} %reshape.219, pred[2,512,640]{2,1,0:T(8,128)(4,1)} %broadcast_compare_fusion), kind=kOutput, calls=%fused_computation.303 | convolution fusion | flops 1036111872 | bytes 35700736 | tf_op jit(solution)/shard_map/bqhd,bkhd->bhqk/dot_general | solution.py:352
  265.0 14.3 fusion
  290.2 14.0 fusion.34
  308.8 145.3 %shard_map.138 = bf16[3072,768]{1,0:T(8,128)(2,1)} custom-call(s32[32,3]{1,0:T(8,128)} %copy-done.27, bf16[4,192,384]{2,1,0:T(8,128)(2,1)} %pad_maximum_fusion.8.refs_0_, bf16[4,192,384]{2,1,0:T(8,128)(2,1)} %collective-permute-done.25.refs_1_, bf16[4,192,384]{2,1,0:T(8,128)(2,1)} %collective-permute-done.26.refs_2_, ...), custom_call_target="tpu_custom_call" | custom-call | tf_op jit(solution)/shard_map/pallas_call | solution.py:186
  455.2 38.1 %shard_map.136 = bf16[768,768]{1,0:T(8,128)(2,1)} custom-call(s32[32,3]{1,0:T(8,128)} %copy-done.27, bf16[4,240,384]{2,1,0:T(8,128)(2,1)} %pad_maximum_fusion.3.refs_0_, bf16[4,240,384]{2,1,0:T(8,128)(2,1)} %collective-permute-done.15.refs_1_, bf16[4,240,384]{2,1,0:T(8,128)(2,1)} %collective-permute-done.16.refs_2_, ...), custom_call_target="tpu_custom_call" | custom-call | tf_op jit(solution)/shard_map/pallas_call | solution.py:186
  498.7 145.4 %shard_map.137 = bf16[3072,768]{1,0:T(8,128)(2,1)} custom-call(s32[32,3]{1,0:T(8,128)} %copy-done.27, bf16[4,240,384]{2,1,0:T(8,128)(2,1)} %pad_maximum_fusion.3.refs_0_, bf16[4,240,384]{2,1,0:T(8,128)(2,1)} %collective-permute-done.15.refs_1_, bf16[4,240,384]{2,1,0:T(8,128)(2,1)} %collective-permute-done.16.refs_2_, ...), custom_call_target="tpu_custom_call" | custom-call | tf_op jit(solution)/shard_map/pallas_call | solution.py:186
  644.1 37.7 %multiply_convert_fusion.1 = (bf16[1024,3072]{1,0:T(8,128)(2,1)}, f32[1024,3072]{1,0:T(8,128)}, f32[1024,3072]{1,0:T(8,128)}) fusion(f32[3072]{0:T(1024)S(1)} %slice.328, bf16[3072,768]{1,0:T(8,128)(2,1)} %shard_map.137, f32[1024,768]{0,1:T(8,128)S(1)} %copy-done.4, f32[768]{0:T(1024)S(1)} %copy-done.82, f32[768]{0:T(1024)S(1)} %get-tuple-element.210, ...), kind=kOutput, calls=%fused_computation.22 | convolution fusion | flops 5043388416 | bytes 39348224 | tf_op jit(solution)/shard_map/dot_general | solution.py:47
  681.8 17.8 %fusion.89 = (bf16[3072]{0:T(1024)(128)(2,1)}, bf16[1024,3072]{1,0:T(8,128)(2,1)}) fusion(f32[1024,3072]{1,0:T(8,128)} %get-tuple-element.164, bf16[3072,768]{1,0:T(8,128)(2,1)} %shard_map.138, bf16[1024,768]{1,0:T(8,128)(2,1)S(1)} %copy-done.16, f32[1024,3072]{1,0:T(8,128)} %get-tuple-element.226, f32[3072]{0:T(1024)S(1)} %slice.328), kind=kOutput, calls=%fused_computation.307 | convolution fusion | flops 4882166784 | bytes 37767168 | tf_op jit(solution)/shard_map/dot_general | solution.py:47
  699.6 9.5 fusion.88
  709.1 7.4 convolution_convert_fusion.1.src
  733.3 12.1 fusion.2
  748.9 22.1 %multiply_reduce_fusion = (f32[2,12,512]{2,1,0:T(8,128)S(1)}, f32[2,12,512,640]{3,2,1,0:T(8,128)}) fusion(f32[2,12,512,640]{3,2,1,0:T(8,128)} %get-tuple-element.223, f32[2,12,512]{2,1,0:T(8,128)S(1)} %copy-done.26, bf16[2,64,12,64]{1,3,2,0:T(8,128)(2,1)S(1)} %bitcast.288, bf16[2,512,12,64]{1,3,2,0:T(8,128)(2,1)S(1)} %copy-done.14, ...), kind=kOutput, calls=%fused_computation.1 | convolution fusion | flops 1036111872 | bytes 66551808 | tf_op jit(solution)/shard_map/bqhd,bkhd->bhqk/dot_general | solution.py:393
  771.0 26.4 %multiply_convert_fusion = bf16[2,12,512,640]{3,2,1,0:T(8,128)(2,1)} fusion(f32[2,12,512,640]{3,2,1,0:T(8,128)} %get-tuple-element.228, f32[2,12,512,640]{3,2,1,0:T(8,128)} %get-tuple-element.223, f32[2,12,512]{2,1,0:T(8,128)S(1)} %get-tuple-element.227, f32[2,12,512]{2,1,0:T(8,128)S(1)} %copy-done.26), kind=kLoop, calls=%fused_computation | loop fusion | flops 31457280 | bytes 78741504 | tf_op jit(solution)/shard_map/convert_element_type | solution.py:398
  797.4 12.0 fusion.33
  809.4 6.8 convolution_multiply_fusion
  843.3 8.3 fusion.87
  853.1 6.0 convolution_convert_fusion.2.src
  859.1 7.4 convolution_convert_fusion.src
  866.5 5.5 add_convert_fusion.4
  873.6 145.3 %shard_map.142 = (bf16[4,192,384]{2,1,0:T(8,128)(2,1)}, bf16[4,192,384]{2,1,0:T(8,128)(2,1)}, bf16[4,192,384]{2,1,0:T(8,128)(2,1)}, bf16[4,192,384]{2,1,0:T(8,12...) custom-call(s32[32,3]{1,0:T(8,128)} %copy-done.27, ...), custom_call_target="tpu_custom_call" | custom-call | tf_op jit(solution)/shard_map/pallas_call | solution.py:186
  1019.3 38.1 %shard_map.140 = (bf16[4,48,384]{2,1,0:T(8,128)(2,1)}, bf16[4,48,384]{2,1,0:T(8,128)(2,1)}, bf16[4,48,384]{2,1,0:T(8,128)(2,1)}, bf16[4,48,384]{2,1,0:T(8,128)(2...) custom-call(s32[32,3]{1,0:T(8,128)} %copy-done.27, ...), custom_call_target="tpu_custom_call" | custom-call | tf_op jit(solution)/shard_map/pallas_call | solution.py:186
  1071.1 109.7 %shard_map.139 = (bf16[4,144,384]{2,1,0:T(8,128)(2,1)}, bf16[4,144,384]{2,1,0:T(8,128)(2,1)}, bf16[4,144,384]{2,1,0:T(8,128)(2,1)}, bf16[4,144,384]{2,1,0:T(8,12...) custom-call(s32[32,3]{1,0:T(8,128)} %copy-done.27, ...), custom_call_target="tpu_custom_call" | custom-call | tf_op jit(solution)/shard_map/pallas_call | solution.py:186
  1199.1 145.3 %shard_map.141 = (bf16[4,192,384]{2,1,0:T(8,128)(2,1)}, bf16[4,192,384]{2,1,0:T(8,128)(2,1)}, bf16[4,192,384]{2,1,0:T(8,128)(2,1)}, bf16[4,192,384]{2,1,0:T(8,12...) custom-call(s32[32,3]{1,0:T(8,128)} %copy-done.27, ...), custom_call_target="tpu_custom_call" | custom-call | tf_op jit(solution)/shard_map/pallas_call | solution.py:186
  1356.3 6.3 collective-permute-done.37
  1365.2 6.5 collective-permute-done.70
  1400.5 5.5 collective-permute-done.67
  1411.9 6.5 collective-permute-done.56
  1424.9 5.1 collective-permute-done.61
  1430.7 5.4 collective-permute-done.62
  (548 shorter events, 284.8 us)
Async XLA Ops:
  6.4 33.3 %collective-permute-start.11 = (bf16[432,192]{1,0:T(8,128)(2,1)}, bf16[432,192]{1,0:T(8,128)(2,1)}, u32[]{:S(2)}, u32[]{:S(2)}) collective-permute-start(bf16[432,192]{1,0:T(8,128)(2,1)} %constant_dynamic-slice_fusion.4), channel_id=1, source_target_pairs={{0,1},{1,0},{2,3},{3,2},{4,5},{5,4},{6,7},{7,6},{8,9},{9,8},{10,11... | collective-permute-start | bytes 497672 | tf_op jit(solution)/shard_map/ppermute | solution.py:135
  40.9 39.7 %collective-permute-start.5 = (bf16[4,160,384]{2,1,0:T(8,128)(2,1)}, bf16[4,160,384]{2,1,0:T(8,128)(2,1)}, u32[]{:S(2)}, u32[]{:S(2)}) collective-permute-start(bf16[4,160,384]{2,1,0:T(8,128)(2,1)} %pad_maximum_fusion.9.refs_0_), channel_id=1, source_target_pairs={{0,2},{1,5},{2,0},{3,7},{4,6},{5,1},{6,4},{7,3},{8,10},{9,13},{10,... | collective-permute-start | bytes 1474568 | tf_op jit(solution)/shard_map/ppermute | solution.py:135
  47.0 33.5 %collective-permute-start.6 = (bf16[4,160,384]{2,1,0:T(8,128)(2,1)}, bf16[4,160,384]{2,1,0:T(8,128)(2,1)}, u32[]{:S(2)}, u32[]{:S(2)}) collective-permute-start(bf16[4,160,384]{2,1,0:T(8,128)(2,1)} %collective-permute-done.4.refs_1_), channel_id=1, source_target_pairs={{0,2},{1,5},{2,0},{3,7},{4,6},{5,1},{6,4},{7,3},{8,10},{9,13},{10,... | collective-permute-start | bytes 1474568 | tf_op jit(solution)/shard_map/ppermute | solution.py:135
  52.5 19.3 %collective-permute-start.24 = (bf16[192,384]{1,0:T(8,128)(2,1)}, bf16[192,384]{1,0:T(8,128)(2,1)}, u32[]{:S(2)}, u32[]{:S(2)}) collective-permute-start(bf16[192,384]{1,0:T(8,128)(2,1)} %pad_maximum_fusion.15), channel_id=1, source_target_pairs={{0,24},{1,25},{2,26},{3,27},{4,28},{5,29},{6,30},{7,31},{8,0},{9,1... | collective-permute-start | bytes 442376 | tf_op jit(solution)/shard_map/ppermute | solution.py:135
  77.3 20.9 %collective-permute-start.25 = (bf16[4,192,384]{2,1,0:T(8,128)(2,1)}, bf16[4,192,384]{2,1,0:T(8,128)(2,1)}, u32[]{:S(2)}, u32[]{:S(2)}) collective-permute-start(bf16[4,192,384]{2,1,0:T(8,128)(2,1)} %pad_maximum_fusion.8.refs_0_), channel_id=1, source_target_pairs={{0,4},{1,3},{2,6},{3,1},{4,0},{5,7},{6,2},{7,5},{8,12},{9,11},{10,... | collective-permute-start | bytes 1769480 | tf_op jit(solution)/shard_map/ppermute | solution.py:135
  91.4 170.9 %collective-permute-start.28 = (bf16[4,192,384]{2,1,0:T(8,128)(2,1)}, bf16[4,192,384]{2,1,0:T(8,128)(2,1)}, u32[]{:S(2)}, u32[]{:S(2)}) collective-permute-start(bf16[4,192,384]{2,1,0:T(8,128)(2,1)} %pad_maximum_fusion.8.refs_0_), channel_id=1, source_target_pairs={{0,1},{1,0},{2,3},{3,2},{4,5},{5,4},{6,7},{7,6},{8,9},{9,8},{10,11... | collective-permute-start | bytes 1769480 | tf_op jit(solution)/shard_map/ppermute | solution.py:135
  93.7 170.4 %collective-permute-start.26 = (bf16[4,192,384]{2,1,0:T(8,128)(2,1)}, bf16[4,192,384]{2,1,0:T(8,128)(2,1)}, u32[]{:S(2)}, u32[]{:S(2)}) collective-permute-start(bf16[4,192,384]{2,1,0:T(8,128)(2,1)} %pad_maximum_fusion.8.refs_0_), channel_id=1, source_target_pairs={{0,2},{1,5},{2,0},{3,7},{4,6},{5,1},{6,4},{7,3},{8,10},{9,13},{10,... | collective-permute-start | bytes 1769480 | tf_op jit(solution)/shard_map/ppermute | solution.py:135
  95.8 193.3 %collective-permute-start.16 = (bf16[4,240,384]{2,1,0:T(8,128)(2,1)}, bf16[4,240,384]{2,1,0:T(8,128)(2,1)}, u32[]{:S(2)}, u32[]{:S(2)}) collective-permute-start(bf16[4,240,384]{2,1,0:T(8,128)(2,1)} %pad_maximum_fusion.3.refs_0_), channel_id=1, source_target_pairs={{0,2},{1,5},{2,0},{3,7},{4,6},{5,1},{6,4},{7,3},{8,10},{9,13},{10,... | collective-permute-start | bytes 2211848 | tf_op jit(solution)/shard_map/ppermute | solution.py:135
  98.2 166.0 %collective-permute-start.15 = (bf16[4,240,384]{2,1,0:T(8,128)(2,1)}, bf16[4,240,384]{2,1,0:T(8,128)(2,1)}, u32[]{:S(2)}, u32[]{:S(2)}) collective-permute-start(bf16[4,240,384]{2,1,0:T(8,128)(2,1)} %pad_maximum_fusion.3.refs_0_), channel_id=1, source_target_pairs={{0,4},{1,3},{2,6},{3,1},{4,0},{5,7},{6,2},{7,5},{8,12},{9,11},{10,... | collective-permute-start | bytes 2211848 | tf_op jit(solution)/shard_map/ppermute | solution.py:135
  98.9 190.7 %collective-permute-start.29 = (bf16[4,192,384]{2,1,0:T(8,128)(2,1)}, bf16[4,192,384]{2,1,0:T(8,128)(2,1)}, u32[]{:S(2)}, u32[]{:S(2)}) collective-permute-start(bf16[4,192,384]{2,1,0:T(8,128)(2,1)} %collective-permute-done.25.refs_1_), channel_id=1, source_target_pairs={{0,1},{1,0},{2,3},{3,2},{4,5},{5,4},{6,7},{7,6},{8,9},{9,8},{10,11... | collective-permute-start | bytes 1769480 | tf_op jit(solution)/shard_map/ppermute | solution.py:135
  262.3 27.4 %collective-permute-start.27 = (bf16[4,192,384]{2,1,0:T(8,128)(2,1)}, bf16[4,192,384]{2,1,0:T(8,128)(2,1)}, u32[]{:S(2)}, u32[]{:S(2)}) collective-permute-start(bf16[4,192,384]{2,1,0:T(8,128)(2,1)} %collective-permute-done.25.refs_1_), channel_id=1, source_target_pairs={{0,2},{1,5},{2,0},{3,7},{4,6},{5,1},{6,4},{7,3},{8,10},{9,13},{10,... | collective-permute-start | bytes 1769480 | tf_op jit(solution)/shard_map/ppermute | solution.py:135
  264.1 25.0 %collective-permute-start.30 = (bf16[4,192,384]{2,1,0:T(8,128)(2,1)}, bf16[4,192,384]{2,1,0:T(8,128)(2,1)}, u32[]{:S(2)}, u32[]{:S(2)}) collective-permute-start(bf16[4,192,384]{2,1,0:T(8,128)(2,1)} %collective-permute-done.26.refs_2_), channel_id=1, source_target_pairs={{0,1},{1,0},{2,3},{3,2},{4,5},{5,4},{6,7},{7,6},{8,9},{9,8},{10,11... | collective-permute-start | bytes 1769480 | tf_op jit(solution)/shard_map/ppermute | solution.py:135
  264.1 26.0 %collective-permute-start.17 = (bf16[4,240,384]{2,1,0:T(8,128)(2,1)}, bf16[4,240,384]{2,1,0:T(8,128)(2,1)}, u32[]{:S(2)}, u32[]{:S(2)}) collective-permute-start(bf16[4,240,384]{2,1,0:T(8,128)(2,1)} %collective-permute-done.15.refs_1_), channel_id=1, source_target_pairs={{0,2},{1,5},{2,0},{3,7},{4,6},{5,1},{6,4},{7,3},{8,10},{9,13},{10,... | collective-permute-start | bytes 2211848 | tf_op jit(solution)/shard_map/ppermute | solution.py:135
  289.1 165.0 %collective-permute-start.18 = (bf16[4,240,384]{2,1,0:T(8,128)(2,1)}, bf16[4,240,384]{2,1,0:T(8,128)(2,1)S(1)}, u32[]{:S(2)}, u32[]{:S(2)}) collective-permute-start(bf16[4,240,384]{2,1,0:T(8,128)(2,1)} %pad_maximum_fusion.3.refs_0_), channel_id=1, source_target_pairs={{0,1},{1,0},{2,3},{3,2},{4,5},{5,4},{6,7},{7,6},{8,9},{9,8},{10,11... | collective-permute-start | bytes 2211848 | tf_op jit(solution)/shard_map/ppermute | solution.py:135
  289.1 165.0 %collective-permute-start.19 = (bf16[4,240,384]{2,1,0:T(8,128)(2,1)}, bf16[4,240,384]{2,1,0:T(8,128)(2,1)S(1)}, u32[]{:S(2)}, u32[]{:S(2)}) collective-permute-start(bf16[4,240,384]{2,1,0:T(8,128)(2,1)} %collective-permute-done.15.refs_1_), channel_id=1, source_target_pairs={{0,1},{1,0},{2,3},{3,2},{4,5},{5,4},{6,7},{7,6},{8,9},{9,8},{10,11... | collective-permute-start | bytes 2211848 | tf_op jit(solution)/shard_map/ppermute | solution.py:135
  289.6 164.5 %collective-permute-start.20 = (bf16[4,240,384]{2,1,0:T(8,128)(2,1)}, bf16[4,240,384]{2,1,0:T(8,128)(2,1)}, u32[]{:S(2)}, u32[]{:S(2)}) collective-permute-start(bf16[4,240,384]{2,1,0:T(8,128)(2,1)} %collective-permute-done.16.refs_2_), channel_id=1, source_target_pairs={{0,1},{1,0},{2,3},{3,2},{4,5},{5,4},{6,7},{7,6},{8,9},{9,8},{10,11... | collective-permute-start | bytes 2211848 | tf_op jit(solution)/shard_map/ppermute | solution.py:135
  289.7 19.1 %collective-permute-start.31 = (bf16[4,192,384]{2,1,0:T(8,128)(2,1)}, bf16[4,192,384]{2,1,0:T(8,128)(2,1)}, u32[]{:S(2)}, u32[]{:S(2)}) collective-permute-start(bf16[4,192,384]{2,1,0:T(8,128)(2,1)} %collective-permute-done.27.refs_3_), channel_id=1, source_target_pairs={{0,1},{1,0},{2,3},{3,2},{4,5},{5,4},{6,7},{7,6},{8,9},{9,8},{10,11... | collective-permute-start | bytes 1769480 | tf_op jit(solution)/shard_map/ppermute | solution.py:135
  290.2 164.0 %collective-permute-start.21 = (bf16[4,240,384]{2,1,0:T(8,128)(2,1)}, bf16[4,240,384]{2,1,0:T(8,128)(2,1)}, u32[]{:S(2)}, u32[]{:S(2)}) collective-permute-start(bf16[4,240,384]{2,1,0:T(8,128)(2,1)} %collective-permute-done.17.refs_3_), channel_id=1, source_target_pairs={{0,1},{1,0},{2,3},{3,2},{4,5},{5,4},{6,7},{7,6},{8,9},{9,8},{10,11... | collective-permute-start | bytes 2211848 | tf_op jit(solution)/shard_map/ppermute | solution.py:135
  1018.8 333.5 %collective-permute-start.66 = (bf16[4,192,384]{2,1,0:T(8,128)(2,1)}, bf16[4,192,384]{2,1,0:T(8,128)(2,1)}, u32[]{:S(2)}, u32[]{:S(2)}) collective-permute-start(bf16[4,192,384]{2,1,0:T(8,128)(2,1)} %get-tuple-element.66), channel_id=1, source_target_pairs={{0,1},{1,0},{2,3},{3,2},{4,5},{5,4},{6,7},{7,6},{8,9},{9,8},{10,11... | collective-permute-start | bytes 1769480 | tf_op jit(solution)/shard_map/ppermute | solution.py:135
  1057.4 136.7 %collective-permute-start.43 = (bf16[4,48,384]{2,1,0:T(8,128)(2,1)}, bf16[4,48,384]{2,1,0:T(8,128)(2,1)}, u32[]{:S(2)}, u32[]{:S(2)}) collective-permute-start(bf16[4,48,384]{2,1,0:T(8,128)(2,1)} %get-tuple-element.48), channel_id=1, source_target_pairs={{0,1},{1,0},{2,3},{3,2},{4,5},{5,4},{6,7},{7,6},{8,9},{9,8},{10,11... | collective-permute-start | bytes 442376 | tf_op jit(solution)/shard_map/ppermute | solution.py:135
  1057.5 126.2 %collective-permute-start.44 = (bf16[4,48,384]{2,1,0:T(8,128)(2,1)}, bf16[4,48,384]{2,1,0:T(8,128)(2,1)S(1)}, u32[]{:S(2)}, u32[]{:S(2)}) collective-permute-start(bf16[4,48,384]{2,1,0:T(8,128)(2,1)} %get-tuple-element.50), channel_id=1, source_target_pairs={{0,1},{1,0},{2,3},{3,2},{4,5},{5,4},{6,7},{7,6},{8,9},{9,8},{10,11... | collective-permute-start | bytes 442376 | tf_op jit(solution)/shard_map/ppermute | solution.py:135
  1058.0 127.1 %collective-permute-start.46 = (bf16[4,48,384]{2,1,0:T(8,128)(2,1)}, bf16[4,48,384]{2,1,0:T(8,128)(2,1)}, u32[]{:S(2)}, u32[]{:S(2)}) collective-permute-start(bf16[4,48,384]{2,1,0:T(8,128)(2,1)} %get-tuple-element.52), channel_id=1, source_target_pairs={{0,1},{1,0},{2,3},{3,2},{4,5},{5,4},{6,7},{7,6},{8,9},{9,8},{10,11... | collective-permute-start | bytes 442376 | tf_op jit(solution)/shard_map/ppermute | solution.py:135
  1058.1 124.7 %collective-permute-start.47 = (bf16[4,48,384]{2,1,0:T(8,128)(2,1)}, bf16[4,48,384]{2,1,0:T(8,128)(2,1)}, u32[]{:S(2)}, u32[]{:S(2)}) collective-permute-start(bf16[4,48,384]{2,1,0:T(8,128)(2,1)} %get-tuple-element.54), channel_id=1, source_target_pairs={{0,1},{1,0},{2,3},{3,2},{4,5},{5,4},{6,7},{7,6},{8,9},{9,8},{10,11... | collective-permute-start | bytes 442376 | tf_op jit(solution)/shard_map/ppermute | solution.py:135
  1182.7 164.0 %collective-permute-start.36 = (bf16[4,160,384]{2,1,0:T(8,128)(2,1)}, bf16[4,160,384]{2,1,0:T(8,128)(2,1)S(1)}, u32[]{:S(2)}, u32[]{:S(2)}) collective-permute-start(bf16[4,160,384]{2,1,0:T(8,128)(2,1)} %pad_maximum_fusion.13), channel_id=1, source_target_pairs={{0,1},{1,0},{2,3},{3,2},{4,5},{5,4},{6,7},{7,6},{8,9},{9,8},{10,11... | collective-permute-start | bytes 1474568 | tf_op jit(solution)/shard_map/ppermute | solution.py:135
  1196.2 149.8 %collective-permute-start.50 = (bf16[48,384]{1,0:T(8,128)(2,1)S(1)}, bf16[48,384]{1,0:T(8,128)(2,1)S(1)}, u32[]{:S(2)}, u32[]{:S(2)}) collective-permute-start(bf16[48,384]{1,0:T(8,128)(2,1)S(1)} %get-tuple-element.195), channel_id=1, source_target_pairs={{0,24},{1,25},{2,26},{3,27},{4,28},{5,29},{6,30},{7,31},{8,0},{9,1... | collective-permute-start | bytes 110600 | tf_op jit(solution)/shard_map/ppermute | solution.py:135
  1196.2 149.8 %collective-permute-start.52 = (bf16[48,384]{1,0:T(8,128)(2,1)S(1)}, bf16[48,384]{1,0:T(8,128)(2,1)S(1)}, u32[]{:S(2)}, u32[]{:S(2)}) collective-permute-start(bf16[48,384]{1,0:T(8,128)(2,1)S(1)} %get-tuple-element.196), channel_id=1, source_target_pairs={{0,8},{1,9},{2,10},{3,11},{4,12},{5,13},{6,14},{7,15},{8,16},{9,17... | collective-permute-start | bytes 110600 | tf_op jit(solution)/shard_map/ppermute | solution.py:135
  1198.3 148.3 %collective-permute-start.51 = (bf16[48,384]{1,0:T(8,128)(2,1)S(1)}, bf16[48,384]{1,0:T(8,128)(2,1)S(1)}, u32[]{:S(2)}, u32[]{:S(2)}) collective-permute-start(bf16[48,384]{1,0:T(8,128)(2,1)S(1)} %get-tuple-element.197), channel_id=1, source_target_pairs={{0,16},{1,17},{2,18},{3,19},{4,20},{5,21},{6,22},{7,23},{8,24},{9,... | collective-permute-start | bytes 110600 | tf_op jit(solution)/shard_map/ppermute | solution.py:135
  1346.0 19.1 %collective-permute-start.68 = (bf16[4,192,384]{2,1,0:T(8,128)(2,1)}, bf16[4,192,384]{2,1,0:T(8,128)(2,1)S(1)}, u32[]{:S(2)}, u32[]{:S(2)}) collective-permute-start(bf16[4,192,384]{2,1,0:T(8,128)(2,1)} %get-tuple-element.68), channel_id=1, source_target_pairs={{0,1},{1,0},{2,3},{3,2},{4,5},{5,4},{6,7},{7,6},{8,9},{9,8},{10,11... | collective-permute-start | bytes 1769480 | tf_op jit(solution)/shard_map/ppermute | solution.py:135
  1374.4 24.3 %collective-permute-start.65 = (bf16[4,192,384]{2,1,0:T(8,128)(2,1)S(1)}, bf16[4,192,384]{2,1,0:T(8,128)(2,1)S(1)}, u32[]{:S(2)}, u32[]{:S(2)}) collective-permute-start(bf16[4,192,384]{2,1,0:T(8,128)(2,1)S(1)} %copy-done.91), channel_id=1, source_target_pairs={{0,1},{1,0},{2,3},{3,2},{4,5},{5,4},{6,7},{7,6},{8,9},{9,8},{10,11... | collective-permute-start | bytes 1769480 | tf_op jit(solution)/shard_map/ppermute | solution.py:135
  1379.4 32.0 %collective-permute-start.54 = (bf16[4,192,384]{2,1,0:T(8,128)(2,1)}, bf16[4,192,384]{2,1,0:T(8,128)(2,1)S(1)}, u32[]{:S(2)}, u32[]{:S(2)}) collective-permute-start(bf16[4,192,384]{2,1,0:T(8,128)(2,1)} %get-tuple-element.56), channel_id=1, source_target_pairs={{0,1},{1,0},{2,3},{3,2},{4,5},{5,4},{6,7},{7,6},{8,9},{9,8},{10,11... | collective-permute-start | bytes 1769480 | tf_op jit(solution)/shard_map/ppermute | solution.py:135
  1397.4 21.0 %collective-permute-start.56 = (bf16[4,192,384]{2,1,0:T(8,128)(2,1)S(1)}, bf16[4,192,384]{2,1,0:T(8,128)(2,1)}, u32[]{:S(2)}, u32[]{:S(2)}) collective-permute-start(bf16[4,192,384]{2,1,0:T(8,128)(2,1)S(1)} %add_convert_fusion.18), channel_id=1, source_target_pairs={{0,2},{1,5},{2,0},{3,7},{4,6},{5,1},{6,4},{7,3},{8,10},{9,13},{10,... | collective-permute-start | bytes 1769480 | tf_op jit(solution)/shard_map/ppermute | solution.py:135
  1398.8 19.6 %collective-permute-start.60 = (bf16[4,192,384]{2,1,0:T(8,128)(2,1)}, bf16[4,192,384]{2,1,0:T(8,128)(2,1)}, u32[]{:S(2)}, u32[]{:S(2)}) collective-permute-start(bf16[4,192,384]{2,1,0:T(8,128)(2,1)} %add_convert_fusion.14), channel_id=1, source_target_pairs={{0,4},{1,3},{2,6},{3,1},{4,0},{5,7},{6,2},{7,5},{8,12},{9,11},{10,... | collective-permute-start | bytes 1769480 | tf_op jit(solution)/shard_map/ppermute | solution.py:135
  (143 other events, 3379.3 us)

commit v2 on v1

--- a/solution.py
+++ b/solution.py
@@ -182,18 +182,26 @@
     return total(stack[0], *[send(stack[k], topo.zp[deep - k]) for k in range(1, deep)])
 
 
-def dma_call(kernel, out_shape, operands, n):
+def dma_call(kernel, out_shape, operands, n, in_spec, out_spec):
     return pl.pallas_call(
         kernel,
         grid_spec=pltpu.PrefetchScalarGridSpec(
             num_scalar_prefetch=1,
             grid=(1,),
-            in_specs=[pl.BlockSpec(memory_space=pl.ANY)] * (len(operands) - 1),
-            out_specs=jax.tree.map(lambda _: pl.BlockSpec(memory_space=pl.ANY), out_shape),
+            in_specs=[in_spec] * (len(operands) - 1),
+            out_specs=jax.tree.map(lambda _: out_spec, out_shape),
             scratch_shapes=[pltpu.SemaphoreType.DMA((n,))],
         ),
         out_shape=out_shape,
+        compiler_params=pltpu.CompilerParams(vmem_limit_bytes=32 * 1024 * 1024),
     )(*operands)
+
+
+ANYWHERE = pl.BlockSpec(memory_space=pl.ANY)
+
+
+def whole_block(shape):
+    return pl.BlockSpec(shape, lambda i, at: (0,) * len(shape))
 
 
 def assemble(pieces, places, low, rows, topo):
@@ -218,7 +226,7 @@
             copy.wait()
 
     shape = jax.ShapeDtypeStruct((topo.wide * 2 * rows, topo.Y * lanes), pieces[0].dtype)
-    return dma_call(kernel, shape, (places, *pieces), len(pieces) * deep)
+    return dma_call(kernel, shape, (places, *pieces), len(pieces) * deep, ANYWHERE, whole_block(shape.shape))
 
 
 def disassemble(whole, places, topo):
@@ -242,7 +250,7 @@
             copy.wait()
 
     shapes = [jax.ShapeDtypeStruct((deep, rows, lanes), whole.dtype)] * count
-    return dma_call(kernel, shapes, (places, whole), count * deep)
+    return dma_call(kernel, shapes, (places, whole), count * deep, whole_block(whole.shape), ANYWHERE)
 
 
 def tail_rows(values, rows, lanes):

time: 1450 us -> 611 us (0.42)
  Pallas kernels: 876 us -> 18 us
  local copies, waits for them, and re-layouts: 109 us -> 138 us
    pallas_call x8, Pallas kernels: 876 us -> 18 us  [dma_call(): pl.pallas_call(kernel, grid_spec=pltpu.PrefetchScalarGridSpec(num_scalar_...]
    unnamed x236 -> x330, local copies, waits for them, and re-layouts: 30.9 us -> 55.9 us
  transfers between devices with their start and end apart: 76 -> 76, of which waited for: 22 -> 24; matrix products, arithmetic and copies ran while one was open for 12% -> 30% of each run, Pallas kernels for 38% -> 2%
where the time goes in v2:
time: 611 us; the launch traced here: 605 us
  matrix products  190 us (31%)
  local copies, waits for them, and re-layouts  138 us (23%)
  other arithmetic  103 us (17%)
  waiting for transfers between devices  80.7 us (13%)
  starting transfers between devices  70.3 us (12%)
  Pallas kernels  18 us (3%)
    ppermute x76, waiting for transfers between devices, send(): return lax.ppermute(values, AXES, perm)  80.7 us
    ppermute x76, starting transfers between devices, send(): return lax.ppermute(values, AXES, perm)  70.3 us
    dot_general x4, matrix products, contract_cols(): lax.dot_general(left, right, (((1,), (1,)), ((), ())), preferred_element_...  57.5 us
    unnamed x330, local copies, waits for them, and re-layouts  55.9 us
    convert_element_type x1, other arithmetic, per_device(): grad_scores = (probs * (grad_probs - jnp.sum(probs * grad_probs, axis=3,...  26.3 us
    dot_general x1, matrix products, per_device(): jnp.einsum('bqhd,bkhd->bhqk', grad_blk, values_win, preferred_element_typ...  22.1 us
    dot_general x4, matrix products, contract_rows(): lax.dot_general(left, right, (((0,), (0,)), ((), ())), preferred_element_...  21.3 us
    pallas_call x8, Pallas kernels, dma_call(): pl.pallas_call(kernel, grid_spec=pltpu.PrefetchScalarGridSpec(num_scalar_...  18 us
  transfers between devices with their start and end apart: 76, of which 24 were waited for; matrix products, arithmetic and copies ran while one was open for 30% of the time, Pallas kernels for 2%

profile of v2, /device:TPU:0, one launch (start us, length us, event | category | flops | bytes accessed | tf_op | source)
XLA Modules:
  0.0 605.0 jit_solution(7516463246352558131)
XLA Ops:
  19.0 4.1 collective-permute-start.2
  27.6 4.9 collective-permute-done.2
  38.4 9.0 %collective-permute-done.4.refs_1_ = bf16[4,160,384]{2,1,0:T(8,128)(2,1)S(1)} collective-permute-done((bf16[4,160,384]{2,1,0:T(8,128)(2,1)S(1)}, bf16[4,160,384]{2,1,0:T(8,128)(2,1)S(1)}, u32[]{:S(2)}, u32[]{:S(2)}) %collective-permute-start.4) | collective-permute-done | bytes 491552 | tf_op jit(solution)/shard_map/ppermute | solution.py:135
  56.8 4.1 collective-permute-done.23
  60.9 6.3 %collective-permute-start.14 = (bf16[240,384]{1,0:T(8,128)(2,1)S(1)}, bf16[240,384]{1,0:T(8,128)(2,1)S(1)}, u32[]{:S(2)}, u32[]{:S(2)}) collective-permute-start(bf16[240,384]{1,0:T(8,128)(2,1)S(1)} %fusion.50), channel_id=1, source_target_pairs={{0,24},{1,25},{2,26},{3,27},{4,28},{5,29},{6,30},{7,31},{8,0},{9,1... | collective-permute-start | bytes 552968 | tf_op jit(solution)/shard_map/ppermute | solution.py:135
  71.6 6.5 %collective-permute-done.13 = bf16[240,384]{1,0:T(8,128)(2,1)S(1)} collective-permute-done((bf16[240,384]{1,0:T(8,128)(2,1)S(1)}, bf16[240,384]{1,0:T(8,128)(2,1)S(1)}, u32[]{:S(2)}, u32[]{:S(2)}) %collective-permute-start.13) | collective-permute-done | bytes 184352 | tf_op jit(solution)/shard_map/ppermute | solution.py:135
  105.0 4.7 add_convert_fusion
  121.0 3.9 reshape.219
  124.9 3.9 concatenate.95
  136.4 16.9 %fusion.85 = (f32[2,12,512]{2,1,0:T(8,128)S(1)}, f32[2,12,512,640]{3,2,1,0:T(8,128)}) fusion(bf16[2,64,12,64]{1,3,2,0:T(8,128)(2,1)S(1)} %bitcast.293, bf16[2,512,12,64]{1,3,2,0:T(8,128)(2,1)} %copy.523, bf16[2,64,12,64]{1,3,2,0:T(8,128)(2,1)} %bitcast.295, bf16[2,512,12,64]{1,0,3,2:T(2,128)(2,1)} %reshape.219, pred[2,512,640]{2,1,0:T(8,128)(4,1)} %broadcast_compare_fusion), kind=kOutput, calls=%fused_computation.303 | convolution fusion | flops 1036111872 | bytes 35700736 | tf_op jit(solution)/shard_map/bqhd,bkhd->bhqk/dot_general | solution.py:360
  155.5 14.3 %fusion = f32[2,12,512]{2,1,0:T(8,128)} fusion(f32[2,12,512,640]{3,2,1,0:T(8,128)} %get-tuple-element.223, f32[2,12,512]{2,1,0:T(8,128)S(1)} %get-tuple-element.222), kind=kLoop, calls=%fused_computation.6 | loop fusion | flops 15716352 | bytes 31555584 | tf_op jit(solution)/shard_map/reduce_sum | solution.py:366
  185.6 14.4 %fusion.34 = bf16[2,512,12,64]{1,3,2,0:T(8,128)(2,1)S(1)} fusion(f32[2,12,512,640]{3,2,1,0:T(8,128)} %get-tuple-element.223, f32[2,12,512]{2,1,0:T(8,128)} %fusion, f32[2,12,512]{2,1,0:T(8,128)} %copy-done.93, bf16[2,64,12,64]{1,3,2,0:T(8,128)(2,1)} %bitcast.287, bf16[2,512,12,64]{1,3,2,0:T(8,128)(2,1)} %copy.518, bf16[2,64,12,64]{1,3,2,0:T(8,128)(2,1)} %bitcast.289), kind=kOutput, calls=%fused_computation.80 | convolution fusion | flops 1036910592 | bytes 35094528 | tf_op jit(solution)/shard_map/bhqk,bkhd->bqhd/dot_general | solution.py:369
  213.4 35.2 %multiply_convert_fusion.1 = (bf16[1024,3072]{1,0:T(8,128)(2,1)}, f32[1024,3072]{1,0:T(8,128)}, f32[1024,3072]{1,0:T(8,128)}) fusion(f32[3072]{0:T(1024)S(1)} %slice.328, bf16[3072,768]{1,0:T(8,128)(2,1)S(1)} %shard_map.137, f32[1024,768]{0,1:T(8,128)S(1)} %get-tuple-element.225, f32[768]{0:T(1024)S(1)} %copy-done.128, f32[768]{0:T(1024)S(1)} %copy-done.122, ...), kind=kOutput, calls=%fused_computation.22 | convolution fusion | flops 5043388416 | bytes 39348224 | tf_op jit(solution)/shard_map/dot_general | solution.py:47
  248.6 16.2 %fusion.89 = (bf16[3072]{0:T(1024)(128)(2,1)}, bf16[1024,3072]{1,0:T(8,128)(2,1)}) fusion(f32[1024,3072]{1,0:T(8,128)} %get-tuple-element.164, bf16[3072,768]{1,0:T(8,128)(2,1)S(1)} %shard_map.138, bf16[1024,768]{1,0:T(8,128)(2,1)S(1)} %copy-done.72, f32[1024,3072]{1,0:T(8,128)} %get-tuple-element.226, f32[3072]{0:T(1024)} %copy-done.124), kind=kOutput, calls=%fused_computation.307 | convolution fusion | flops 4882166784 | bytes 37767168 | tf_op jit(solution)/shard_map/dot_general | solution.py:47
  264.8 9.3 %fusion.88 = (bf16[768]{0:T(1024)(128)(2,1)}, f32[1024,768]{1,0:T(8,128)}) fusion(bf16[1024,3072]{1,0:T(8,128)(2,1)} %get-tuple-element.234, bf16[3072,768]{1,0:T(8,128)(2,1)S(1)} %copy-done.3), kind=kOutput, calls=%fused_computation.306 | convolution fusion | flops 4832623616 | bytes 14157312 | tf_op jit(solution)/shard_map/dot_general | solution.py:387
  274.1 7.6 %convolution_convert_fusion.1.src = bf16[3072,768]{1,0:T(8,128)(2,1)} fusion(bf16[1024,3072]{1,0:T(8,128)(2,1)S(1)} %copy-done.141, f32[1024,768]{0,1:T(8,128)S(1)} %copy-done.59, f32[768]{0:T(1024)S(1)} %copy-done.128, f32[768]{0:T(1024)S(1)} %copy-done.122, f32[1024]{0:T(1024)S(1)} %fusion.65, f32[1024]{0:T(1024)S(1)} %broadcast_multiply_fusion), kind=kOutput, calls=%fused_computation.38 | convolution fusion | flops 4838129664 | bytes 14170112 | tf_op jit(solution)/shard_map/dot_general | solution.py:41
  298.2 12.5 %fusion.2 = f32[2,12,64,640]{3,2,1,0:T(8,128)S(1)} fusion(f32[2,12,512,640]{3,2,1,0:T(8,128)} %get-tuple-element.223, f32[2,12,512]{2,1,0:T(8,128)S(1)} %copy-done.78, bf16[2,512,12,64]{1,0,3,2:T(2,128)(2,1)S(1)} %reshape.222), kind=kOutput, calls=%fused_computation.9 | convolution fusion | flops 1022361600 | bytes 37011456 | tf_op jit(solution)/shard_map/bhqk,bqhd->bkhd/dot_general | solution.py:415
  314.2 22.1 %multiply_reduce_fusion = (f32[2,12,512]{2,1,0:T(8,128)S(1)}, f32[2,12,512,640]{3,2,1,0:T(8,128)}) fusion(f32[2,12,512,640]{3,2,1,0:T(8,128)} %get-tuple-element.223, f32[2,12,512]{2,1,0:T(8,128)S(1)} %copy-done.78, bf16[2,64,12,64]{1,3,2,0:T(8,128)(2,1)S(1)} %bitcast.288, bf16[2,512,12,64]{1,3,2,0:T(8,128)(2,1)S(1)} %copy-done.71, ...), kind=kOutput, calls=%fused_computation.1 | convolution fusion | flops 1036111872 | bytes 66551808 | tf_op jit(solution)/shard_map/bqhd,bkhd->bhqk/dot_general | solution.py:401
  336.2 26.3 %multiply_convert_fusion = bf16[2,12,512,640]{3,2,1,0:T(8,128)(2,1)} fusion(f32[2,12,512,640]{3,2,1,0:T(8,128)} %get-tuple-element.228, f32[2,12,512,640]{3,2,1,0:T(8,128)} %get-tuple-element.223, f32[2,12,512]{2,1,0:T(8,128)S(1)} %get-tuple-element.227, f32[2,12,512]{2,1,0:T(8,128)S(1)} %copy-done.78), kind=kLoop, calls=%fused_computation | loop fusion | flops 31457280 | bytes 78741504 | tf_op jit(solution)/shard_map/convert_element_type | solution.py:406
  362.5 12.0 %fusion.33 = bf16[2,512,12,64]{1,3,2,0:T(8,128)(2,1)} fusion(bf16[2,12,512,640]{3,2,1,0:T(8,128)(2,1)} %multiply_convert_fusion, bf16[2,64,12,64]{1,3,2,0:T(8,128)(2,1)} %bitcast.294, bf16[2,512,12,64]{1,3,2,0:T(8,128)(2,1)S(1)} %copy-done.74, bf16[2,64,12,64]{1,3,2,0:T(8,128)(2,1)} %bitcast.296), kind=kOutput, calls=%fused_computation.79 | convolution fusion | flops 1014104064 | bytes 19267584 | tf_op jit(solution)/shard_map/bhqk,bkhd->bqhd/dot_general | solution.py:408
  374.5 6.8 %convolution_multiply_fusion = f32[2,12,64,640]{3,2,1,0:T(8,128)S(1)} fusion(bf16[2,12,512,640]{3,2,1,0:T(8,128)(2,1)} %multiply_convert_fusion, bf16[2,512,12,64]{1,0,3,2:T(2,128)(2,1)S(1)} %copy-done.70), kind=kOutput, calls=%fused_computation.68 | convolution fusion | flops 1007616000 | bytes 21233664 | tf_op jit(solution)/shard_map/bhqk,bqhd->bkhd/dot_general | solution.py:412
  408.4 8.7 %fusion.87 = (bf16[768]{0:T(1024)(128)(2,1)}, f32[1024,768]{1,0:T(8,128)}) fusion(bf16[2304,768]{1,0:T(8,128)(2,1)S(1)} %copy-done.6, bf16[1024,768]{0,1:T(8,128)(2,1)} %copy.543, bf16[1024,768]{0,1:T(8,128)(2,1)} %copy.542, bf16[1024,768]{0,1:T(8,128)(2,1)} %bitcast.276), kind=kOutput, calls=%fused_computation.305 | convolution fusion | flops 3638820096 | bytes 11404800 | tf_op jit(solution)/shard_map/dot_general | solution.py:425
  418.5 4.2 convolution_convert_fusion.2.src
  422.8 7.2 %convolution_convert_fusion.src = bf16[3072,768]{1,0:T(8,128)(2,1)} fusion(bf16[1024,3072]{1,0:T(8,128)(2,1)S(1)} %bitcast.319, bf16[1024,768]{1,0:T(8,128)(2,1)S(1)} %copy-done.73), kind=kOutput, calls=%fused_computation.37 | convolution fusion | flops 4834197504 | bytes 12582912 | tf_op jit(solution)/shard_map/dot_general | solution.py:41
  430.0 6.3 %add_convert_fusion.4 = bf16[1024,768]{0,1:T(8,128)(2,1)} fusion(f32[1024,768]{0,1:T(8,128)S(1)} %copy-done.61, bf16[1024,3072]{1,0:T(8,128)(2,1)S(1)} %bitcast.319, bf16[3072,768]{1,0:T(8,128)(2,1)S(1)} %bitcast.271, f32[768]{0:T(1024)S(1)} %copy-done.125), kind=kOutput, calls=%fused_computation.65 | convolution fusion | flops 4834197504 | bytes 15731712 | tf_op jit(solution)/shard_map/dot_general | solution.py:377
  523.3 5.5 collective-permute-done.37
  531.4 6.3 %collective-permute-done.70 = bf16[4,192,384]{2,1,0:T(8,128)(2,1)S(1)} collective-permute-done((bf16[4,192,384]{2,1,0:T(8,128)(2,1)S(1)}, bf16[4,192,384]{2,1,0:T(8,128)(2,1)S(1)}, u32[]{:S(2)}, u32[]{:S(2)}) %collective-permute-start.70) | collective-permute-done | bytes 589856 | tf_op jit(solution)/shard_map/ppermute | solution.py:135
  541.3 4.3 collective-permute-done.34
  566.9 4.4 collective-permute-done.67
  577.6 6.4 %collective-permute-done.56 = bf16[4,192,384]{2,1,0:T(8,128)(2,1)} collective-permute-done((bf16[4,192,384]{2,1,0:T(8,128)(2,1)}, bf16[4,192,384]{2,1,0:T(8,128)(2,1)}, u32[]{:S(2)}, u32[]{:S(2)}) %collective-permute-start.56) | collective-permute-done | bytes 589856 | tf_op jit(solution)/shard_map/ppermute | solution.py:135
  590.3 5.6 collective-permute-done.61
  596.1 5.7 collective-permute-done.62
  (642 shorter events, 295.5 us)
Async XLA Ops:
  7.0 29.7 %collective-permute-start.11 = (bf16[432,192]{1,0:T(8,128)(2,1)}, bf16[432,192]{1,0:T(8,128)(2,1)S(1)}, u32[]{:S(2)}, u32[]{:S(2)}) collective-permute-start(bf16[432,192]{1,0:T(8,128)(2,1)} %constant_dynamic-slice_fusion.4), channel_id=1, source_target_pairs={{0,1},{1,0},{2,3},{3,2},{4,5},{5,4},{6,7},{7,6},{8,9},{9,8},{10,11... | collective-permute-start | bytes 497672 | tf_op jit(solution)/shard_map/ppermute | solution.py:135
  36.8 41.8 %collective-permute-start.5 = (bf16[4,160,384]{2,1,0:T(8,128)(2,1)S(1)}, bf16[4,160,384]{2,1,0:T(8,128)(2,1)S(1)}, u32[]{:S(2)}, u32[]{:S(2)}) collective-permute-start(bf16[4,160,384]{2,1,0:T(8,128)(2,1)S(1)} %pad_maximum_fusion.9.refs_0_), channel_id=1, source_target_pairs={{0,2},{1,5},{2,0},{3,7},{4,6},{5,1},{6,4},{7,3},{8,10},{9,13},{10,... | collective-permute-start | bytes 1474568 | tf_op jit(solution)/shard_map/ppermute | solution.py:135
  47.4 31.8 %collective-permute-start.6 = (bf16[4,160,384]{2,1,0:T(8,128)(2,1)S(1)}, bf16[4,160,384]{2,1,0:T(8,128)(2,1)}, u32[]{:S(2)}, u32[]{:S(2)}) collective-permute-start(bf16[4,160,384]{2,1,0:T(8,128)(2,1)S(1)} %collective-permute-done.4.refs_1_), channel_id=1, source_target_pairs={{0,2},{1,5},{2,0},{3,7},{4,6},{5,1},{6,4},{7,3},{8,10},{9,13},{10,... | collective-permute-start | bytes 1474568 | tf_op jit(solution)/shard_map/ppermute | solution.py:135
  52.2 17.3 %collective-permute-start.24 = (bf16[192,384]{1,0:T(8,128)(2,1)S(1)}, bf16[192,384]{1,0:T(8,128)(2,1)S(1)}, u32[]{:S(2)}, u32[]{:S(2)}) collective-permute-start(bf16[192,384]{1,0:T(8,128)(2,1)S(1)} %pad_maximum_fusion.15), channel_id=1, source_target_pairs={{0,24},{1,25},{2,26},{3,27},{4,28},{5,29},{6,30},{7,31},{8,0},{9,1... | collective-permute-start | bytes 442376 | tf_op jit(solution)/shard_map/ppermute | solution.py:135
  71.5 18.2 %collective-permute-start.7 = (bf16[4,160,384]{2,1,0:T(8,128)(2,1)S(1)}, bf16[4,160,384]{2,1,0:T(8,128)(2,1)S(1)}, u32[]{:S(2)}, u32[]{:S(2)}) collective-permute-start(bf16[4,160,384]{2,1,0:T(8,128)(2,1)S(1)} %pad_maximum_fusion.9.refs_0_), channel_id=1, source_target_pairs={{0,1},{1,0},{2,3},{3,2},{4,5},{5,4},{6,7},{7,6},{8,9},{9,8},{10,11... | collective-permute-start | bytes 1474568 | tf_op jit(solution)/shard_map/ppermute | solution.py:135
  78.1 17.4 %collective-permute-start.25 = (bf16[4,192,384]{2,1,0:T(8,128)(2,1)S(1)}, bf16[4,192,384]{2,1,0:T(8,128)(2,1)}, u32[]{:S(2)}, u32[]{:S(2)}) collective-permute-start(bf16[4,192,384]{2,1,0:T(8,128)(2,1)S(1)} %pad_maximum_fusion.8.refs_0_), channel_id=1, source_target_pairs={{0,4},{1,3},{2,6},{3,1},{4,0},{5,7},{6,2},{7,5},{8,12},{9,11},{10,... | collective-permute-start | bytes 1769480 | tf_op jit(solution)/shard_map/ppermute | solution.py:135
  79.1 18.0 %collective-permute-start.10 = (bf16[4,160,384]{2,1,0:T(8,128)(2,1)}, bf16[4,160,384]{2,1,0:T(8,128)(2,1)}, u32[]{:S(2)}, u32[]{:S(2)}) collective-permute-start(bf16[4,160,384]{2,1,0:T(8,128)(2,1)} %collective-permute-done.6.refs_3_), channel_id=1, source_target_pairs={{0,1},{1,0},{2,3},{3,2},{4,5},{5,4},{6,7},{7,6},{8,9},{9,8},{10,11... | collective-permute-start | bytes 1474568 | tf_op jit(solution)/shard_map/ppermute | solution.py:135
  89.7 63.5 %collective-permute-start.28 = (bf16[4,192,384]{2,1,0:T(8,128)(2,1)S(1)}, bf16[4,192,384]{2,1,0:T(8,128)(2,1)}, u32[]{:S(2)}, u32[]{:S(2)}) collective-permute-start(bf16[4,192,384]{2,1,0:T(8,128)(2,1)S(1)} %pad_maximum_fusion.8.refs_0_), channel_id=1, source_target_pairs={{0,1},{1,0},{2,3},{3,2},{4,5},{5,4},{6,7},{7,6},{8,9},{9,8},{10,11... | collective-permute-start | bytes 1769480 | tf_op jit(solution)/shard_map/ppermute | solution.py:135
  91.1 63.8 %collective-permute-start.26 = (bf16[4,192,384]{2,1,0:T(8,128)(2,1)S(1)}, bf16[4,192,384]{2,1,0:T(8,128)(2,1)}, u32[]{:S(2)}, u32[]{:S(2)}) collective-permute-start(bf16[4,192,384]{2,1,0:T(8,128)(2,1)S(1)} %pad_maximum_fusion.8.refs_0_), channel_id=1, source_target_pairs={{0,2},{1,5},{2,0},{3,7},{4,6},{5,1},{6,4},{7,3},{8,10},{9,13},{10,... | collective-permute-start | bytes 1769480 | tf_op jit(solution)/shard_map/ppermute | solution.py:135
  93.0 91.5 %collective-permute-start.16 = (bf16[4,240,384]{2,1,0:T(8,128)(2,1)S(1)}, bf16[4,240,384]{2,1,0:T(8,128)(2,1)S(1)}, u32[]{:S(2)}, u32[]{:S(2)}) collective-permute-start(bf16[4,240,384]{2,1,0:T(8,128)(2,1)S(1)} %pad_maximum_fusion.3.refs_0_), channel_id=1, source_target_pairs={{0,2},{1,5},{2,0},{3,7},{4,6},{5,1},{6,4},{7,3},{8,10},{9,13},{10,... | collective-permute-start | bytes 2211848 | tf_op jit(solution)/shard_map/ppermute | solution.py:135
  95.5 59.3 %collective-permute-start.15 = (bf16[4,240,384]{2,1,0:T(8,128)(2,1)S(1)}, bf16[4,240,384]{2,1,0:T(8,128)(2,1)S(1)}, u32[]{:S(2)}, u32[]{:S(2)}) collective-permute-start(bf16[4,240,384]{2,1,0:T(8,128)(2,1)S(1)} %pad_maximum_fusion.3.refs_0_), channel_id=1, source_target_pairs={{0,4},{1,3},{2,6},{3,1},{4,0},{5,7},{6,2},{7,5},{8,12},{9,11},{10,... | collective-permute-start | bytes 2211848 | tf_op jit(solution)/shard_map/ppermute | solution.py:135
  97.1 88.0 %collective-permute-start.29 = (bf16[4,192,384]{2,1,0:T(8,128)(2,1)}, bf16[4,192,384]{2,1,0:T(8,128)(2,1)}, u32[]{:S(2)}, u32[]{:S(2)}) collective-permute-start(bf16[4,192,384]{2,1,0:T(8,128)(2,1)} %collective-permute-done.25.refs_1_), channel_id=1, source_target_pairs={{0,1},{1,0},{2,3},{3,2},{4,5},{5,4},{6,7},{7,6},{8,9},{9,8},{10,11... | collective-permute-start | bytes 1769480 | tf_op jit(solution)/shard_map/ppermute | solution.py:135
  153.3 31.9 %collective-permute-start.27 = (bf16[4,192,384]{2,1,0:T(8,128)(2,1)}, bf16[4,192,384]{2,1,0:T(8,128)(2,1)}, u32[]{:S(2)}, u32[]{:S(2)}) collective-permute-start(bf16[4,192,384]{2,1,0:T(8,128)(2,1)} %collective-permute-done.25.refs_1_), channel_id=1, source_target_pairs={{0,2},{1,5},{2,0},{3,7},{4,6},{5,1},{6,4},{7,3},{8,10},{9,13},{10,... | collective-permute-start | bytes 1769480 | tf_op jit(solution)/shard_map/ppermute | solution.py:135
  154.9 29.7 %collective-permute-start.30 = (bf16[4,192,384]{2,1,0:T(8,128)(2,1)}, bf16[4,192,384]{2,1,0:T(8,128)(2,1)}, u32[]{:S(2)}, u32[]{:S(2)}) collective-permute-start(bf16[4,192,384]{2,1,0:T(8,128)(2,1)} %collective-permute-done.26.refs_2_), channel_id=1, source_target_pairs={{0,1},{1,0},{2,3},{3,2},{4,5},{5,4},{6,7},{7,6},{8,9},{9,8},{10,11... | collective-permute-start | bytes 1769480 | tf_op jit(solution)/shard_map/ppermute | solution.py:135
  154.9 30.7 %collective-permute-start.17 = (bf16[4,240,384]{2,1,0:T(8,128)(2,1)S(1)}, bf16[4,240,384]{2,1,0:T(8,128)(2,1)S(1)}, u32[]{:S(2)}, u32[]{:S(2)}) collective-permute-start(bf16[4,240,384]{2,1,0:T(8,128)(2,1)S(1)} %collective-permute-done.15.refs_1_), channel_id=1, source_target_pairs={{0,2},{1,5},{2,0},{3,7},{4,6},{5,1},{6,4},{7,3},{8,10},{9,13},{10,... | collective-permute-start | bytes 2211848 | tf_op jit(solution)/shard_map/ppermute | solution.py:135
  184.5 22.3 %collective-permute-start.18 = (bf16[4,240,384]{2,1,0:T(8,128)(2,1)S(1)}, bf16[4,240,384]{2,1,0:T(8,128)(2,1)S(1)}, u32[]{:S(2)}, u32[]{:S(2)}) collective-permute-start(bf16[4,240,384]{2,1,0:T(8,128)(2,1)S(1)} %pad_maximum_fusion.3.refs_0_), channel_id=1, source_target_pairs={{0,1},{1,0},{2,3},{3,2},{4,5},{5,4},{6,7},{7,6},{8,9},{9,8},{10,11... | collective-permute-start | bytes 2211848 | tf_op jit(solution)/shard_map/ppermute | solution.py:135
  184.6 22.3 %collective-permute-start.19 = (bf16[4,240,384]{2,1,0:T(8,128)(2,1)S(1)}, bf16[4,240,384]{2,1,0:T(8,128)(2,1)S(1)}, u32[]{:S(2)}, u32[]{:S(2)}) collective-permute-start(bf16[4,240,384]{2,1,0:T(8,128)(2,1)S(1)} %collective-permute-done.15.refs_1_), channel_id=1, source_target_pairs={{0,1},{1,0},{2,3},{3,2},{4,5},{5,4},{6,7},{7,6},{8,9},{9,8},{10,11... | collective-permute-start | bytes 2211848 | tf_op jit(solution)/shard_map/ppermute | solution.py:135
  185.1 21.8 %collective-permute-start.20 = (bf16[4,240,384]{2,1,0:T(8,128)(2,1)S(1)}, bf16[4,240,384]{2,1,0:T(8,128)(2,1)S(1)}, u32[]{:S(2)}, u32[]{:S(2)}) collective-permute-start(bf16[4,240,384]{2,1,0:T(8,128)(2,1)S(1)} %collective-permute-done.16.refs_2_), channel_id=1, source_target_pairs={{0,1},{1,0},{2,3},{3,2},{4,5},{5,4},{6,7},{7,6},{8,9},{9,8},{10,11... | collective-permute-start | bytes 2211848 | tf_op jit(solution)/shard_map/ppermute | solution.py:135
  185.1 18.4 %collective-permute-start.31 = (bf16[4,192,384]{2,1,0:T(8,128)(2,1)}, bf16[4,192,384]{2,1,0:T(8,128)(2,1)S(1)}, u32[]{:S(2)}, u32[]{:S(2)}) collective-permute-start(bf16[4,192,384]{2,1,0:T(8,128)(2,1)} %collective-permute-done.27.refs_3_), channel_id=1, source_target_pairs={{0,1},{1,0},{2,3},{3,2},{4,5},{5,4},{6,7},{7,6},{8,9},{9,8},{10,11... | collective-permute-start | bytes 1769480 | tf_op jit(solution)/shard_map/ppermute | solution.py:135
  185.6 21.3 %collective-permute-start.21 = (bf16[4,240,384]{2,1,0:T(8,128)(2,1)S(1)}, bf16[4,240,384]{2,1,0:T(8,128)(2,1)S(1)}, u32[]{:S(2)}, u32[]{:S(2)}) collective-permute-start(bf16[4,240,384]{2,1,0:T(8,128)(2,1)S(1)} %collective-permute-done.17.refs_3_), channel_id=1, source_target_pairs={{0,1},{1,0},{2,3},{3,2},{4,5},{5,4},{6,7},{7,6},{8,9},{9,8},{10,11... | collective-permute-start | bytes 2211848 | tf_op jit(solution)/shard_map/ppermute | solution.py:135
  446.4 71.1 %collective-permute-start.66 = (bf16[4,192,384]{2,1,0:T(8,128)(2,1)}, bf16[4,192,384]{2,1,0:T(8,128)(2,1)}, u32[]{:S(2)}, u32[]{:S(2)}) collective-permute-start(bf16[4,192,384]{2,1,0:T(8,128)(2,1)} %get-tuple-element.66), channel_id=1, source_target_pairs={{0,1},{1,0},{2,3},{3,2},{4,5},{5,4},{6,7},{7,6},{8,9},{9,8},{10,11... | collective-permute-start | bytes 1769480 | tf_op jit(solution)/shard_map/ppermute | solution.py:135
  451.6 43.3 %collective-permute-start.43 = (bf16[4,48,384]{2,1,0:T(8,128)(2,1)}, bf16[4,48,384]{2,1,0:T(8,128)(2,1)}, u32[]{:S(2)}, u32[]{:S(2)}) collective-permute-start(bf16[4,48,384]{2,1,0:T(8,128)(2,1)} %get-tuple-element.48), channel_id=1, source_target_pairs={{0,1},{1,0},{2,3},{3,2},{4,5},{5,4},{6,7},{7,6},{8,9},{9,8},{10,11... | collective-permute-start | bytes 442376 | tf_op jit(solution)/shard_map/ppermute | solution.py:135
  451.7 33.6 %collective-permute-start.44 = (bf16[4,48,384]{2,1,0:T(8,128)(2,1)}, bf16[4,48,384]{2,1,0:T(8,128)(2,1)}, u32[]{:S(2)}, u32[]{:S(2)}) collective-permute-start(bf16[4,48,384]{2,1,0:T(8,128)(2,1)} %get-tuple-element.50), channel_id=1, source_target_pairs={{0,1},{1,0},{2,3},{3,2},{4,5},{5,4},{6,7},{7,6},{8,9},{9,8},{10,11... | collective-permute-start | bytes 442376 | tf_op jit(solution)/shard_map/ppermute | solution.py:135
  452.1 35.7 %collective-permute-start.46 = (bf16[4,48,384]{2,1,0:T(8,128)(2,1)}, bf16[4,48,384]{2,1,0:T(8,128)(2,1)}, u32[]{:S(2)}, u32[]{:S(2)}) collective-permute-start(bf16[4,48,384]{2,1,0:T(8,128)(2,1)} %get-tuple-element.52), channel_id=1, source_target_pairs={{0,1},{1,0},{2,3},{3,2},{4,5},{5,4},{6,7},{7,6},{8,9},{9,8},{10,11... | collective-permute-start | bytes 442376 | tf_op jit(solution)/shard_map/ppermute | solution.py:135
  452.2 32.0 %collective-permute-start.47 = (bf16[4,48,384]{2,1,0:T(8,128)(2,1)}, bf16[4,48,384]{2,1,0:T(8,128)(2,1)}, u32[]{:S(2)}, u32[]{:S(2)}) collective-permute-start(bf16[4,48,384]{2,1,0:T(8,128)(2,1)} %get-tuple-element.54), channel_id=1, source_target_pairs={{0,1},{1,0},{2,3},{3,2},{4,5},{5,4},{6,7},{7,6},{8,9},{9,8},{10,11... | collective-permute-start | bytes 442376 | tf_op jit(solution)/shard_map/ppermute | solution.py:135
  484.2 28.9 %collective-permute-start.36 = (bf16[4,160,384]{2,1,0:T(8,128)(2,1)}, bf16[4,160,384]{2,1,0:T(8,128)(2,1)}, u32[]{:S(2)}, u32[]{:S(2)}) collective-permute-start(bf16[4,160,384]{2,1,0:T(8,128)(2,1)} %pad_maximum_fusion.13), channel_id=1, source_target_pairs={{0,1},{1,0},{2,3},{3,2},{4,5},{5,4},{6,7},{7,6},{8,9},{9,8},{10,11... | collective-permute-start | bytes 1474568 | tf_op jit(solution)/shard_map/ppermute | solution.py:135
  511.6 19.8 %collective-permute-start.68 = (bf16[4,192,384]{2,1,0:T(8,128)(2,1)}, bf16[4,192,384]{2,1,0:T(8,128)(2,1)S(1)}, u32[]{:S(2)}, u32[]{:S(2)}) collective-permute-start(bf16[4,192,384]{2,1,0:T(8,128)(2,1)} %copy-done.43), channel_id=1, source_target_pairs={{0,1},{1,0},{2,3},{3,2},{4,5},{5,4},{6,7},{7,6},{8,9},{9,8},{10,11... | collective-permute-start | bytes 1769480 | tf_op jit(solution)/shard_map/ppermute | solution.py:135
  523.2 18.1 %collective-permute-start.32 = (bf16[4,160,384]{2,1,0:T(8,128)(2,1)S(1)}, bf16[4,160,384]{2,1,0:T(8,128)(2,1)S(1)}, u32[]{:S(2)}, u32[]{:S(2)}) collective-permute-start(bf16[4,160,384]{2,1,0:T(8,128)(2,1)S(1)} %copy-done.91), channel_id=1, source_target_pairs={{0,1},{1,0},{2,3},{3,2},{4,5},{5,4},{6,7},{7,6},{8,9},{9,8},{10,11... | collective-permute-start | bytes 1474568 | tf_op jit(solution)/shard_map/ppermute | solution.py:135
  541.3 23.9 %collective-permute-start.65 = (bf16[4,192,384]{2,1,0:T(8,128)(2,1)S(1)}, bf16[4,192,384]{2,1,0:T(8,128)(2,1)S(1)}, u32[]{:S(2)}, u32[]{:S(2)}) collective-permute-start(bf16[4,192,384]{2,1,0:T(8,128)(2,1)S(1)} %copy-done.42), channel_id=1, source_target_pairs={{0,1},{1,0},{2,3},{3,2},{4,5},{5,4},{6,7},{7,6},{8,9},{9,8},{10,11... | collective-permute-start | bytes 1769480 | tf_op jit(solution)/shard_map/ppermute | solution.py:135
  545.6 31.0 %collective-permute-start.54 = (bf16[4,192,384]{2,1,0:T(8,128)(2,1)S(1)}, bf16[4,192,384]{2,1,0:T(8,128)(2,1)}, u32[]{:S(2)}, u32[]{:S(2)}) collective-permute-start(bf16[4,192,384]{2,1,0:T(8,128)(2,1)S(1)} %copy-done.46), channel_id=1, source_target_pairs={{0,1},{1,0},{2,3},{3,2},{4,5},{5,4},{6,7},{7,6},{8,9},{9,8},{10,11... | collective-permute-start | bytes 1769480 | tf_op jit(solution)/shard_map/ppermute | solution.py:135
  563.6 20.4 %collective-permute-start.56 = (bf16[4,192,384]{2,1,0:T(8,128)(2,1)}, bf16[4,192,384]{2,1,0:T(8,128)(2,1)}, u32[]{:S(2)}, u32[]{:S(2)}) collective-permute-start(bf16[4,192,384]{2,1,0:T(8,128)(2,1)} %add_convert_fusion.18), channel_id=1, source_target_pairs={{0,2},{1,5},{2,0},{3,7},{4,6},{5,1},{6,4},{7,3},{8,10},{9,13},{10,... | collective-permute-start | bytes 1769480 | tf_op jit(solution)/shard_map/ppermute | solution.py:135
  565.2 18.8 %collective-permute-start.60 = (bf16[4,192,384]{2,1,0:T(8,128)(2,1)S(1)}, bf16[4,192,384]{2,1,0:T(8,128)(2,1)}, u32[]{:S(2)}, u32[]{:S(2)}) collective-permute-start(bf16[4,192,384]{2,1,0:T(8,128)(2,1)S(1)} %add_convert_fusion.14), channel_id=1, source_target_pairs={{0,4},{1,3},{2,6},{3,1},{4,0},{5,7},{6,2},{7,5},{8,12},{9,11},{10,... | collective-permute-start | bytes 1769480 | tf_op jit(solution)/shard_map/ppermute | solution.py:135
  (190 other events, 1911.4 us)

commit v3 on v0

--- a/solution.py
+++ b/solution.py
@@ -1,6 +1,8 @@
 import jax
 import jax.numpy as jnp
 from jax import lax
+from jax.experimental import pallas as pl
+from jax.experimental.pallas import tpu as pltpu
 from jax.sharding import PartitionSpec as P
 
 HEADS = 12
@@ -71,7 +73,904 @@
     return (middle + before + after).reshape(blocks * block_rows, width)
 
 
+BF = jnp.bfloat16
+F32 = jnp.float32
+AXES = ("wide", "narrow")
+
+
+class Topo:
+    def __init__(self, wide, narrow):
+        self.wide, self.narrow = wide, narrow
+        self.Y = narrow // 2
+        self.X = self.Y
+        self.Z = wide // self.X
+        side, deep = self.X, self.Z
+        self.zp = [self.perm(lambda z, x, y, c, k=k: ((z + k) % deep, x, y, c)) for k in range(deep)]
+        self.ap = [
+            self.perm(
+                lambda z, x, y, c, k=k: (z, (x + k) % side, y, c) if c == 0 else (z, x, (y + k) % side, c)
+            )
+            for k in range(side)
+        ]
+        self.bp = [
+            self.perm(
+                lambda z, x, y, c, k=k: (z, x, (y + k) % side, c) if c == 0 else (z, (x + k) % side, y, c)
+            )
+            for k in range(side)
+        ]
+        self.cp = self.perm(lambda z, x, y, c: (z, x, y, 1 - c))
+
+    def did(self, z, x, y, c):
+        return ((z * self.X + x) * self.Y + y) * 2 + c
+
+    def perm(self, target):
+        return [
+            (self.did(z, x, y, c), self.did(*target(z, x, y, c)))
+            for z in range(self.Z)
+            for x in range(self.X)
+            for y in range(self.Y)
+            for c in range(2)
+        ]
+
+    def here(self):
+        wide, narrow = lax.axis_index("wide"), lax.axis_index("narrow")
+        return wide // self.X, wide % self.X, narrow // 2, narrow % 2
+
+    def origins(self):
+        z0, x0, y0, c0 = self.here()
+        rows = []
+        for other in range(2):
+            c = (c0 + other) % 2
+            for kb in range(self.X):
+                for ka in range(self.X):
+                    x = (x0 + self.X - jnp.where(c == 0, ka, kb)) % self.X
+                    y = (y0 + self.Y - jnp.where(c == 0, kb, ka)) % self.Y
+                    for kz in range(self.Z):
+                        z = (z0 + self.Z - kz) % self.Z
+                        rows.append(jnp.stack([z * self.X + x, y, c]))
+        return jnp.stack(rows).astype(jnp.int32)
+
+
+def send(values, perm):
+    return lax.ppermute(values, AXES, perm)
+
+
+def pick_half(values, axis, index):
+    half = values.shape[axis] // 2
+    return lax.dynamic_slice_in_dim(values, index * half, half, axis)
+
+
+def pair_up(shard, topo, core):
+    mine = pick_half(shard, 0, core)
+    other = send(pick_half(shard, 0, 1 - core), topo.cp)
+    first = jnp.where(core == 0, mine, other)
+    second = jnp.where(core == 0, other, mine)
+    return jnp.concatenate([first, second], axis=1)
+
+
+def unpair(piece, topo, core):
+    mine = pick_half(piece, 1, core)
+    other = send(pick_half(piece, 1, 1 - core), topo.cp)
+    first = jnp.where(core == 0, mine, other)
+    second = jnp.where(core == 0, other, mine)
+    return jnp.concatenate([first, second], axis=0)
+
+
+def gather(piece, topo):
+    stack = jnp.stack([piece] + [send(piece, topo.zp[k]) for k in range(1, topo.Z)])
+    line = [stack] + [send(stack, topo.ap[k]) for k in range(1, topo.X)]
+    own = [p for k in range(topo.X) for p in (line if k == 0 else [send(q, topo.bp[k]) for q in line])]
+    return own + [send(p, topo.cp) for p in own]
+
+
+def nn(a, b):
+    return lax.dot_general(a, b, (((1,), (0,)), ((), ())), preferred_element_type=F32)
+
+
+def nt(a, b):
+    return lax.dot_general(a, b, (((1,), (1,)), ((), ())), preferred_element_type=F32)
+
+
+def tn(a, b):
+    return lax.dot_general(a, b, (((0,), (0,)), ((), ())), preferred_element_type=F32)
+
+
+def normed(values):
+    center = values - jnp.mean(values, axis=-1, keepdims=True)
+    spread = jnp.mean(center * center, axis=-1, keepdims=True)
+    inverse = lax.rsqrt(spread + EPS)
+    return center * inverse, inverse
+
+
+def norm_back(grad, hat, inverse, gain):
+    scaled = grad * gain
+    first = jnp.mean(scaled, axis=-1, keepdims=True)
+    second = jnp.mean(scaled * hat, axis=-1, keepdims=True)
+    return inverse * (scaled - first - hat * second)
+
+
+ROOT_HALF = 0.7071067811865476
+ROOT_TAU = 0.3989422804014327
+MIB = 1024 * 1024
+
+
+def cdf_pdf(u):
+    bell = jnp.exp(-0.5 * (u * u))
+    t = 1.0 / (1.0 + (0.3275911 * ROOT_HALF) * jnp.abs(u))
+    poly = 1.061405429 * 0.5
+    for coef in (-1.453152027, 1.421413741, -0.284496736, 0.254829592):
+        poly = poly * t + coef * 0.5
+    upper = poly * t * bell
+    return jnp.where(u < 0, upper, 1.0 - upper), ROOT_TAU * bell
+
+
+def call(kernel, grid, in_specs, out_specs, out_shape, scratch, vmem, flops, bytes_accessed, operands, prefetch=0, aliases=None, after=()):
+    first, count = len(operands), len(after)
+
+    def body(*refs):
+        kernel(*refs[:first], *refs[first + count :])
+
+    return pl.pallas_call(
+        body,
+        grid_spec=pltpu.PrefetchScalarGridSpec(
+            num_scalar_prefetch=prefetch,
+            grid=grid,
+            in_specs=in_specs + [ANYWHERE] * count,
+            out_specs=out_specs,
+            scratch_shapes=scratch,
+        ),
+        out_shape=out_shape,
+        input_output_aliases=aliases or {},
+        compiler_params=pltpu.CompilerParams(vmem_limit_bytes=vmem * MIB),
+        cost_estimate=pl.CostEstimate(flops=flops, bytes_accessed=bytes_accessed, transcendentals=0),
+    )(*operands, *after)
+
+
+ANYWHERE = pl.BlockSpec(memory_space=pl.ANY)
+
+
+def full(shape):
+    return pl.BlockSpec(shape, lambda *unused: (0,) * len(shape))
+
+
+def rows_of(shape):
+    return pl.BlockSpec(shape, lambda i, *unused: (i,) + (0,) * (len(shape) - 1))
+
+
+def lanes_of(shape):
+    return pl.BlockSpec(shape, lambda i, *unused: (0, i))
+
+
+def piece_place(at, j, rows, lanes):
+    row = pl.multiple_of((at[j, 0] * 2 + at[j, 2]) * rows, 16)
+    lane = pl.multiple_of(at[j, 1] * lanes, 128)
+    return pl.ds(row, rows), pl.ds(lane, lanes)
+
+
+def load_pieces(at, pieces, low, rows, whole, sem):
+    copies = []
+    deep, lanes = pieces[0].shape[0], pieces[0].shape[2]
+    for i, piece in enumerate(pieces):
+        for k in range(deep):
+            place = piece_place(at, i * deep + k, rows, lanes)
+            copy = pltpu.make_async_copy(piece.at[k, pl.ds(low, rows), :], whole.at[place], sem.at[i * deep + k])
+            copy.start()
+            copies.append(copy)
+    return copies
+
+
+def store_pieces(at, whole, rows, own, far, low, sem):
+    copies = []
+    count, deep, lanes = own.shape[0], own.shape[1], own.shape[3]
+    for i in range(2 * count):
+        for k in range(deep):
+            place = piece_place(at, i * deep + k, rows, lanes)
+            target = own.at[i, k] if i < count else far.at[i - count, k]
+            copy = pltpu.make_async_copy(whole.at[place], target.at[pl.ds(low, rows), :], sem.at[i * deep + k])
+            copy.start()
+            copies.append(copy)
+    return copies
+
+
+def wait_all(copies):
+    for copy in copies:
+        copy.wait()
+
+
+def unpack_vectors(pieces, places, low, share, width, wide, narrow):
+    n, deep, lanes = len(pieces), pieces[0].shape[0], pieces[0].shape[2]
+    hidden = wide * narrow * share - 8 * width
+    group = hidden // (2 * wide)
+    unit = group // 2
+    lines = 8 + hidden // width
+
+    def kernel(at, *refs):
+        parts, (vecs, bias, up_a, up_b, slots, flat, sem) = refs[:n], refs[n:]
+        copies = []
+        for i, piece in enumerate(parts):
+            for k in range(deep):
+                j = i * deep + k
+                slot = at[j, 0] * narrow + at[j, 1] * 2 + at[j, 2]
+                copy = pltpu.make_async_copy(piece.at[k, pl.ds(low, 16), :], slots.at[slot], sem.at[j])
+                copy.start()
+                copies.append(copy)
+        wait_all(copies)
+        for j in range(wide * narrow):
+            values = slots[j].astype(F32)[0:1, :]
+            done = 0
+            while done < share:
+                line, lane = divmod(j * share + done, width)
+                take = min(share - done, width - lane)
+                flat[line : line + 1, lane : lane + take] = values[:, done : done + take]
+                done += take
+        vecs[...] = flat[0:8, :]
+        columns = lambda line: jnp.broadcast_to(flat[line : line + 1, :], (128, width)).T[:, 0:1]
+        bias[0:width, :] = columns(2)
+        bias[width : 2 * width, :] = jnp.zeros((width, 1), F32)
+        bias[2 * width :, :] = columns(3)
+        up = jnp.concatenate([columns(line) for line in range(8, lines)], axis=0)
+        for k in range(2 * wide):
+            up_a[k * unit : (k + 1) * unit, :] = up[k * group : k * group + unit, :]
+            up_b[k * unit : (k + 1) * unit, :] = up[k * group + unit : (k + 1) * group, :]
+
+    column = jax.ShapeDtypeStruct((hidden // 2, 1), F32)
+    return call(
+        kernel,
+        (1,),
+        [ANYWHERE] * n,
+        [full((8, width)), full((3 * width, 1)), full(column.shape), full(column.shape)],
+        [jax.ShapeDtypeStruct((8, width), F32), jax.ShapeDtypeStruct((3 * width, 1), F32), column, column],
+        [
+            pltpu.VMEM((wide * narrow, 16, lanes), BF),
+            pltpu.VMEM((16, width), F32),
+            pltpu.SemaphoreType.DMA((n * deep,)),
+        ],
+        16,
+        1000,
+        1000,
+        (places, *pieces),
+        prefetch=1,
+    )
+
+
+def project_qkv(tokens, vecs, bias, pieces, places, shape):
+    rows, width = tokens.shape
+    half, wide = shape
+    n, block, steps = len(pieces), 256, 3 * width // 256
+
+    def kernel(at, tok, vec, bias_ref, *refs):
+        parts, (hid_out, out, weight, hid, sem) = refs[:n], refs[n:]
+        step = pl.program_id(0)
+
+        @pl.when(step == 0)
+        def first():
+            copies = load_pieces(at, parts, 0, half, weight, sem)
+            hat, unused = normed(tok[...].astype(F32))
+            hid[...] = (hat * vec[0:1, :] + vec[1:2, :]).astype(BF)
+            hid_out[...] = hid[...]
+            wait_all(copies)
+
+        start = pl.multiple_of(step * block, block)
+        out[...] = (nt(weight[pl.ds(start, block), :], hid[...]) + bias_ref[...]).astype(BF)
+
+    return call(
+        kernel,
+        (steps,),
+        [full((rows, width)), full(vecs.shape), rows_of((block, 1))] + [ANYWHERE] * n,
+        [full((rows, width)), rows_of((block, rows))],
+        [jax.ShapeDtypeStruct((rows, width), BF), jax.ShapeDtypeStruct((3 * width, rows), BF)],
+        [
+            pltpu.VMEM((3 * width, width), BF),
+            pltpu.VMEM((rows, width), BF),
+            pltpu.SemaphoreType.DMA((n * pieces[0].shape[0],)),
+        ],
+        32,
+        6 * rows * width * width,
+        12 * MIB,
+        (places, tokens, vecs, bias, *pieces),
+        prefetch=1,
+    )
+
+
+QB = 128
+KB = 256
+PARTS = 2
+
+
+def window_bias(seg_row, seg_col):
+    return jnp.where(seg_col == seg_row, 0.0, NEG).astype(F32)
+
+
+def shift_in(dst, src):
+    count, rows = src.shape
+    half = KB // 4
+    zero = jnp.zeros((count, half), src.dtype)
+    dst[...] = jnp.concatenate([zero, src, zero], axis=1)
+
+
+def head_parts(width, rows, part):
+    half = width // PARTS
+    return [
+        pl.BlockSpec((half, QB), lambda i, *unused: (part, i)),
+        pl.BlockSpec((half, rows), lambda i, *unused: (PARTS + part, 0)),
+        pl.BlockSpec((half, rows), lambda i, *unused: (2 * PARTS + part, 0)),
+    ]
+
+
+def attend(qkv_t, seg_row, seg_col, width, part, after=()):
+    rows = qkv_t.shape[1]
+    half = width // PARTS
+    heads = half // HEAD_DIM
+
+    def kernel(q_ref, k_ref, v_ref, seg_r, seg_c, o_ref, lse_ref, keys, values):
+        step = pl.program_id(0)
+
+        @pl.when(step == 0)
+        def first():
+            shift_in(keys, k_ref[...])
+            shift_in(values, v_ref[...])
+
+        start = pl.multiple_of(step * QB, QB)
+        window = pl.ds(start, KB)
+        bias = window_bias(seg_r[0:1, :], seg_c[window, :])
+        ats = [slice(h * HEAD_DIM, (h + 1) * HEAD_DIM) for h in range(heads)]
+        scores = [tn(keys[at, window], q_ref[at, :] * BF(HEAD_DIM**-0.5)) + bias for at in ats]
+        tops = [jnp.max(s, axis=0, keepdims=True) for s in scores]
+        expos = [jnp.exp(s - t) for s, t in zip(scores, tops)]
+        sums = [jnp.sum(e, axis=0, keepdims=True) for e in expos]
+        probs = [(e * (1.0 / s)).astype(BF) for e, s in zip(expos, sums)]
+        for at, p in zip(ats, probs):
+            o_ref[at, :] = nn(values[at, window], p).astype(BF)
+        for h, (t, s) in enumerate(zip(tops, sums)):
+            lse_ref[h : h + 1, :] = t + jnp.log(s)
+
+    return call(
+        kernel,
+        (rows // QB,),
+        head_parts(width, rows, part) + [lanes_of((8, QB)), full(seg_col.shape)],
+        [lanes_of((half, QB)), lanes_of((16, QB))],
+        [jax.ShapeDtypeStruct((half, rows), BF), jax.ShapeDtypeStruct((16, rows), F32)],
+        [pltpu.VMEM((half, rows + QB), BF), pltpu.VMEM((half, rows + QB), BF)],
+        40,
+        4 * rows * KB * half * 4,
+        8 * MIB,
+        (qkv_t, qkv_t, qkv_t, seg_row, seg_col),
+        after=after,
+    )
+
+
+def project_out(o_parts, tokens, vecs, pieces, places, rows_piece, after=()):
+    rows, width = tokens.shape
+    n, block = len(pieces), 256
+
+    def kernel(at, o_a, o_b, tok, vec, *refs):
+        parts, (mid_out, hid_out, weight, sem) = refs[:n], refs[n:]
+
+        @pl.when(pl.program_id(0) == 0)
+        def first():
+            wait_all(load_pieces(at, parts, 0, rows_piece, weight, sem))
+
+        both = jnp.concatenate([o_a[...], o_b[...]], axis=0)
+        mid = tok[...].astype(F32) + tn(both, weight[...]) + vec[4:5, :]
+        mid_out[...] = mid
+        hat, unused = normed(mid)
+        hid_out[...] = (hat * vec[5:6, :] + vec[6:7, :]).astype(BF)
+
+    return call(
+        kernel,
+        (rows // block,),
+        [lanes_of((width // PARTS, block))] * PARTS + [rows_of((block, width)), full(vecs.shape)] + [ANYWHERE] * n,
+        [rows_of((block, width)), rows_of((block, width))],
+        [jax.ShapeDtypeStruct((rows, width), F32), jax.ShapeDtypeStruct((rows, width), BF)],
+        [pltpu.VMEM((width, width), BF), pltpu.SemaphoreType.DMA((n * pieces[0].shape[0],))],
+        32,
+        2 * rows * width * width,
+        12 * MIB,
+        (places, *o_parts, tokens, vecs, *pieces),
+        prefetch=1,
+        after=after,
+    )
+
+
+def mlp_half(hidden, cot, bias, pieces, places, low, unit_rows, group_rows, wide, after=()):
+    rows, width = hidden.shape
+    n, deep, lanes = len(pieces), pieces[0].shape[0], pieces[0].shape[2]
+    units = 2 * wide * unit_rows
+    block = min(384, units)
+
+    def kernel(at, hid, cot_ref, bias_ref, *refs):
+        parts = refs[:n]
+        act_out, grad_out, sum_out, own, far, up, down, d_up, d_down, sem_a, sem_b = refs[n:]
+        step = pl.program_id(0)
+
+        @pl.when(step == 0)
+        def first():
+            one = load_pieces(at, parts, low, unit_rows, up, sem_a)
+            two = load_pieces(at, parts, low + unit_rows, unit_rows, down, sem_b)
+            wait_all(one)
+            wait_all(two)
+
+        here = pl.ds(pl.multiple_of(step * block, block), block)
+        pre = nt(up[here, :], hid[...]) + bias_ref[...]
+        grad_act = nt(down[here, :], cot_ref[...])
+        cdf, pdf = cdf_pdf(pre)
+        act = (pre * cdf).astype(BF)
+        grad = (grad_act * (cdf + pre * pdf)).astype(BF)
+        act_out[...] = act
+        grad_out[...] = grad
+        sum_out[...] = jnp.sum(grad.astype(F32), axis=1, keepdims=True)
+        d_down[here, :] = nn(act, cot_ref[...]).astype(BF)
+        d_up[here, :] = nn(grad, hid[...]).astype(BF)
+
+        @pl.when(step == pl.num_programs(0) - 1)
+        def last():
+            one = store_pieces(at, d_up, unit_rows, own, far, 0, sem_a)
+            two = store_pieces(at, d_down, unit_rows, own, far, unit_rows, sem_b)
+            wait_all(one)
+            wait_all(two)
+
+    piece_shape = jax.ShapeDtypeStruct((n // 2, deep, group_rows, lanes), BF)
+    return call(
+        kernel,
+        (units // block,),
+        [full((rows, width)), full((rows, width)), rows_of((block, 1))] + [ANYWHERE] * n,
+        [rows_of((block, rows)), rows_of((block, rows)), rows_of((block, 1)), ANYWHERE, ANYWHERE],
+        [
+            jax.ShapeDtypeStruct((units, rows), BF),
+            jax.ShapeDtypeStruct((units, rows), BF),
+            jax.ShapeDtypeStruct((units, 1), F32),
+            piece_shape,
+            piece_shape,
+        ],
+        [pltpu.VMEM((units, width), BF)] * 4
+        + [pltpu.SemaphoreType.DMA((n * deep,))] * 2,
+        48,
+        8 * rows * units * width,
+        16 * MIB,
+        (places, hidden, cot, bias, *pieces),
+        prefetch=1,
+        after=after,
+    )
+
+
+def second_norm_back(grads, mid, cot, vecs, groups, places, unit_rows, wide, after=()):
+    rows, width = mid.shape
+    block = 256
+    n, deep = len(groups[0][0]), groups[0][0][0].shape[0]
+    units = 2 * wide * unit_rows
+
+    def kernel(at, ga, gb, mid_ref, cot_ref, vec, *refs):
+        parts = refs[: 2 * n]
+        out, low_out, sums, up_a, up_b, sem = refs[2 * n :]
+        step = pl.program_id(0)
+
+        @pl.when(step == 0)
+        def first():
+            one = load_pieces(at, parts[:n], groups[0][1], unit_rows, up_a, sem.at[0])
+            two = load_pieces(at, parts[n:], groups[1][1], unit_rows, up_b, sem.at[1])
+            wait_all(one)
+            wait_all(two)
+            sums[...] = jnp.zeros_like(sums)
+
+        grad = tn(ga[...], up_a[...]) + tn(gb[...], up_b[...])
+        hat, inverse = normed(mid_ref[...])
+        top = cot_ref[...].astype(F32)
+        total_grad = top + norm_back(grad, hat, inverse, vec[5:6, :])
+        out[...] = total_grad
+        lower = total_grad.astype(BF)
+        low_out[...] = lower
+        sums[0:1, :] += jnp.sum(grad * hat, axis=0, keepdims=True)
+        sums[1:2, :] += jnp.sum(grad, axis=0, keepdims=True)
+        sums[2:3, :] += jnp.sum(lower.astype(F32), axis=0, keepdims=True)
+        sums[3:4, :] += jnp.sum(top, axis=0, keepdims=True)
+
+    return call(
+        kernel,
+        (rows // block,),
+        [lanes_of((units, block)), lanes_of((units, block)), rows_of((block, width)), rows_of((block, width)), full(vecs.shape)]
+        + [ANYWHERE] * (2 * n),
+        [rows_of((block, width)), rows_of((block, width)), full((8, width))],
+        [
+            jax.ShapeDtypeStruct((rows, width), F32),
+            jax.ShapeDtypeStruct((rows, width), BF),
+            jax.ShapeDtypeStruct((8, width), F32),
+        ],
+        [pltpu.VMEM((units, width), BF)] * 2 + [pltpu.SemaphoreType.DMA((2, n * deep))],
+        48,
+        4 * rows * units * width,
+        20 * MIB,
+        (places, *grads, mid, cot, vecs, *groups[0][0], *groups[1][0]),
+        prefetch=1,
+        after=after,
+    )
+
+
+def out_back(o_parts, grad_low, pieces, places, rows_piece, own, far, low, after=()):
+    rows, width = grad_low.shape
+    half = width // PARTS
+    n, deep = len(pieces), pieces[0].shape[0]
+
+    def kernel(at, o_a, o_b, grad, own_in, far_in, *refs):
+        parts, (do_ref, own_ref, far_ref, weight, d_weight, sem) = refs[:n], refs[n:]
+        copies = load_pieces(at, parts, 0, rows_piece, weight, sem)
+        d_weight[:half, :] = nn(o_a[...], grad[...]).astype(BF)
+        d_weight[half:, :] = nn(o_b[...], grad[...]).astype(BF)
+        wait_all(copies)
+        copies = store_pieces(at, d_weight, rows_piece, own_ref, far_ref, low, sem)
+        do_ref[...] = nt(weight[...], grad[...]).astype(BF)
+        wait_all(copies)
+
+    return call(
+        kernel,
+        (1,),
+        [full((half, rows))] * PARTS + [full((rows, width)), ANYWHERE, ANYWHERE] + [ANYWHERE] * n,
+        [full((width, rows)), ANYWHERE, ANYWHERE],
+        [
+            jax.ShapeDtypeStruct((width, rows), BF),
+            jax.ShapeDtypeStruct(own.shape, BF),
+            jax.ShapeDtypeStruct(far.shape, BF),
+        ],
+        [pltpu.VMEM((width, width), BF)] * 2 + [pltpu.SemaphoreType.DMA((n * deep,))],
+        32,
+        4 * rows * width * width,
+        8 * MIB,
+        (places, *o_parts, grad_low, own, far, *pieces),
+        prefetch=1,
+        aliases={4: 1, 5: 2},
+        after=after,
+    )
+
+
+def attend_back(qkv_t, do_t, lse, seg_row, seg_col, width, part, after=()):
+    rows = qkv_t.shape[1]
+    half = width // PARTS
+    heads = half // HEAD_DIM
+    scale = HEAD_DIM**-0.5
+
+    def kernel(q_ref, k_ref, v_ref, do_ref, lse_ref, seg_r, seg_c, out, sums, keys, values, d_keys, d_values):
+        step = pl.program_id(0)
+
+        @pl.when(step == 0)
+        def first():
+            shift_in(keys, k_ref[...])
+            shift_in(values, v_ref[...])
+            d_keys[...] = jnp.zeros_like(d_keys)
+            d_values[...] = jnp.zeros_like(d_values)
+
+        start = pl.multiple_of(step * QB, QB)
+        window = pl.ds(start, KB)
+        bias = window_bias(seg_r[0:1, :], seg_c[window, :])
+        ats = [slice(h * HEAD_DIM, (h + 1) * HEAD_DIM) for h in range(heads)]
+        queries = [q_ref[at, :] * BF(scale) for at in ats]
+        raw = [tn(keys[at, window], q) for at, q in zip(ats, queries)]
+        grad_probs = [tn(values[at, window], do_ref[at, :]) for at in ats]
+        probs = [jnp.exp(r + (bias - lse_ref[h : h + 1, :])) for h, r in enumerate(raw)]
+        weighted = [p * g for p, g in zip(probs, grad_probs)]
+        deltas = [jnp.sum(w, axis=0, keepdims=True) for w in weighted]
+        scores = [(w - p * d).astype(BF) for w, p, d in zip(weighted, probs, deltas)]
+        for at, s in zip(ats, scores):
+            out[at, pl.ds(start, QB)] = (nn(keys[at, window], s) * scale).astype(BF)
+        for at, q, s in zip(ats, queries, scores):
+            d_keys[at, window] += nt(q, s)
+        for at, p in zip(ats, probs):
+            d_values[at, window] += nt(do_ref[at, :], p.astype(BF))
+
+        @pl.when(step == pl.num_programs(0) - 1)
+        def last():
+            edge = KB // 4
+            out[half : 2 * half, :] = d_keys[...][:, edge : edge + rows].astype(BF)
+            out[2 * half : 3 * half, :] = d_values[...][:, edge : edge + rows].astype(BF)
+            sums[...] = jnp.sum(out[...].astype(F32), axis=1, keepdims=True)
+
+    return call(
+        kernel,
+        (rows // QB,),
+        head_parts(width, rows, part)
+        + [
+            pl.BlockSpec((half, QB), lambda i, *unused: (part, i)),
+            lanes_of((16, QB)),
+            lanes_of((8, QB)),
+            full(seg_col.shape),
+        ],
+        [full((3 * half, rows)), full((3 * half, 1))],
+        [jax.ShapeDtypeStruct((3 * half, rows), BF), jax.ShapeDtypeStruct((3 * half, 1), F32)],
+        [pltpu.VMEM((half, rows + QB), BF)] * 2 + [pltpu.VMEM((half, rows + QB), F32)] * 2,
+        48,
+        10 * rows * KB * half * 4,
+        16 * MIB,
+        (qkv_t, qkv_t, qkv_t, do_t, lse, seg_row, seg_col),
+        after=after,
+    )
+
+
+def qkv_back(grad_parts, hidden, places, rows_piece, topo, after=()):
+    rows, width = hidden.shape
+    half = width // PARTS
+    count = 3 * width
+    sites, lanes = topo.X * topo.X, width // topo.Y
+
+    def kernel(at, grad_a, grad_b, hid, own, far, whole, sem):
+        step = pl.program_id(0)
+        for part, grad in enumerate((grad_a, grad_b)):
+            here = pl.ds(pl.multiple_of(step * width + part * half, half), half)
+            whole[here, :] = nn(grad[...], hid[...]).astype(BF)
+
+        @pl.when(step == pl.num_programs(0) - 1)
+        def last():
+            wait_all(store_pieces(at, whole, rows_piece, own, far, 0, sem))
+
+    piece_shape = jax.ShapeDtypeStruct((sites, topo.Z, rows_piece, lanes), BF)
+    return call(
+        kernel,
+        (3,),
+        [rows_of((half, rows))] * PARTS + [full((rows, width))],
+        [ANYWHERE, ANYWHERE],
+        [piece_shape, piece_shape],
+        [pltpu.VMEM((count, width), BF), pltpu.SemaphoreType.DMA((2 * sites * topo.Z,))],
+        32,
+        2 * rows * count * width,
+        12 * MIB,
+        (places, *grad_parts, hidden),
+        prefetch=1,
+        after=after,
+    )
+
+
+def first_norm_back(grad_parts, tokens, grad_mid, vecs, pieces, places, rows_piece, after=()):
+    rows, width = tokens.shape
+    count, half = 3 * width, width // PARTS
+    block = 256
+    n = len(pieces)
+
+    def kernel(at, grad_a, grad_b, tok, mid, vec, *refs):
+        parts, (out, sums, weight, sem) = refs[:n], refs[n:]
+
+        @pl.when(pl.program_id(0) == 0)
+        def first():
+            wait_all(load_pieces(at, parts, 0, rows_piece, weight, sem))
+            sums[...] = jnp.zeros_like(sums)
+
+        both = jnp.concatenate([g[k * half : (k + 1) * half, :] for k in range(3) for g in (grad_a, grad_b)], axis=0)
+        grad = tn(both, weight[...])
+        hat, inverse = normed(tok[...].astype(F32))
+        out[...] = (mid[...] + norm_back(grad, hat, inverse, vec[0:1, :])).astype(BF)
+        sums[0:1, :] += jnp.sum(grad * hat, axis=0, keepdims=True)
+        sums[1:2, :] += jnp.sum(grad, axis=0, keepdims=True)
+
+    return call(
+        kernel,
+        (rows // block,),
+        [lanes_of((count // PARTS, block))] * PARTS
+        + [rows_of((block, width)), rows_of((block, width)), full(vecs.shape)]
+        + [ANYWHERE] * n,
+        [rows_of((block, width)), full((8, width))],
+        [jax.ShapeDtypeStruct((rows, width), BF), jax.ShapeDtypeStruct((8, width), F32)],
+        [pltpu.VMEM((count, width), BF), pltpu.SemaphoreType.DMA((n * pieces[0].shape[0],))],
+        40,
+        2 * rows * count * width,
+        16 * MIB,
+        (places, *grad_parts, tokens, grad_mid, vecs, *pieces),
+        prefetch=1,
+        after=after,
+    )
+
+
+def finish_out(acts, mid, vecs, groups, places, unit_rows, wide, after=()):
+    rows, width = mid.shape
+    block = 256
+    n, deep = len(groups[0][0]), groups[0][0][0].shape[0]
+    units = 2 * wide * unit_rows
+
+    def kernel(at, act_a, act_b, mid_ref, vec, *refs):
+        parts = refs[: 2 * n]
+        out, down_a, down_b, sem = refs[2 * n :]
+
+        @pl.when(pl.program_id(0) == 0)
+        def first():
+            one = load_pieces(at, parts[:n], groups[0][1], unit_rows, down_a, sem.at[0])
+            two = load_pieces(at, parts[n:], groups[1][1], unit_rows, down_b, sem.at[1])
+            wait_all(one)
+            wait_all(two)
+
+        result = tn(act_a[...], down_a[...]) + tn(act_b[...], down_b[...])
+        out[...] = (mid_ref[...] + result + vec[7:8, :]).astype(BF)
+
+    return call(
+        kernel,
+        (rows // block,),
+        [lanes_of((units, block)), lanes_of((units, block)), rows_of((block, width)), full(vecs.shape)]
+        + [ANYWHERE] * (2 * n),
+        rows_of((block, width)),
+        jax.ShapeDtypeStruct((rows, width), BF),
+        [pltpu.VMEM((units, width), BF)] * 2 + [pltpu.SemaphoreType.DMA((2, n * deep))],
+        48,
+        4 * rows * units * width,
+        16 * MIB,
+        (places, *acts, mid, vecs, *groups[0][0], *groups[1][0]),
+        prefetch=1,
+        after=after,
+    )
+
+
+def total(first, *rest):
+    result = first.astype(F32)
+    for other in rest:
+        result = result + other.astype(F32)
+    return result
+
+
+class Chain:
+    def __init__(self, own, far, topo):
+        self.topo, self.held = topo, own
+        self.coming = [send(far, topo.cp)]
+
+    def arrived(self):
+        return tuple(self.coming)
+
+    def fold(self):
+        return total(self.held, *self.coming)
+
+    def across(self):
+        topo, side = self.topo, self.topo.X
+        own = self.fold().astype(BF).reshape(side, side, *self.held.shape[1:])
+        self.held = own[0]
+        self.coming = [send(own[k], topo.bp[side - k]) for k in range(1, side)]
+
+    def along(self):
+        topo, side = self.topo, self.topo.X
+        line = self.fold().astype(BF)
+        self.held = line[0]
+        self.coming = [send(line[k], topo.ap[side - k]) for k in range(1, side)]
+
+    def down(self):
+        topo, deep = self.topo, self.topo.Z
+        stack = self.fold().astype(BF)
+        self.held = stack[0]
+        self.coming = [send(stack[k], topo.zp[deep - k]) for k in range(1, deep)]
+
+    def result(self):
+        return self.fold()
+
+
+def scatter(own, far, topo):
+    chain = Chain(own, far, topo)
+    chain.across()
+    chain.along()
+    chain.down()
+    return chain.result()
+
+
+def tail_rows(values, rows, lanes):
+    return jnp.pad(values[None], ((0, rows - 1), (0, lanes - values.shape[0])))
+
+
+def vector_slots(places, topo):
+    slot = places[:, 0] * topo.narrow + places[:, 1] * 2 + places[:, 2]
+    return (slot[:, None] == jnp.arange(topo.wide * topo.narrow)[None]).astype(BF)
+
+
+def fits(topo, rows, width, hidden):
+    lanes = 2 * width // topo.narrow
+    return (
+        lanes % 128 == 0
+        and rows % 256 == 0
+        and (width // topo.wide) % 32 == 0
+        and (hidden // topo.wide) % 64 == 0
+        and 2 * P_THREE == QB
+    )
+
+
+def fast_device(
+    tokens, qkv_weight, out_weight, up_weight, down_weight, vectors, bucket_counts, cotangent, topo
+):
+    rows, width = tokens.shape
+    wide = topo.wide
+    places = topo.origins()
+    core = topo.here()[3]
+    shards = [qkv_weight.astype(BF).T, out_weight.astype(BF), up_weight.astype(BF).T, down_weight.astype(BF)]
+    r_qkv, r_out, r_unit = shards[0].shape[0] // 2, shards[1].shape[0] // 2, shards[2].shape[0] // 4
+    first = pair_up(shards[0], topo, core)
+    rest = pair_up(
+        jnp.concatenate([pick_half(s, 0, h) for h in range(2) for s in shards[1:]], axis=0), topo, core
+    )
+    lanes = first.shape[1]
+    low_vec = vectors.astype(BF)
+    out_end, up_end = r_out, r_out + 2 * r_unit
+    one = gather(jnp.concatenate([first, tail_rows(low_vec, 16, lanes)], axis=0), topo)
+    two = gather(
+        jnp.concatenate([rest[: out_end + r_unit], rest[up_end : up_end + r_unit]], axis=0), topo
+    )
+    three = gather(
+        jnp.concatenate([rest[out_end + r_unit : up_end], rest[up_end + r_unit :]], axis=0), topo
+    )
+    slots = vector_slots(places, topo)
+    vecs, bias_qkv, *bias_up = unpack_vectors(one, places, r_qkv, vectors.shape[0], width, wide, topo.narrow)
+    segment = image_ids(bucket_counts[0], rows)
+    seg_row = jnp.broadcast_to(segment[None], (8, rows))
+    seg_col = jnp.pad(segment, (QB // 2, QB // 2), constant_values=-1)[:, None]
+
+    hidden_one, qkv_t = project_qkv(tokens, vecs, bias_qkv, one, places, (r_qkv, wide))
+    attn = [attend(qkv_t, seg_row, seg_col, width, part) for part in range(PARTS)]
+    attn_t, lse = [a[0] for a in attn], [a[1] for a in attn]
+    mid, hidden_two = project_out(attn_t, tokens, vecs, two, places, r_out)
+    act_a, grad_a, sum_a, own_a, far_a = mlp_half(
+        hidden_two, cotangent, bias_up[0], two, places, r_out, r_unit, 2 * r_unit, wide
+    )
+    chain_a = Chain(own_a, far_a, topo)
+    act_b, grad_b, sum_b, own_b, far_b = mlp_half(
+        hidden_two, cotangent, bias_up[1], three, places, 0, r_unit, 2 * r_unit + r_out, wide
+    )
+    grad_mid, grad_mid_low, sums_two = second_norm_back(
+        (grad_a, grad_b), mid, cotangent, vecs, ((two, r_out), (three, 0)), places, r_unit, wide,
+        after=chain_a.arrived(),
+    )
+    chain_a.across()
+    do_t, own_b, far_b = out_back(attn_t, grad_mid_low, two, places, r_out, own_b, far_b, 2 * r_unit)
+    chain_b = Chain(own_b, far_b, topo)
+    grads_0, sums_0 = attend_back(
+        qkv_t, do_t, lse[0], seg_row, seg_col, width, 0, after=chain_a.arrived()
+    )
+    chain_a.along()
+    grads_1, sums_1 = attend_back(
+        qkv_t, do_t, lse[1], seg_row, seg_col, width, 1, after=chain_a.arrived() + chain_b.arrived()
+    )
+    chain_a.down()
+    chain_b.across()
+    grad_t = (grads_0, grads_1)
+    own_q, far_q = qkv_back(
+        grad_t, hidden_one, places, r_qkv, topo, after=chain_b.arrived()
+    )
+    chain_q = Chain(own_q, far_q, topo)
+    chain_b.along()
+    input_grad, sums_one = first_norm_back(
+        grad_t, tokens, grad_mid, vecs, one, places, r_qkv, after=chain_a.arrived() + chain_q.arrived()
+    )
+    chain_q.across()
+    block_out = finish_out(
+        (act_a, act_b), mid, vecs, ((two, r_out + r_unit), (three, r_unit)), places, r_unit, wide,
+        after=chain_b.arrived(),
+    )
+    chain_b.down()
+    chain_q.along()
+    chain_q.down()
+    half = width // PARTS
+    sums_qkv = [[s[k * half : (k + 1) * half, 0] for s in (sums_0, sums_1)] for k in (0, 2)]
+    sums_up = jnp.stack([s.reshape(2 * wide, r_unit) for s in (sum_a, sum_b)], axis=1).reshape(-1)
+    d_vector = jnp.concatenate(
+        [
+            sums_one[0],
+            sums_one[1],
+            *sums_qkv[0],
+            *sums_qkv[1],
+            sums_two[2],
+            sums_two[0],
+            sums_two[1],
+            sums_two[3],
+            sums_up,
+        ]
+    )
+    part_a, part_b, part_q = chain_a.result(), chain_b.result(), chain_q.result()
+    rel = jnp.dot(slots, d_vector.astype(BF).reshape(slots.shape[1], -1), preferred_element_type=F32).astype(BF)
+    rel = jnp.pad(rel, ((0, 0), (0, lanes - rel.shape[1]))).reshape(2, topo.X * topo.X, topo.Z, 1, lanes)
+    vector_grad = scatter(rel[0], rel[1], topo)[0, : vectors.shape[0]]
+    down = jnp.concatenate([part_a[r_unit:], part_b[r_unit : 2 * r_unit]], axis=0)
+    up = jnp.concatenate([part_a[:r_unit], part_b[:r_unit]], axis=0)
+    out = part_b[2 * r_unit :]
+    grads = [unpair(g, topo, core) for g in (part_q, out, up, down)]
+    return (block_out, input_grad, grads[0].T, grads[1], grads[2].T, grads[3], vector_grad)
+
+
 def per_device(
+    tokens, qkv_weight, out_weight, up_weight, down_weight, vectors, bucket_counts, cotangent
+):
+    topo = Topo(lax.axis_size("wide"), lax.axis_size("narrow"))
+    operands = (tokens, qkv_weight, out_weight, up_weight, down_weight, vectors, bucket_counts, cotangent)
+    if fits(topo, *tokens.shape, up_weight.shape[1] * topo.wide):
+        return fast_device(*operands, topo)
+    return plain_device(*operands)
+
+
+def plain_device(
     tokens, qkv_weight, out_weight, up_weight, down_weight, vectors, bucket_counts, cotangent
 ):
     rows, width = tokens.shape

time: 841 us -> 380 us (0.45)
  waiting for transfers between devices: 305 us -> 84.4 us
  matrix products: 208 us -> 0.19 us
  Pallas kernels: 0 us -> 148 us
  blocking collectives: 110 us -> 0 us
  local copies, waits for them, and re-layouts: 118 us -> 44 us
  starting transfers between devices: 0.67 us -> 58.8 us
  other arithmetic: 71.1 us -> 35.9 us
  between operations: 18.4 us -> 4.03 us
    dot_general x18 -> x1, matrix products: 208 us -> 0.19 us  [fast_device(): jnp.dot(slots, d_vector.astype(BF).reshape(slots.shape[1], -1), preferred...]
    pallas_call x0 -> x14, Pallas kernels: none -> 148 us  [call(): pl.pallas_call(body, grid_spec=pltpu.PrefetchScalarGridSpec(num_scalar_pr...]
    reduce_scatter x4 -> x0, waiting for transfers between devices: 139 us -> none  [the longest x1 84.1 us: per_device(): lax.psum_scatter(d_down.astype(jnp.bfloat16), 'wide', scatter_dimension=0...]
    unnamed x16 -> x0, waiting for transfers between devices: 104 us -> none
    ppermute x0 -> x60, waiting for transfers between devices: none -> 84.4 us  [send(): return lax.ppermute(values, AXES, perm)]
    all_gather x5 -> x0, blocking collectives: 62.1 us -> none  [the longest x1 31.3 us: per_device(): lax.all_gather(halves[4], 'wide', axis=0, tiled=True)]
    all_gather x4 -> x0, waiting for transfers between devices: 61.6 us -> none  [the longest x1 43 us: per_device(): lax.all_gather(halves[3], 'wide', axis=0, tiled=True)]
    ppermute x0 -> x60, starting transfers between devices: none -> 58.8 us  [send(): return lax.ppermute(values, AXES, perm)]
  transfers between devices with their start and end apart: 12 -> 60, of which waited for: 7 -> 18; matrix products, arithmetic and copies ran while one was open for 37% -> 13% of each run, Pallas kernels for 0% -> 34%
where the time goes in v3:
time: 380 us; the launch traced here: 375 us
  Pallas kernels  148 us (39%)
  waiting for transfers between devices  84.4 us (22%)
  starting transfers between devices  58.8 us (15%)
  local copies, waits for them, and re-layouts  44 us (12%)
  other arithmetic  35.9 us (9%)
  between operations  4.03 us (1%)
    pallas_call x14, Pallas kernels, call(): pl.pallas_call(body, grid_spec=pltpu.PrefetchScalarGridSpec(num_scalar_pr...  148 us
    ppermute x60, waiting for transfers between devices, send(): return lax.ppermute(values, AXES, perm)  84.4 us
    ppermute x60, starting transfers between devices, send(): return lax.ppermute(values, AXES, perm)  58.8 us
    unnamed x238, local copies, waits for them, and re-layouts  31.4 us
    another operation x16, other arithmetic, origins(): return jnp.stack(rows).astype(jnp.int32)  10.3 us
  transfers between devices with their start and end apart: 60, of which 18 were waited for; matrix products, arithmetic and copies ran while one was open for 13% of the time, Pallas kernels for 34%

profile of v3, /device:TPU:0, one launch (start us, length us, event | category | flops | bytes accessed | tf_op | source)
XLA Modules:
  0.0 375.0 jit_solution(7969373735013618909)
XLA Ops:
  9.2 4.0 %collective-permute-start.2 = (bf16[160,384]{1,0:T(8,128)(2,1)S(1)}, bf16[160,384]{1,0:T(8,128)(2,1)S(1)}, u32[]{:S(2)}, u32[]{:S(2)}) collective-permute-start(bf16[160,384]{1,0:T(8,128)(2,1)S(1)} %fusion.18), channel_id=1, source_target_pairs={{0,16},{1,17},{2,18},{3,19},{4,20},{5,21},{6,22},{7,23},{8,24},{9,... | collective-permute-start | bytes 368648 | tf_op jit(solution)/shard_map/ppermute | solution.py:135
  18.0 4.6 %collective-permute-done.2 = bf16[160,384]{1,0:T(8,128)(2,1)S(1)} collective-permute-done((bf16[160,384]{1,0:T(8,128)(2,1)S(1)}, bf16[160,384]{1,0:T(8,128)(2,1)S(1)}, u32[]{:S(2)}, u32[]{:S(2)}) %collective-permute-start.2) | collective-permute-done | bytes 122912 | tf_op jit(solution)/shard_map/ppermute | solution.py:135
  22.6 6.4 %collective-permute-start.14 = (bf16[240,384]{1,0:T(8,128)(2,1)S(1)}, bf16[240,384]{1,0:T(8,128)(2,1)S(1)}, u32[]{:S(2)}, u32[]{:S(2)}) collective-permute-start(bf16[240,384]{1,0:T(8,128)(2,1)S(1)} %get-tuple-element.150), channel_id=1, source_target_pairs={{0,24},{1,25},{2,26},{3,27},{4,28},{5,29},{6,30},{7,31},{8,0},{9,1... | collective-permute-start | bytes 552968 | tf_op jit(solution)/shard_map/ppermute | solution.py:135
  30.8 6.3 %collective-permute-done.13 = bf16[240,384]{1,0:T(8,128)(2,1)S(1)} collective-permute-done((bf16[240,384]{1,0:T(8,128)(2,1)S(1)}, bf16[240,384]{1,0:T(8,128)(2,1)S(1)}, u32[]{:S(2)}, u32[]{:S(2)}) %collective-permute-start.13) | collective-permute-done | bytes 184352 | tf_op jit(solution)/shard_map/ppermute | solution.py:135
  43.4 3.0 collective-permute-start.23
  49.2 6.6 %collective-permute-done.23 = bf16[192,384]{1,0:T(8,128)(2,1)S(1)} collective-permute-done((bf16[192,384]{1,0:T(8,128)(2,1)S(1)}, bf16[192,384]{1,0:T(8,128)(2,1)S(1)}, u32[]{:S(2)}, u32[]{:S(2)}) %collective-permute-start.23) | collective-permute-done | bytes 147488 | tf_op jit(solution)/shard_map/ppermute | solution.py:135
  59.1 3.8 %collective-permute-done.22 = bf16[192,384]{1,0:T(8,128)(2,1)} collective-permute-done((bf16[192,384]{1,0:T(8,128)(2,1)S(1)}, bf16[192,384]{1,0:T(8,128)(2,1)}, u32[]{:S(2)}, u32[]{:S(2)}) %collective-permute-start.22) | collective-permute-done | bytes 147488 | tf_op jit(solution)/shard_map/ppermute | solution.py:135
  69.9 2.9 stack.500.refs_0_
  74.9 7.3 %collective-permute-done.17.refs_8_.refs_7_.refs_9_ = bf16[4,240,384]{2,1,0:T(8,128)(2,1)S(1)} collective-permute-done((bf16[4,240,384]{2,1,0:T(8,128)(2,1)S(1)}, bf16[4,240,384]{2,1,0:T(8,128)(2,1)S(1)}, u32[]{:S(2)}, u32[]{:S(2)}) %collective-permute-start.17) | collective-permute-done | bytes 737312 | tf_op jit(solution)/shard_map/ppermute | solution.py:135
  87.0 3.2 shard_map.135
  92.0 9.3 %shard_map.136 = (bf16[1024,768]{1,0:T(8,128)(2,1)S(1)}, bf16[2304,1024]{1,0:T(8,128)(2,1)S(1)}) custom-call(s32[32,3]{1,0:T(8,128)S(1)} %stack.500.refs_0_, bf16[1024,768]{1,0:T(8,128)(2,1)S(1)} %copy-done.20, f32[8,768]{1,0:T(8,128)S(1)} %get-tuple-element.43.refs_2_.refs_4_.refs_5_, f32[2304,1]{1,0:T(8,128)S(1)} %get-tuple-element.44.refs_3_, ...), custom_call_target="tpu_custom_call" | custom-call | flops 3623878656 | bytes 12582912 | tf_op jit(solution)/shard_map/pallas_call | solution.py:213
  102.4 5.9 %shard_map.138 = (bf16[384,1024]{1,0:T(8,128)(2,1)S(1)}, f32[16,1024]{1,0:T(8,128)S(1)}) custom-call(bf16[2304,1024]{1,0:T(8,128)(2,1)S(1)} %get-tuple-element.45.refs_0_.refs_1_.refs_2_, bf16[2304,1024]{1,0:T(8,128)(2,1)S(1)} %get-tuple-element.45.refs_0_.refs_1_.refs_2_, bf16[2304,1024]{1,0:T(8,128)(2,1)S(1)} %get-tuple-element.45.refs_0_.refs_1_.refs_2_, ...), custom_call_target="tpu_custom_call" | custom-call | flops 1610612736 | bytes 8388608 | tf_op jit(solution)/shard_map/pallas_call | solution.py:213
  109.0 5.9 %shard_map.137 = (bf16[384,1024]{1,0:T(8,128)(2,1)S(1)}, f32[16,1024]{1,0:T(8,128)S(1)}) custom-call(bf16[2304,1024]{1,0:T(8,128)(2,1)S(1)} %get-tuple-element.45.refs_0_.refs_1_.refs_2_, bf16[2304,1024]{1,0:T(8,128)(2,1)S(1)} %get-tuple-element.45.refs_0_.refs_1_.refs_2_, bf16[2304,1024]{1,0:T(8,128)(2,1)S(1)} %get-tuple-element.45.refs_0_.refs_1_.refs_2_, ...), custom_call_target="tpu_custom_call" | custom-call | flops 1610612736 | bytes 8388608 | tf_op jit(solution)/shard_map/pallas_call | solution.py:213
  115.1 4.9 %shard_map.139 = (f32[1024,768]{1,0:T(8,128)S(1)}, bf16[1024,768]{1,0:T(8,128)(2,1)S(1)}) custom-call(s32[32,3]{1,0:T(8,128)S(1)} %stack.500.refs_0_, bf16[384,1024]{1,0:T(8,128)(2,1)S(1)} %get-tuple-element.46.refs_1_, bf16[384,1024]{1,0:T(8,128)(2,1)S(1)} %get-tuple-element.47.refs_2_, bf16[1024,768]{1,0:T(8,128)(2,1)S(1)} %copy-done.20, ...), custom_call_target="tpu_custom_call" | custom-call | flops 1207959552 | bytes 12582912 | tf_op jit(solution)/shard_map/pallas_call | solution.py:213
  122.9 21.8 %shard_map.140 = (bf16[1536,1024]{1,0:T(8,128)(2,1)}, bf16[1536,1024]{1,0:T(8,128)(2,1)}, f32[1536,1]{1,0:T(8,128)}, bf16[4,4,192,384]{3,2,1,0:T(8,128)(2,1)}, bf16[4,4,192,384]{3,2,1,0:T(8,128)(2,1)}) custom-call(s32[32,3]{1,0:T(8,128)S(1)} %stack.500.refs_0_, bf16[1024,768]{1,0:T(8,128)(2,1)} %copy-done.67, bf16[1024,768]{1,0:T(8,128)(2,1)} %refs_4_.1, ...), custom_call_target="tpu_custom_call" | custom-call | flops 9663676416 | bytes 16777216 | tf_op jit(solution)/shard_map/pallas_call | solution.py:213
  147.4 7.3 %collective-permute-done.26.refs_6_.refs_16_.refs_15_ = bf16[4,192,384]{2,1,0:T(8,128)(2,1)S(1)} collective-permute-done((bf16[4,192,384]{2,1,0:T(8,128)(2,1)S(1)}, bf16[4,192,384]{2,1,0:T(8,128)(2,1)S(1)}, u32[]{:S(2)}, u32[]{:S(2)}) %collective-permute-start.26) | collective-permute-done | bytes 589856 | tf_op jit(solution)/shard_map/ppermute | solution.py:135
  154.8 6.3 %collective-permute-done.27.refs_7_.refs_17_.refs_16_ = bf16[4,192,384]{2,1,0:T(8,128)(2,1)S(1)} collective-permute-done((bf16[4,192,384]{2,1,0:T(8,128)(2,1)S(1)}, bf16[4,192,384]{2,1,0:T(8,128)(2,1)S(1)}, u32[]{:S(2)}, u32[]{:S(2)}) %collective-permute-start.27) | collective-permute-done | bytes 589856 | tf_op jit(solution)/shard_map/ppermute | solution.py:135
  163.1 22.4 %shard_map.141 = (bf16[1536,1024]{1,0:T(8,128)(2,1)}, bf16[1536,1024]{1,0:T(8,128)(2,1)}, f32[1536,1]{1,0:T(8,128)S(1)}, bf16[4,4,240,384]{3,2,1,0:T(8,128)(2,1)}, bf16[4,4,240,384]{3,2,1,0:T(8,128)(2,1)}) custom-call(s32[32,3]{1,0:T(8,128)S(1)} %stack.500.refs_0_, bf16[1024,768]{1,0:T(8,128)(2,1)} %copy-done.67, bf16[1024,768]{1,0:T(8,128)(2,1)} %refs_4_.1, ...), custom_call_target="tpu_custom_call" | custom-call | flops 9663676416 | bytes 16777216 | tf_op jit(solution)/shard_map/pallas_call | solution.py:213
  195.4 14.8 %shard_map.142 = (f32[1024,768]{1,0:T(8,128)}, bf16[1024,768]{1,0:T(8,128)(2,1)}, f32[8,768]{1,0:T(8,128)S(1)}) custom-call(s32[32,3]{1,0:T(8,128)S(1)} %stack.500.refs_0_, bf16[1536,1024]{1,0:T(8,128)(2,1)} %get-tuple-element.54.refs_1_, bf16[1536,1024]{1,0:T(8,128)(2,1)} %get-tuple-element.55.refs_2_, f32[1024,768]{1,0:T(8,128)} %copy-done.1, ...), custom_call_target="tpu_custom_call" | custom-call | flops 4831838208 | bytes 20971520 | tf_op jit(solution)/shard_map/pallas_call | solution.py:213
  211.7 5.1 %shard_map.143 = (bf16[768,1024]{1,0:T(8,128)(2,1)S(1)}, bf16[4,4,240,384]{3,2,1,0:T(8,128)(2,1)S(1)}, bf16[4,4,240,384]{3,2,1,0:T(8,128)(2,1)}) custom-call(s32[32,3]{1,0:T(8,128)S(1)} %stack.500.refs_0_, bf16[384,1024]{1,0:T(8,128)(2,1)S(1)} %copy-done.31, bf16[384,1024]{1,0:T(8,128)(2,1)S(1)} %copy-done.29, ...), custom_call_target="tpu_custom_call", output_to_operand_aliasing={{1}: (4, {}), {2}: (5, {})} | custom-call | flops 2415919104 | bytes 8388608 | tf_op jit(solution)/shard_map/pallas_call | solution.py:213
  224.5 12.7 %collective-permute-done.36.refs_7_ = bf16[2,4,192,384]{3,2,1,0:T(8,128)(2,1)S(1)} collective-permute-done((bf16[2,4,192,384]{3,2,1,0:T(8,128)(2,1)}, bf16[2,4,192,384]{3,2,1,0:T(8,128)(2,1)S(1)}, u32[]{:S(2)}, u32[]{:S(2)}) %collective-permute-start.36) | collective-permute-done | bytes 1179680 | tf_op jit(solution)/shard_map/ppermute | solution.py:135
  242.4 3.4 add_convert_fusion
  247.7 6.2 %collective-permute-done.37.refs_7_ = bf16[4,192,384]{2,1,0:T(8,128)(2,1)S(1)} collective-permute-done((bf16[4,192,384]{2,1,0:T(8,128)(2,1)}, bf16[4,192,384]{2,1,0:T(8,128)(2,1)S(1)}, u32[]{:S(2)}, u32[]{:S(2)}) %collective-permute-start.37) | collective-permute-done | bytes 589856 | tf_op jit(solution)/shard_map/ppermute | solution.py:135
  258.0 13.0 %shard_map.145 = (bf16[1152,1024]{1,0:T(8,128)(2,1)}, f32[1152,1]{1,0:T(8,128)S(1)}) custom-call(bf16[2304,1024]{1,0:T(8,128)(2,1)} %copy-done, bf16[2304,1024]{1,0:T(8,128)(2,1)} %copy-done, bf16[2304,1024]{1,0:T(8,128)(2,1)} %copy-done, bf16[768,1024]{1,0:T(8,128)(2,1)S(1)} %copy-done.19, f32[16,1024]{1,0:T(8,128)S(1)} %copy-done.66, ...), custom_call_target="tpu_custom_call" | custom-call | flops 4026531840 | bytes 16777216 | tf_op jit(solution)/shard_map/pallas_call | solution.py:213
  274.5 11.7 %shard_map.146 = (bf16[1152,1024]{1,0:T(8,128)(2,1)S(1)}, f32[1152,1]{1,0:T(8,128)S(1)}) custom-call(bf16[2304,1024]{1,0:T(8,128)(2,1)} %copy-done, bf16[2304,1024]{1,0:T(8,128)(2,1)} %copy-done, bf16[2304,1024]{1,0:T(8,128)(2,1)} %copy-done, bf16[768,1024]{1,0:T(8,128)(2,1)S(1)} %copy-done.19, f32[16,1024]{1,0:T(8,128)S(1)} %copy-done.64, ...), custom_call_target="tpu_custom_call" | custom-call | flops 4026531840 | bytes 16777216 | tf_op jit(solution)/shard_map/pallas_call | solution.py:213
  287.0 6.9 %shard_map.147 = (bf16[4,4,144,384]{3,2,1,0:T(8,128)(2,1)S(1)}, bf16[4,4,144,384]{3,2,1,0:T(8,128)(2,1)}) custom-call(s32[32,3]{1,0:T(8,128)S(1)} %stack.500.refs_0_, bf16[1152,1024]{1,0:T(8,128)(2,1)S(1)} %copy-done.53, bf16[1152,1024]{1,0:T(8,128)(2,1)S(1)} %get-tuple-element.67.refs_2_, bf16[1024,768]{1,0:T(8,128)(2,1)S(1)} %copy-done.71, ...), custom_call_target="tpu_custom_call" | custom-call | flops 3623878656 | bytes 12582912 | tf_op jit(solution)/shard_map/pallas_call | solution.py:213
  301.2 11.6 %shard_map.144 = bf16[1024,768]{1,0:T(8,128)(2,1)} custom-call(s32[32,3]{1,0:T(8,128)S(1)} %stack.500.refs_0_, bf16[1536,1024]{1,0:T(8,128)(2,1)} %get-tuple-element.50.refs_1_, bf16[1536,1024]{1,0:T(8,128)(2,1)} %get-tuple-element.52.refs_2_, f32[1024,768]{1,0:T(8,128)} %copy-done.1, f32[8,768]{1,0:T(8,128)S(1)} %copy-done.62, ...), custom_call_target="tpu_custom_call" | custom-call | flops 4831838208 | bytes 16777216 | tf_op jit(solution)/shard_map/pallas_call | solution.py:213
  312.9 3.0 collective-permute-done.49
  319.5 11.1 %shard_map.148 = (bf16[1024,768]{1,0:T(8,128)(2,1)}, f32[8,768]{1,0:T(8,128)S(1)}) custom-call(s32[32,3]{1,0:T(8,128)S(1)} %stack.500.refs_0_, bf16[1152,1024]{1,0:T(8,128)(2,1)S(1)} %copy-done.53, bf16[1152,1024]{1,0:T(8,128)(2,1)S(1)} %get-tuple-element.67.refs_2_, bf16[1024,768]{1,0:T(8,128)(2,1)S(1)} %copy-done.21, ...), custom_call_target="tpu_custom_call" | custom-call | flops 3623878656 | bytes 16777216 | tf_op jit(solution)/shard_map/pallas_call | solution.py:213
  342.3 7.8 %collective-permute-done.55 = bf16[2,4,1,384]{3,1,0,2:T(4,128)(2,1)S(1)} collective-permute-done((bf16[2,4,1,384]{3,1,0,2:T(4,128)(2,1)S(1)}, bf16[2,4,1,384]{3,1,0,2:T(4,128)(2,1)S(1)}, u32[]{:S(2)}, u32[]{:S(2)}) %collective-permute-start.55) | collective-permute-done | bytes 6176 | tf_op jit(solution)/shard_map/ppermute | solution.py:135
  355.5 4.5 %collective-permute-done.56 = bf16[4,1,384]{2,0,1:T(4,128)(2,1)S(1)} collective-permute-done((bf16[4,1,384]{2,0,1:T(4,128)(2,1)S(1)}, bf16[4,1,384]{2,0,1:T(4,128)(2,1)S(1)}, u32[]{:S(2)}, u32[]{:S(2)}) %collective-permute-start.56) | collective-permute-done | bytes 3104 | tf_op jit(solution)/shard_map/ppermute | solution.py:135
  363.6 3.2 collective-permute-start.57
  (447 shorter events, 123.9 us)
Async XLA Ops:
  13.2 15.9 %collective-permute-start.1 = (bf16[160,384]{1,0:T(8,128)(2,1)S(1)}, bf16[160,384]{1,0:T(8,128)(2,1)S(1)}, u32[]{:S(2)}, u32[]{:S(2)}) collective-permute-start(bf16[160,384]{1,0:T(8,128)(2,1)S(1)} %fusion.18), channel_id=1, source_target_pairs={{0,8},{1,9},{2,10},{3,11},{4,12},{5,13},{6,14},{7,15},{8,16},{9,17... | collective-permute-start | bytes 368648 | tf_op jit(solution)/shard_map/ppermute | solution.py:135
  14.7 14.4 %collective-permute-start.3 = (bf16[160,384]{1,0:T(8,128)(2,1)S(1)}, bf16[160,384]{1,0:T(8,128)(2,1)S(1)}, u32[]{:S(2)}, u32[]{:S(2)}) collective-permute-start(bf16[160,384]{1,0:T(8,128)(2,1)S(1)} %fusion.18), channel_id=1, source_target_pairs={{0,24},{1,25},{2,26},{3,27},{4,28},{5,29},{6,30},{7,31},{8,0},{9,1... | collective-permute-start | bytes 368648 | tf_op jit(solution)/shard_map/ppermute | solution.py:135
  17.3 19.7 %collective-permute-start.13 = (bf16[240,384]{1,0:T(8,128)(2,1)S(1)}, bf16[240,384]{1,0:T(8,128)(2,1)S(1)}, u32[]{:S(2)}, u32[]{:S(2)}) collective-permute-start(bf16[240,384]{1,0:T(8,128)(2,1)S(1)} %get-tuple-element.150), channel_id=1, source_target_pairs={{0,16},{1,17},{2,18},{3,19},{4,20},{5,21},{6,22},{7,23},{8,24},{9,... | collective-permute-start | bytes 552968 | tf_op jit(solution)/shard_map/ppermute | solution.py:135
  17.4 19.6 %collective-permute-start.12 = (bf16[240,384]{1,0:T(8,128)(2,1)S(1)}, bf16[240,384]{1,0:T(8,128)(2,1)S(1)}, u32[]{:S(2)}, u32[]{:S(2)}) collective-permute-start(bf16[240,384]{1,0:T(8,128)(2,1)S(1)} %get-tuple-element.150), channel_id=1, source_target_pairs={{0,8},{1,9},{2,10},{3,11},{4,12},{5,13},{6,14},{7,15},{8,16},{9,17... | collective-permute-start | bytes 552968 | tf_op jit(solution)/shard_map/ppermute | solution.py:135
  22.6 14.5 %collective-permute-start.14 = (bf16[240,384]{1,0:T(8,128)(2,1)S(1)}, bf16[240,384]{1,0:T(8,128)(2,1)S(1)}, u32[]{:S(2)}, u32[]{:S(2)}) collective-permute-start(bf16[240,384]{1,0:T(8,128)(2,1)S(1)} %get-tuple-element.150), channel_id=1, source_target_pairs={{0,24},{1,25},{2,26},{3,27},{4,28},{5,29},{6,30},{7,31},{8,0},{9,1... | collective-permute-start | bytes 552968 | tf_op jit(solution)/shard_map/ppermute | solution.py:135
  29.2 26.7 %collective-permute-start.4 = (bf16[4,160,384]{2,1,0:T(8,128)(2,1)S(1)}, bf16[4,160,384]{2,1,0:T(8,128)(2,1)}, u32[]{:S(2)}, u32[]{:S(2)}) collective-permute-start(bf16[4,160,384]{2,1,0:T(8,128)(2,1)S(1)} %pad_maximum_fusion.2.refs_1_.refs_4_.refs_6_), channel_id=1, source_target_pairs={{0,4},{1,3},{2,6},{3,1},{4,0},{5,7},{6,2},{7,5},{8,12},{9,11},{10,... | collective-permute-start | bytes 1474568 | tf_op jit(solution)/shard_map/ppermute | solution.py:135
  37.2 26.2 %collective-permute-start.15 = (bf16[4,240,384]{2,1,0:T(8,128)(2,1)S(1)}, bf16[4,240,384]{2,1,0:T(8,128)(2,1)S(1)}, u32[]{:S(2)}, u32[]{:S(2)}) collective-permute-start(bf16[4,240,384]{2,1,0:T(8,128)(2,1)S(1)} %pad_maximum_fusion.refs_5_.refs_4_.refs_6_), channel_id=1, source_target_pairs={{0,4},{1,3},{2,6},{3,1},{4,0},{5,7},{6,2},{7,5},{8,12},{9,11},{10,... | collective-permute-start | bytes 2211848 | tf_op jit(solution)/shard_map/ppermute | solution.py:135
  47.0 18.6 %collective-permute-start.7 = (bf16[4,160,384]{2,1,0:T(8,128)(2,1)S(1)}, bf16[4,160,384]{2,1,0:T(8,128)(2,1)}, u32[]{:S(2)}, u32[]{:S(2)}) collective-permute-start(bf16[4,160,384]{2,1,0:T(8,128)(2,1)S(1)} %pad_maximum_fusion.2.refs_1_.refs_4_.refs_6_), channel_id=1, source_target_pairs={{0,1},{1,0},{2,3},{3,2},{4,5},{5,4},{6,7},{7,6},{8,9},{9,8},{10,11... | collective-permute-start | bytes 1474568 | tf_op jit(solution)/shard_map/ppermute | solution.py:135
  47.6 18.1 %collective-permute-start.5 = (bf16[4,160,384]{2,1,0:T(8,128)(2,1)S(1)}, bf16[4,160,384]{2,1,0:T(8,128)(2,1)}, u32[]{:S(2)}, u32[]{:S(2)}) collective-permute-start(bf16[4,160,384]{2,1,0:T(8,128)(2,1)S(1)} %pad_maximum_fusion.2.refs_1_.refs_4_.refs_6_), channel_id=1, source_target_pairs={{0,2},{1,5},{2,0},{3,7},{4,6},{5,1},{6,4},{7,3},{8,10},{9,13},{10,... | collective-permute-start | bytes 1474568 | tf_op jit(solution)/shard_map/ppermute | solution.py:135
  63.4 18.9 %collective-permute-start.17 = (bf16[4,240,384]{2,1,0:T(8,128)(2,1)S(1)}, bf16[4,240,384]{2,1,0:T(8,128)(2,1)S(1)}, u32[]{:S(2)}, u32[]{:S(2)}) collective-permute-start(bf16[4,240,384]{2,1,0:T(8,128)(2,1)S(1)} %collective-permute-done.15.refs_6_.refs_5_.refs_7_), channel_id=1, source_target_pairs={{0,2},{1,5},{2,0},{3,7},{4,6},{5,1},{6,4},{7,3},{8,10},{9,13},{10,... | collective-permute-start | bytes 2211848 | tf_op jit(solution)/shard_map/ppermute | solution.py:135
  66.9 16.9 %collective-permute-start.10 = (bf16[4,160,384]{2,1,0:T(8,128)(2,1)}, bf16[4,160,384]{2,1,0:T(8,128)(2,1)}, u32[]{:S(2)}, u32[]{:S(2)}) collective-permute-start(bf16[4,160,384]{2,1,0:T(8,128)(2,1)} %collective-permute-done.6.refs_4_.refs_7_.refs_9_), channel_id=1, source_target_pairs={{0,1},{1,0},{2,3},{3,2},{4,5},{5,4},{6,7},{7,6},{8,9},{9,8},{10,11... | collective-permute-start | bytes 1474568 | tf_op jit(solution)/shard_map/ppermute | solution.py:135
  74.3 40.7 %collective-permute-start.18 = (bf16[4,240,384]{2,1,0:T(8,128)(2,1)S(1)}, bf16[4,240,384]{2,1,0:T(8,128)(2,1)S(1)}, u32[]{:S(2)}, u32[]{:S(2)}) collective-permute-start(bf16[4,240,384]{2,1,0:T(8,128)(2,1)S(1)} %pad_maximum_fusion.refs_5_.refs_4_.refs_6_), channel_id=1, source_target_pairs={{0,1},{1,0},{2,3},{3,2},{4,5},{5,4},{6,7},{7,6},{8,9},{9,8},{10,11... | collective-permute-start | bytes 2211848 | tf_op jit(solution)/shard_map/ppermute | solution.py:135
  74.3 40.7 %collective-permute-start.19 = (bf16[4,240,384]{2,1,0:T(8,128)(2,1)S(1)}, bf16[4,240,384]{2,1,0:T(8,128)(2,1)S(1)}, u32[]{:S(2)}, u32[]{:S(2)}) collective-permute-start(bf16[4,240,384]{2,1,0:T(8,128)(2,1)S(1)} %collective-permute-done.15.refs_6_.refs_5_.refs_7_), channel_id=1, source_target_pairs={{0,1},{1,0},{2,3},{3,2},{4,5},{5,4},{6,7},{7,6},{8,9},{9,8},{10,11... | collective-permute-start | bytes 2211848 | tf_op jit(solution)/shard_map/ppermute | solution.py:135
  74.8 40.2 %collective-permute-start.20 = (bf16[4,240,384]{2,1,0:T(8,128)(2,1)S(1)}, bf16[4,240,384]{2,1,0:T(8,128)(2,1)S(1)}, u32[]{:S(2)}, u32[]{:S(2)}) collective-permute-start(bf16[4,240,384]{2,1,0:T(8,128)(2,1)S(1)} %collective-permute-done.16.refs_7_.refs_6_.refs_8_), channel_id=1, source_target_pairs={{0,1},{1,0},{2,3},{3,2},{4,5},{5,4},{6,7},{7,6},{8,9},{9,8},{10,11... | collective-permute-start | bytes 2211848 | tf_op jit(solution)/shard_map/ppermute | solution.py:135
  82.2 32.8 %collective-permute-start.21 = (bf16[4,240,384]{2,1,0:T(8,128)(2,1)S(1)}, bf16[4,240,384]{2,1,0:T(8,128)(2,1)S(1)}, u32[]{:S(2)}, u32[]{:S(2)}) collective-permute-start(bf16[4,240,384]{2,1,0:T(8,128)(2,1)S(1)} %collective-permute-done.17.refs_8_.refs_7_.refs_9_), channel_id=1, source_target_pairs={{0,1},{1,0},{2,3},{3,2},{4,5},{5,4},{6,7},{7,6},{8,9},{9,8},{10,11... | collective-permute-start | bytes 2211848 | tf_op jit(solution)/shard_map/ppermute | solution.py:135
  83.8 61.1 %collective-permute-start.25 = (bf16[4,192,384]{2,1,0:T(8,128)(2,1)S(1)}, bf16[4,192,384]{2,1,0:T(8,128)(2,1)S(1)}, u32[]{:S(2)}, u32[]{:S(2)}) collective-permute-start(bf16[4,192,384]{2,1,0:T(8,128)(2,1)S(1)} %pad_maximum_fusion.1.refs_4_.refs_14_.refs_13_), channel_id=1, source_target_pairs={{0,4},{1,3},{2,6},{3,1},{4,0},{5,7},{6,2},{7,5},{8,12},{9,11},{10,... | collective-permute-start | bytes 1769480 | tf_op jit(solution)/shard_map/ppermute | solution.py:135
  144.7 41.7 %collective-permute-start.32 = (bf16[4,4,192,384]{3,2,1,0:T(8,128)(2,1)}, bf16[4,4,192,384]{3,2,1,0:T(8,128)(2,1)S(1)}, u32[]{:S(2)}, u32[]{:S(2)}) collective-permute-start(bf16[4,4,192,384]{3,2,1,0:T(8,128)(2,1)} %get-tuple-element.56), channel_id=1, source_target_pairs={{0,1},{1,0},{2,3},{3,2},{4,5},{5,4},{6,7},{7,6},{8,9},{9,8},{10,11... | collective-permute-start | bytes 7077896 | tf_op jit(solution)/shard_map/ppermute | solution.py:135
  144.9 16.2 %collective-permute-start.27 = (bf16[4,192,384]{2,1,0:T(8,128)(2,1)S(1)}, bf16[4,192,384]{2,1,0:T(8,128)(2,1)S(1)}, u32[]{:S(2)}, u32[]{:S(2)}) collective-permute-start(bf16[4,192,384]{2,1,0:T(8,128)(2,1)S(1)} %collective-permute-done.25.refs_5_.refs_15_.refs_14_), channel_id=1, source_target_pairs={{0,2},{1,5},{2,0},{3,7},{4,6},{5,1},{6,4},{7,3},{8,10},{9,13},{10,... | collective-permute-start | bytes 1769480 | tf_op jit(solution)/shard_map/ppermute | solution.py:135
  146.9 14.2 %collective-permute-start.28 = (bf16[4,192,384]{2,1,0:T(8,128)(2,1)S(1)}, bf16[4,192,384]{2,1,0:T(8,128)(2,1)S(1)}, u32[]{:S(2)}, u32[]{:S(2)}) collective-permute-start(bf16[4,192,384]{2,1,0:T(8,128)(2,1)S(1)} %pad_maximum_fusion.1.refs_4_.refs_14_.refs_13_), channel_id=1, source_target_pairs={{0,1},{1,0},{2,3},{3,2},{4,5},{5,4},{6,7},{7,6},{8,9},{9,8},{10,11... | collective-permute-start | bytes 1769480 | tf_op jit(solution)/shard_map/ppermute | solution.py:135
  146.9 14.2 %collective-permute-start.29 = (bf16[4,192,384]{2,1,0:T(8,128)(2,1)S(1)}, bf16[4,192,384]{2,1,0:T(8,128)(2,1)S(1)}, u32[]{:S(2)}, u32[]{:S(2)}) collective-permute-start(bf16[4,192,384]{2,1,0:T(8,128)(2,1)S(1)} %collective-permute-done.25.refs_5_.refs_15_.refs_14_), channel_id=1, source_target_pairs={{0,1},{1,0},{2,3},{3,2},{4,5},{5,4},{6,7},{7,6},{8,9},{9,8},{10,11... | collective-permute-start | bytes 1769480 | tf_op jit(solution)/shard_map/ppermute | solution.py:135
  216.9 25.5 %collective-permute-start.33 = (bf16[4,4,240,384]{3,2,1,0:T(8,128)(2,1)}, bf16[4,4,240,384]{3,2,1,0:T(8,128)(2,1)}, u32[]{:S(2)}, u32[]{:S(2)}) collective-permute-start(bf16[4,4,240,384]{3,2,1,0:T(8,128)(2,1)} %get-tuple-element.61), channel_id=1, source_target_pairs={{0,1},{1,0},{2,3},{3,2},{4,5},{5,4},{6,7},{7,6},{8,9},{9,8},{10,11... | collective-permute-start | bytes 8847368 | tf_op jit(solution)/shard_map/ppermute | solution.py:135
  220.7 16.4 %collective-permute-start.36 = (bf16[2,4,192,384]{3,2,1,0:T(8,128)(2,1)}, bf16[2,4,192,384]{3,2,1,0:T(8,128)(2,1)S(1)}, u32[]{:S(2)}, u32[]{:S(2)}) collective-permute-start(bf16[2,4,192,384]{3,2,1,0:T(8,128)(2,1)} %slice.267), channel_id=1, source_target_pairs={{0,2},{1,5},{2,0},{3,7},{4,6},{5,1},{6,4},{7,3},{8,10},{9,13},{10,... | collective-permute-start | bytes 3538952 | tf_op jit(solution)/shard_map/ppermute | solution.py:135
  246.1 26.5 %collective-permute-start.34 = (bf16[2,4,240,384]{3,2,1,0:T(8,128)(2,1)S(1)}, bf16[2,4,240,384]{3,2,1,0:T(8,128)(2,1)S(1)}, u32[]{:S(2)}, u32[]{:S(2)}) collective-permute-start(bf16[2,4,240,384]{3,2,1,0:T(8,128)(2,1)S(1)} %slice.265), channel_id=1, source_target_pairs={{0,2},{1,5},{2,0},{3,7},{4,6},{5,1},{6,4},{7,3},{8,10},{9,13},{10,... | collective-permute-start | bytes 4423688 | tf_op jit(solution)/shard_map/ppermute | solution.py:135
  254.1 17.7 %collective-permute-start.40 = (bf16[192,384]{1,0:T(8,128)(2,1)S(1)}, bf16[192,384]{1,0:T(8,128)(2,1)S(1)}, u32[]{:S(2)}, u32[]{:S(2)}) collective-permute-start(bf16[192,384]{1,0:T(8,128)(2,1)S(1)} %get-tuple-element.129), channel_id=1, source_target_pairs={{0,8},{1,9},{2,10},{3,11},{4,12},{5,13},{6,14},{7,15},{8,16},{9,17... | collective-permute-start | bytes 442376 | tf_op jit(solution)/shard_map/ppermute | solution.py:135
  254.8 17.0 %collective-permute-start.39 = (bf16[192,384]{1,0:T(8,128)(2,1)S(1)}, bf16[192,384]{1,0:T(8,128)(2,1)S(1)}, u32[]{:S(2)}, u32[]{:S(2)}) collective-permute-start(bf16[192,384]{1,0:T(8,128)(2,1)S(1)} %get-tuple-element.130), channel_id=1, source_target_pairs={{0,16},{1,17},{2,18},{3,19},{4,20},{5,21},{6,22},{7,23},{8,24},{9,... | collective-permute-start | bytes 442376 | tf_op jit(solution)/shard_map/ppermute | solution.py:135
  255.9 15.9 %collective-permute-start.38 = (bf16[192,384]{1,0:T(8,128)(2,1)S(1)}, bf16[192,384]{1,0:T(8,128)(2,1)S(1)}, u32[]{:S(2)}, u32[]{:S(2)}) collective-permute-start(bf16[192,384]{1,0:T(8,128)(2,1)S(1)} %get-tuple-element.131), channel_id=1, source_target_pairs={{0,24},{1,25},{2,26},{3,27},{4,28},{5,29},{6,30},{7,31},{8,0},{9,1... | collective-permute-start | bytes 442376 | tf_op jit(solution)/shard_map/ppermute | solution.py:135
  274.2 21.1 %collective-permute-start.35 = (bf16[4,240,384]{2,1,0:T(8,128)(2,1)}, bf16[4,240,384]{2,1,0:T(8,128)(2,1)}, u32[]{:S(2)}, u32[]{:S(2)}) collective-permute-start(bf16[4,240,384]{2,1,0:T(8,128)(2,1)} %slice_bitcast_fusion.1), channel_id=1, source_target_pairs={{0,4},{1,3},{2,6},{3,1},{4,0},{5,7},{6,2},{7,5},{8,12},{9,11},{10,... | collective-permute-start | bytes 2211848 | tf_op jit(solution)/shard_map/ppermute | solution.py:135
  295.2 24.2 %collective-permute-start.41 = (bf16[4,4,144,384]{3,2,1,0:T(8,128)(2,1)}, bf16[4,4,144,384]{3,2,1,0:T(8,128)(2,1)S(1)}, u32[]{:S(2)}, u32[]{:S(2)}) collective-permute-start(bf16[4,4,144,384]{3,2,1,0:T(8,128)(2,1)} %get-tuple-element.70), channel_id=1, source_target_pairs={{0,1},{1,0},{2,3},{3,2},{4,5},{5,4},{6,7},{7,6},{8,9},{9,8},{10,11... | collective-permute-start | bytes 5308424 | tf_op jit(solution)/shard_map/ppermute | solution.py:135
  296.8 16.1 %collective-permute-start.48 = (bf16[240,384]{1,0:T(8,128)(2,1)S(1)}, bf16[240,384]{1,0:T(8,128)(2,1)S(1)}, u32[]{:S(2)}, u32[]{:S(2)}) collective-permute-start(bf16[240,384]{1,0:T(8,128)(2,1)S(1)} %get-tuple-element.124), channel_id=1, source_target_pairs={{0,24},{1,25},{2,26},{3,27},{4,28},{5,29},{6,30},{7,31},{8,0},{9,1... | collective-permute-start | bytes 552968 | tf_op jit(solution)/shard_map/ppermute | solution.py:135
  298.0 14.8 %collective-permute-start.50 = (bf16[240,384]{1,0:T(8,128)(2,1)S(1)}, bf16[240,384]{1,0:T(8,128)(2,1)S(1)}, u32[]{:S(2)}, u32[]{:S(2)}) collective-permute-start(bf16[240,384]{1,0:T(8,128)(2,1)S(1)} %get-tuple-element.125), channel_id=1, source_target_pairs={{0,8},{1,9},{2,10},{3,11},{4,12},{5,13},{6,14},{7,15},{8,16},{9,17... | collective-permute-start | bytes 552968 | tf_op jit(solution)/shard_map/ppermute | solution.py:135
  299.1 16.8 %collective-permute-start.49 = (bf16[240,384]{1,0:T(8,128)(2,1)S(1)}, bf16[240,384]{1,0:T(8,128)(2,1)S(1)}, u32[]{:S(2)}, u32[]{:S(2)}) collective-permute-start(bf16[240,384]{1,0:T(8,128)(2,1)S(1)} %get-tuple-element.126), channel_id=1, source_target_pairs={{0,16},{1,17},{2,18},{3,19},{4,20},{5,21},{6,22},{7,23},{8,24},{9,... | collective-permute-start | bytes 552968 | tf_op jit(solution)/shard_map/ppermute | solution.py:135
  317.7 21.5 %collective-permute-start.53 = (f32[192,192]{1,0:T(8,128)}, f32[192,192]{1,0:T(8,128)}, u32[]{:S(2)}, u32[]{:S(2)}) collective-permute-start(f32[192,192]{1,0:T(8,128)} %fusion.12), channel_id=1, source_target_pairs={{0,1},{1,0},{2,3},{3,2},{4,5},{5,4},{6,7},{7,6},{8,9},{9,8},{10,11... | collective-permute-start | bytes 442376 | tf_op jit(solution)/shard_map/ppermute | solution.py:135
  (137 other events, 1526.3 us)

commit v4 on v3

--- a/solution.py
+++ b/solution.py
@@ -118,17 +118,14 @@
 
     def origins(self):
         z0, x0, y0, c0 = self.here()
-        rows = []
-        for other in range(2):
-            c = (c0 + other) % 2
-            for kb in range(self.X):
-                for ka in range(self.X):
-                    x = (x0 + self.X - jnp.where(c == 0, ka, kb)) % self.X
-                    y = (y0 + self.Y - jnp.where(c == 0, kb, ka)) % self.Y
-                    for kz in range(self.Z):
-                        z = (z0 + self.Z - kz) % self.Z
-                        rows.append(jnp.stack([z * self.X + x, y, c]))
-        return jnp.stack(rows).astype(jnp.int32)
+        side, deep = self.X, self.Z
+        index = jnp.arange(2 * side * side * deep, dtype=jnp.int32)
+        kz, ka, kb = index % deep, index // deep % side, index // (deep * side) % side
+        c = (c0 + index // (deep * side * side)) % 2
+        x = (x0 + side - jnp.where(c == 0, ka, kb)) % side
+        y = (y0 + side - jnp.where(c == 0, kb, ka)) % side
+        z = (z0 + deep - kz) % deep
+        return jnp.stack([z * side + x, y, c], axis=1).astype(jnp.int32)
 
 
 def send(values, perm):
@@ -192,6 +189,8 @@
 ROOT_HALF = 0.7071067811865476
 ROOT_TAU = 0.3989422804014327
 MIB = 1024 * 1024
+SCALE = 1.0
+BACK = 3
 
 
 def cdf_pdf(u):
@@ -204,7 +203,7 @@
     return jnp.where(u < 0, upper, 1.0 - upper), ROOT_TAU * bell
 
 
-def call(kernel, grid, in_specs, out_specs, out_shape, scratch, vmem, flops, bytes_accessed, operands, prefetch=0, aliases=None, after=()):
+def call(kernel, grid, in_specs, out_specs, out_shape, scratch, vmem, us, operands, prefetch=0, aliases=None, after=()):
     first, count = len(operands), len(after)
 
     def body(*refs):
@@ -222,11 +221,11 @@
         out_shape=out_shape,
         input_output_aliases=aliases or {},
         compiler_params=pltpu.CompilerParams(vmem_limit_bytes=vmem * MIB),
-        cost_estimate=pl.CostEstimate(flops=flops, bytes_accessed=bytes_accessed, transcendentals=0),
+        cost_estimate=pl.CostEstimate(flops=int(us * SCALE * 1.0e9), bytes_accessed=int(us * SCALE * 3.0e6), transcendentals=0),
     )(*operands, *after)
 
 
-ANYWHERE = pl.BlockSpec(memory_space=pl.ANY)
+ANYWHERE = pl.BlockSpec(memory_space=pltpu.HBM)
 
 
 def full(shape):
@@ -326,14 +325,13 @@
             pltpu.SemaphoreType.DMA((n * deep,)),
         ],
         16,
-        1000,
-        1000,
+        3,
         (places, *pieces),
         prefetch=1,
     )
 
 
-def project_qkv(tokens, vecs, bias, pieces, places, shape):
+def project_qkv(tokens, vecs, bias, pieces, places, shape, after=()):
     rows, width = tokens.shape
     half, wide = shape
     n, block, steps = len(pieces), 256, 3 * width // 256
@@ -365,10 +363,10 @@
             pltpu.SemaphoreType.DMA((n * pieces[0].shape[0],)),
         ],
         32,
-        6 * rows * width * width,
-        12 * MIB,
+        9,
         (places, tokens, vecs, bias, *pieces),
         prefetch=1,
+        after=after,
     )
 
 
@@ -432,14 +430,13 @@
         [jax.ShapeDtypeStruct((half, rows), BF), jax.ShapeDtypeStruct((16, rows), F32)],
         [pltpu.VMEM((half, rows + QB), BF), pltpu.VMEM((half, rows + QB), BF)],
         40,
-        4 * rows * KB * half * 4,
-        8 * MIB,
+        6,
         (qkv_t, qkv_t, qkv_t, seg_row, seg_col),
         after=after,
     )
 
 
-def project_out(o_parts, tokens, vecs, pieces, places, rows_piece, after=()):
+def project_out(o_parts, tokens, vecs, pieces, places, low, rows_piece, after=()):
     rows, width = tokens.shape
     n, block = len(pieces), 256
 
@@ -448,7 +445,7 @@
 
         @pl.when(pl.program_id(0) == 0)
         def first():
-            wait_all(load_pieces(at, parts, 0, rows_piece, weight, sem))
+            wait_all(load_pieces(at, parts, low, rows_piece, weight, sem))
 
         both = jnp.concatenate([o_a[...], o_b[...]], axis=0)
         mid = tok[...].astype(F32) + tn(both, weight[...]) + vec[4:5, :]
@@ -464,8 +461,7 @@
         [jax.ShapeDtypeStruct((rows, width), F32), jax.ShapeDtypeStruct((rows, width), BF)],
         [pltpu.VMEM((width, width), BF), pltpu.SemaphoreType.DMA((n * pieces[0].shape[0],))],
         32,
-        2 * rows * width * width,
-        12 * MIB,
+        5,
         (places, *o_parts, tokens, vecs, *pieces),
         prefetch=1,
         after=after,
@@ -498,7 +494,7 @@
         grad = (grad_act * (cdf + pre * pdf)).astype(BF)
         act_out[...] = act
         grad_out[...] = grad
-        sum_out[...] = jnp.sum(grad.astype(F32), axis=1, keepdims=True)
+        sum_out[...] = nt(jnp.ones((8, rows), BF), grad)
         d_down[here, :] = nn(act, cot_ref[...]).astype(BF)
         d_up[here, :] = nn(grad, hid[...]).astype(BF)
 
@@ -514,19 +510,18 @@
         kernel,
         (units // block,),
         [full((rows, width)), full((rows, width)), rows_of((block, 1))] + [ANYWHERE] * n,
-        [rows_of((block, rows)), rows_of((block, rows)), rows_of((block, 1)), ANYWHERE, ANYWHERE],
+        [rows_of((block, rows)), rows_of((block, rows)), lanes_of((8, block)), ANYWHERE, ANYWHERE],
         [
             jax.ShapeDtypeStruct((units, rows), BF),
             jax.ShapeDtypeStruct((units, rows), BF),
-            jax.ShapeDtypeStruct((units, 1), F32),
+            jax.ShapeDtypeStruct((8, units), F32),
             piece_shape,
             piece_shape,
         ],
         [pltpu.VMEM((units, width), BF)] * 4
         + [pltpu.SemaphoreType.DMA((n * deep,))] * 2,
         48,
-        8 * rows * units * width,
-        16 * MIB,
+        22,
         (places, hidden, cot, bias, *pieces),
         prefetch=1,
         after=after,
@@ -577,22 +572,21 @@
         ],
         [pltpu.VMEM((units, width), BF)] * 2 + [pltpu.SemaphoreType.DMA((2, n * deep))],
         48,
-        4 * rows * units * width,
-        20 * MIB,
+        14 * BACK,
         (places, *grads, mid, cot, vecs, *groups[0][0], *groups[1][0]),
         prefetch=1,
         after=after,
     )
 
 
-def out_back(o_parts, grad_low, pieces, places, rows_piece, own, far, low, after=()):
+def out_back(o_parts, grad_low, pieces, places, low_in, rows_piece, own, far, low, after=()):
     rows, width = grad_low.shape
     half = width // PARTS
     n, deep = len(pieces), pieces[0].shape[0]
 
     def kernel(at, o_a, o_b, grad, own_in, far_in, *refs):
         parts, (do_ref, own_ref, far_ref, weight, d_weight, sem) = refs[:n], refs[n:]
-        copies = load_pieces(at, parts, 0, rows_piece, weight, sem)
+        copies = load_pieces(at, parts, low_in, rows_piece, weight, sem)
         d_weight[:half, :] = nn(o_a[...], grad[...]).astype(BF)
         d_weight[half:, :] = nn(o_b[...], grad[...]).astype(BF)
         wait_all(copies)
@@ -612,8 +606,7 @@
         ],
         [pltpu.VMEM((width, width), BF)] * 2 + [pltpu.SemaphoreType.DMA((n * deep,))],
         32,
-        4 * rows * width * width,
-        8 * MIB,
+        5 * BACK,
         (places, *o_parts, grad_low, own, far, *pieces),
         prefetch=1,
         aliases={4: 1, 5: 2},
@@ -660,7 +653,7 @@
             edge = KB // 4
             out[half : 2 * half, :] = d_keys[...][:, edge : edge + rows].astype(BF)
             out[2 * half : 3 * half, :] = d_values[...][:, edge : edge + rows].astype(BF)
-            sums[...] = jnp.sum(out[...].astype(F32), axis=1, keepdims=True)
+            sums[...] = nt(jnp.ones((8, rows), BF), out[...])
 
     return call(
         kernel,
@@ -672,12 +665,11 @@
             lanes_of((8, QB)),
             full(seg_col.shape),
         ],
-        [full((3 * half, rows)), full((3 * half, 1))],
-        [jax.ShapeDtypeStruct((3 * half, rows), BF), jax.ShapeDtypeStruct((3 * half, 1), F32)],
+        [full((3 * half, rows)), full((8, 3 * half))],
+        [jax.ShapeDtypeStruct((3 * half, rows), BF), jax.ShapeDtypeStruct((8, 3 * half), F32)],
         [pltpu.VMEM((half, rows + QB), BF)] * 2 + [pltpu.VMEM((half, rows + QB), F32)] * 2,
         48,
-        10 * rows * KB * half * 4,
-        16 * MIB,
+        12 * BACK,
         (qkv_t, qkv_t, qkv_t, do_t, lse, seg_row, seg_col),
         after=after,
     )
@@ -708,8 +700,7 @@
         [piece_shape, piece_shape],
         [pltpu.VMEM((count, width), BF), pltpu.SemaphoreType.DMA((2 * sites * topo.Z,))],
         32,
-        2 * rows * count * width,
-        12 * MIB,
+        7 * BACK,
         (places, *grad_parts, hidden),
         prefetch=1,
         after=after,
@@ -747,8 +738,7 @@
         [jax.ShapeDtypeStruct((rows, width), BF), jax.ShapeDtypeStruct((8, width), F32)],
         [pltpu.VMEM((count, width), BF), pltpu.SemaphoreType.DMA((n * pieces[0].shape[0],))],
         40,
-        2 * rows * count * width,
-        16 * MIB,
+        11 * BACK,
         (places, *grad_parts, tokens, grad_mid, vecs, *pieces),
         prefetch=1,
         after=after,
@@ -784,9 +774,65 @@
         jax.ShapeDtypeStruct((rows, width), BF),
         [pltpu.VMEM((units, width), BF)] * 2 + [pltpu.SemaphoreType.DMA((2, n * deep))],
         48,
-        4 * rows * units * width,
-        16 * MIB,
+        11 * BACK,
         (places, *acts, mid, vecs, *groups[0][0], *groups[1][0]),
+        prefetch=1,
+        after=after,
+    )
+
+
+def pack_vectors(sums_one, sums_two, sums_qkv, sums_up, places, topo, share, after=()):
+    width = sums_one.shape[1]
+    half = width // PARTS
+    hidden = PARTS * sums_up[0].shape[1]
+    group = hidden // (2 * topo.wide)
+    unit = group // 2
+    sites, deep, lanes = topo.X * topo.X, topo.Z, width // topo.Y
+    lines = 8 + hidden // width
+
+    def kernel(at, one, two, qkv_a, qkv_b, up_a, up_b, own, far, flat, ups, slots):
+        flat[0:2, :] = one[0:2, :]
+        for part, ref in enumerate((qkv_a, qkv_b)):
+            lane = slice(part * half, (part + 1) * half)
+            flat[2:3, lane] = ref[0:1, 0:half]
+            flat[3:4, lane] = ref[0:1, 2 * half : 3 * half]
+        flat[4:5, :] = two[2:3, :]
+        flat[5:7, :] = two[0:2, :]
+        flat[7:8, :] = two[3:4, :]
+        for k in range(2 * topo.wide):
+            for part, ref in enumerate((up_a, up_b)):
+                ups[0:1, k * group + part * unit : k * group + (part + 1) * unit] = ref[0:1, k * unit : (k + 1) * unit]
+        for line in range(8, lines):
+            flat[line : line + 1, :] = ups[0:1, (line - 8) * width : (line - 7) * width]
+        slots[...] = jnp.zeros_like(slots)
+        for j in range(topo.wide * topo.narrow):
+            done = 0
+            while done < share:
+                line, lane = divmod(j * share + done, width)
+                take = min(share - done, width - lane)
+                slots[j, 0:1, done : done + take] = flat[line : line + 1, lane : lane + take]
+                done += take
+        for j in range(2 * sites * deep):
+            i, k = divmod(j, deep)
+            slot = at[j, 0] * topo.narrow + at[j, 1] * 2 + at[j, 2]
+            target = own.at[i, k] if i < sites else far.at[i - sites, k]
+            target[...] = jnp.broadcast_to(slots[slot, 0:1, :], (16, lanes)).astype(BF)
+
+    shape = (sites, deep, 16, lanes)
+    return call(
+        kernel,
+        (1,),
+        [full(a.shape) for a in (sums_one, sums_two, *sums_qkv, *sums_up)],
+        [full(shape)] * 2,
+        [jax.ShapeDtypeStruct(shape, BF)] * 2,
+        [
+            pltpu.VMEM((16, width), F32),
+            pltpu.VMEM((8, hidden), F32),
+            pltpu.VMEM((topo.wide * topo.narrow, 8, lanes), F32),
+        ],
+        16,
+        3 * BACK,
+        (places, sums_one, sums_two, *sums_qkv, *sums_up),
         prefetch=1,
         after=after,
     )
@@ -799,6 +845,30 @@
     return result
 
 
+def tied(values, others):
+    return lax.optimization_barrier((values, tuple(others)))[0] if others else values
+
+
+class Spread:
+    def __init__(self, piece, topo):
+        self.topo, self.piece = topo, piece
+        self.coming = tuple(send(piece, topo.zp[k]) for k in range(1, topo.Z))
+
+    def along(self, others=()):
+        stack = tied(jnp.stack((self.piece, *self.coming)), others)
+        self.coming = tuple(send(stack, self.topo.ap[k]) for k in range(1, self.topo.X))
+        self.line = (stack, *self.coming)
+
+    def across(self, others=()):
+        self.near = tuple(send(p, self.topo.cp) for p in self.line)
+        line = tied(self.line, others)
+        self.coming = tuple(send(q, self.topo.bp[k]) for k in range(1, self.topo.X) for q in line)
+
+    def core(self, others=()):
+        coming = tied(self.coming, others)
+        self.pieces = [*self.line, *coming, *self.near, *[send(p, self.topo.cp) for p in coming]]
+
+
 class Chain:
     def __init__(self, own, far, topo):
         self.topo, self.held = topo, own
@@ -807,46 +877,35 @@
     def arrived(self):
         return tuple(self.coming)
 
-    def fold(self):
-        return total(self.held, *self.coming)
-
-    def across(self):
-        topo, side = self.topo, self.topo.X
-        own = self.fold().astype(BF).reshape(side, side, *self.held.shape[1:])
-        self.held = own[0]
-        self.coming = [send(own[k], topo.bp[side - k]) for k in range(1, side)]
-
-    def along(self):
-        topo, side = self.topo, self.topo.X
-        line = self.fold().astype(BF)
-        self.held = line[0]
-        self.coming = [send(line[k], topo.ap[side - k]) for k in range(1, side)]
-
-    def down(self):
-        topo, deep = self.topo, self.topo.Z
-        stack = self.fold().astype(BF)
-        self.held = stack[0]
-        self.coming = [send(stack[k], topo.zp[deep - k]) for k in range(1, deep)]
-
-    def result(self):
+    def fold(self, part=None):
+        terms = (self.held, *self.coming)
+        return total(*(terms if part is None else [t[part] for t in terms]))
+
+    def stage(self, count, perms, others):
+        self.held, self.coming = tied((self.held, self.coming), others)
+        self.held, *sent = [self.fold(k).astype(BF) for k in range(count)]
+        self.sent = tuple(sent)
+        self.coming = [send(values, perms[count - 1 - k]) for k, values in enumerate(sent)]
+
+    def across(self, others=()):
+        side = self.topo.X
+        split = lambda values: values.reshape(side, side, *values.shape[1:])
+        self.held, self.coming = split(self.held), [split(c) for c in self.coming]
+        self.stage(side, self.topo.bp, others)
+
+    def along(self, others=()):
+        self.stage(self.topo.X, self.topo.ap, others)
+
+    def down(self, others=()):
+        self.stage(self.topo.Z, self.topo.zp, others)
+
+    def result(self, others=()):
+        self.held, self.coming = tied((self.held, self.coming), others)
         return self.fold()
-
-
-def scatter(own, far, topo):
-    chain = Chain(own, far, topo)
-    chain.across()
-    chain.along()
-    chain.down()
-    return chain.result()
 
 
 def tail_rows(values, rows, lanes):
     return jnp.pad(values[None], ((0, rows - 1), (0, lanes - values.shape[0])))
-
-
-def vector_slots(places, topo):
-    slot = places[:, 0] * topo.narrow + places[:, 1] * 2 + places[:, 2]
-    return (slot[:, None] == jnp.arange(topo.wide * topo.narrow)[None]).astype(BF)
 
 
 def fits(topo, rows, width, hidden):
@@ -869,90 +928,86 @@
     core = topo.here()[3]
     shards = [qkv_weight.astype(BF).T, out_weight.astype(BF), up_weight.astype(BF).T, down_weight.astype(BF)]
     r_qkv, r_out, r_unit = shards[0].shape[0] // 2, shards[1].shape[0] // 2, shards[2].shape[0] // 4
-    first = pair_up(shards[0], topo, core)
-    rest = pair_up(
-        jnp.concatenate([pick_half(s, 0, h) for h in range(2) for s in shards[1:]], axis=0), topo, core
-    )
-    lanes = first.shape[1]
-    low_vec = vectors.astype(BF)
-    out_end, up_end = r_out, r_out + 2 * r_unit
-    one = gather(jnp.concatenate([first, tail_rows(low_vec, 16, lanes)], axis=0), topo)
-    two = gather(
-        jnp.concatenate([rest[: out_end + r_unit], rest[up_end : up_end + r_unit]], axis=0), topo
-    )
-    three = gather(
-        jnp.concatenate([rest[out_end + r_unit : up_end], rest[up_end + r_unit :]], axis=0), topo
-    )
-    slots = vector_slots(places, topo)
-    vecs, bias_qkv, *bias_up = unpack_vectors(one, places, r_qkv, vectors.shape[0], width, wide, topo.narrow)
+    lanes = 2 * out_weight.shape[1]
+    halves = [jnp.concatenate([pick_half(s, 0, h) for h in range(2) for s in pair], axis=0) for pair in (shards[:2], shards[2:])]
+    first = pair_up(halves[0], topo, core)
+    vec_low, out_low = r_qkv, r_qkv + 16
+    one = Spread(
+        jnp.concatenate([first[:r_qkv], tail_rows(vectors.astype(BF), 16, lanes), first[r_qkv:]], axis=0), topo
+    )
+    rest = pair_up(tied(halves[1], one.coming), topo, core)
+    piece_two = jnp.concatenate([rest[:r_unit], rest[2 * r_unit : 3 * r_unit]], axis=0)
+    piece_three = jnp.concatenate([rest[r_unit : 2 * r_unit], rest[3 * r_unit :]], axis=0)
+    one.along()
+    two = Spread(tied(piece_two, one.line[:1]), topo)
+    one.across()
+    one.core()
+    one = one.pieces
+    vecs, bias_qkv, *bias_up = unpack_vectors(one, places, vec_low, vectors.shape[0], width, wide, topo.narrow)
     segment = image_ids(bucket_counts[0], rows)
     seg_row = jnp.broadcast_to(segment[None], (8, rows))
     seg_col = jnp.pad(segment, (QB // 2, QB // 2), constant_values=-1)[:, None]
 
     hidden_one, qkv_t = project_qkv(tokens, vecs, bias_qkv, one, places, (r_qkv, wide))
-    attn = [attend(qkv_t, seg_row, seg_col, width, part) for part in range(PARTS)]
-    attn_t, lse = [a[0] for a in attn], [a[1] for a in attn]
-    mid, hidden_two = project_out(attn_t, tokens, vecs, two, places, r_out)
+    two.along((hidden_one,))
+    three = Spread(tied(piece_three, (hidden_one,)), topo)
+    attn_a, lse_a = attend(qkv_t, seg_row, seg_col, width, 0, after=two.line[:1])
+    two.across((lse_a,))
+    attn_b, lse_b = attend(qkv_t, seg_row, seg_col, width, 1)
+    attn_t, lse = (attn_a, attn_b), (lse_a, lse_b)
+    three.along((lse_b,))
+    mid, hidden_two = project_out(attn_t, tokens, vecs, one, places, out_low, r_out, after=three.line[:1])
+    two.core((hidden_two,))
+    three.across((hidden_two,))
+    two = two.pieces
+    three_along = three.line
     act_a, grad_a, sum_a, own_a, far_a = mlp_half(
-        hidden_two, cotangent, bias_up[0], two, places, r_out, r_unit, 2 * r_unit, wide
-    )
+        hidden_two, cotangent, bias_up[0], two, places, 0, r_unit, 2 * r_unit, wide, after=three_along
+    )
+    three.core((sum_a,))
+    three = three.pieces
     chain_a = Chain(own_a, far_a, topo)
     act_b, grad_b, sum_b, own_b, far_b = mlp_half(
         hidden_two, cotangent, bias_up[1], three, places, 0, r_unit, 2 * r_unit + r_out, wide
     )
+    chain_a.across((sum_b,))
     grad_mid, grad_mid_low, sums_two = second_norm_back(
-        (grad_a, grad_b), mid, cotangent, vecs, ((two, r_out), (three, 0)), places, r_unit, wide,
-        after=chain_a.arrived(),
-    )
-    chain_a.across()
-    do_t, own_b, far_b = out_back(attn_t, grad_mid_low, two, places, r_out, own_b, far_b, 2 * r_unit)
+        (grad_a, grad_b), mid, cotangent, vecs, ((two, 0), (three, 0)), places, r_unit, wide,
+        after=chain_a.sent,
+    )
+    do_t, own_b, far_b = out_back(attn_t, grad_mid_low, one, places, out_low, r_out, own_b, far_b, 2 * r_unit)
     chain_b = Chain(own_b, far_b, topo)
-    grads_0, sums_0 = attend_back(
-        qkv_t, do_t, lse[0], seg_row, seg_col, width, 0, after=chain_a.arrived()
-    )
-    chain_a.along()
+    chain_a.along((do_t,))
+    grads_0, sums_0 = attend_back(qkv_t, do_t, lse[0], seg_row, seg_col, width, 0, after=chain_a.sent)
+    chain_a.down((sums_0,))
+    chain_b.across((sums_0,))
     grads_1, sums_1 = attend_back(
-        qkv_t, do_t, lse[1], seg_row, seg_col, width, 1, after=chain_a.arrived() + chain_b.arrived()
-    )
-    chain_a.down()
-    chain_b.across()
+        qkv_t, do_t, lse[1], seg_row, seg_col, width, 1, after=chain_a.sent + chain_b.sent
+    )
     grad_t = (grads_0, grads_1)
-    own_q, far_q = qkv_back(
-        grad_t, hidden_one, places, r_qkv, topo, after=chain_b.arrived()
-    )
+    own_q, far_q = qkv_back(grad_t, hidden_one, places, r_qkv, topo)
     chain_q = Chain(own_q, far_q, topo)
-    chain_b.along()
+    chain_b.along((far_q,))
+    chain_q.across()
     input_grad, sums_one = first_norm_back(
-        grad_t, tokens, grad_mid, vecs, one, places, r_qkv, after=chain_a.arrived() + chain_q.arrived()
-    )
-    chain_q.across()
+        grad_t, tokens, grad_mid, vecs, one, places, r_qkv, after=chain_q.sent + chain_b.sent
+    )
+    chain_q.along((sums_one,))
+    chain_b.down((sums_one,))
+    own_v, far_v = pack_vectors(
+        sums_one, sums_two, (sums_0, sums_1), (sum_a, sum_b), places, topo, vectors.shape[0], after=chain_q.sent
+    )
+    chain_v = Chain(own_v, far_v, topo)
+    chain_v.across()
+    chain_q.down()
     block_out = finish_out(
-        (act_a, act_b), mid, vecs, ((two, r_out + r_unit), (three, r_unit)), places, r_unit, wide,
-        after=chain_b.arrived(),
-    )
-    chain_b.down()
-    chain_q.along()
-    chain_q.down()
-    half = width // PARTS
-    sums_qkv = [[s[k * half : (k + 1) * half, 0] for s in (sums_0, sums_1)] for k in (0, 2)]
-    sums_up = jnp.stack([s.reshape(2 * wide, r_unit) for s in (sum_a, sum_b)], axis=1).reshape(-1)
-    d_vector = jnp.concatenate(
-        [
-            sums_one[0],
-            sums_one[1],
-            *sums_qkv[0],
-            *sums_qkv[1],
-            sums_two[2],
-            sums_two[0],
-            sums_two[1],
-            sums_two[3],
-            sums_up,
-        ]
-    )
-    part_a, part_b, part_q = chain_a.result(), chain_b.result(), chain_q.result()
-    rel = jnp.dot(slots, d_vector.astype(BF).reshape(slots.shape[1], -1), preferred_element_type=F32).astype(BF)
-    rel = jnp.pad(rel, ((0, 0), (0, lanes - rel.shape[1]))).reshape(2, topo.X * topo.X, topo.Z, 1, lanes)
-    vector_grad = scatter(rel[0], rel[1], topo)[0, : vectors.shape[0]]
+        (act_a, act_b), mid, vecs, ((two, r_unit), (three, r_unit)), places, r_unit, wide,
+        after=chain_q.sent + chain_v.sent,
+    )
+    chain_v.along((block_out,))
+    chain_v.down()
+    part_a, part_b, part_q = chain_a.result((sums_one,)), chain_b.result((block_out,)), chain_q.result()
+    vector_grad = chain_v.result()[0, : vectors.shape[0]]
     down = jnp.concatenate([part_a[r_unit:], part_b[r_unit : 2 * r_unit]], axis=0)
     up = jnp.concatenate([part_a[:r_unit], part_b[:r_unit]], axis=0)
     out = part_b[2 * r_unit :]

time: 380 us -> 317 us (0.83)
  local copies, waits for them, and re-layouts: 44 us -> 17.7 us
  waiting for transfers between devices: 84.4 us -> 63.9 us
  other arithmetic: 35.9 us -> 22 us
    ppermute x60, waiting for transfers between devices: 84.4 us -> 63.9 us  [send(): return lax.ppermute(values, AXES, perm)]
    unnamed x238 -> x107, local copies, waits for them, and re-layouts: 31.4 us -> 14.3 us
    another operation x28 -> x4, other arithmetic: 15.1 us -> 1.92 us  [the longest x3 1.34 us: along(): stack = tied(jnp.stack((self.piece, *self.coming)), others)]
    pallas_call x14 -> x15, Pallas kernels: 148 us -> 148 us  [call(): pl.pallas_call(body, grid_spec=pltpu.PrefetchScalarGridSpec(num_scalar_pr...]
  transfers between devices with their start and end apart: 60 -> 60, of which waited for: 18 -> 19; matrix products, arithmetic and copies ran while one was open for 13% -> 6% of each run, Pallas kernels for 34% -> 44%
where the time goes in v4:
time: 317 us; the launch traced here: 311 us
  Pallas kernels  148 us (47%)
  waiting for transfers between devices  63.9 us (20%)
  starting transfers between devices  55.7 us (18%)
  other arithmetic  22 us (7%)
  local copies, waits for them, and re-layouts  17.7 us (6%)
  between operations  3.23 us (1%)
    pallas_call x15, Pallas kernels, call(): pl.pallas_call(body, grid_spec=pltpu.PrefetchScalarGridSpec(num_scalar_pr...  148 us
    ppermute x60, waiting for transfers between devices, send(): return lax.ppermute(values, AXES, perm)  63.9 us
    ppermute x60, starting transfers between devices, send(): return lax.ppermute(values, AXES, perm)  55.7 us
    unnamed x107, local copies, waits for them, and re-layouts  14.3 us
    convert_element_type x12, other arithmetic, stage(): self.held, *sent = [self.fold(k).astype(BF) for k in range(count)]  12.8 us
  transfers between devices with their start and end apart: 60, of which 19 were waited for; matrix products, arithmetic and copies ran while one was open for 6% of the time, Pallas kernels for 44%

profile of v4, /device:TPU:0, one launch (start us, length us, event | category | flops | bytes accessed | tf_op | source)
XLA Modules:
  0.0 310.6 jit_solution(3713617110418381263)
XLA Ops:
  4.5 5.0 %collective-permute-start.3 = (bf16[208,384]{1,0:T(8,128)(2,1)S(1)}, bf16[208,384]{1,0:T(8,128)(2,1)S(1)}, u32[]{:S(2)}, u32[]{:S(2)}) collective-permute-start(bf16[208,384]{1,0:T(8,128)(2,1)S(1)} %fusion.30), channel_id=1, source_target_pairs={{0,24},{1,25},{2,26},{3,27},{4,28},{5,29},{6,30},{7,31},{8,0},{9,1... | collective-permute-start | bytes 479240 | tf_op jit(solution)/shard_map/ppermute | solution.py:132
  10.4 3.5 %collective-permute-done.3 = bf16[208,384]{1,0:T(8,128)(2,1)S(1)} collective-permute-done((bf16[208,384]{1,0:T(8,128)(2,1)S(1)}, bf16[208,384]{1,0:T(8,128)(2,1)S(1)}, u32[]{:S(2)}, u32[]{:S(2)}) %collective-permute-start.3) | collective-permute-done | bytes 159776 | tf_op jit(solution)/shard_map/ppermute | solution.py:132
  14.0 9.3 %collective-permute-done.2 = bf16[208,384]{1,0:T(8,128)(2,1)S(1)} collective-permute-done((bf16[208,384]{1,0:T(8,128)(2,1)S(1)}, bf16[208,384]{1,0:T(8,128)(2,1)S(1)}, u32[]{:S(2)}, u32[]{:S(2)}) %collective-permute-start.2) | collective-permute-done | bytes 159776 | tf_op jit(solution)/shard_map/ppermute | solution.py:132
  27.1 12.1 %collective-permute-done.4.refs_2_.refs_5_.refs_6_.refs_7_ = bf16[4,208,384]{2,1,0:T(8,128)(2,1)S(1)} collective-permute-done((bf16[4,208,384]{2,1,0:T(8,128)(2,1)S(1)}, bf16[4,208,384]{2,1,0:T(8,128)(2,1)S(1)}, u32[]{:S(2)}, u32[]{:S(2)}) %collective-permute-start.4) | collective-permute-done | bytes 639008 | tf_op jit(solution)/shard_map/ppermute | solution.py:132
  45.4 4.2 %collective-permute-done.6.refs_4_.refs_7_.refs_8_.refs_9_ = bf16[4,208,384]{2,1,0:T(8,128)(2,1)S(1)} collective-permute-done((bf16[4,208,384]{2,1,0:T(8,128)(2,1)S(1)}, bf16[4,208,384]{2,1,0:T(8,128)(2,1)S(1)}, u32[]{:S(2)}, u32[]{:S(2)}) %collective-permute-start.6) | collective-permute-done | bytes 639008 | tf_op jit(solution)/shard_map/ppermute | solution.py:132
  49.6 2.9 collective-permute-start.13
  53.9 6.3 %collective-permute-done.13 = bf16[192,384]{1,0:T(8,128)(2,1)} collective-permute-done((bf16[192,384]{1,0:T(8,128)(2,1)S(1)}, bf16[192,384]{1,0:T(8,128)(2,1)}, u32[]{:S(2)}, u32[]{:S(2)}) %collective-permute-start.13) | collective-permute-done | bytes 147488 | tf_op jit(solution)/shard_map/ppermute | solution.py:132
  64.2 3.6 %collective-permute-done.12 = bf16[192,384]{1,0:T(8,128)(2,1)} collective-permute-done((bf16[192,384]{1,0:T(8,128)(2,1)S(1)}, bf16[192,384]{1,0:T(8,128)(2,1)}, u32[]{:S(2)}, u32[]{:S(2)}) %collective-permute-start.12) | collective-permute-done | bytes 147488 | tf_op jit(solution)/shard_map/ppermute | solution.py:132
  69.0 3.2 %shard_map.135 = (f32[8,768]{1,0:T(8,128)S(1)}, f32[2304,1]{1,0:T(8,128)S(1)}, f32[1536,1]{1,0:T(8,128)S(1)}, f32[1536,1]{1,0:T(8,128)S(1)}) custom-call(s32[32,3]{1,0:T(8,128)S(1)} %copy.71.refs_0_, bf16[4,208,384]{2,1,0:T(8,128)(2,1)S(1)} %pad_maximum_fusion.refs_1_.refs_4_.refs_5_.refs_6_, ...), custom_call_target="tpu_custom_call" | custom-call | flops 3000000000 | bytes 9000000 | tf_op jit(solution)/shard_map/pallas_call | solution.py:212
  73.1 8.5 %shard_map.136 = (bf16[1024,768]{1,0:T(8,128)(2,1)S(1)}, bf16[2304,1024]{1,0:T(8,128)(2,1)S(1)}) custom-call(s32[32,3]{1,0:T(8,128)S(1)} %copy.71.refs_0_, bf16[1024,768]{1,0:T(8,128)(2,1)S(1)} %copy-done.1, f32[8,768]{1,0:T(8,128)S(1)} %get-tuple-element.82.refs_2_.refs_4_.refs_5_, f32[2304,1]{1,0:T(8,128)S(1)} %get-tuple-element.83.refs_3_, ...), custom_call_target="tpu_custom_call" | custom-call | flops 8999999488 | bytes 27000000 | tf_op jit(solution)/shard_map/pallas_call | solution.py:212
  85.0 2.5 collective-permute-start.18
  87.4 6.0 %shard_map.137 = (bf16[384,1024]{1,0:T(8,128)(2,1)S(1)}, f32[16,1024]{1,0:T(8,128)S(1)}) custom-call(bf16[2304,1024]{1,0:T(8,128)(2,1)S(1)} %get-tuple-element.84.refs_0_.refs_1_.refs_2_, bf16[2304,1024]{1,0:T(8,128)(2,1)S(1)} %get-tuple-element.84.refs_0_.refs_1_.refs_2_, bf16[2304,1024]{1,0:T(8,128)(2,1)S(1)} %get-tuple-element.84.refs_0_.refs_1_.refs_2_, ...), custom_call_target="tpu_custom_call" | custom-call | flops 6000000000 | bytes 18000000 | tf_op jit(solution)/shard_map/pallas_call | solution.py:212
  93.4 6.0 %shard_map.138 = (bf16[384,1024]{1,0:T(8,128)(2,1)S(1)}, f32[16,1024]{1,0:T(8,128)S(1)}) custom-call(bf16[2304,1024]{1,0:T(8,128)(2,1)S(1)} %get-tuple-element.84.refs_0_.refs_1_.refs_2_, bf16[2304,1024]{1,0:T(8,128)(2,1)S(1)} %get-tuple-element.84.refs_0_.refs_1_.refs_2_, bf16[2304,1024]{1,0:T(8,128)(2,1)S(1)} %get-tuple-element.84.refs_0_.refs_1_.refs_2_, ...), custom_call_target="tpu_custom_call" | custom-call | flops 6000000000 | bytes 18000000 | tf_op jit(solution)/shard_map/pallas_call | solution.py:212
  101.8 5.7 %shard_map.139 = (f32[1024,768]{1,0:T(8,128)S(1)}, bf16[1024,768]{1,0:T(8,128)(2,1)S(1)}) custom-call(s32[32,3]{1,0:T(8,128)S(1)} %copy.71.refs_0_, bf16[384,1024]{1,0:T(8,128)(2,1)S(1)} %get-tuple-element.89.refs_1_, bf16[384,1024]{1,0:T(8,128)(2,1)S(1)} %get-tuple-element.90.refs_2_, bf16[1024,768]{1,0:T(8,128)(2,1)S(1)} %copy-done.1, ...), custom_call_target="tpu_custom_call" | custom-call | flops 5000000000 | bytes 15000000 | tf_op jit(solution)/shard_map/pallas_call | solution.py:212
  110.3 4.7 %collective-permute-done.19.refs_6_.refs_8_.refs_7_ = bf16[4,192,384]{2,1,0:T(8,128)(2,1)S(1)} collective-permute-done((bf16[4,192,384]{2,1,0:T(8,128)(2,1)S(1)}, bf16[4,192,384]{2,1,0:T(8,128)(2,1)S(1)}, u32[]{:S(2)}, u32[]{:S(2)}) %collective-permute-start.19) | collective-permute-done | bytes 589856 | tf_op jit(solution)/shard_map/ppermute | solution.py:132
  115.0 7.0 %collective-permute-done.20.refs_7_.refs_9_.refs_8_ = bf16[4,192,384]{2,1,0:T(8,128)(2,1)S(1)} collective-permute-done((bf16[4,192,384]{2,1,0:T(8,128)(2,1)S(1)}, bf16[4,192,384]{2,1,0:T(8,128)(2,1)S(1)}, u32[]{:S(2)}, u32[]{:S(2)}) %collective-permute-start.20) | collective-permute-done | bytes 589856 | tf_op jit(solution)/shard_map/ppermute | solution.py:132
  124.9 21.9 %shard_map.140 = (bf16[1536,1024]{1,0:T(8,128)(2,1)}, bf16[1536,1024]{1,0:T(8,128)(2,1)}, f32[8,1536]{1,0:T(8,128)S(1)}, bf16[4,4,192,384]{3,2,1,0:T(8,128)(2,1)}, bf16[4,4,192,384]{3,2,1,0:T(8,128)(2,1)}) custom-call(s32[32,3]{1,0:T(8,128)S(1)} %copy.71.refs_0_, bf16[1024,768]{1,0:T(8,128)(2,1)} %copy-done.30, bf16[1024,768]{1,0:T(8,128)(2,1)} %refs_4_.1, ...), custom_call_target="tpu_custom_call" | custom-call | flops 22000001024 | bytes 66000000 | tf_op jit(solution)/shard_map/pallas_call | solution.py:212
  152.0 22.0 %shard_map.141 = (bf16[1536,1024]{1,0:T(8,128)(2,1)}, bf16[1536,1024]{1,0:T(8,128)(2,1)}, f32[8,1536]{1,0:T(8,128)S(1)}, bf16[4,4,240,384]{3,2,1,0:T(8,128)(2,1)}, bf16[4,4,240,384]{3,2,1,0:T(8,128)(2,1)}) custom-call(s32[32,3]{1,0:T(8,128)S(1)} %copy.71.refs_0_, bf16[1024,768]{1,0:T(8,128)(2,1)} %copy-done.30, bf16[1024,768]{1,0:T(8,128)(2,1)} %refs_4_.1, ...), custom_call_target="tpu_custom_call" | custom-call | flops 22000001024 | bytes 66000000 | tf_op jit(solution)/shard_map/pallas_call | solution.py:212
  174.1 3.8 %fusion.3 = (bf16[2,4,192,384]{3,2,1,0:T(8,128)(2,1)}, bf16[2,4,192,384]{3,2,1,0:T(8,128)(2,1)}) fusion(bf16[2,2,4,192,384]{4,3,2,1,0:T(8,128)(2,1)} %bitcast.17, bf16[2,2,4,192,384]{4,3,2,1,0:T(8,128)(2,1)S(1)} %bitcast.123), kind=kLoop, calls=%fused_computation.11 | loop fusion | flops 4718592 | bytes 7077888 | tf_op jit(solution)/shard_map/convert_element_type | solution.py:886
  179.3 14.4 %shard_map.142 = (f32[1024,768]{1,0:T(8,128)}, bf16[1024,768]{1,0:T(8,128)(2,1)}, f32[8,768]{1,0:T(8,128)S(1)}) custom-call(s32[32,3]{1,0:T(8,128)S(1)} %copy.71.refs_0_, bf16[1536,1024]{1,0:T(8,128)(2,1)} %get-tuple-element.110.refs_1_, bf16[1536,1024]{1,0:T(8,128)(2,1)} %get-tuple-element.111.refs_2_, f32[1024,768]{1,0:T(8,128)} %copy-done.26, ...), custom_call_target="tpu_custom_call" | custom-call | flops 41999998976 | bytes 126000000 | tf_op jit(solution)/shard_map/pallas_call | solution.py:212
  195.1 5.2 %shard_map.143 = (bf16[768,1024]{1,0:T(8,128)(2,1)S(1)}, bf16[4,4,240,384]{3,2,1,0:T(8,128)(2,1)S(1)}, bf16[4,4,240,384]{3,2,1,0:T(8,128)(2,1)}) custom-call(s32[32,3]{1,0:T(8,128)S(1)} %copy.71.refs_0_, bf16[384,1024]{1,0:T(8,128)(2,1)S(1)} %copy-done.32, bf16[384,1024]{1,0:T(8,128)(2,1)S(1)} %copy-done.34, ...), custom_call_target="tpu_custom_call", output_to_operand_aliasing={{1}: (4, {}), {2}: (5, {})} | custom-call | flops 15000000512 | bytes 45000000 | tf_op jit(solution)/shard_map/pallas_call | solution.py:212
  202.7 11.9 %shard_map.144 = (bf16[1152,1024]{1,0:T(8,128)(2,1)S(1)}, f32[8,1152]{1,0:T(8,128)S(1)}) custom-call(bf16[2304,1024]{1,0:T(8,128)(2,1)} %copy-done.25, bf16[2304,1024]{1,0:T(8,128)(2,1)} %copy-done.25, bf16[2304,1024]{1,0:T(8,128)(2,1)} %copy-done.25, bf16[768,1024]{1,0:T(8,128)(2,1)S(1)} %get-tuple-element.120.refs_3_, ...), custom_call_target="tpu_custom_call" | custom-call | flops 35999997952 | bytes 108000000 | tf_op jit(solution)/shard_map/pallas_call | solution.py:212
  214.8 4.3 %fusion.1 = (bf16[2,4,240,384]{3,2,1,0:T(8,128)(2,1)}, bf16[2,4,240,384]{3,2,1,0:T(8,128)(2,1)S(1)}) fusion(bf16[2,2,4,240,384]{4,3,2,1,0:T(8,128)(2,1)} %bitcast.26, bf16[2,2,4,240,384]{4,3,2,1,0:T(8,128)(2,1)S(1)} %bitcast.122), kind=kLoop, calls=%fused_computation.7 | loop fusion | flops 5898240 | bytes 8847360 | tf_op jit(solution)/shard_map/convert_element_type | solution.py:886
  220.4 13.1 %shard_map.145 = (bf16[1152,1024]{1,0:T(8,128)(2,1)}, f32[8,1152]{1,0:T(8,128)S(1)}) custom-call(bf16[2304,1024]{1,0:T(8,128)(2,1)} %copy-done.25, bf16[2304,1024]{1,0:T(8,128)(2,1)} %copy-done.25, bf16[2304,1024]{1,0:T(8,128)(2,1)} %copy-done.25, bf16[768,1024]{1,0:T(8,128)(2,1)S(1)} %get-tuple-element.120.refs_3_, ...), custom_call_target="tpu_custom_call" | custom-call | flops 35999997952 | bytes 108000000 | tf_op jit(solution)/shard_map/pallas_call | solution.py:212
  235.2 6.1 %shard_map.146 = (bf16[4,4,144,384]{3,2,1,0:T(8,128)(2,1)S(1)}, bf16[4,4,144,384]{3,2,1,0:T(8,128)(2,1)S(1)}) custom-call(s32[32,3]{1,0:T(8,128)S(1)} %copy.71.refs_0_, bf16[1152,1024]{1,0:T(8,128)(2,1)S(1)} %get-tuple-element.123.refs_1_, bf16[1152,1024]{1,0:T(8,128)(2,1)S(1)} %copy-done.40, bf16[1024,768]{1,0:T(8,128)(2,1)S(1)} %copy-done.36), custom_call_target="tpu_custom_call" | custom-call | flops 20999999488 | bytes 63000000 | tf_op jit(solution)/shard_map/pallas_call | solution.py:212
  244.4 2.8 collective-permute-start.50
  252.1 11.0 %shard_map.147 = (bf16[1024,768]{1,0:T(8,128)(2,1)}, f32[8,768]{1,0:T(8,128)S(1)}) custom-call(s32[32,3]{1,0:T(8,128)S(1)} %copy.71.refs_0_, bf16[1152,1024]{1,0:T(8,128)(2,1)S(1)} %copy-done.39, bf16[1152,1024]{1,0:T(8,128)(2,1)S(1)} %copy-done.41, bf16[1024,768]{1,0:T(8,128)(2,1)S(1)} %copy-done.2, f32[1024,768]{1,0:T(8,128)} %get-tuple-element.134.refs_4_, ...), custom_call_target="tpu_custom_call" | custom-call | flops 32999999488 | bytes 99000000 | tf_op jit(solution)/shard_map/pallas_call | solution.py:212
  263.2 5.2 %collective-permute-done.45 = bf16[4,240,384]{2,1,0:T(8,128)(2,1)S(1)} collective-permute-done((bf16[4,240,384]{2,1,0:T(8,128)(2,1)S(1)}, bf16[4,240,384]{2,1,0:T(8,128)(2,1)S(1)}, u32[]{:S(2)}, u32[]{:S(2)}) %collective-permute-start.45) | collective-permute-done | bytes 737312 | tf_op jit(solution)/shard_map/ppermute | solution.py:132
  273.0 3.0 collective-permute-start.46
  277.5 12.3 %shard_map.149 = bf16[1024,768]{1,0:T(8,128)(2,1)} custom-call(s32[32,3]{1,0:T(8,128)S(1)} %copy.71.refs_0_, bf16[1536,1024]{1,0:T(8,128)(2,1)} %get-tuple-element.101.refs_1_, bf16[1536,1024]{1,0:T(8,128)(2,1)} %get-tuple-element.108.refs_2_, f32[1024,768]{1,0:T(8,128)} %copy-done.26, f32[8,768]{1,0:T(8,128)S(1)} %get-tuple-element.82.refs_2_.refs_4_.refs_5_, ...), custom_call_target="tpu_custom_call" | custom-call | flops 32999999488 | bytes 99000000 | tf_op jit(solution)/shard_map/pallas_call | solution.py:212
  296.5 2.5 collective-permute-start.57
  299.0 2.5 collective-permute-start.58
  (272 shorter events, 75.1 us)
Async XLA Ops:
  23.4 15.8 %collective-permute-start.4 = (bf16[4,208,384]{2,1,0:T(8,128)(2,1)S(1)}, bf16[4,208,384]{2,1,0:T(8,128)(2,1)S(1)}, u32[]{:S(2)}, u32[]{:S(2)}) collective-permute-start(bf16[4,208,384]{2,1,0:T(8,128)(2,1)S(1)} %pad_maximum_fusion.refs_1_.refs_4_.refs_5_.refs_6_), channel_id=1, source_target_pairs={{0,4},{1,3},{2,6},{3,1},{4,0},{5,7},{6,2},{7,5},{8,12},{9,11},{10,... | collective-permute-start | bytes 1916936 | tf_op jit(solution)/shard_map/ppermute | solution.py:132
  25.4 15.3 %collective-permute-start.11 = (bf16[384,192]{1,0:T(8,128)(2,1)S(1)}, bf16[384,192]{1,0:T(8,128)(2,1)}, u32[]{:S(2)}, u32[]{:S(2)}) collective-permute-start(bf16[384,192]{1,0:T(8,128)(2,1)S(1)} %constant_dynamic-slice_fusion.2), channel_id=1, source_target_pairs={{0,1},{1,0},{2,3},{3,2},{4,5},{5,4},{6,7},{7,6},{8,9},{9,8},{10,11... | collective-permute-start | bytes 442376 | tf_op jit(solution)/shard_map/ppermute | solution.py:132
  25.5 19.9 %collective-permute-start.5 = (bf16[4,208,384]{2,1,0:T(8,128)(2,1)S(1)}, bf16[4,208,384]{2,1,0:T(8,128)(2,1)S(1)}, u32[]{:S(2)}, u32[]{:S(2)}) collective-permute-start(bf16[4,208,384]{2,1,0:T(8,128)(2,1)S(1)} %pad_maximum_fusion.refs_1_.refs_4_.refs_5_.refs_6_), channel_id=1, source_target_pairs={{0,2},{1,5},{2,0},{3,7},{4,6},{5,1},{6,4},{7,3},{8,10},{9,13},{10,... | collective-permute-start | bytes 1916936 | tf_op jit(solution)/shard_map/ppermute | solution.py:132
  44.9 24.1 %collective-permute-start.7 = (bf16[4,208,384]{2,1,0:T(8,128)(2,1)S(1)}, bf16[4,208,384]{2,1,0:T(8,128)(2,1)S(1)}, u32[]{:S(2)}, u32[]{:S(2)}) collective-permute-start(bf16[4,208,384]{2,1,0:T(8,128)(2,1)S(1)} %pad_maximum_fusion.refs_1_.refs_4_.refs_5_.refs_6_), channel_id=1, source_target_pairs={{0,1},{1,0},{2,3},{3,2},{4,5},{5,4},{6,7},{7,6},{8,9},{9,8},{10,11... | collective-permute-start | bytes 1916936 | tf_op jit(solution)/shard_map/ppermute | solution.py:132
  44.9 24.1 %collective-permute-start.8 = (bf16[4,208,384]{2,1,0:T(8,128)(2,1)S(1)}, bf16[4,208,384]{2,1,0:T(8,128)(2,1)}, u32[]{:S(2)}, u32[]{:S(2)}) collective-permute-start(bf16[4,208,384]{2,1,0:T(8,128)(2,1)S(1)} %collective-permute-done.4.refs_2_.refs_5_.refs_6_.refs_7_), channel_id=1, source_target_pairs={{0,1},{1,0},{2,3},{3,2},{4,5},{5,4},{6,7},{7,6},{8,9},{9,8},{10,11... | collective-permute-start | bytes 1916936 | tf_op jit(solution)/shard_map/ppermute | solution.py:132
  45.4 23.6 %collective-permute-start.9 = (bf16[4,208,384]{2,1,0:T(8,128)(2,1)S(1)}, bf16[4,208,384]{2,1,0:T(8,128)(2,1)}, u32[]{:S(2)}, u32[]{:S(2)}) collective-permute-start(bf16[4,208,384]{2,1,0:T(8,128)(2,1)S(1)} %collective-permute-done.5.refs_3_.refs_6_.refs_7_.refs_8_), channel_id=1, source_target_pairs={{0,1},{1,0},{2,3},{3,2},{4,5},{5,4},{6,7},{7,6},{8,9},{9,8},{10,11... | collective-permute-start | bytes 1916936 | tf_op jit(solution)/shard_map/ppermute | solution.py:132
  49.6 19.4 %collective-permute-start.10 = (bf16[4,208,384]{2,1,0:T(8,128)(2,1)S(1)}, bf16[4,208,384]{2,1,0:T(8,128)(2,1)}, u32[]{:S(2)}, u32[]{:S(2)}) collective-permute-start(bf16[4,208,384]{2,1,0:T(8,128)(2,1)S(1)} %collective-permute-done.6.refs_4_.refs_7_.refs_8_.refs_9_), channel_id=1, source_target_pairs={{0,1},{1,0},{2,3},{3,2},{4,5},{5,4},{6,7},{7,6},{8,9},{9,8},{10,11... | collective-permute-start | bytes 1916936 | tf_op jit(solution)/shard_map/ppermute | solution.py:132
  82.8 18.3 %collective-permute-start.17 = (bf16[192,384]{1,0:T(8,128)(2,1)S(1)}, bf16[192,384]{1,0:T(8,128)(2,1)S(1)}, u32[]{:S(2)}, u32[]{:S(2)}) collective-permute-start(bf16[192,384]{1,0:T(8,128)(2,1)S(1)} %fusion.37), channel_id=1, source_target_pairs={{0,24},{1,25},{2,26},{3,27},{4,28},{5,29},{6,30},{7,31},{8,0},{9,1... | collective-permute-start | bytes 442376 | tf_op jit(solution)/shard_map/ppermute | solution.py:132
  83.1 18.5 %collective-permute-start.16 = (bf16[192,384]{1,0:T(8,128)(2,1)S(1)}, bf16[192,384]{1,0:T(8,128)(2,1)S(1)}, u32[]{:S(2)}, u32[]{:S(2)}) collective-permute-start(bf16[192,384]{1,0:T(8,128)(2,1)S(1)} %fusion.37), channel_id=1, source_target_pairs={{0,16},{1,17},{2,18},{3,19},{4,20},{5,21},{6,22},{7,23},{8,24},{9,... | collective-permute-start | bytes 442376 | tf_op jit(solution)/shard_map/ppermute | solution.py:132
  83.1 18.5 %collective-permute-start.15 = (bf16[192,384]{1,0:T(8,128)(2,1)S(1)}, bf16[192,384]{1,0:T(8,128)(2,1)S(1)}, u32[]{:S(2)}, u32[]{:S(2)}) collective-permute-start(bf16[192,384]{1,0:T(8,128)(2,1)S(1)} %fusion.37), channel_id=1, source_target_pairs={{0,8},{1,9},{2,10},{3,11},{4,12},{5,13},{6,14},{7,15},{8,16},{9,17... | collective-permute-start | bytes 442376 | tf_op jit(solution)/shard_map/ppermute | solution.py:132
  85.0 37.7 %collective-permute-start.21 = (bf16[4,192,384]{2,1,0:T(8,128)(2,1)S(1)}, bf16[4,192,384]{2,1,0:T(8,128)(2,1)S(1)}, u32[]{:S(2)}, u32[]{:S(2)}) collective-permute-start(bf16[4,192,384]{2,1,0:T(8,128)(2,1)S(1)} %pad_maximum_fusion.1.refs_5_.refs_4_.refs_6_), channel_id=1, source_target_pairs={{0,1},{1,0},{2,3},{3,2},{4,5},{5,4},{6,7},{7,6},{8,9},{9,8},{10,11... | collective-permute-start | bytes 1769480 | tf_op jit(solution)/shard_map/ppermute | solution.py:132
  99.5 15.6 %collective-permute-start.19 = (bf16[4,192,384]{2,1,0:T(8,128)(2,1)S(1)}, bf16[4,192,384]{2,1,0:T(8,128)(2,1)S(1)}, u32[]{:S(2)}, u32[]{:S(2)}) collective-permute-start(bf16[4,192,384]{2,1,0:T(8,128)(2,1)S(1)} %pad_maximum_fusion.1.refs_5_.refs_4_.refs_6_), channel_id=1, source_target_pairs={{0,2},{1,5},{2,0},{3,7},{4,6},{5,1},{6,4},{7,3},{8,10},{9,13},{10,... | collective-permute-start | bytes 1769480 | tf_op jit(solution)/shard_map/ppermute | solution.py:132
  101.1 21.0 %collective-permute-start.20 = (bf16[4,192,384]{2,1,0:T(8,128)(2,1)S(1)}, bf16[4,192,384]{2,1,0:T(8,128)(2,1)S(1)}, u32[]{:S(2)}, u32[]{:S(2)}) collective-permute-start(bf16[4,192,384]{2,1,0:T(8,128)(2,1)S(1)} %collective-permute-done.18.refs_5_.refs_7_.refs_6_), channel_id=1, source_target_pairs={{0,2},{1,5},{2,0},{3,7},{4,6},{5,1},{6,4},{7,3},{8,10},{9,13},{10,... | collective-permute-start | bytes 1769480 | tf_op jit(solution)/shard_map/ppermute | solution.py:132
  101.7 20.9 %collective-permute-start.25 = (bf16[4,192,384]{2,1,0:T(8,128)(2,1)S(1)}, bf16[4,192,384]{2,1,0:T(8,128)(2,1)S(1)}, u32[]{:S(2)}, u32[]{:S(2)}) collective-permute-start(bf16[4,192,384]{2,1,0:T(8,128)(2,1)S(1)} %pad_maximum_fusion.2.refs_13_.refs_12_.refs_4_.refs_14_), channel_id=1, source_target_pairs={{0,4},{1,3},{2,6},{3,1},{4,0},{5,7},{6,2},{7,5},{8,12},{9,11},{10,... | collective-permute-start | bytes 1769480 | tf_op jit(solution)/shard_map/ppermute | solution.py:132
  122.6 25.2 %collective-permute-start.28 = (bf16[4,192,384]{2,1,0:T(8,128)(2,1)S(1)}, bf16[4,192,384]{2,1,0:T(8,128)(2,1)S(1)}, u32[]{:S(2)}, u32[]{:S(2)}) collective-permute-start(bf16[4,192,384]{2,1,0:T(8,128)(2,1)S(1)} %pad_maximum_fusion.2.refs_13_.refs_12_.refs_4_.refs_14_), channel_id=1, source_target_pairs={{0,1},{1,0},{2,3},{3,2},{4,5},{5,4},{6,7},{7,6},{8,9},{9,8},{10,11... | collective-permute-start | bytes 1769480 | tf_op jit(solution)/shard_map/ppermute | solution.py:132
  122.6 24.2 %collective-permute-start.26 = (bf16[4,192,384]{2,1,0:T(8,128)(2,1)S(1)}, bf16[4,192,384]{2,1,0:T(8,128)(2,1)S(1)}, u32[]{:S(2)}, u32[]{:S(2)}) collective-permute-start(bf16[4,192,384]{2,1,0:T(8,128)(2,1)S(1)} %pad_maximum_fusion.2.refs_13_.refs_12_.refs_4_.refs_14_), channel_id=1, source_target_pairs={{0,2},{1,5},{2,0},{3,7},{4,6},{5,1},{6,4},{7,3},{8,10},{9,13},{10,... | collective-permute-start | bytes 1769480 | tf_op jit(solution)/shard_map/ppermute | solution.py:132
  123.9 22.9 %collective-permute-start.27 = (bf16[4,192,384]{2,1,0:T(8,128)(2,1)S(1)}, bf16[4,192,384]{2,1,0:T(8,128)(2,1)S(1)}, u32[]{:S(2)}, u32[]{:S(2)}) collective-permute-start(bf16[4,192,384]{2,1,0:T(8,128)(2,1)S(1)} %collective-permute-done.25.refs_13_.refs_5_.refs_15_.refs_14_), channel_id=1, source_target_pairs={{0,2},{1,5},{2,0},{3,7},{4,6},{5,1},{6,4},{7,3},{8,10},{9,13},{10,... | collective-permute-start | bytes 1769480 | tf_op jit(solution)/shard_map/ppermute | solution.py:132
  124.7 23.1 %collective-permute-start.29 = (bf16[4,192,384]{2,1,0:T(8,128)(2,1)S(1)}, bf16[4,192,384]{2,1,0:T(8,128)(2,1)S(1)}, u32[]{:S(2)}, u32[]{:S(2)}) collective-permute-start(bf16[4,192,384]{2,1,0:T(8,128)(2,1)S(1)} %collective-permute-done.25.refs_13_.refs_5_.refs_15_.refs_14_), channel_id=1, source_target_pairs={{0,1},{1,0},{2,3},{3,2},{4,5},{5,4},{6,7},{7,6},{8,9},{9,8},{10,11... | collective-permute-start | bytes 1769480 | tf_op jit(solution)/shard_map/ppermute | solution.py:132
  147.4 26.6 %collective-permute-start.32 = (bf16[4,4,192,384]{3,2,1,0:T(8,128)(2,1)}, bf16[4,4,192,384]{3,2,1,0:T(8,128)(2,1)}, u32[]{:S(2)}, u32[]{:S(2)}) collective-permute-start(bf16[4,4,192,384]{3,2,1,0:T(8,128)(2,1)} %get-tuple-element.113), channel_id=1, source_target_pairs={{0,1},{1,0},{2,3},{3,2},{4,5},{5,4},{6,7},{7,6},{8,9},{9,8},{10,11... | collective-permute-start | bytes 7077896 | tf_op jit(solution)/shard_map/ppermute | solution.py:132
  177.9 22.5 %collective-permute-start.33 = (bf16[2,4,192,384]{3,2,1,0:T(8,128)(2,1)}, bf16[2,4,192,384]{3,2,1,0:T(8,128)(2,1)}, u32[]{:S(2)}, u32[]{:S(2)}) collective-permute-start(bf16[2,4,192,384]{3,2,1,0:T(8,128)(2,1)} %get-tuple-element.188.refs_22_), channel_id=1, source_target_pairs={{0,2},{1,5},{2,0},{3,7},{4,6},{5,1},{6,4},{7,3},{8,10},{9,13},{10,... | collective-permute-start | bytes 3538952 | tf_op jit(solution)/shard_map/ppermute | solution.py:132
  200.3 14.5 %collective-permute-start.35 = (bf16[4,4,240,384]{3,2,1,0:T(8,128)(2,1)}, bf16[4,4,240,384]{3,2,1,0:T(8,128)(2,1)}, u32[]{:S(2)}, u32[]{:S(2)}) collective-permute-start(bf16[4,4,240,384]{3,2,1,0:T(8,128)(2,1)} %get-tuple-element.128), channel_id=1, source_target_pairs={{0,1},{1,0},{2,3},{3,2},{4,5},{5,4},{6,7},{7,6},{8,9},{9,8},{10,11... | collective-permute-start | bytes 8847368 | tf_op jit(solution)/shard_map/ppermute | solution.py:132
  219.1 28.1 %collective-permute-start.38 = (bf16[2,4,240,384]{3,2,1,0:T(8,128)(2,1)S(1)}, bf16[2,4,240,384]{3,2,1,0:T(8,128)(2,1)}, u32[]{:S(2)}, u32[]{:S(2)}) collective-permute-start(bf16[2,4,240,384]{3,2,1,0:T(8,128)(2,1)S(1)} %get-tuple-element.186.refs_10_), channel_id=1, source_target_pairs={{0,2},{1,5},{2,0},{3,7},{4,6},{5,1},{6,4},{7,3},{8,10},{9,13},{10,... | collective-permute-start | bytes 4423688 | tf_op jit(solution)/shard_map/ppermute | solution.py:132
  241.3 21.8 %collective-permute-start.52 = (bf16[192,384]{1,0:T(8,128)(2,1)S(1)}, bf16[192,384]{1,0:T(8,128)(2,1)S(1)}, u32[]{:S(2)}, u32[]{:S(2)}) collective-permute-start(bf16[192,384]{1,0:T(8,128)(2,1)S(1)} %get-tuple-element.202.refs_9_), channel_id=1, source_target_pairs={{0,8},{1,9},{2,10},{3,11},{4,12},{5,13},{6,14},{7,15},{8,16},{9,17... | collective-permute-start | bytes 442376 | tf_op jit(solution)/shard_map/ppermute | solution.py:132
  243.1 20.0 %collective-permute-start.51 = (bf16[192,384]{1,0:T(8,128)(2,1)S(1)}, bf16[192,384]{1,0:T(8,128)(2,1)S(1)}, u32[]{:S(2)}, u32[]{:S(2)}) collective-permute-start(bf16[192,384]{1,0:T(8,128)(2,1)S(1)} %get-tuple-element.203.refs_8_), channel_id=1, source_target_pairs={{0,16},{1,17},{2,18},{3,19},{4,20},{5,21},{6,22},{7,23},{8,24},{9,... | collective-permute-start | bytes 442376 | tf_op jit(solution)/shard_map/ppermute | solution.py:132
  244.4 18.7 %collective-permute-start.50 = (bf16[192,384]{1,0:T(8,128)(2,1)S(1)}, bf16[192,384]{1,0:T(8,128)(2,1)S(1)}, u32[]{:S(2)}, u32[]{:S(2)}) collective-permute-start(bf16[192,384]{1,0:T(8,128)(2,1)S(1)} %get-tuple-element.204.refs_7_), channel_id=1, source_target_pairs={{0,24},{1,25},{2,26},{3,27},{4,28},{5,29},{6,30},{7,31},{8,0},{9,1... | collective-permute-start | bytes 442376 | tf_op jit(solution)/shard_map/ppermute | solution.py:132
  249.1 19.3 %collective-permute-start.45 = (bf16[4,240,384]{2,1,0:T(8,128)(2,1)S(1)}, bf16[4,240,384]{2,1,0:T(8,128)(2,1)S(1)}, u32[]{:S(2)}, u32[]{:S(2)}) collective-permute-start(bf16[4,240,384]{2,1,0:T(8,128)(2,1)S(1)} %get-tuple-element.192.refs_15_), channel_id=1, source_target_pairs={{0,4},{1,3},{2,6},{3,1},{4,0},{5,7},{6,2},{7,5},{8,12},{9,11},{10,... | collective-permute-start | bytes 2211848 | tf_op jit(solution)/shard_map/ppermute | solution.py:132
  250.4 18.3 %collective-permute-start.37 = (bf16[2,4,144,384]{3,2,1,0:T(8,128)(2,1)S(1)}, bf16[2,4,144,384]{3,2,1,0:T(8,128)(2,1)S(1)}, u32[]{:S(2)}, u32[]{:S(2)}) collective-permute-start(bf16[2,4,144,384]{3,2,1,0:T(8,128)(2,1)S(1)} %get-tuple-element.189.refs_14_), channel_id=1, source_target_pairs={{0,2},{1,5},{2,0},{3,7},{4,6},{5,1},{6,4},{7,3},{8,10},{9,13},{10,... | collective-permute-start | bytes 2654216 | tf_op jit(solution)/shard_map/ppermute | solution.py:132
  272.1 17.7 %collective-permute-start.48 = (bf16[240,384]{1,0:T(8,128)(2,1)S(1)}, bf16[240,384]{1,0:T(8,128)(2,1)S(1)}, u32[]{:S(2)}, u32[]{:S(2)}) collective-permute-start(bf16[240,384]{1,0:T(8,128)(2,1)S(1)} %get-tuple-element.197), channel_id=1, source_target_pairs={{0,8},{1,9},{2,10},{3,11},{4,12},{5,13},{6,14},{7,15},{8,16},{9,17... | collective-permute-start | bytes 552968 | tf_op jit(solution)/shard_map/ppermute | solution.py:132
  272.1 17.6 %collective-permute-start.47 = (bf16[240,384]{1,0:T(8,128)(2,1)S(1)}, bf16[240,384]{1,0:T(8,128)(2,1)S(1)}, u32[]{:S(2)}, u32[]{:S(2)}) collective-permute-start(bf16[240,384]{1,0:T(8,128)(2,1)S(1)} %get-tuple-element.198), channel_id=1, source_target_pairs={{0,16},{1,17},{2,18},{3,19},{4,20},{5,21},{6,22},{7,23},{8,24},{9,... | collective-permute-start | bytes 552968 | tf_op jit(solution)/shard_map/ppermute | solution.py:132
  273.0 16.8 %collective-permute-start.46 = (bf16[240,384]{1,0:T(8,128)(2,1)S(1)}, bf16[240,384]{1,0:T(8,128)(2,1)S(1)}, u32[]{:S(2)}, u32[]{:S(2)}) collective-permute-start(bf16[240,384]{1,0:T(8,128)(2,1)S(1)} %get-tuple-element.199), channel_id=1, source_target_pairs={{0,24},{1,25},{2,26},{3,27},{4,28},{5,29},{6,30},{7,31},{8,0},{9,1... | collective-permute-start | bytes 552968 | tf_op jit(solution)/shard_map/ppermute | solution.py:132
  276.0 16.3 %collective-permute-start.55 = (bf16[2,4,16,384]{3,2,1,0:T(8,128)(2,1)S(1)}, bf16[2,4,16,384]{3,2,1,0:T(8,128)(2,1)S(1)}, u32[]{:S(2)}, u32[]{:S(2)}) collective-permute-start(bf16[2,4,16,384]{3,2,1,0:T(8,128)(2,1)S(1)} %get-tuple-element.215.refs_24_), channel_id=1, source_target_pairs={{0,2},{1,5},{2,0},{3,7},{4,6},{5,1},{6,4},{7,3},{8,10},{9,13},{10,... | collective-permute-start | bytes 294920 | tf_op jit(solution)/shard_map/ppermute | solution.py:132
  289.9 15.8 %collective-permute-start.43 = (bf16[144,384]{1,0:T(8,128)(2,1)S(1)}, bf16[144,384]{1,0:T(8,128)(2,1)S(1)}, u32[]{:S(2)}, u32[]{:S(2)}) collective-permute-start(bf16[144,384]{1,0:T(8,128)(2,1)S(1)} %get-tuple-element.205.refs_23_), channel_id=1, source_target_pairs={{0,8},{1,9},{2,10},{3,11},{4,12},{5,13},{6,14},{7,15},{8,16},{9,17... | collective-permute-start | bytes 331784 | tf_op jit(solution)/shard_map/ppermute | solution.py:132
  (79 other events, 971.0 us)

commit v5 on v4

--- a/solution.py
+++ b/solution.py
@@ -1,3 +1,5 @@
+import math
+
 import jax
 import jax.numpy as jnp
 from jax import lax
@@ -189,6 +191,7 @@
 ROOT_HALF = 0.7071067811865476
 ROOT_TAU = 0.3989422804014327
 MIB = 1024 * 1024
+WIDTH = HEADS * HEAD_DIM
 SCALE = 1.0
 BACK = 3
 
@@ -246,28 +249,40 @@
     return pl.ds(row, rows), pl.ds(lane, lanes)
 
 
+def sites_of(at, pieces, rows, lanes):
+    if len(pieces) == 1:
+        (piece,) = pieces
+        narrow = 2 * (WIDTH // lanes)
+        for j in range(piece.shape[0]):
+            wide, y, core = j // narrow, j % narrow // 2, j % 2
+            yield piece.at[j], (pl.ds((wide * 2 + core) * rows, rows), pl.ds(y * lanes, lanes))
+    else:
+        side, deep = pieces[0].shape[:2]
+        for i, piece in enumerate(pieces):
+            for a in range(side):
+                for k in range(deep):
+                    yield piece.at[a, k], piece_place(at, (i * side + a) * deep + k, rows, lanes)
+
+
+def count_of(pieces):
+    return len(pieces) * math.prod(pieces[0].shape[:-2])
+
+
 def load_pieces(at, pieces, low, rows, whole, sem):
     copies = []
-    deep, lanes = pieces[0].shape[0], pieces[0].shape[2]
-    for i, piece in enumerate(pieces):
-        for k in range(deep):
-            place = piece_place(at, i * deep + k, rows, lanes)
-            copy = pltpu.make_async_copy(piece.at[k, pl.ds(low, rows), :], whole.at[place], sem.at[i * deep + k])
-            copy.start()
-            copies.append(copy)
+    for j, (piece, place) in enumerate(sites_of(at, pieces, rows, pieces[0].shape[-1])):
+        copy = pltpu.make_async_copy(piece.at[pl.ds(low, rows), :], whole.at[place], sem.at[j])
+        copy.start()
+        copies.append(copy)
     return copies
 
 
-def store_pieces(at, whole, rows, own, far, low, sem):
+def store_pieces(at, whole, rows, outs, low, sem):
     copies = []
-    count, deep, lanes = own.shape[0], own.shape[1], own.shape[3]
-    for i in range(2 * count):
-        for k in range(deep):
-            place = piece_place(at, i * deep + k, rows, lanes)
-            target = own.at[i, k] if i < count else far.at[i - count, k]
-            copy = pltpu.make_async_copy(whole.at[place], target.at[pl.ds(low, rows), :], sem.at[i * deep + k])
-            copy.start()
-            copies.append(copy)
+    for j, (piece, place) in enumerate(sites_of(at, outs, rows, outs[0].shape[-1])):
+        copy = pltpu.make_async_copy(whole.at[place], piece.at[pl.ds(low, rows), :], sem.at[j])
+        copy.start()
+        copies.append(copy)
     return copies
 
 
@@ -277,7 +292,7 @@
 
 
 def unpack_vectors(pieces, places, low, share, width, wide, narrow):
-    n, deep, lanes = len(pieces), pieces[0].shape[0], pieces[0].shape[2]
+    n, lanes = len(pieces), pieces[0].shape[-1]
     hidden = wide * narrow * share - 8 * width
     group = hidden // (2 * wide)
     unit = group // 2
@@ -286,13 +301,11 @@
     def kernel(at, *refs):
         parts, (vecs, bias, up_a, up_b, slots, flat, sem) = refs[:n], refs[n:]
         copies = []
-        for i, piece in enumerate(parts):
-            for k in range(deep):
-                j = i * deep + k
-                slot = at[j, 0] * narrow + at[j, 1] * 2 + at[j, 2]
-                copy = pltpu.make_async_copy(piece.at[k, pl.ds(low, 16), :], slots.at[slot], sem.at[j])
-                copy.start()
-                copies.append(copy)
+        for j, (piece, unused) in enumerate(sites_of(at, parts, 16, lanes)):
+            slot = at[j, 0] * narrow + at[j, 1] * 2 + at[j, 2]
+            copy = pltpu.make_async_copy(piece.at[pl.ds(low, 16), :], slots.at[slot], sem.at[j])
+            copy.start()
+            copies.append(copy)
         wait_all(copies)
         for j in range(wide * narrow):
             values = slots[j].astype(F32)[0:1, :]
@@ -322,7 +335,7 @@
         [
             pltpu.VMEM((wide * narrow, 16, lanes), BF),
             pltpu.VMEM((16, width), F32),
-            pltpu.SemaphoreType.DMA((n * deep,)),
+            pltpu.SemaphoreType.DMA((count_of(pieces),)),
         ],
         16,
         3,
@@ -360,9 +373,9 @@
         [
             pltpu.VMEM((3 * width, width), BF),
             pltpu.VMEM((rows, width), BF),
-            pltpu.SemaphoreType.DMA((n * pieces[0].shape[0],)),
+            pltpu.SemaphoreType.DMA((count_of(pieces),)),
         ],
-        32,
+        20,
         9,
         (places, tokens, vecs, bias, *pieces),
         prefetch=1,
@@ -429,7 +442,7 @@
         [lanes_of((half, QB)), lanes_of((16, QB))],
         [jax.ShapeDtypeStruct((half, rows), BF), jax.ShapeDtypeStruct((16, rows), F32)],
         [pltpu.VMEM((half, rows + QB), BF), pltpu.VMEM((half, rows + QB), BF)],
-        40,
+        20,
         6,
         (qkv_t, qkv_t, qkv_t, seg_row, seg_col),
         after=after,
@@ -459,8 +472,8 @@
         [lanes_of((width // PARTS, block))] * PARTS + [rows_of((block, width)), full(vecs.shape)] + [ANYWHERE] * n,
         [rows_of((block, width)), rows_of((block, width))],
         [jax.ShapeDtypeStruct((rows, width), F32), jax.ShapeDtypeStruct((rows, width), BF)],
-        [pltpu.VMEM((width, width), BF), pltpu.SemaphoreType.DMA((n * pieces[0].shape[0],))],
-        32,
+        [pltpu.VMEM((width, width), BF), pltpu.SemaphoreType.DMA((count_of(pieces),))],
+        16,
         5,
         (places, *o_parts, tokens, vecs, *pieces),
         prefetch=1,
@@ -468,15 +481,17 @@
     )
 
 
-def mlp_half(hidden, cot, bias, pieces, places, low, unit_rows, group_rows, wide, after=()):
+def mlp_half(hidden, cot, bias, pieces, places, low, unit_rows, out_shapes, wide, after=()):
     rows, width = hidden.shape
-    n, deep, lanes = len(pieces), pieces[0].shape[0], pieces[0].shape[2]
+    n, m, count = len(pieces), len(out_shapes), count_of(pieces)
     units = 2 * wide * unit_rows
     block = min(384, units)
 
     def kernel(at, hid, cot_ref, bias_ref, *refs):
         parts = refs[:n]
-        act_out, grad_out, sum_out, own, far, up, down, d_up, d_down, sem_a, sem_b = refs[n:]
+        act_out, grad_out, sum_out = refs[n : n + 3]
+        outs = refs[n + 3 : n + 3 + m]
+        up, down, d_up, d_down, sem_a, sem_b = refs[n + 3 + m :]
         step = pl.program_id(0)
 
         @pl.when(step == 0)
@@ -500,27 +515,25 @@
 
         @pl.when(step == pl.num_programs(0) - 1)
         def last():
-            one = store_pieces(at, d_up, unit_rows, own, far, 0, sem_a)
-            two = store_pieces(at, d_down, unit_rows, own, far, unit_rows, sem_b)
+            one = store_pieces(at, d_up, unit_rows, outs, 0, sem_a)
+            two = store_pieces(at, d_down, unit_rows, outs, unit_rows, sem_b)
             wait_all(one)
             wait_all(two)
 
-    piece_shape = jax.ShapeDtypeStruct((n // 2, deep, group_rows, lanes), BF)
     return call(
         kernel,
         (units // block,),
         [full((rows, width)), full((rows, width)), rows_of((block, 1))] + [ANYWHERE] * n,
-        [rows_of((block, rows)), rows_of((block, rows)), lanes_of((8, block)), ANYWHERE, ANYWHERE],
+        [rows_of((block, rows)), rows_of((block, rows)), lanes_of((8, block))] + [ANYWHERE] * m,
         [
             jax.ShapeDtypeStruct((units, rows), BF),
             jax.ShapeDtypeStruct((units, rows), BF),
             jax.ShapeDtypeStruct((8, units), F32),
-            piece_shape,
-            piece_shape,
+            *[jax.ShapeDtypeStruct(shape, BF) for shape in out_shapes],
         ],
         [pltpu.VMEM((units, width), BF)] * 4
-        + [pltpu.SemaphoreType.DMA((n * deep,))] * 2,
-        48,
+        + [pltpu.SemaphoreType.DMA((count,))] * 2,
+        32,
         22,
         (places, hidden, cot, bias, *pieces),
         prefetch=1,
@@ -531,12 +544,12 @@
 def second_norm_back(grads, mid, cot, vecs, groups, places, unit_rows, wide, after=()):
     rows, width = mid.shape
     block = 256
-    n, deep = len(groups[0][0]), groups[0][0][0].shape[0]
+    n, total_n, count = len(groups[0][0]), len(groups[0][0]) + len(groups[1][0]), count_of(groups[0][0])
     units = 2 * wide * unit_rows
 
     def kernel(at, ga, gb, mid_ref, cot_ref, vec, *refs):
-        parts = refs[: 2 * n]
-        out, low_out, sums, up_a, up_b, sem = refs[2 * n :]
+        parts = refs[:total_n]
+        out, low_out, sums, up_a, up_b, sem = refs[total_n:]
         step = pl.program_id(0)
 
         @pl.when(step == 0)
@@ -563,15 +576,15 @@
         kernel,
         (rows // block,),
         [lanes_of((units, block)), lanes_of((units, block)), rows_of((block, width)), rows_of((block, width)), full(vecs.shape)]
-        + [ANYWHERE] * (2 * n),
+        + [ANYWHERE] * total_n,
         [rows_of((block, width)), rows_of((block, width)), full((8, width))],
         [
             jax.ShapeDtypeStruct((rows, width), F32),
             jax.ShapeDtypeStruct((rows, width), BF),
             jax.ShapeDtypeStruct((8, width), F32),
         ],
-        [pltpu.VMEM((units, width), BF)] * 2 + [pltpu.SemaphoreType.DMA((2, n * deep))],
-        48,
+        [pltpu.VMEM((units, width), BF)] * 2 + [pltpu.SemaphoreType.DMA((2, count))],
+        32,
         14 * BACK,
         (places, *grads, mid, cot, vecs, *groups[0][0], *groups[1][0]),
         prefetch=1,
@@ -582,7 +595,7 @@
 def out_back(o_parts, grad_low, pieces, places, low_in, rows_piece, own, far, low, after=()):
     rows, width = grad_low.shape
     half = width // PARTS
-    n, deep = len(pieces), pieces[0].shape[0]
+    n = len(pieces)
 
     def kernel(at, o_a, o_b, grad, own_in, far_in, *refs):
         parts, (do_ref, own_ref, far_ref, weight, d_weight, sem) = refs[:n], refs[n:]
@@ -590,7 +603,7 @@
         d_weight[:half, :] = nn(o_a[...], grad[...]).astype(BF)
         d_weight[half:, :] = nn(o_b[...], grad[...]).astype(BF)
         wait_all(copies)
-        copies = store_pieces(at, d_weight, rows_piece, own_ref, far_ref, low, sem)
+        copies = store_pieces(at, d_weight, rows_piece, (own_ref, far_ref), low, sem)
         do_ref[...] = nt(weight[...], grad[...]).astype(BF)
         wait_all(copies)
 
@@ -604,8 +617,8 @@
             jax.ShapeDtypeStruct(own.shape, BF),
             jax.ShapeDtypeStruct(far.shape, BF),
         ],
-        [pltpu.VMEM((width, width), BF)] * 2 + [pltpu.SemaphoreType.DMA((n * deep,))],
-        32,
+        [pltpu.VMEM((width, width), BF)] * 2 + [pltpu.SemaphoreType.DMA((count_of(pieces),))],
+        20,
         5 * BACK,
         (places, *o_parts, grad_low, own, far, *pieces),
         prefetch=1,
@@ -668,7 +681,7 @@
         [full((3 * half, rows)), full((8, 3 * half))],
         [jax.ShapeDtypeStruct((3 * half, rows), BF), jax.ShapeDtypeStruct((8, 3 * half), F32)],
         [pltpu.VMEM((half, rows + QB), BF)] * 2 + [pltpu.VMEM((half, rows + QB), F32)] * 2,
-        48,
+        28,
         12 * BACK,
         (qkv_t, qkv_t, qkv_t, do_t, lse, seg_row, seg_col),
         after=after,
@@ -689,7 +702,7 @@
 
         @pl.when(step == pl.num_programs(0) - 1)
         def last():
-            wait_all(store_pieces(at, whole, rows_piece, own, far, 0, sem))
+            wait_all(store_pieces(at, whole, rows_piece, (own, far), 0, sem))
 
     piece_shape = jax.ShapeDtypeStruct((sites, topo.Z, rows_piece, lanes), BF)
     return call(
@@ -699,7 +712,7 @@
         [ANYWHERE, ANYWHERE],
         [piece_shape, piece_shape],
         [pltpu.VMEM((count, width), BF), pltpu.SemaphoreType.DMA((2 * sites * topo.Z,))],
-        32,
+        24,
         7 * BACK,
         (places, *grad_parts, hidden),
         prefetch=1,
@@ -736,8 +749,8 @@
         + [ANYWHERE] * n,
         [rows_of((block, width)), full((8, width))],
         [jax.ShapeDtypeStruct((rows, width), BF), jax.ShapeDtypeStruct((8, width), F32)],
-        [pltpu.VMEM((count, width), BF), pltpu.SemaphoreType.DMA((n * pieces[0].shape[0],))],
-        40,
+        [pltpu.VMEM((count, width), BF), pltpu.SemaphoreType.DMA((count_of(pieces),))],
+        28,
         11 * BACK,
         (places, *grad_parts, tokens, grad_mid, vecs, *pieces),
         prefetch=1,
@@ -748,12 +761,12 @@
 def finish_out(acts, mid, vecs, groups, places, unit_rows, wide, after=()):
     rows, width = mid.shape
     block = 256
-    n, deep = len(groups[0][0]), groups[0][0][0].shape[0]
+    n, total_n, count = len(groups[0][0]), len(groups[0][0]) + len(groups[1][0]), count_of(groups[0][0])
     units = 2 * wide * unit_rows
 
     def kernel(at, act_a, act_b, mid_ref, vec, *refs):
-        parts = refs[: 2 * n]
-        out, down_a, down_b, sem = refs[2 * n :]
+        parts = refs[:total_n]
+        out, down_a, down_b, sem = refs[total_n:]
 
         @pl.when(pl.program_id(0) == 0)
         def first():
@@ -769,11 +782,11 @@
         kernel,
         (rows // block,),
         [lanes_of((units, block)), lanes_of((units, block)), rows_of((block, width)), full(vecs.shape)]
-        + [ANYWHERE] * (2 * n),
+        + [ANYWHERE] * total_n,
         rows_of((block, width)),
         jax.ShapeDtypeStruct((rows, width), BF),
-        [pltpu.VMEM((units, width), BF)] * 2 + [pltpu.SemaphoreType.DMA((2, n * deep))],
-        48,
+        [pltpu.VMEM((units, width), BF)] * 2 + [pltpu.SemaphoreType.DMA((2, count))],
+        32,
         11 * BACK,
         (places, *acts, mid, vecs, *groups[0][0], *groups[1][0]),
         prefetch=1,
@@ -856,17 +869,17 @@
 
     def along(self, others=()):
         stack = tied(jnp.stack((self.piece, *self.coming)), others)
+        self.first = stack
         self.coming = tuple(send(stack, self.topo.ap[k]) for k in range(1, self.topo.X))
-        self.line = (stack, *self.coming)
 
     def across(self, others=()):
-        self.near = tuple(send(p, self.topo.cp) for p in self.line)
-        line = tied(self.line, others)
-        self.coming = tuple(send(q, self.topo.bp[k]) for k in range(1, self.topo.X) for q in line)
+        self.line = tied(jnp.stack((self.first, *self.coming)), others)
+        self.coming = tuple(send(self.line, self.topo.bp[k]) for k in range(1, self.topo.X))
+        self.near = send(self.line, self.topo.cp)
 
     def core(self, others=()):
         coming = tied(self.coming, others)
-        self.pieces = [*self.line, *coming, *self.near, *[send(p, self.topo.cp) for p in coming]]
+        self.pieces = [self.line, *coming, self.near, *[send(p, self.topo.cp) for p in coming]]
 
 
 class Chain:
@@ -935,40 +948,44 @@
     one = Spread(
         jnp.concatenate([first[:r_qkv], tail_rows(vectors.astype(BF), 16, lanes), first[r_qkv:]], axis=0), topo
     )
-    rest = pair_up(tied(halves[1], one.coming), topo, core)
+    rest = pair_up(tied(halves[1], (first,)), topo, core)
     piece_two = jnp.concatenate([rest[:r_unit], rest[2 * r_unit : 3 * r_unit]], axis=0)
     piece_three = jnp.concatenate([rest[r_unit : 2 * r_unit], rest[3 * r_unit :]], axis=0)
-    one.along()
-    two = Spread(tied(piece_two, one.line[:1]), topo)
+    one.along((rest,))
+    two = Spread(tied(piece_two, one.coming), topo)
     one.across()
-    one.core()
+    two.along(one.coming)
+    one.core((two.first,))
     one = one.pieces
+    sites = topo.X * topo.X
+    shapes_a = [(sites, topo.Z, 2 * r_unit, lanes)] * 2
+    shapes_b = [(sites, topo.Z, 2 * r_unit + r_out, lanes)] * 2
     vecs, bias_qkv, *bias_up = unpack_vectors(one, places, vec_low, vectors.shape[0], width, wide, topo.narrow)
     segment = image_ids(bucket_counts[0], rows)
     seg_row = jnp.broadcast_to(segment[None], (8, rows))
     seg_col = jnp.pad(segment, (QB // 2, QB // 2), constant_values=-1)[:, None]
 
+    two_along = two.coming
+    two.across()
     hidden_one, qkv_t = project_qkv(tokens, vecs, bias_qkv, one, places, (r_qkv, wide))
-    two.along((hidden_one,))
     three = Spread(tied(piece_three, (hidden_one,)), topo)
-    attn_a, lse_a = attend(qkv_t, seg_row, seg_col, width, 0, after=two.line[:1])
-    two.across((lse_a,))
+    attn_a, lse_a = attend(qkv_t, seg_row, seg_col, width, 0, after=two_along)
+    two.core((lse_a,))
     attn_b, lse_b = attend(qkv_t, seg_row, seg_col, width, 1)
     attn_t, lse = (attn_a, attn_b), (lse_a, lse_b)
     three.along((lse_b,))
-    mid, hidden_two = project_out(attn_t, tokens, vecs, one, places, out_low, r_out, after=three.line[:1])
-    two.core((hidden_two,))
+    two = two.pieces
+    mid, hidden_two = project_out(attn_t, tokens, vecs, one, places, out_low, r_out, after=(three.first,))
     three.across((hidden_two,))
-    two = two.pieces
-    three_along = three.line
+    three_along = (three.line,)
     act_a, grad_a, sum_a, own_a, far_a = mlp_half(
-        hidden_two, cotangent, bias_up[0], two, places, 0, r_unit, 2 * r_unit, wide, after=three_along
+        hidden_two, cotangent, bias_up[0], two, places, 0, r_unit, shapes_a, wide, after=three_along
     )
     three.core((sum_a,))
     three = three.pieces
     chain_a = Chain(own_a, far_a, topo)
     act_b, grad_b, sum_b, own_b, far_b = mlp_half(
-        hidden_two, cotangent, bias_up[1], three, places, 0, r_unit, 2 * r_unit + r_out, wide
+        hidden_two, cotangent, bias_up[1], three, places, 0, r_unit, shapes_b, wide
     )
     chain_a.across((sum_b,))
     grad_mid, grad_mid_low, sums_two = second_norm_back(
@@ -985,7 +1002,7 @@
         qkv_t, do_t, lse[1], seg_row, seg_col, width, 1, after=chain_a.sent + chain_b.sent
     )
     grad_t = (grads_0, grads_1)
-    own_q, far_q = qkv_back(grad_t, hidden_one, places, r_qkv, topo)
+    own_q, far_q = qkv_back(grad_t, hidden_one, places, r_qkv, topo, after=chain_a.arrived())
     chain_q = Chain(own_q, far_q, topo)
     chain_b.along((far_q,))
     chain_q.across()
@@ -1006,7 +1023,7 @@
     )
     chain_v.along((block_out,))
     chain_v.down()
-    part_a, part_b, part_q = chain_a.result((sums_one,)), chain_b.result((block_out,)), chain_q.result()
+    part_a, part_b, part_q = chain_a.result((sums_one,)), chain_b.result((block_out,)), chain_q.result((block_out,))
     vector_grad = chain_v.result()[0, : vectors.shape[0]]
     down = jnp.concatenate([part_a[r_unit:], part_b[r_unit : 2 * r_unit]], axis=0)
     up = jnp.concatenate([part_a[:r_unit], part_b[:r_unit]], axis=0)

time: 317 us -> 293 us (0.924)
  Pallas kernels: 148 us -> 132 us
  other arithmetic: 22 us -> 9.14 us
  local copies, waits for them, and re-layouts: 17.7 us -> 23.4 us
    pallas_call x15, Pallas kernels: 148 us -> 132 us  [call(): pl.pallas_call(body, grid_spec=pltpu.PrefetchScalarGridSpec(num_scalar_pr...]
    convert_element_type x12, other arithmetic: 12.8 us -> 4.29 us  [stage(): self.held, *sent = [self.fold(k).astype(BF) for k in range(count)]]
    unnamed x107 -> x99, local copies, waits for them, and re-layouts: 14.3 us -> 21.9 us
    ppermute x60 -> x51, starting transfers between devices: 55.7 us -> 56.7 us  [send(): return lax.ppermute(values, AXES, perm)]
    ppermute x60 -> x51, waiting for transfers between devices: 63.9 us -> 63.4 us  [send(): return lax.ppermute(values, AXES, perm)]
  transfers between devices with their start and end apart: 60 -> 51, of which waited for: 19 -> 17; matrix products, arithmetic and copies ran while one was open for 6% -> 3% of each run, Pallas kernels for 44% -> 46%
where the time goes in v5:
time: 293 us; the launch traced here: 287 us
  Pallas kernels  132 us (45%)
  waiting for transfers between devices  63.4 us (22%)
  starting transfers between devices  56.7 us (19%)
  local copies, waits for them, and re-layouts  23.4 us (8%)
  other arithmetic  9.14 us (3%)
  between operations  3.16 us (1%)
    pallas_call x15, Pallas kernels, call(): pl.pallas_call(body, grid_spec=pltpu.PrefetchScalarGridSpec(num_scalar_pr...  132 us
    ppermute x51, waiting for transfers between devices, send(): return lax.ppermute(values, AXES, perm)  63.4 us
    ppermute x51, starting transfers between devices, send(): return lax.ppermute(values, AXES, perm)  56.7 us
    unnamed x99, local copies, waits for them, and re-layouts  21.9 us
  transfers between devices with their start and end apart: 51, of which 17 were waited for; matrix products, arithmetic and copies ran while one was open for 3% of the time, Pallas kernels for 46%

profile of v5, /device:TPU:0, one launch (start us, length us, event | category | flops | bytes accessed | tf_op | source)
XLA Modules:
  0.0 287.3 jit_solution(5172250430292760586)
XLA Ops:
  4.5 4.0 %collective-permute-start.2 = (bf16[208,384]{1,0:T(8,128)(2,1)S(1)}, bf16[208,384]{1,0:T(8,128)(2,1)S(1)}, u32[]{:S(2)}, u32[]{:S(2)}) collective-permute-start(bf16[208,384]{1,0:T(8,128)(2,1)S(1)} %fusion.24), channel_id=1, source_target_pairs={{0,16},{1,17},{2,18},{3,19},{4,20},{5,21},{6,22},{7,23},{8,24},{9,... | collective-permute-start | bytes 479240 | tf_op jit(solution)/shard_map/ppermute | solution.py:134
  10.1 2.2 collective-permute-start.3
  12.3 7.9 %collective-permute-done.2 = bf16[208,384]{1,0:T(8,128)(2,1)S(1)} collective-permute-done((bf16[208,384]{1,0:T(8,128)(2,1)S(1)}, bf16[208,384]{1,0:T(8,128)(2,1)S(1)}, u32[]{:S(2)}, u32[]{:S(2)}) %collective-permute-start.2) | collective-permute-done | bytes 159776 | tf_op jit(solution)/shard_map/ppermute | solution.py:134
  23.4 8.5 %collective-permute-done.5 = bf16[4,208,384]{2,1,0:T(8,128)(2,1)S(1)} collective-permute-done((bf16[4,208,384]{2,1,0:T(8,128)(2,1)S(1)}, bf16[4,208,384]{2,1,0:T(8,128)(2,1)S(1)}, u32[]{:S(2)}, u32[]{:S(2)}) %collective-permute-start.5) | collective-permute-done | bytes 639008 | tf_op jit(solution)/shard_map/ppermute | solution.py:134
  35.6 2.1 collective-permute-start.9
  37.7 2.5 collective-permute-start.8
  40.2 1.9 collective-permute-start.7
  42.3 11.4 %collective-permute-done.8 = bf16[192,384]{1,0:T(8,128)(2,1)S(1)} collective-permute-done((bf16[192,384]{1,0:T(8,128)(2,1)S(1)}, bf16[192,384]{1,0:T(8,128)(2,1)S(1)}, u32[]{:S(2)}, u32[]{:S(2)}) %collective-permute-start.8) | collective-permute-done | bytes 147488 | tf_op jit(solution)/shard_map/ppermute | solution.py:134
  58.0 5.9 %collective-permute-done.12.refs_5_ = bf16[4,192,384]{2,1,0:T(8,128)(2,1)S(1)} collective-permute-done((bf16[4,192,384]{2,1,0:T(8,128)(2,1)S(1)}, bf16[4,192,384]{2,1,0:T(8,128)(2,1)S(1)}, u32[]{:S(2)}, u32[]{:S(2)}) %collective-permute-start.12) | collective-permute-done | bytes 589856 | tf_op jit(solution)/shard_map/ppermute | solution.py:134
  64.7 3.0 %shard_map.135 = (f32[8,768]{1,0:T(8,128)S(1)}, f32[2304,1]{1,0:T(8,128)S(1)}, f32[1536,1]{1,0:T(8,128)S(1)}, f32[1536,1]{1,0:T(8,128)S(1)}) custom-call(s32[32,3]{1,0:T(8,128)S(1)} %copy.71.refs_0_, bf16[2,4,208,384]{3,2,1,0:T(8,128)(2,1)S(1)} %pad_maximum_fusion.refs_1_.refs_4_.refs_5_.refs_6_, ...), custom_call_target="tpu_custom_call" | custom-call | flops 3000000000 | bytes 9000000 | tf_op jit(solution)/shard_map/pallas_call | solution.py:215
  67.7 9.2 %shard_map.136 = (bf16[1024,768]{1,0:T(8,128)(2,1)S(1)}, bf16[2304,1024]{1,0:T(8,128)(2,1)S(1)}) custom-call(s32[32,3]{1,0:T(8,128)S(1)} %copy.71.refs_0_, bf16[1024,768]{1,0:T(8,128)(2,1)S(1)} %copy-done.2, f32[8,768]{1,0:T(8,128)S(1)} %get-tuple-element.88.refs_2_.refs_4_.refs_5_, f32[2304,1]{1,0:T(8,128)S(1)} %get-tuple-element.89.refs_3_, ...), custom_call_target="tpu_custom_call" | custom-call | flops 8999999488 | bytes 27000000 | tf_op jit(solution)/shard_map/pallas_call | solution.py:215
  78.1 2.1 collective-permute-start.13
  80.2 6.0 %shard_map.137 = (bf16[384,1024]{1,0:T(8,128)(2,1)S(1)}, f32[16,1024]{1,0:T(8,128)S(1)}) custom-call(bf16[2304,1024]{1,0:T(8,128)(2,1)S(1)} %get-tuple-element.90.refs_0_.refs_1_.refs_2_, bf16[2304,1024]{1,0:T(8,128)(2,1)S(1)} %get-tuple-element.90.refs_0_.refs_1_.refs_2_, bf16[2304,1024]{1,0:T(8,128)(2,1)S(1)} %get-tuple-element.90.refs_0_.refs_1_.refs_2_, ...), custom_call_target="tpu_custom_call" | custom-call | flops 6000000000 | bytes 18000000 | tf_op jit(solution)/shard_map/pallas_call | solution.py:215
  86.3 6.0 %shard_map.138 = (bf16[384,1024]{1,0:T(8,128)(2,1)S(1)}, f32[16,1024]{1,0:T(8,128)S(1)}) custom-call(bf16[2304,1024]{1,0:T(8,128)(2,1)S(1)} %get-tuple-element.90.refs_0_.refs_1_.refs_2_, bf16[2304,1024]{1,0:T(8,128)(2,1)S(1)} %get-tuple-element.90.refs_0_.refs_1_.refs_2_, bf16[2304,1024]{1,0:T(8,128)(2,1)S(1)} %get-tuple-element.90.refs_0_.refs_1_.refs_2_, ...), custom_call_target="tpu_custom_call" | custom-call | flops 6000000000 | bytes 18000000 | tf_op jit(solution)/shard_map/pallas_call | solution.py:215
  94.0 5.6 %shard_map.139 = (f32[1024,768]{1,0:T(8,128)S(1)}, bf16[1024,768]{1,0:T(8,128)(2,1)S(1)}) custom-call(s32[32,3]{1,0:T(8,128)S(1)} %copy.71.refs_0_, bf16[384,1024]{1,0:T(8,128)(2,1)S(1)} %get-tuple-element.91.refs_1_, bf16[384,1024]{1,0:T(8,128)(2,1)S(1)} %get-tuple-element.92.refs_2_, bf16[1024,768]{1,0:T(8,128)(2,1)S(1)} %copy-done.2, ...), custom_call_target="tpu_custom_call" | custom-call | flops 5000000000 | bytes 15000000 | tf_op jit(solution)/shard_map/pallas_call | solution.py:215
  103.5 18.2 %shard_map.140 = (bf16[1536,1024]{1,0:T(8,128)(2,1)S(1)}, bf16[1536,1024]{1,0:T(8,128)(2,1)S(1)}, f32[8,1536]{1,0:T(8,128)S(1)}, bf16[4,4,192,384]{3,2,1,0:T(8,128)(2,1)S(1)}, bf16[4,4,192,384]{3,2,1,0:T(8,128)(2,1)}) custom-call(s32[32,3]{1,0:T(8,128)S(1)} %copy.71.refs_0_, bf16[1024,768]{1,0:T(8,128)(2,1)S(1)} %get-tuple-element.97.refs_1_, ...), custom_call_target="tpu_custom_call" | custom-call | flops 22000001024 | bytes 66000000 | tf_op jit(solution)/shard_map/pallas_call | solution.py:215
  130.1 18.3 %shard_map.141 = (bf16[1536,1024]{1,0:T(8,128)(2,1)S(1)}, bf16[1536,1024]{1,0:T(8,128)(2,1)S(1)}, f32[8,1536]{1,0:T(8,128)S(1)}, bf16[4,4,240,384]{3,2,1,0:T(8,128)(2,1)S(1)}, bf16[4,4,240,384]{3,2,1,0:T(8,128)(2,1)}) custom-call(s32[32,3]{1,0:T(8,128)S(1)} %copy.71.refs_0_, bf16[1024,768]{1,0:T(8,128)(2,1)S(1)} %get-tuple-element.97.refs_1_, ...), custom_call_target="tpu_custom_call" | custom-call | flops 22000001024 | bytes 66000000 | tf_op jit(solution)/shard_map/pallas_call | solution.py:215
  156.9 11.7 %shard_map.142 = (f32[1024,768]{1,0:T(8,128)S(1)}, bf16[1024,768]{1,0:T(8,128)(2,1)S(1)}, f32[8,768]{1,0:T(8,128)S(1)}) custom-call(s32[32,3]{1,0:T(8,128)S(1)} %copy.71.refs_0_, bf16[1536,1024]{1,0:T(8,128)(2,1)S(1)} %copy-done.34, bf16[1536,1024]{1,0:T(8,128)(2,1)} %copy-done.37, f32[1024,768]{1,0:T(8,128)} %copy-done.23, bf16[1024,768]{1,0:T(8,128)(2,1)S(1)} %copy-done.1, ...), custom_call_target="tpu_custom_call" | custom-call | flops 41999998976 | bytes 126000000 | tf_op jit(solution)/shard_map/pallas_call | solution.py:215
  170.2 5.2 %shard_map.143 = (bf16[768,1024]{1,0:T(8,128)(2,1)S(1)}, bf16[4,4,240,384]{3,2,1,0:T(8,128)(2,1)S(1)}, bf16[4,4,240,384]{3,2,1,0:T(8,128)(2,1)}) custom-call(s32[32,3]{1,0:T(8,128)S(1)} %copy.71.refs_0_, bf16[384,1024]{1,0:T(8,128)(2,1)S(1)} %copy-done.26, bf16[384,1024]{1,0:T(8,128)(2,1)S(1)} %copy-done.28, ...), custom_call_target="tpu_custom_call", output_to_operand_aliasing={{1}: (4, {}), {2}: (5, {})} | custom-call | flops 15000000512 | bytes 45000000 | tf_op jit(solution)/shard_map/pallas_call | solution.py:215
  177.0 2.3 copy-done.22
  179.4 10.7 %shard_map.144 = (bf16[1152,1024]{1,0:T(8,128)(2,1)S(1)}, f32[8,1152]{1,0:T(8,128)S(1)}) custom-call(bf16[2304,1024]{1,0:T(8,128)(2,1)S(1)} %copy-done.22, bf16[2304,1024]{1,0:T(8,128)(2,1)S(1)} %copy-done.22, bf16[2304,1024]{1,0:T(8,128)(2,1)S(1)} %copy-done.22, bf16[768,1024]{1,0:T(8,128)(2,1)S(1)} %get-tuple-element.118.refs_3_, ...), custom_call_target="tpu_custom_call" | custom-call | flops 35999997952 | bytes 108000000 | tf_op jit(solution)/shard_map/pallas_call | solution.py:215
  193.0 2.8 collective-permute-start.27
  196.6 10.3 %shard_map.145 = (bf16[1152,1024]{1,0:T(8,128)(2,1)S(1)}, f32[8,1152]{1,0:T(8,128)S(1)}) custom-call(bf16[2304,1024]{1,0:T(8,128)(2,1)S(1)} %bitcast.131, bf16[2304,1024]{1,0:T(8,128)(2,1)S(1)} %bitcast.131, bf16[2304,1024]{1,0:T(8,128)(2,1)S(1)} %bitcast.131, bf16[768,1024]{1,0:T(8,128)(2,1)S(1)} %get-tuple-element.118.refs_3_, ...), custom_call_target="tpu_custom_call" | custom-call | flops 35999997952 | bytes 108000000 | tf_op jit(solution)/shard_map/pallas_call | solution.py:215
  207.5 6.0 %shard_map.146 = (bf16[4,4,144,384]{3,2,1,0:T(8,128)(2,1)S(1)}, bf16[4,4,144,384]{3,2,1,0:T(8,128)(2,1)S(1)}) custom-call(s32[32,3]{1,0:T(8,128)S(1)} %copy.71.refs_0_, bf16[1152,1024]{1,0:T(8,128)(2,1)S(1)} %get-tuple-element.121.refs_1_, bf16[1152,1024]{1,0:T(8,128)(2,1)S(1)} %get-tuple-element.129.refs_2_, bf16[1024,768]{1,0:T(8,128)(2,1)S(1)} %copy-done.30, ...), custom_call_target="tpu_custom_call" | custom-call | flops 20999999488 | bytes 63000000 | tf_op jit(solution)/shard_map/pallas_call | solution.py:215
  213.6 12.7 %collective-permute-done.32 = bf16[2,4,240,384]{3,2,1,0:T(8,128)(2,1)S(1)} collective-permute-done((bf16[2,4,240,384]{3,2,1,0:T(8,128)(2,1)S(1)}, bf16[2,4,240,384]{3,2,1,0:T(8,128)(2,1)S(1)}, u32[]{:S(2)}, u32[]{:S(2)}) %collective-permute-start.32) | collective-permute-done | bytes 1474592 | tf_op jit(solution)/shard_map/ppermute | solution.py:134
  229.6 10.2 %shard_map.147 = (bf16[1024,768]{1,0:T(8,128)(2,1)}, f32[8,768]{1,0:T(8,128)S(1)}) custom-call(s32[32,3]{1,0:T(8,128)S(1)} %copy.71.refs_0_, bf16[1152,1024]{1,0:T(8,128)(2,1)S(1)} %get-tuple-element.121.refs_1_, bf16[1152,1024]{1,0:T(8,128)(2,1)S(1)} %get-tuple-element.129.refs_2_, bf16[1024,768]{1,0:T(8,128)(2,1)S(1)} %copy-done.3, ...), custom_call_target="tpu_custom_call" | custom-call | flops 32999999488 | bytes 99000000 | tf_op jit(solution)/shard_map/pallas_call | solution.py:215
  240.0 5.9 %collective-permute-done.39 = bf16[4,240,384]{2,1,0:T(8,128)(2,1)S(1)} collective-permute-done((bf16[4,240,384]{2,1,0:T(8,128)(2,1)S(1)}, bf16[4,240,384]{2,1,0:T(8,128)(2,1)S(1)}, u32[]{:S(2)}, u32[]{:S(2)}) %collective-permute-start.39) | collective-permute-done | bytes 737312 | tf_op jit(solution)/shard_map/ppermute | solution.py:134
  249.5 2.8 collective-permute-start.40
  254.6 10.1 %shard_map.149 = bf16[1024,768]{1,0:T(8,128)(2,1)} custom-call(s32[32,3]{1,0:T(8,128)S(1)} %copy.71.refs_0_, bf16[1536,1024]{1,0:T(8,128)(2,1)S(1)} %copy-done.32, bf16[1536,1024]{1,0:T(8,128)(2,1)S(1)} %copy-done.36, f32[1024,768]{1,0:T(8,128)S(1)} %copy-done.24, f32[8,768]{1,0:T(8,128)S(1)} %get-tuple-element.88.refs_2_.refs_4_.refs_5_, ...), custom_call_target="tpu_custom_call" | custom-call | flops 32999999488 | bytes 99000000 | tf_op jit(solution)/shard_map/pallas_call | solution.py:215
  264.9 4.1 %collective-permute-start.37 = (bf16[144,384]{1,0:T(8,128)(2,1)S(1)}, bf16[144,384]{1,0:T(8,128)(2,1)S(1)}, u32[]{:S(2)}, u32[]{:S(2)}) collective-permute-start(bf16[144,384]{1,0:T(8,128)(2,1)S(1)} %get-tuple-element.208.refs_15_), channel_id=1, source_target_pairs={{0,8},{1,9},{2,10},{3,11},{4,12},{5,13},{6,14},{7,15},{8,16},{9,17... | collective-permute-start | bytes 331784 | tf_op jit(solution)/shard_map/ppermute | solution.py:134
  276.2 2.0 collective-permute-start.49
  278.9 2.3 collective-permute-start.35
  (252 shorter events, 69.9 us)
Async XLA Ops:
  4.5 15.8 %collective-permute-start.2 = (bf16[208,384]{1,0:T(8,128)(2,1)S(1)}, bf16[208,384]{1,0:T(8,128)(2,1)S(1)}, u32[]{:S(2)}, u32[]{:S(2)}) collective-permute-start(bf16[208,384]{1,0:T(8,128)(2,1)S(1)} %fusion.24), channel_id=1, source_target_pairs={{0,16},{1,17},{2,18},{3,19},{4,20},{5,21},{6,22},{7,23},{8,24},{9,... | collective-permute-start | bytes 479240 | tf_op jit(solution)/shard_map/ppermute | solution.py:134
  8.5 11.8 %collective-permute-start.1 = (bf16[208,384]{1,0:T(8,128)(2,1)S(1)}, bf16[208,384]{1,0:T(8,128)(2,1)S(1)}, u32[]{:S(2)}, u32[]{:S(2)}) collective-permute-start(bf16[208,384]{1,0:T(8,128)(2,1)S(1)} %fusion.24), channel_id=1, source_target_pairs={{0,8},{1,9},{2,10},{3,11},{4,12},{5,13},{6,14},{7,15},{8,16},{9,17... | collective-permute-start | bytes 479240 | tf_op jit(solution)/shard_map/ppermute | solution.py:134
  10.1 11.3 %collective-permute-start.3 = (bf16[208,384]{1,0:T(8,128)(2,1)S(1)}, bf16[208,384]{1,0:T(8,128)(2,1)S(1)}, u32[]{:S(2)}, u32[]{:S(2)}) collective-permute-start(bf16[208,384]{1,0:T(8,128)(2,1)S(1)} %fusion.24), channel_id=1, source_target_pairs={{0,24},{1,25},{2,26},{3,27},{4,28},{5,29},{6,30},{7,31},{8,0},{9,1... | collective-permute-start | bytes 479240 | tf_op jit(solution)/shard_map/ppermute | solution.py:134
  32.1 21.7 %collective-permute-start.6 = (bf16[2,4,208,384]{3,2,1,0:T(8,128)(2,1)S(1)}, bf16[2,4,208,384]{3,2,1,0:T(8,128)(2,1)}, u32[]{:S(2)}, u32[]{:S(2)}) collective-permute-start(bf16[2,4,208,384]{3,2,1,0:T(8,128)(2,1)S(1)} %pad_maximum_fusion.refs_1_.refs_4_.refs_5_.refs_6_), channel_id=1, source_target_pairs={{0,2},{1,5},{2,0},{3,7},{4,6},{5,1},{6,4},{7,3},{8,10},{9,13},{10,... | collective-permute-start | bytes 3833864 | tf_op jit(solution)/shard_map/ppermute | solution.py:134
  37.7 16.0 %collective-permute-start.8 = (bf16[192,384]{1,0:T(8,128)(2,1)S(1)}, bf16[192,384]{1,0:T(8,128)(2,1)S(1)}, u32[]{:S(2)}, u32[]{:S(2)}) collective-permute-start(bf16[192,384]{1,0:T(8,128)(2,1)S(1)} %pad_maximum_fusion.11), channel_id=1, source_target_pairs={{0,16},{1,17},{2,18},{3,19},{4,20},{5,21},{6,22},{7,23},{8,24},{9,... | collective-permute-start | bytes 442376 | tf_op jit(solution)/shard_map/ppermute | solution.py:134
  40.2 13.6 %collective-permute-start.7 = (bf16[192,384]{1,0:T(8,128)(2,1)S(1)}, bf16[192,384]{1,0:T(8,128)(2,1)S(1)}, u32[]{:S(2)}, u32[]{:S(2)}) collective-permute-start(bf16[192,384]{1,0:T(8,128)(2,1)S(1)} %pad_maximum_fusion.11), channel_id=1, source_target_pairs={{0,8},{1,9},{2,10},{3,11},{4,12},{5,13},{6,14},{7,15},{8,16},{9,17... | collective-permute-start | bytes 442376 | tf_op jit(solution)/shard_map/ppermute | solution.py:134
  42.1 22.5 %collective-permute-start.10 = (bf16[2,4,208,384]{3,2,1,0:T(8,128)(2,1)S(1)}, bf16[2,4,208,384]{3,2,1,0:T(8,128)(2,1)}, u32[]{:S(2)}, u32[]{:S(2)}) collective-permute-start(bf16[2,4,208,384]{3,2,1,0:T(8,128)(2,1)S(1)} %pad_maximum_fusion.refs_1_.refs_4_.refs_5_.refs_6_), channel_id=1, source_target_pairs={{0,1},{1,0},{2,3},{3,2},{4,5},{5,4},{6,7},{7,6},{8,9},{9,8},{10,11... | collective-permute-start | bytes 3833864 | tf_op jit(solution)/shard_map/ppermute | solution.py:134
  64.0 39.4 %collective-permute-start.17 = (bf16[2,4,192,384]{3,2,1,0:T(8,128)(2,1)S(1)}, bf16[2,4,192,384]{3,2,1,0:T(8,128)(2,1)S(1)}, u32[]{:S(2)}, u32[]{:S(2)}) collective-permute-start(bf16[2,4,192,384]{3,2,1,0:T(8,128)(2,1)S(1)} %pad_maximum_fusion.1.refs_4_.refs_6_.refs_5_), channel_id=1, source_target_pairs={{0,1},{1,0},{2,3},{3,2},{4,5},{5,4},{6,7},{7,6},{8,9},{9,8},{10,11... | collective-permute-start | bytes 3538952 | tf_op jit(solution)/shard_map/ppermute | solution.py:134
  64.1 22.1 %collective-permute-start.16 = (bf16[2,4,192,384]{3,2,1,0:T(8,128)(2,1)S(1)}, bf16[2,4,192,384]{3,2,1,0:T(8,128)(2,1)S(1)}, u32[]{:S(2)}, u32[]{:S(2)}) collective-permute-start(bf16[2,4,192,384]{3,2,1,0:T(8,128)(2,1)S(1)} %pad_maximum_fusion.1.refs_4_.refs_6_.refs_5_), channel_id=1, source_target_pairs={{0,2},{1,5},{2,0},{3,7},{4,6},{5,1},{6,4},{7,3},{8,10},{9,13},{10,... | collective-permute-start | bytes 3538952 | tf_op jit(solution)/shard_map/ppermute | solution.py:134
  76.9 15.4 %collective-permute-start.15 = (bf16[192,384]{1,0:T(8,128)(2,1)S(1)}, bf16[192,384]{1,0:T(8,128)(2,1)S(1)}, u32[]{:S(2)}, u32[]{:S(2)}) collective-permute-start(bf16[192,384]{1,0:T(8,128)(2,1)S(1)} %pad_maximum_fusion.12), channel_id=1, source_target_pairs={{0,24},{1,25},{2,26},{3,27},{4,28},{5,29},{6,30},{7,31},{8,0},{9,1... | collective-permute-start | bytes 442376 | tf_op jit(solution)/shard_map/ppermute | solution.py:134
  77.0 15.3 %collective-permute-start.14 = (bf16[192,384]{1,0:T(8,128)(2,1)S(1)}, bf16[192,384]{1,0:T(8,128)(2,1)S(1)}, u32[]{:S(2)}, u32[]{:S(2)}) collective-permute-start(bf16[192,384]{1,0:T(8,128)(2,1)S(1)} %pad_maximum_fusion.12), channel_id=1, source_target_pairs={{0,16},{1,17},{2,18},{3,19},{4,20},{5,21},{6,22},{7,23},{8,24},{9,... | collective-permute-start | bytes 442376 | tf_op jit(solution)/shard_map/ppermute | solution.py:134
  78.1 14.2 %collective-permute-start.13 = (bf16[192,384]{1,0:T(8,128)(2,1)S(1)}, bf16[192,384]{1,0:T(8,128)(2,1)S(1)}, u32[]{:S(2)}, u32[]{:S(2)}) collective-permute-start(bf16[192,384]{1,0:T(8,128)(2,1)S(1)} %pad_maximum_fusion.12), channel_id=1, source_target_pairs={{0,8},{1,9},{2,10},{3,11},{4,12},{5,13},{6,14},{7,15},{8,16},{9,17... | collective-permute-start | bytes 442376 | tf_op jit(solution)/shard_map/ppermute | solution.py:134
  86.2 17.2 %collective-permute-start.18 = (bf16[2,4,192,384]{3,2,1,0:T(8,128)(2,1)S(1)}, bf16[2,4,192,384]{3,2,1,0:T(8,128)(2,1)S(1)}, u32[]{:S(2)}, u32[]{:S(2)}) collective-permute-start(bf16[2,4,192,384]{3,2,1,0:T(8,128)(2,1)S(1)} %collective-permute-done.16.refs_5_.refs_7_.refs_6_), channel_id=1, source_target_pairs={{0,1},{1,0},{2,3},{3,2},{4,5},{5,4},{6,7},{7,6},{8,9},{9,8},{10,11... | collective-permute-start | bytes 3538952 | tf_op jit(solution)/shard_map/ppermute | solution.py:134
  102.5 24.4 %collective-permute-start.21 = (bf16[2,4,192,384]{3,2,1,0:T(8,128)(2,1)S(1)}, bf16[2,4,192,384]{3,2,1,0:T(8,128)(2,1)S(1)}, u32[]{:S(2)}, u32[]{:S(2)}) collective-permute-start(bf16[2,4,192,384]{3,2,1,0:T(8,128)(2,1)S(1)} %pad_maximum_fusion.2.refs_8_.refs_4_.refs_10_.refs_9_), channel_id=1, source_target_pairs={{0,1},{1,0},{2,3},{3,2},{4,5},{5,4},{6,7},{7,6},{8,9},{9,8},{10,11... | collective-permute-start | bytes 3538952 | tf_op jit(solution)/shard_map/ppermute | solution.py:134
  102.6 22.4 %collective-permute-start.20 = (bf16[2,4,192,384]{3,2,1,0:T(8,128)(2,1)S(1)}, bf16[2,4,192,384]{3,2,1,0:T(8,128)(2,1)S(1)}, u32[]{:S(2)}, u32[]{:S(2)}) collective-permute-start(bf16[2,4,192,384]{3,2,1,0:T(8,128)(2,1)S(1)} %pad_maximum_fusion.2.refs_8_.refs_4_.refs_10_.refs_9_), channel_id=1, source_target_pairs={{0,2},{1,5},{2,0},{3,7},{4,6},{5,1},{6,4},{7,3},{8,10},{9,13},{10,... | collective-permute-start | bytes 3538952 | tf_op jit(solution)/shard_map/ppermute | solution.py:134
  126.9 24.9 %collective-permute-start.23 = (bf16[4,4,192,384]{3,2,1,0:T(8,128)(2,1)}, bf16[4,4,192,384]{3,2,1,0:T(8,128)(2,1)S(1)}, u32[]{:S(2)}, u32[]{:S(2)}) collective-permute-start(bf16[4,4,192,384]{3,2,1,0:T(8,128)(2,1)} %get-tuple-element.111), channel_id=1, source_target_pairs={{0,1},{1,0},{2,3},{3,2},{4,5},{5,4},{6,7},{7,6},{8,9},{9,8},{10,11... | collective-permute-start | bytes 7077896 | tf_op jit(solution)/shard_map/ppermute | solution.py:134
  153.5 22.4 %collective-permute-start.24 = (bf16[2,4,192,384]{3,2,1,0:T(8,128)(2,1)S(1)}, bf16[2,4,192,384]{3,2,1,0:T(8,128)(2,1)S(1)}, u32[]{:S(2)}, u32[]{:S(2)}) collective-permute-start(bf16[2,4,192,384]{3,2,1,0:T(8,128)(2,1)S(1)} %get-tuple-element.190.refs_14_), channel_id=1, source_target_pairs={{0,2},{1,5},{2,0},{3,7},{4,6},{5,1},{6,4},{7,3},{8,10},{9,13},{10,... | collective-permute-start | bytes 3538952 | tf_op jit(solution)/shard_map/ppermute | solution.py:134
  175.4 20.4 %collective-permute-start.26 = (bf16[4,4,240,384]{3,2,1,0:T(8,128)(2,1)}, bf16[4,4,240,384]{3,2,1,0:T(8,128)(2,1)S(1)}, u32[]{:S(2)}, u32[]{:S(2)}) collective-permute-start(bf16[4,4,240,384]{3,2,1,0:T(8,128)(2,1)} %get-tuple-element.126), channel_id=1, source_target_pairs={{0,1},{1,0},{2,3},{3,2},{4,5},{5,4},{6,7},{7,6},{8,9},{9,8},{10,11... | collective-permute-start | bytes 8847368 | tf_op jit(solution)/shard_map/ppermute | solution.py:134
  176.2 13.9 %collective-permute-start.25 = (bf16[4,192,384]{2,1,0:T(8,128)(2,1)S(1)}, bf16[4,192,384]{2,1,0:T(8,128)(2,1)S(1)}, u32[]{:S(2)}, u32[]{:S(2)}) collective-permute-start(bf16[4,192,384]{2,1,0:T(8,128)(2,1)S(1)} %get-tuple-element.196.refs_7_), channel_id=1, source_target_pairs={{0,4},{1,3},{2,6},{3,1},{4,0},{5,7},{6,2},{7,5},{8,12},{9,11},{10,... | collective-permute-start | bytes 1769480 | tf_op jit(solution)/shard_map/ppermute | solution.py:134
  190.2 17.2 %collective-permute-start.29 = (bf16[192,384]{1,0:T(8,128)(2,1)S(1)}, bf16[192,384]{1,0:T(8,128)(2,1)S(1)}, u32[]{:S(2)}, u32[]{:S(2)}) collective-permute-start(bf16[192,384]{1,0:T(8,128)(2,1)S(1)} %get-tuple-element.204.refs_9_), channel_id=1, source_target_pairs={{0,8},{1,9},{2,10},{3,11},{4,12},{5,13},{6,14},{7,15},{8,16},{9,17... | collective-permute-start | bytes 442376 | tf_op jit(solution)/shard_map/ppermute | solution.py:134
  191.5 15.9 %collective-permute-start.28 = (bf16[192,384]{1,0:T(8,128)(2,1)S(1)}, bf16[192,384]{1,0:T(8,128)(2,1)S(1)}, u32[]{:S(2)}, u32[]{:S(2)}) collective-permute-start(bf16[192,384]{1,0:T(8,128)(2,1)S(1)} %get-tuple-element.205.refs_8_), channel_id=1, source_target_pairs={{0,16},{1,17},{2,18},{3,19},{4,20},{5,21},{6,22},{7,23},{8,24},{9,... | collective-permute-start | bytes 442376 | tf_op jit(solution)/shard_map/ppermute | solution.py:134
  193.0 14.5 %collective-permute-start.27 = (bf16[192,384]{1,0:T(8,128)(2,1)S(1)}, bf16[192,384]{1,0:T(8,128)(2,1)S(1)}, u32[]{:S(2)}, u32[]{:S(2)}) collective-permute-start(bf16[192,384]{1,0:T(8,128)(2,1)S(1)} %get-tuple-element.206.refs_7_), channel_id=1, source_target_pairs={{0,24},{1,25},{2,26},{3,27},{4,28},{5,29},{6,30},{7,31},{8,0},{9,1... | collective-permute-start | bytes 442376 | tf_op jit(solution)/shard_map/ppermute | solution.py:134
  206.9 19.4 %collective-permute-start.32 = (bf16[2,4,240,384]{3,2,1,0:T(8,128)(2,1)S(1)}, bf16[2,4,240,384]{3,2,1,0:T(8,128)(2,1)S(1)}, u32[]{:S(2)}, u32[]{:S(2)}) collective-permute-start(bf16[2,4,240,384]{3,2,1,0:T(8,128)(2,1)S(1)} %get-tuple-element.188.refs_10_), channel_id=1, source_target_pairs={{0,2},{1,5},{2,0},{3,7},{4,6},{5,1},{6,4},{7,3},{8,10},{9,13},{10,... | collective-permute-start | bytes 4423688 | tf_op jit(solution)/shard_map/ppermute | solution.py:134
  213.5 13.8 %collective-permute-start.30 = (bf16[4,4,144,384]{3,2,1,0:T(8,128)(2,1)S(1)}, bf16[4,4,144,384]{3,2,1,0:T(8,128)(2,1)S(1)}, u32[]{:S(2)}, u32[]{:S(2)}) collective-permute-start(bf16[4,4,144,384]{3,2,1,0:T(8,128)(2,1)S(1)} %get-tuple-element.131), channel_id=1, source_target_pairs={{0,1},{1,0},{2,3},{3,2},{4,5},{5,4},{6,7},{7,6},{8,9},{9,8},{10,11... | collective-permute-start | bytes 5308424 | tf_op jit(solution)/shard_map/ppermute | solution.py:134
  226.7 19.2 %collective-permute-start.39 = (bf16[4,240,384]{2,1,0:T(8,128)(2,1)S(1)}, bf16[4,240,384]{2,1,0:T(8,128)(2,1)S(1)}, u32[]{:S(2)}, u32[]{:S(2)}) collective-permute-start(bf16[4,240,384]{2,1,0:T(8,128)(2,1)S(1)} %get-tuple-element.194.refs_11_), channel_id=1, source_target_pairs={{0,4},{1,3},{2,6},{3,1},{4,0},{5,7},{6,2},{7,5},{8,12},{9,11},{10,... | collective-permute-start | bytes 2211848 | tf_op jit(solution)/shard_map/ppermute | solution.py:134
  227.7 18.1 %collective-permute-start.31 = (bf16[2,4,144,384]{3,2,1,0:T(8,128)(2,1)S(1)}, bf16[2,4,144,384]{3,2,1,0:T(8,128)(2,1)S(1)}, u32[]{:S(2)}, u32[]{:S(2)}) collective-permute-start(bf16[2,4,144,384]{3,2,1,0:T(8,128)(2,1)S(1)} %get-tuple-element.191.refs_10_), channel_id=1, source_target_pairs={{0,2},{1,5},{2,0},{3,7},{4,6},{5,1},{6,4},{7,3},{8,10},{9,13},{10,... | collective-permute-start | bytes 2654216 | tf_op jit(solution)/shard_map/ppermute | solution.py:134
  248.3 16.5 %collective-permute-start.42 = (bf16[240,384]{1,0:T(8,128)(2,1)S(1)}, bf16[240,384]{1,0:T(8,128)(2,1)S(1)}, u32[]{:S(2)}, u32[]{:S(2)}) collective-permute-start(bf16[240,384]{1,0:T(8,128)(2,1)S(1)} %get-tuple-element.199), channel_id=1, source_target_pairs={{0,8},{1,9},{2,10},{3,11},{4,12},{5,13},{6,14},{7,15},{8,16},{9,17... | collective-permute-start | bytes 552968 | tf_op jit(solution)/shard_map/ppermute | solution.py:134
  248.4 16.4 %collective-permute-start.41 = (bf16[240,384]{1,0:T(8,128)(2,1)S(1)}, bf16[240,384]{1,0:T(8,128)(2,1)S(1)}, u32[]{:S(2)}, u32[]{:S(2)}) collective-permute-start(bf16[240,384]{1,0:T(8,128)(2,1)S(1)} %get-tuple-element.200), channel_id=1, source_target_pairs={{0,16},{1,17},{2,18},{3,19},{4,20},{5,21},{6,22},{7,23},{8,24},{9,... | collective-permute-start | bytes 552968 | tf_op jit(solution)/shard_map/ppermute | solution.py:134
  249.5 15.3 %collective-permute-start.40 = (bf16[240,384]{1,0:T(8,128)(2,1)S(1)}, bf16[240,384]{1,0:T(8,128)(2,1)S(1)}, u32[]{:S(2)}, u32[]{:S(2)}) collective-permute-start(bf16[240,384]{1,0:T(8,128)(2,1)S(1)} %get-tuple-element.201), channel_id=1, source_target_pairs={{0,24},{1,25},{2,26},{3,27},{4,28},{5,29},{6,30},{7,31},{8,0},{9,1... | collective-permute-start | bytes 552968 | tf_op jit(solution)/shard_map/ppermute | solution.py:134
  252.4 17.5 %collective-permute-start.46 = (bf16[2,4,16,384]{3,2,1,0:T(8,128)(2,1)S(1)}, bf16[2,4,16,384]{3,2,1,0:T(8,128)(2,1)S(1)}, u32[]{:S(2)}, u32[]{:S(2)}) collective-permute-start(bf16[2,4,16,384]{3,2,1,0:T(8,128)(2,1)S(1)} %get-tuple-element.218.refs_16_), channel_id=1, source_target_pairs={{0,2},{1,5},{2,0},{3,7},{4,6},{5,1},{6,4},{7,3},{8,10},{9,13},{10,... | collective-permute-start | bytes 294920 | tf_op jit(solution)/shard_map/ppermute | solution.py:134
  264.9 17.5 %collective-permute-start.37 = (bf16[144,384]{1,0:T(8,128)(2,1)S(1)}, bf16[144,384]{1,0:T(8,128)(2,1)S(1)}, u32[]{:S(2)}, u32[]{:S(2)}) collective-permute-start(bf16[144,384]{1,0:T(8,128)(2,1)S(1)} %get-tuple-element.208.refs_15_), channel_id=1, source_target_pairs={{0,8},{1,9},{2,10},{3,11},{4,12},{5,13},{6,14},{7,15},{8,16},{9,17... | collective-permute-start | bytes 331784 | tf_op jit(solution)/shard_map/ppermute | solution.py:134
  269.0 13.4 %collective-permute-start.36 = (bf16[144,384]{1,0:T(8,128)(2,1)S(1)}, bf16[144,384]{1,0:T(8,128)(2,1)S(1)}, u32[]{:S(2)}, u32[]{:S(2)}) collective-permute-start(bf16[144,384]{1,0:T(8,128)(2,1)S(1)} %get-tuple-element.209.refs_14_), channel_id=1, source_target_pairs={{0,16},{1,17},{2,18},{3,19},{4,20},{5,21},{6,22},{7,23},{8,24},{9,... | collective-permute-start | bytes 331784 | tf_op jit(solution)/shard_map/ppermute | solution.py:134
  (66 other events, 547.4 us)

commit v6 on v5

--- a/solution.py
+++ b/solution.py
@@ -193,7 +193,7 @@
 MIB = 1024 * 1024
 WIDTH = HEADS * HEAD_DIM
 SCALE = 1.0
-BACK = 3
+BACK = 5
 
 
 def cdf_pdf(u):
@@ -1002,9 +1002,9 @@
         qkv_t, do_t, lse[1], seg_row, seg_col, width, 1, after=chain_a.sent + chain_b.sent
     )
     grad_t = (grads_0, grads_1)
-    own_q, far_q = qkv_back(grad_t, hidden_one, places, r_qkv, topo, after=chain_a.arrived())
+    chain_b.along((sums_1,))
+    own_q, far_q = qkv_back(grad_t, hidden_one, places, r_qkv, topo, after=(*chain_a.arrived(), *chain_b.sent))
     chain_q = Chain(own_q, far_q, topo)
-    chain_b.along((far_q,))
     chain_q.across()
     input_grad, sums_one = first_norm_back(
         grad_t, tokens, grad_mid, vecs, one, places, r_qkv, after=chain_q.sent + chain_b.sent

time: 293 us -> 290 us (0.990)
    unnamed x99 -> x113, local copies, waits for them, and re-layouts: 21.9 us -> 19.8 us
  transfers between devices with their start and end apart: 51 -> 51, of which waited for: 17 -> 20; matrix products, arithmetic and copies ran while one was open for 3% -> 4% of each run, Pallas kernels for 46% -> 44%
where the time goes in v6:
time: 290 us; the launch traced here: 284 us
  Pallas kernels  131 us (45%)
  waiting for transfers between devices  62.6 us (22%)
  starting transfers between devices  55.8 us (19%)
  local copies, waits for them, and re-layouts  21.2 us (7%)
  other arithmetic  10.7 us (4%)
  between operations  3.18 us (1%)
    pallas_call x15, Pallas kernels, call(): pl.pallas_call(body, grid_spec=pltpu.PrefetchScalarGridSpec(num_scalar_pr...  131 us
    ppermute x51, waiting for transfers between devices, send(): return lax.ppermute(values, AXES, perm)  62.6 us
    ppermute x51, starting transfers between devices, send(): return lax.ppermute(values, AXES, perm)  55.8 us
    unnamed x113, local copies, waits for them, and re-layouts  19.8 us
  transfers between devices with their start and end apart: 51, of which 20 were waited for; matrix products, arithmetic and copies ran while one was open for 4% of the time, Pallas kernels for 44%

profile of v6, /device:TPU:0, one launch (start us, length us, event | category | flops | bytes accessed | tf_op | source)
XLA Modules:
  0.0 284.2 jit_solution(4933319757236417694)
XLA Ops:
  4.5 4.0 %collective-permute-start.2 = (bf16[208,384]{1,0:T(8,128)(2,1)S(1)}, bf16[208,384]{1,0:T(8,128)(2,1)S(1)}, u32[]{:S(2)}, u32[]{:S(2)}) collective-permute-start(bf16[208,384]{1,0:T(8,128)(2,1)S(1)} %fusion.24), channel_id=1, source_target_pairs={{0,16},{1,17},{2,18},{3,19},{4,20},{5,21},{6,22},{7,23},{8,24},{9,... | collective-permute-start | bytes 479240 | tf_op jit(solution)/shard_map/ppermute | solution.py:134
  10.1 2.2 collective-permute-start.3
  12.3 7.9 %collective-permute-done.2 = bf16[208,384]{1,0:T(8,128)(2,1)S(1)} collective-permute-done((bf16[208,384]{1,0:T(8,128)(2,1)S(1)}, bf16[208,384]{1,0:T(8,128)(2,1)S(1)}, u32[]{:S(2)}, u32[]{:S(2)}) %collective-permute-start.2) | collective-permute-done | bytes 159776 | tf_op jit(solution)/shard_map/ppermute | solution.py:134
  23.4 8.5 %collective-permute-done.5 = bf16[4,208,384]{2,1,0:T(8,128)(2,1)S(1)} collective-permute-done((bf16[4,208,384]{2,1,0:T(8,128)(2,1)S(1)}, bf16[4,208,384]{2,1,0:T(8,128)(2,1)S(1)}, u32[]{:S(2)}, u32[]{:S(2)}) %collective-permute-start.5) | collective-permute-done | bytes 639008 | tf_op jit(solution)/shard_map/ppermute | solution.py:134
  37.7 2.5 collective-permute-start.8
  42.3 11.4 %collective-permute-done.8 = bf16[192,384]{1,0:T(8,128)(2,1)S(1)} collective-permute-done((bf16[192,384]{1,0:T(8,128)(2,1)S(1)}, bf16[192,384]{1,0:T(8,128)(2,1)S(1)}, u32[]{:S(2)}, u32[]{:S(2)}) %collective-permute-start.8) | collective-permute-done | bytes 147488 | tf_op jit(solution)/shard_map/ppermute | solution.py:134
  58.7 6.1 %collective-permute-done.12.refs_5_ = bf16[4,192,384]{2,1,0:T(8,128)(2,1)S(1)} collective-permute-done((bf16[4,192,384]{2,1,0:T(8,128)(2,1)}, bf16[4,192,384]{2,1,0:T(8,128)(2,1)S(1)}, u32[]{:S(2)}, u32[]{:S(2)}) %collective-permute-start.12) | collective-permute-done | bytes 589856 | tf_op jit(solution)/shard_map/ppermute | solution.py:134
  66.7 3.1 %shard_map.135 = (f32[8,768]{1,0:T(8,128)S(1)}, f32[2304,1]{1,0:T(8,128)S(1)}, f32[1536,1]{1,0:T(8,128)S(1)}, f32[1536,1]{1,0:T(8,128)S(1)}) custom-call(s32[32,3]{1,0:T(8,128)S(1)} %copy.71.refs_0_, bf16[2,4,208,384]{3,2,1,0:T(8,128)(2,1)S(1)} %pad_maximum_fusion.refs_1_.refs_4_.refs_5_.refs_6_, ...), custom_call_target="tpu_custom_call" | custom-call | flops 3000000000 | bytes 9000000 | tf_op jit(solution)/shard_map/pallas_call | solution.py:215
  69.8 8.6 %shard_map.136 = (bf16[1024,768]{1,0:T(8,128)(2,1)S(1)}, bf16[2304,1024]{1,0:T(8,128)(2,1)S(1)}) custom-call(s32[32,3]{1,0:T(8,128)S(1)} %copy.71.refs_0_, bf16[1024,768]{1,0:T(8,128)(2,1)S(1)} %copy-done.5, f32[8,768]{1,0:T(8,128)S(1)} %get-tuple-element.88.refs_2_.refs_4_.refs_5_, f32[2304,1]{1,0:T(8,128)S(1)} %get-tuple-element.89.refs_3_, ...), custom_call_target="tpu_custom_call" | custom-call | flops 8999999488 | bytes 27000000 | tf_op jit(solution)/shard_map/pallas_call | solution.py:215
  79.8 2.2 collective-permute-start.13
  82.0 5.9 %shard_map.137 = (bf16[384,1024]{1,0:T(8,128)(2,1)S(1)}, f32[16,1024]{1,0:T(8,128)S(1)}) custom-call(bf16[2304,1024]{1,0:T(8,128)(2,1)S(1)} %get-tuple-element.90.refs_0_.refs_1_.refs_2_, bf16[2304,1024]{1,0:T(8,128)(2,1)S(1)} %get-tuple-element.90.refs_0_.refs_1_.refs_2_, bf16[2304,1024]{1,0:T(8,128)(2,1)S(1)} %get-tuple-element.90.refs_0_.refs_1_.refs_2_, ...), custom_call_target="tpu_custom_call" | custom-call | flops 6000000000 | bytes 18000000 | tf_op jit(solution)/shard_map/pallas_call | solution.py:215
  88.4 5.9 %shard_map.138 = (bf16[384,1024]{1,0:T(8,128)(2,1)S(1)}, f32[16,1024]{1,0:T(8,128)S(1)}) custom-call(bf16[2304,1024]{1,0:T(8,128)(2,1)S(1)} %get-tuple-element.90.refs_0_.refs_1_.refs_2_, bf16[2304,1024]{1,0:T(8,128)(2,1)S(1)} %get-tuple-element.90.refs_0_.refs_1_.refs_2_, bf16[2304,1024]{1,0:T(8,128)(2,1)S(1)} %get-tuple-element.90.refs_0_.refs_1_.refs_2_, ...), custom_call_target="tpu_custom_call" | custom-call | flops 6000000000 | bytes 18000000 | tf_op jit(solution)/shard_map/pallas_call | solution.py:215
  95.7 5.7 %shard_map.139 = (f32[1024,768]{1,0:T(8,128)S(1)}, bf16[1024,768]{1,0:T(8,128)(2,1)S(1)}) custom-call(s32[32,3]{1,0:T(8,128)S(1)} %copy.71.refs_0_, bf16[384,1024]{1,0:T(8,128)(2,1)S(1)} %get-tuple-element.91.refs_1_, bf16[384,1024]{1,0:T(8,128)(2,1)S(1)} %get-tuple-element.92.refs_2_, bf16[1024,768]{1,0:T(8,128)(2,1)S(1)} %copy-done.5, ...), custom_call_target="tpu_custom_call" | custom-call | flops 5000000000 | bytes 15000000 | tf_op jit(solution)/shard_map/pallas_call | solution.py:215
  106.0 18.1 %shard_map.140 = (bf16[1536,1024]{1,0:T(8,128)(2,1)S(1)}, bf16[1536,1024]{1,0:T(8,128)(2,1)S(1)}, f32[8,1536]{1,0:T(8,128)S(1)}, bf16[4,4,192,384]{3,2,1,0:T(8,128)(2,1)S(1)}, bf16[4,4,192,384]{3,2,1,0:T(8,128)(2,1)}) custom-call(s32[32,3]{1,0:T(8,128)S(1)} %copy.71.refs_0_, bf16[1024,768]{1,0:T(8,128)(2,1)S(1)} %get-tuple-element.97.refs_1_, ...), custom_call_target="tpu_custom_call" | custom-call | flops 22000001024 | bytes 66000000 | tf_op jit(solution)/shard_map/pallas_call | solution.py:215
  128.0 2.8 collective-permute-done.22.refs_7_.refs_13_.refs_12_
  130.8 18.5 %shard_map.141 = (bf16[1536,1024]{1,0:T(8,128)(2,1)S(1)}, bf16[1536,1024]{1,0:T(8,128)(2,1)S(1)}, f32[8,1536]{1,0:T(8,128)S(1)}, bf16[4,4,240,384]{3,2,1,0:T(8,128)(2,1)S(1)}, bf16[4,4,240,384]{3,2,1,0:T(8,128)(2,1)}) custom-call(s32[32,3]{1,0:T(8,128)S(1)} %copy.71.refs_0_, bf16[1024,768]{1,0:T(8,128)(2,1)S(1)} %get-tuple-element.97.refs_1_, ...), custom_call_target="tpu_custom_call" | custom-call | flops 22000001024 | bytes 66000000 | tf_op jit(solution)/shard_map/pallas_call | solution.py:215
  156.8 11.7 %shard_map.142 = (f32[1024,768]{1,0:T(8,128)S(1)}, bf16[1024,768]{1,0:T(8,128)(2,1)S(1)}, f32[8,768]{1,0:T(8,128)S(1)}) custom-call(s32[32,3]{1,0:T(8,128)S(1)} %copy.71.refs_0_, bf16[1536,1024]{1,0:T(8,128)(2,1)S(1)} %copy-done.43, bf16[1536,1024]{1,0:T(8,128)(2,1)} %copy-done.46, f32[1024,768]{1,0:T(8,128)} %copy-done.30, bf16[1024,768]{1,0:T(8,128)(2,1)S(1)} %copy-done.4, ...), custom_call_target="tpu_custom_call" | custom-call | flops 70000001024 | bytes 210000000 | tf_op jit(solution)/shard_map/pallas_call | solution.py:215
  168.5 5.2 %shard_map.143 = (bf16[768,1024]{1,0:T(8,128)(2,1)S(1)}, bf16[4,4,240,384]{3,2,1,0:T(8,128)(2,1)S(1)}, bf16[4,4,240,384]{3,2,1,0:T(8,128)(2,1)}) custom-call(s32[32,3]{1,0:T(8,128)S(1)} %copy.71.refs_0_, bf16[384,1024]{1,0:T(8,128)(2,1)S(1)} %copy-done.33, bf16[384,1024]{1,0:T(8,128)(2,1)S(1)} %copy-done.35, ...), custom_call_target="tpu_custom_call", output_to_operand_aliasing={{1}: (4, {}), {2}: (5, {})} | custom-call | flops 24999999488 | bytes 75000000 | tf_op jit(solution)/shard_map/pallas_call | solution.py:215
  174.2 2.1 collective-permute-start.25
  176.3 2.3 copy-done.28
  178.7 10.3 %shard_map.144 = (bf16[1152,1024]{1,0:T(8,128)(2,1)S(1)}, f32[8,1152]{1,0:T(8,128)S(1)}) custom-call(bf16[2304,1024]{1,0:T(8,128)(2,1)S(1)} %copy-done.28, bf16[2304,1024]{1,0:T(8,128)(2,1)S(1)} %copy-done.28, bf16[2304,1024]{1,0:T(8,128)(2,1)S(1)} %copy-done.28, bf16[768,1024]{1,0:T(8,128)(2,1)S(1)} %get-tuple-element.118.refs_3_, ...), custom_call_target="tpu_custom_call" | custom-call | flops 60000002048 | bytes 180000000 | tf_op jit(solution)/shard_map/pallas_call | solution.py:215
  192.5 2.9 %collective-permute-start.27 = (bf16[192,384]{1,0:T(8,128)(2,1)S(1)}, bf16[192,384]{1,0:T(8,128)(2,1)S(1)}, u32[]{:S(2)}, u32[]{:S(2)}) collective-permute-start(bf16[192,384]{1,0:T(8,128)(2,1)S(1)} %get-tuple-element.206.refs_7_), channel_id=1, source_target_pairs={{0,24},{1,25},{2,26},{3,27},{4,28},{5,29},{6,30},{7,31},{8,0},{9,1... | collective-permute-start | bytes 442376 | tf_op jit(solution)/shard_map/ppermute | solution.py:134
  197.7 10.5 %shard_map.145 = (bf16[1152,1024]{1,0:T(8,128)(2,1)S(1)}, f32[8,1152]{1,0:T(8,128)S(1)}) custom-call(bf16[2304,1024]{1,0:T(8,128)(2,1)S(1)} %copy-done.29, bf16[2304,1024]{1,0:T(8,128)(2,1)S(1)} %copy-done.29, bf16[2304,1024]{1,0:T(8,128)(2,1)S(1)} %copy-done.29, bf16[768,1024]{1,0:T(8,128)(2,1)S(1)} %get-tuple-element.118.refs_3_, ...), custom_call_target="tpu_custom_call" | custom-call | flops 60000002048 | bytes 180000000 | tf_op jit(solution)/shard_map/pallas_call | solution.py:215
  208.2 7.3 %collective-permute-done.30 = bf16[2,4,240,384]{3,2,1,0:T(8,128)(2,1)S(1)} collective-permute-done((bf16[2,4,240,384]{3,2,1,0:T(8,128)(2,1)S(1)}, bf16[2,4,240,384]{3,2,1,0:T(8,128)(2,1)S(1)}, u32[]{:S(2)}, u32[]{:S(2)}) %collective-permute-start.30) | collective-permute-done | bytes 1474592 | tf_op jit(solution)/shard_map/ppermute | solution.py:134
  216.9 6.1 %shard_map.146 = (bf16[4,4,144,384]{3,2,1,0:T(8,128)(2,1)S(1)}, bf16[4,4,144,384]{3,2,1,0:T(8,128)(2,1)S(1)}) custom-call(s32[32,3]{1,0:T(8,128)S(1)} %copy.71.refs_0_, bf16[1152,1024]{1,0:T(8,128)(2,1)S(1)} %get-tuple-element.121.refs_1_, bf16[1152,1024]{1,0:T(8,128)(2,1)S(1)} %get-tuple-element.129.refs_2_, bf16[1024,768]{1,0:T(8,128)(2,1)S(1)} %copy-done.37, ...), custom_call_target="tpu_custom_call" | custom-call | flops 35000000512 | bytes 105000000 | tf_op jit(solution)/shard_map/pallas_call | solution.py:215
  223.9 2.9 %collective-permute-done.31 = bf16[4,4,144,384]{3,2,1,0:T(8,128)(2,1)S(1)} collective-permute-done((bf16[4,4,144,384]{3,2,1,0:T(8,128)(2,1)S(1)}, bf16[4,4,144,384]{3,2,1,0:T(8,128)(2,1)S(1)}, u32[]{:S(2)}, u32[]{:S(2)}) %collective-permute-start.31) | collective-permute-done | bytes 1769504 | tf_op jit(solution)/shard_map/ppermute | solution.py:134
  228.6 10.1 %shard_map.147 = (bf16[1024,768]{1,0:T(8,128)(2,1)}, f32[8,768]{1,0:T(8,128)S(1)}) custom-call(s32[32,3]{1,0:T(8,128)S(1)} %copy.71.refs_0_, bf16[1152,1024]{1,0:T(8,128)(2,1)S(1)} %get-tuple-element.121.refs_1_, bf16[1152,1024]{1,0:T(8,128)(2,1)S(1)} %get-tuple-element.129.refs_2_, bf16[1024,768]{1,0:T(8,128)(2,1)S(1)} %copy-done.6, ...), custom_call_target="tpu_custom_call" | custom-call | flops 54999998464 | bytes 165000000 | tf_op jit(solution)/shard_map/pallas_call | solution.py:215
  240.0 3.2 %collective-permute-start.40 = (bf16[240,384]{1,0:T(8,128)(2,1)S(1)}, bf16[240,384]{1,0:T(8,128)(2,1)S(1)}, u32[]{:S(2)}, u32[]{:S(2)}) collective-permute-start(bf16[240,384]{1,0:T(8,128)(2,1)S(1)} %get-tuple-element.201), channel_id=1, source_target_pairs={{0,24},{1,25},{2,26},{3,27},{4,28},{5,29},{6,30},{7,31},{8,0},{9,1... | collective-permute-start | bytes 552968 | tf_op jit(solution)/shard_map/ppermute | solution.py:134
  248.7 4.6 %collective-permute-done.33 = bf16[4,144,384]{2,1,0:T(8,128)(2,1)S(1)} collective-permute-done((bf16[4,144,384]{2,1,0:T(8,128)(2,1)S(1)}, bf16[4,144,384]{2,1,0:T(8,128)(2,1)S(1)}, u32[]{:S(2)}, u32[]{:S(2)}) %collective-permute-start.33) | collective-permute-done | bytes 442400 | tf_op jit(solution)/shard_map/ppermute | solution.py:134
  253.5 10.0 %shard_map.149 = bf16[1024,768]{1,0:T(8,128)(2,1)} custom-call(s32[32,3]{1,0:T(8,128)S(1)} %copy.71.refs_0_, bf16[1536,1024]{1,0:T(8,128)(2,1)S(1)} %copy-done.41, bf16[1536,1024]{1,0:T(8,128)(2,1)S(1)} %copy-done.45, f32[1024,768]{1,0:T(8,128)S(1)} %copy-done.31, f32[8,768]{1,0:T(8,128)S(1)} %copy-done.39, ...), custom_call_target="tpu_custom_call" | custom-call | flops 54999998464 | bytes 165000000 | tf_op jit(solution)/shard_map/pallas_call | solution.py:215
  269.8 2.9 %collective-permute-start.48 = (bf16[16,384]{1,0:T(8,128)(2,1)S(1)}, bf16[16,384]{1,0:T(8,128)(2,1)S(1)}, u32[]{:S(2)}, u32[]{:S(2)}) collective-permute-start(bf16[16,384]{1,0:T(8,128)(2,1)S(1)} %get-tuple-element.241), channel_id=1, source_target_pairs={{0,24},{1,25},{2,26},{3,27},{4,28},{5,29},{6,30},{7,31},{8,0},{9,1... | collective-permute-start | bytes 36872 | tf_op jit(solution)/shard_map/ppermute | solution.py:134
  274.4 3.7 %collective-permute-start.35 = (bf16[144,384]{1,0:T(8,128)(2,1)S(1)}, bf16[144,384]{1,0:T(8,128)(2,1)S(1)}, u32[]{:S(2)}, u32[]{:S(2)}) collective-permute-start(bf16[144,384]{1,0:T(8,128)(2,1)S(1)} %get-tuple-element.210.refs_13_), channel_id=1, source_target_pairs={{0,24},{1,25},{2,26},{3,27},{4,28},{5,29},{6,30},{7,31},{8,0},{9,1... | collective-permute-start | bytes 331784 | tf_op jit(solution)/shard_map/ppermute | solution.py:134
  (265 shorter events, 71.7 us)
Async XLA Ops:
  4.5 15.8 %collective-permute-start.2 = (bf16[208,384]{1,0:T(8,128)(2,1)S(1)}, bf16[208,384]{1,0:T(8,128)(2,1)S(1)}, u32[]{:S(2)}, u32[]{:S(2)}) collective-permute-start(bf16[208,384]{1,0:T(8,128)(2,1)S(1)} %fusion.24), channel_id=1, source_target_pairs={{0,16},{1,17},{2,18},{3,19},{4,20},{5,21},{6,22},{7,23},{8,24},{9,... | collective-permute-start | bytes 479240 | tf_op jit(solution)/shard_map/ppermute | solution.py:134
  8.5 11.8 %collective-permute-start.1 = (bf16[208,384]{1,0:T(8,128)(2,1)S(1)}, bf16[208,384]{1,0:T(8,128)(2,1)S(1)}, u32[]{:S(2)}, u32[]{:S(2)}) collective-permute-start(bf16[208,384]{1,0:T(8,128)(2,1)S(1)} %fusion.24), channel_id=1, source_target_pairs={{0,8},{1,9},{2,10},{3,11},{4,12},{5,13},{6,14},{7,15},{8,16},{9,17... | collective-permute-start | bytes 479240 | tf_op jit(solution)/shard_map/ppermute | solution.py:134
  10.1 11.3 %collective-permute-start.3 = (bf16[208,384]{1,0:T(8,128)(2,1)S(1)}, bf16[208,384]{1,0:T(8,128)(2,1)S(1)}, u32[]{:S(2)}, u32[]{:S(2)}) collective-permute-start(bf16[208,384]{1,0:T(8,128)(2,1)S(1)} %fusion.24), channel_id=1, source_target_pairs={{0,24},{1,25},{2,26},{3,27},{4,28},{5,29},{6,30},{7,31},{8,0},{9,1... | collective-permute-start | bytes 479240 | tf_op jit(solution)/shard_map/ppermute | solution.py:134
  32.1 22.6 %collective-permute-start.6 = (bf16[2,4,208,384]{3,2,1,0:T(8,128)(2,1)S(1)}, bf16[2,4,208,384]{3,2,1,0:T(8,128)(2,1)S(1)}, u32[]{:S(2)}, u32[]{:S(2)}) collective-permute-start(bf16[2,4,208,384]{3,2,1,0:T(8,128)(2,1)S(1)} %pad_maximum_fusion.refs_1_.refs_4_.refs_5_.refs_6_), channel_id=1, source_target_pairs={{0,2},{1,5},{2,0},{3,7},{4,6},{5,1},{6,4},{7,3},{8,10},{9,13},{10,... | collective-permute-start | bytes 3833864 | tf_op jit(solution)/shard_map/ppermute | solution.py:134
  37.7 16.0 %collective-permute-start.8 = (bf16[192,384]{1,0:T(8,128)(2,1)S(1)}, bf16[192,384]{1,0:T(8,128)(2,1)S(1)}, u32[]{:S(2)}, u32[]{:S(2)}) collective-permute-start(bf16[192,384]{1,0:T(8,128)(2,1)S(1)} %pad_maximum_fusion.11), channel_id=1, source_target_pairs={{0,16},{1,17},{2,18},{3,19},{4,20},{5,21},{6,22},{7,23},{8,24},{9,... | collective-permute-start | bytes 442376 | tf_op jit(solution)/shard_map/ppermute | solution.py:134
  40.2 13.6 %collective-permute-start.7 = (bf16[192,384]{1,0:T(8,128)(2,1)S(1)}, bf16[192,384]{1,0:T(8,128)(2,1)S(1)}, u32[]{:S(2)}, u32[]{:S(2)}) collective-permute-start(bf16[192,384]{1,0:T(8,128)(2,1)S(1)} %pad_maximum_fusion.11), channel_id=1, source_target_pairs={{0,8},{1,9},{2,10},{3,11},{4,12},{5,13},{6,14},{7,15},{8,16},{9,17... | collective-permute-start | bytes 442376 | tf_op jit(solution)/shard_map/ppermute | solution.py:134
  42.1 24.6 %collective-permute-start.10 = (bf16[2,4,208,384]{3,2,1,0:T(8,128)(2,1)S(1)}, bf16[2,4,208,384]{3,2,1,0:T(8,128)(2,1)}, u32[]{:S(2)}, u32[]{:S(2)}) collective-permute-start(bf16[2,4,208,384]{3,2,1,0:T(8,128)(2,1)S(1)} %pad_maximum_fusion.refs_1_.refs_4_.refs_5_.refs_6_), channel_id=1, source_target_pairs={{0,1},{1,0},{2,3},{3,2},{4,5},{5,4},{6,7},{7,6},{8,9},{9,8},{10,11... | collective-permute-start | bytes 3833864 | tf_op jit(solution)/shard_map/ppermute | solution.py:134
  54.7 12.0 %collective-permute-start.11 = (bf16[2,4,208,384]{3,2,1,0:T(8,128)(2,1)S(1)}, bf16[2,4,208,384]{3,2,1,0:T(8,128)(2,1)}, u32[]{:S(2)}, u32[]{:S(2)}) collective-permute-start(bf16[2,4,208,384]{3,2,1,0:T(8,128)(2,1)S(1)} %collective-permute-done.6.refs_2_.refs_5_.refs_6_.refs_7_), channel_id=1, source_target_pairs={{0,1},{1,0},{2,3},{3,2},{4,5},{5,4},{6,7},{7,6},{8,9},{9,8},{10,11... | collective-permute-start | bytes 3833864 | tf_op jit(solution)/shard_map/ppermute | solution.py:134
  66.0 39.9 %collective-permute-start.17 = (bf16[2,4,192,384]{3,2,1,0:T(8,128)(2,1)S(1)}, bf16[2,4,192,384]{3,2,1,0:T(8,128)(2,1)S(1)}, u32[]{:S(2)}, u32[]{:S(2)}) collective-permute-start(bf16[2,4,192,384]{3,2,1,0:T(8,128)(2,1)S(1)} %pad_maximum_fusion.1.refs_4_.refs_6_.refs_5_), channel_id=1, source_target_pairs={{0,1},{1,0},{2,3},{3,2},{4,5},{5,4},{6,7},{7,6},{8,9},{9,8},{10,11... | collective-permute-start | bytes 3538952 | tf_op jit(solution)/shard_map/ppermute | solution.py:134
  66.1 21.8 %collective-permute-start.16 = (bf16[2,4,192,384]{3,2,1,0:T(8,128)(2,1)S(1)}, bf16[2,4,192,384]{3,2,1,0:T(8,128)(2,1)S(1)}, u32[]{:S(2)}, u32[]{:S(2)}) collective-permute-start(bf16[2,4,192,384]{3,2,1,0:T(8,128)(2,1)S(1)} %pad_maximum_fusion.1.refs_4_.refs_6_.refs_5_), channel_id=1, source_target_pairs={{0,2},{1,5},{2,0},{3,7},{4,6},{5,1},{6,4},{7,3},{8,10},{9,13},{10,... | collective-permute-start | bytes 3538952 | tf_op jit(solution)/shard_map/ppermute | solution.py:134
  79.5 14.8 %collective-permute-start.15 = (bf16[192,384]{1,0:T(8,128)(2,1)S(1)}, bf16[192,384]{1,0:T(8,128)(2,1)S(1)}, u32[]{:S(2)}, u32[]{:S(2)}) collective-permute-start(bf16[192,384]{1,0:T(8,128)(2,1)S(1)} %pad_maximum_fusion.12), channel_id=1, source_target_pairs={{0,24},{1,25},{2,26},{3,27},{4,28},{5,29},{6,30},{7,31},{8,0},{9,1... | collective-permute-start | bytes 442376 | tf_op jit(solution)/shard_map/ppermute | solution.py:134
  79.6 14.8 %collective-permute-start.14 = (bf16[192,384]{1,0:T(8,128)(2,1)S(1)}, bf16[192,384]{1,0:T(8,128)(2,1)S(1)}, u32[]{:S(2)}, u32[]{:S(2)}) collective-permute-start(bf16[192,384]{1,0:T(8,128)(2,1)S(1)} %pad_maximum_fusion.12), channel_id=1, source_target_pairs={{0,16},{1,17},{2,18},{3,19},{4,20},{5,21},{6,22},{7,23},{8,24},{9,... | collective-permute-start | bytes 442376 | tf_op jit(solution)/shard_map/ppermute | solution.py:134
  79.8 14.5 %collective-permute-start.13 = (bf16[192,384]{1,0:T(8,128)(2,1)S(1)}, bf16[192,384]{1,0:T(8,128)(2,1)S(1)}, u32[]{:S(2)}, u32[]{:S(2)}) collective-permute-start(bf16[192,384]{1,0:T(8,128)(2,1)S(1)} %pad_maximum_fusion.12), channel_id=1, source_target_pairs={{0,8},{1,9},{2,10},{3,11},{4,12},{5,13},{6,14},{7,15},{8,16},{9,17... | collective-permute-start | bytes 442376 | tf_op jit(solution)/shard_map/ppermute | solution.py:134
  88.0 18.0 %collective-permute-start.18 = (bf16[2,4,192,384]{3,2,1,0:T(8,128)(2,1)S(1)}, bf16[2,4,192,384]{3,2,1,0:T(8,128)(2,1)S(1)}, u32[]{:S(2)}, u32[]{:S(2)}) collective-permute-start(bf16[2,4,192,384]{3,2,1,0:T(8,128)(2,1)S(1)} %collective-permute-done.16.refs_5_.refs_7_.refs_6_), channel_id=1, source_target_pairs={{0,1},{1,0},{2,3},{3,2},{4,5},{5,4},{6,7},{7,6},{8,9},{9,8},{10,11... | collective-permute-start | bytes 3538952 | tf_op jit(solution)/shard_map/ppermute | solution.py:134
  104.5 23.5 %collective-permute-start.21 = (bf16[2,4,192,384]{3,2,1,0:T(8,128)(2,1)S(1)}, bf16[2,4,192,384]{3,2,1,0:T(8,128)(2,1)S(1)}, u32[]{:S(2)}, u32[]{:S(2)}) collective-permute-start(bf16[2,4,192,384]{3,2,1,0:T(8,128)(2,1)S(1)} %pad_maximum_fusion.2.refs_8_.refs_4_.refs_10_.refs_9_), channel_id=1, source_target_pairs={{0,1},{1,0},{2,3},{3,2},{4,5},{5,4},{6,7},{7,6},{8,9},{9,8},{10,11... | collective-permute-start | bytes 3538952 | tf_op jit(solution)/shard_map/ppermute | solution.py:134
  104.6 22.9 %collective-permute-start.20 = (bf16[2,4,192,384]{3,2,1,0:T(8,128)(2,1)S(1)}, bf16[2,4,192,384]{3,2,1,0:T(8,128)(2,1)S(1)}, u32[]{:S(2)}, u32[]{:S(2)}) collective-permute-start(bf16[2,4,192,384]{3,2,1,0:T(8,128)(2,1)S(1)} %pad_maximum_fusion.2.refs_8_.refs_4_.refs_10_.refs_9_), channel_id=1, source_target_pairs={{0,2},{1,5},{2,0},{3,7},{4,6},{5,1},{6,4},{7,3},{8,10},{9,13},{10,... | collective-permute-start | bytes 3538952 | tf_op jit(solution)/shard_map/ppermute | solution.py:134
  127.7 23.4 %collective-permute-start.23 = (bf16[4,4,192,384]{3,2,1,0:T(8,128)(2,1)}, bf16[4,4,192,384]{3,2,1,0:T(8,128)(2,1)S(1)}, u32[]{:S(2)}, u32[]{:S(2)}) collective-permute-start(bf16[4,4,192,384]{3,2,1,0:T(8,128)(2,1)} %get-tuple-element.111), channel_id=1, source_target_pairs={{0,1},{1,0},{2,3},{3,2},{4,5},{5,4},{6,7},{7,6},{8,9},{9,8},{10,11... | collective-permute-start | bytes 7077896 | tf_op jit(solution)/shard_map/ppermute | solution.py:134
  152.7 21.2 %collective-permute-start.24 = (bf16[2,4,192,384]{3,2,1,0:T(8,128)(2,1)S(1)}, bf16[2,4,192,384]{3,2,1,0:T(8,128)(2,1)S(1)}, u32[]{:S(2)}, u32[]{:S(2)}) collective-permute-start(bf16[2,4,192,384]{3,2,1,0:T(8,128)(2,1)S(1)} %get-tuple-element.190.refs_14_), channel_id=1, source_target_pairs={{0,2},{1,5},{2,0},{3,7},{4,6},{5,1},{6,4},{7,3},{8,10},{9,13},{10,... | collective-permute-start | bytes 3538952 | tf_op jit(solution)/shard_map/ppermute | solution.py:134
  173.7 21.7 %collective-permute-start.26 = (bf16[4,4,240,384]{3,2,1,0:T(8,128)(2,1)}, bf16[4,4,240,384]{3,2,1,0:T(8,128)(2,1)S(1)}, u32[]{:S(2)}, u32[]{:S(2)}) collective-permute-start(bf16[4,4,240,384]{3,2,1,0:T(8,128)(2,1)} %get-tuple-element.126), channel_id=1, source_target_pairs={{0,1},{1,0},{2,3},{3,2},{4,5},{5,4},{6,7},{7,6},{8,9},{9,8},{10,11... | collective-permute-start | bytes 8847368 | tf_op jit(solution)/shard_map/ppermute | solution.py:134
  174.2 14.8 %collective-permute-start.25 = (bf16[4,192,384]{2,1,0:T(8,128)(2,1)S(1)}, bf16[4,192,384]{2,1,0:T(8,128)(2,1)S(1)}, u32[]{:S(2)}, u32[]{:S(2)}) collective-permute-start(bf16[4,192,384]{2,1,0:T(8,128)(2,1)S(1)} %get-tuple-element.196.refs_7_), channel_id=1, source_target_pairs={{0,4},{1,3},{2,6},{3,1},{4,0},{5,7},{6,2},{7,5},{8,12},{9,11},{10,... | collective-permute-start | bytes 1769480 | tf_op jit(solution)/shard_map/ppermute | solution.py:134
  189.8 26.1 %collective-permute-start.29 = (bf16[192,384]{1,0:T(8,128)(2,1)S(1)}, bf16[192,384]{1,0:T(8,128)(2,1)S(1)}, u32[]{:S(2)}, u32[]{:S(2)}) collective-permute-start(bf16[192,384]{1,0:T(8,128)(2,1)S(1)} %get-tuple-element.204.refs_9_), channel_id=1, source_target_pairs={{0,8},{1,9},{2,10},{3,11},{4,12},{5,13},{6,14},{7,15},{8,16},{9,17... | collective-permute-start | bytes 442376 | tf_op jit(solution)/shard_map/ppermute | solution.py:134
  191.0 24.9 %collective-permute-start.28 = (bf16[192,384]{1,0:T(8,128)(2,1)S(1)}, bf16[192,384]{1,0:T(8,128)(2,1)S(1)}, u32[]{:S(2)}, u32[]{:S(2)}) collective-permute-start(bf16[192,384]{1,0:T(8,128)(2,1)S(1)} %get-tuple-element.205.refs_8_), channel_id=1, source_target_pairs={{0,16},{1,17},{2,18},{3,19},{4,20},{5,21},{6,22},{7,23},{8,24},{9,... | collective-permute-start | bytes 442376 | tf_op jit(solution)/shard_map/ppermute | solution.py:134
  192.5 23.4 %collective-permute-start.27 = (bf16[192,384]{1,0:T(8,128)(2,1)S(1)}, bf16[192,384]{1,0:T(8,128)(2,1)S(1)}, u32[]{:S(2)}, u32[]{:S(2)}) collective-permute-start(bf16[192,384]{1,0:T(8,128)(2,1)S(1)} %get-tuple-element.206.refs_7_), channel_id=1, source_target_pairs={{0,24},{1,25},{2,26},{3,27},{4,28},{5,29},{6,30},{7,31},{8,0},{9,1... | collective-permute-start | bytes 442376 | tf_op jit(solution)/shard_map/ppermute | solution.py:134
  196.1 19.4 %collective-permute-start.30 = (bf16[2,4,240,384]{3,2,1,0:T(8,128)(2,1)S(1)}, bf16[2,4,240,384]{3,2,1,0:T(8,128)(2,1)S(1)}, u32[]{:S(2)}, u32[]{:S(2)}) collective-permute-start(bf16[2,4,240,384]{3,2,1,0:T(8,128)(2,1)S(1)} %get-tuple-element.188.refs_10_), channel_id=1, source_target_pairs={{0,2},{1,5},{2,0},{3,7},{4,6},{5,1},{6,4},{7,3},{8,10},{9,13},{10,... | collective-permute-start | bytes 4423688 | tf_op jit(solution)/shard_map/ppermute | solution.py:134
  223.1 16.1 %collective-permute-start.39 = (bf16[4,240,384]{2,1,0:T(8,128)(2,1)S(1)}, bf16[4,240,384]{2,1,0:T(8,128)(2,1)S(1)}, u32[]{:S(2)}, u32[]{:S(2)}) collective-permute-start(bf16[4,240,384]{2,1,0:T(8,128)(2,1)S(1)} %get-tuple-element.194.refs_7_.refs_11_), channel_id=1, source_target_pairs={{0,4},{1,3},{2,6},{3,1},{4,0},{5,7},{6,2},{7,5},{8,12},{9,11},{10,... | collective-permute-start | bytes 2211848 | tf_op jit(solution)/shard_map/ppermute | solution.py:134
  227.2 16.4 %collective-permute-start.32 = (bf16[2,4,144,384]{3,2,1,0:T(8,128)(2,1)S(1)}, bf16[2,4,144,384]{3,2,1,0:T(8,128)(2,1)S(1)}, u32[]{:S(2)}, u32[]{:S(2)}) collective-permute-start(bf16[2,4,144,384]{3,2,1,0:T(8,128)(2,1)S(1)} %get-tuple-element.191.refs_10_), channel_id=1, source_target_pairs={{0,2},{1,5},{2,0},{3,7},{4,6},{5,1},{6,4},{7,3},{8,10},{9,13},{10,... | collective-permute-start | bytes 2654216 | tf_op jit(solution)/shard_map/ppermute | solution.py:134
  239.4 24.1 %collective-permute-start.42 = (bf16[240,384]{1,0:T(8,128)(2,1)S(1)}, bf16[240,384]{1,0:T(8,128)(2,1)S(1)}, u32[]{:S(2)}, u32[]{:S(2)}) collective-permute-start(bf16[240,384]{1,0:T(8,128)(2,1)S(1)} %get-tuple-element.199), channel_id=1, source_target_pairs={{0,8},{1,9},{2,10},{3,11},{4,12},{5,13},{6,14},{7,15},{8,16},{9,17... | collective-permute-start | bytes 552968 | tf_op jit(solution)/shard_map/ppermute | solution.py:134
  239.5 24.0 %collective-permute-start.41 = (bf16[240,384]{1,0:T(8,128)(2,1)S(1)}, bf16[240,384]{1,0:T(8,128)(2,1)S(1)}, u32[]{:S(2)}, u32[]{:S(2)}) collective-permute-start(bf16[240,384]{1,0:T(8,128)(2,1)S(1)} %get-tuple-element.200), channel_id=1, source_target_pairs={{0,16},{1,17},{2,18},{3,19},{4,20},{5,21},{6,22},{7,23},{8,24},{9,... | collective-permute-start | bytes 552968 | tf_op jit(solution)/shard_map/ppermute | solution.py:134
  240.0 23.5 %collective-permute-start.40 = (bf16[240,384]{1,0:T(8,128)(2,1)S(1)}, bf16[240,384]{1,0:T(8,128)(2,1)S(1)}, u32[]{:S(2)}, u32[]{:S(2)}) collective-permute-start(bf16[240,384]{1,0:T(8,128)(2,1)S(1)} %get-tuple-element.201), channel_id=1, source_target_pairs={{0,24},{1,25},{2,26},{3,27},{4,28},{5,29},{6,30},{7,31},{8,0},{9,1... | collective-permute-start | bytes 552968 | tf_op jit(solution)/shard_map/ppermute | solution.py:134
  247.3 18.3 %collective-permute-start.46 = (bf16[2,4,16,384]{3,2,1,0:T(8,128)(2,1)S(1)}, bf16[2,4,16,384]{3,2,1,0:T(8,128)(2,1)S(1)}, u32[]{:S(2)}, u32[]{:S(2)}) collective-permute-start(bf16[2,4,16,384]{3,2,1,0:T(8,128)(2,1)S(1)} %get-tuple-element.218.refs_16_), channel_id=1, source_target_pairs={{0,2},{1,5},{2,0},{3,7},{4,6},{5,1},{6,4},{7,3},{8,10},{9,13},{10,... | collective-permute-start | bytes 294920 | tf_op jit(solution)/shard_map/ppermute | solution.py:134
  263.6 15.8 %collective-permute-start.37 = (bf16[144,384]{1,0:T(8,128)(2,1)S(1)}, bf16[144,384]{1,0:T(8,128)(2,1)S(1)}, u32[]{:S(2)}, u32[]{:S(2)}) collective-permute-start(bf16[144,384]{1,0:T(8,128)(2,1)S(1)} %get-tuple-element.208.refs_15_), channel_id=1, source_target_pairs={{0,8},{1,9},{2,10},{3,11},{4,12},{5,13},{6,14},{7,15},{8,16},{9,17... | collective-permute-start | bytes 331784 | tf_op jit(solution)/shard_map/ppermute | solution.py:134
  264.0 15.4 %collective-permute-start.36 = (bf16[144,384]{1,0:T(8,128)(2,1)S(1)}, bf16[144,384]{1,0:T(8,128)(2,1)S(1)}, u32[]{:S(2)}, u32[]{:S(2)}) collective-permute-start(bf16[144,384]{1,0:T(8,128)(2,1)S(1)} %get-tuple-element.209.refs_14_), channel_id=1, source_target_pairs={{0,16},{1,17},{2,18},{3,19},{4,20},{5,21},{6,22},{7,23},{8,24},{9,... | collective-permute-start | bytes 331784 | tf_op jit(solution)/shard_map/ppermute | solution.py:134
  (73 other events, 649.5 us)

commit v7 on v6

--- a/solution.py
+++ b/solution.py
@@ -198,7 +198,9 @@
 
 def cdf_pdf(u):
     bell = jnp.exp(-0.5 * (u * u))
-    t = 1.0 / (1.0 + (0.3275911 * ROOT_HALF) * jnp.abs(u))
+    below = 1.0 + (0.3275911 * ROOT_HALF) * jnp.abs(u)
+    t = pltpu.reciprocal(below, approx=True)
+    t = t * (2.0 - below * t)
     poly = 1.061405429 * 0.5
     for coef in (-1.453152027, 1.421413741, -0.284496736, 0.254829592):
         poly = poly * t + coef * 0.5

time: 290 us -> 291 us (level)
  no operation moved by 1% of the time
where the time goes in v7:
time: 291 us; the launch traced here: 286 us
  Pallas kernels  132 us (45%)
  waiting for transfers between devices  62.7 us (22%)
  starting transfers between devices  55.7 us (19%)
  local copies, waits for them, and re-layouts  21.3 us (7%)
  other arithmetic  10.7 us (4%)
  between operations  3.17 us (1%)
    pallas_call x15, Pallas kernels, call(): pl.pallas_call(body, grid_spec=pltpu.PrefetchScalarGridSpec(num_scalar_pr...  132 us
    ppermute x51, waiting for transfers between devices, send(): return lax.ppermute(values, AXES, perm)  62.7 us
    ppermute x51, starting transfers between devices, send(): return lax.ppermute(values, AXES, perm)  55.7 us
    unnamed x113, local copies, waits for them, and re-layouts  19.8 us
  transfers between devices with their start and end apart: 51, of which 20 were waited for; matrix products, arithmetic and copies ran while one was open for 4% of the time, Pallas kernels for 44%

profile of v7, /device:TPU:0, one launch (start us, length us, event | category | flops | bytes accessed | tf_op | source)
XLA Modules:
  0.0 285.6 jit_solution(15632456204583266071)
XLA Ops:
  4.5 4.0 %collective-permute-start.2 = (bf16[208,384]{1,0:T(8,128)(2,1)S(1)}, bf16[208,384]{1,0:T(8,128)(2,1)S(1)}, u32[]{:S(2)}, u32[]{:S(2)}) collective-permute-start(bf16[208,384]{1,0:T(8,128)(2,1)S(1)} %fusion.24), channel_id=1, source_target_pairs={{0,16},{1,17},{2,18},{3,19},{4,20},{5,21},{6,22},{7,23},{8,24},{9,... | collective-permute-start | bytes 479240 | tf_op jit(solution)/shard_map/ppermute | solution.py:134
  10.1 2.2 collective-permute-start.3
  12.3 7.9 %collective-permute-done.2 = bf16[208,384]{1,0:T(8,128)(2,1)S(1)} collective-permute-done((bf16[208,384]{1,0:T(8,128)(2,1)S(1)}, bf16[208,384]{1,0:T(8,128)(2,1)S(1)}, u32[]{:S(2)}, u32[]{:S(2)}) %collective-permute-start.2) | collective-permute-done | bytes 159776 | tf_op jit(solution)/shard_map/ppermute | solution.py:134
  23.4 8.5 %collective-permute-done.5 = bf16[4,208,384]{2,1,0:T(8,128)(2,1)S(1)} collective-permute-done((bf16[4,208,384]{2,1,0:T(8,128)(2,1)S(1)}, bf16[4,208,384]{2,1,0:T(8,128)(2,1)S(1)}, u32[]{:S(2)}, u32[]{:S(2)}) %collective-permute-start.5) | collective-permute-done | bytes 639008 | tf_op jit(solution)/shard_map/ppermute | solution.py:134
  35.6 2.1 collective-permute-start.9
  37.7 2.5 collective-permute-start.8
  42.3 11.4 %collective-permute-done.8 = bf16[192,384]{1,0:T(8,128)(2,1)S(1)} collective-permute-done((bf16[192,384]{1,0:T(8,128)(2,1)S(1)}, bf16[192,384]{1,0:T(8,128)(2,1)S(1)}, u32[]{:S(2)}, u32[]{:S(2)}) %collective-permute-start.8) | collective-permute-done | bytes 147488 | tf_op jit(solution)/shard_map/ppermute | solution.py:134
  58.7 6.1 %collective-permute-done.12.refs_5_ = bf16[4,192,384]{2,1,0:T(8,128)(2,1)S(1)} collective-permute-done((bf16[4,192,384]{2,1,0:T(8,128)(2,1)}, bf16[4,192,384]{2,1,0:T(8,128)(2,1)S(1)}, u32[]{:S(2)}, u32[]{:S(2)}) %collective-permute-start.12) | collective-permute-done | bytes 589856 | tf_op jit(solution)/shard_map/ppermute | solution.py:134
  66.7 3.1 %shard_map.135 = (f32[8,768]{1,0:T(8,128)S(1)}, f32[2304,1]{1,0:T(8,128)S(1)}, f32[1536,1]{1,0:T(8,128)S(1)}, f32[1536,1]{1,0:T(8,128)S(1)}) custom-call(s32[32,3]{1,0:T(8,128)S(1)} %copy.71.refs_0_, bf16[2,4,208,384]{3,2,1,0:T(8,128)(2,1)S(1)} %pad_maximum_fusion.refs_1_.refs_4_.refs_5_.refs_6_, ...), custom_call_target="tpu_custom_call" | custom-call | flops 3000000000 | bytes 9000000 | tf_op jit(solution)/shard_map/pallas_call | solution.py:217
  69.8 8.6 %shard_map.136 = (bf16[1024,768]{1,0:T(8,128)(2,1)S(1)}, bf16[2304,1024]{1,0:T(8,128)(2,1)S(1)}) custom-call(s32[32,3]{1,0:T(8,128)S(1)} %copy.71.refs_0_, bf16[1024,768]{1,0:T(8,128)(2,1)S(1)} %copy-done.5, f32[8,768]{1,0:T(8,128)S(1)} %get-tuple-element.88.refs_2_.refs_4_.refs_5_, f32[2304,1]{1,0:T(8,128)S(1)} %get-tuple-element.89.refs_3_, ...), custom_call_target="tpu_custom_call" | custom-call | flops 8999999488 | bytes 27000000 | tf_op jit(solution)/shard_map/pallas_call | solution.py:217
  79.8 2.2 collective-permute-start.13
  82.0 5.9 %shard_map.137 = (bf16[384,1024]{1,0:T(8,128)(2,1)S(1)}, f32[16,1024]{1,0:T(8,128)S(1)}) custom-call(bf16[2304,1024]{1,0:T(8,128)(2,1)S(1)} %get-tuple-element.90.refs_0_.refs_1_.refs_2_, bf16[2304,1024]{1,0:T(8,128)(2,1)S(1)} %get-tuple-element.90.refs_0_.refs_1_.refs_2_, bf16[2304,1024]{1,0:T(8,128)(2,1)S(1)} %get-tuple-element.90.refs_0_.refs_1_.refs_2_, ...), custom_call_target="tpu_custom_call" | custom-call | flops 6000000000 | bytes 18000000 | tf_op jit(solution)/shard_map/pallas_call | solution.py:217
  88.4 5.9 %shard_map.138 = (bf16[384,1024]{1,0:T(8,128)(2,1)S(1)}, f32[16,1024]{1,0:T(8,128)S(1)}) custom-call(bf16[2304,1024]{1,0:T(8,128)(2,1)S(1)} %get-tuple-element.90.refs_0_.refs_1_.refs_2_, bf16[2304,1024]{1,0:T(8,128)(2,1)S(1)} %get-tuple-element.90.refs_0_.refs_1_.refs_2_, bf16[2304,1024]{1,0:T(8,128)(2,1)S(1)} %get-tuple-element.90.refs_0_.refs_1_.refs_2_, ...), custom_call_target="tpu_custom_call" | custom-call | flops 6000000000 | bytes 18000000 | tf_op jit(solution)/shard_map/pallas_call | solution.py:217
  95.7 5.7 %shard_map.139 = (f32[1024,768]{1,0:T(8,128)S(1)}, bf16[1024,768]{1,0:T(8,128)(2,1)S(1)}) custom-call(s32[32,3]{1,0:T(8,128)S(1)} %copy.71.refs_0_, bf16[384,1024]{1,0:T(8,128)(2,1)S(1)} %get-tuple-element.91.refs_1_, bf16[384,1024]{1,0:T(8,128)(2,1)S(1)} %get-tuple-element.92.refs_2_, bf16[1024,768]{1,0:T(8,128)(2,1)S(1)} %copy-done.5, ...), custom_call_target="tpu_custom_call" | custom-call | flops 5000000000 | bytes 15000000 | tf_op jit(solution)/shard_map/pallas_call | solution.py:217
  106.0 18.9 %shard_map.140 = (bf16[1536,1024]{1,0:T(8,128)(2,1)S(1)}, bf16[1536,1024]{1,0:T(8,128)(2,1)S(1)}, f32[8,1536]{1,0:T(8,128)S(1)}, bf16[4,4,192,384]{3,2,1,0:T(8,128)(2,1)S(1)}, bf16[4,4,192,384]{3,2,1,0:T(8,128)(2,1)}) custom-call(s32[32,3]{1,0:T(8,128)S(1)} %copy.71.refs_0_, bf16[1024,768]{1,0:T(8,128)(2,1)S(1)} %get-tuple-element.97.refs_1_, ...), custom_call_target="tpu_custom_call" | custom-call | flops 22000001024 | bytes 66000000 | tf_op jit(solution)/shard_map/pallas_call | solution.py:217
  128.8 2.8 collective-permute-done.22.refs_7_.refs_13_.refs_12_
  131.6 19.2 %shard_map.141 = (bf16[1536,1024]{1,0:T(8,128)(2,1)S(1)}, bf16[1536,1024]{1,0:T(8,128)(2,1)S(1)}, f32[8,1536]{1,0:T(8,128)S(1)}, bf16[4,4,240,384]{3,2,1,0:T(8,128)(2,1)S(1)}, bf16[4,4,240,384]{3,2,1,0:T(8,128)(2,1)}) custom-call(s32[32,3]{1,0:T(8,128)S(1)} %copy.71.refs_0_, bf16[1024,768]{1,0:T(8,128)(2,1)S(1)} %get-tuple-element.97.refs_1_, ...), custom_call_target="tpu_custom_call" | custom-call | flops 22000001024 | bytes 66000000 | tf_op jit(solution)/shard_map/pallas_call | solution.py:217
  158.3 11.7 %shard_map.142 = (f32[1024,768]{1,0:T(8,128)S(1)}, bf16[1024,768]{1,0:T(8,128)(2,1)S(1)}, f32[8,768]{1,0:T(8,128)S(1)}) custom-call(s32[32,3]{1,0:T(8,128)S(1)} %copy.71.refs_0_, bf16[1536,1024]{1,0:T(8,128)(2,1)S(1)} %copy-done.43, bf16[1536,1024]{1,0:T(8,128)(2,1)} %copy-done.46, f32[1024,768]{1,0:T(8,128)} %copy-done.30, bf16[1024,768]{1,0:T(8,128)(2,1)S(1)} %copy-done.4, ...), custom_call_target="tpu_custom_call" | custom-call | flops 70000001024 | bytes 210000000 | tf_op jit(solution)/shard_map/pallas_call | solution.py:217
  170.0 5.2 %shard_map.143 = (bf16[768,1024]{1,0:T(8,128)(2,1)S(1)}, bf16[4,4,240,384]{3,2,1,0:T(8,128)(2,1)S(1)}, bf16[4,4,240,384]{3,2,1,0:T(8,128)(2,1)}) custom-call(s32[32,3]{1,0:T(8,128)S(1)} %copy.71.refs_0_, bf16[384,1024]{1,0:T(8,128)(2,1)S(1)} %copy-done.33, bf16[384,1024]{1,0:T(8,128)(2,1)S(1)} %copy-done.35, ...), custom_call_target="tpu_custom_call", output_to_operand_aliasing={{1}: (4, {}), {2}: (5, {})} | custom-call | flops 24999999488 | bytes 75000000 | tf_op jit(solution)/shard_map/pallas_call | solution.py:217
  177.7 2.3 copy-done.28
  180.1 10.3 %shard_map.144 = (bf16[1152,1024]{1,0:T(8,128)(2,1)S(1)}, f32[8,1152]{1,0:T(8,128)S(1)}) custom-call(bf16[2304,1024]{1,0:T(8,128)(2,1)S(1)} %copy-done.28, bf16[2304,1024]{1,0:T(8,128)(2,1)S(1)} %copy-done.28, bf16[2304,1024]{1,0:T(8,128)(2,1)S(1)} %copy-done.28, bf16[768,1024]{1,0:T(8,128)(2,1)S(1)} %get-tuple-element.118.refs_3_, ...), custom_call_target="tpu_custom_call" | custom-call | flops 60000002048 | bytes 180000000 | tf_op jit(solution)/shard_map/pallas_call | solution.py:217
  193.9 2.9 %collective-permute-start.27 = (bf16[192,384]{1,0:T(8,128)(2,1)S(1)}, bf16[192,384]{1,0:T(8,128)(2,1)S(1)}, u32[]{:S(2)}, u32[]{:S(2)}) collective-permute-start(bf16[192,384]{1,0:T(8,128)(2,1)S(1)} %get-tuple-element.206.refs_7_), channel_id=1, source_target_pairs={{0,24},{1,25},{2,26},{3,27},{4,28},{5,29},{6,30},{7,31},{8,0},{9,1... | collective-permute-start | bytes 442376 | tf_op jit(solution)/shard_map/ppermute | solution.py:134
  199.1 10.5 %shard_map.145 = (bf16[1152,1024]{1,0:T(8,128)(2,1)S(1)}, f32[8,1152]{1,0:T(8,128)S(1)}) custom-call(bf16[2304,1024]{1,0:T(8,128)(2,1)S(1)} %copy-done.29, bf16[2304,1024]{1,0:T(8,128)(2,1)S(1)} %copy-done.29, bf16[2304,1024]{1,0:T(8,128)(2,1)S(1)} %copy-done.29, bf16[768,1024]{1,0:T(8,128)(2,1)S(1)} %get-tuple-element.118.refs_3_, ...), custom_call_target="tpu_custom_call" | custom-call | flops 60000002048 | bytes 180000000 | tf_op jit(solution)/shard_map/pallas_call | solution.py:217
  209.6 7.3 %collective-permute-done.30 = bf16[2,4,240,384]{3,2,1,0:T(8,128)(2,1)S(1)} collective-permute-done((bf16[2,4,240,384]{3,2,1,0:T(8,128)(2,1)S(1)}, bf16[2,4,240,384]{3,2,1,0:T(8,128)(2,1)S(1)}, u32[]{:S(2)}, u32[]{:S(2)}) %collective-permute-start.30) | collective-permute-done | bytes 1474592 | tf_op jit(solution)/shard_map/ppermute | solution.py:134
  218.4 6.1 %shard_map.146 = (bf16[4,4,144,384]{3,2,1,0:T(8,128)(2,1)S(1)}, bf16[4,4,144,384]{3,2,1,0:T(8,128)(2,1)S(1)}) custom-call(s32[32,3]{1,0:T(8,128)S(1)} %copy.71.refs_0_, bf16[1152,1024]{1,0:T(8,128)(2,1)S(1)} %get-tuple-element.121.refs_1_, bf16[1152,1024]{1,0:T(8,128)(2,1)S(1)} %get-tuple-element.129.refs_2_, bf16[1024,768]{1,0:T(8,128)(2,1)S(1)} %copy-done.37, ...), custom_call_target="tpu_custom_call" | custom-call | flops 35000000512 | bytes 105000000 | tf_op jit(solution)/shard_map/pallas_call | solution.py:217
  225.3 2.9 %collective-permute-done.31 = bf16[4,4,144,384]{3,2,1,0:T(8,128)(2,1)S(1)} collective-permute-done((bf16[4,4,144,384]{3,2,1,0:T(8,128)(2,1)S(1)}, bf16[4,4,144,384]{3,2,1,0:T(8,128)(2,1)S(1)}, u32[]{:S(2)}, u32[]{:S(2)}) %collective-permute-start.31) | collective-permute-done | bytes 1769504 | tf_op jit(solution)/shard_map/ppermute | solution.py:134
  230.0 10.1 %shard_map.147 = (bf16[1024,768]{1,0:T(8,128)(2,1)}, f32[8,768]{1,0:T(8,128)S(1)}) custom-call(s32[32,3]{1,0:T(8,128)S(1)} %copy.71.refs_0_, bf16[1152,1024]{1,0:T(8,128)(2,1)S(1)} %get-tuple-element.121.refs_1_, bf16[1152,1024]{1,0:T(8,128)(2,1)S(1)} %get-tuple-element.129.refs_2_, bf16[1024,768]{1,0:T(8,128)(2,1)S(1)} %copy-done.6, ...), custom_call_target="tpu_custom_call" | custom-call | flops 54999998464 | bytes 165000000 | tf_op jit(solution)/shard_map/pallas_call | solution.py:217
  241.5 3.2 %collective-permute-start.40 = (bf16[240,384]{1,0:T(8,128)(2,1)S(1)}, bf16[240,384]{1,0:T(8,128)(2,1)S(1)}, u32[]{:S(2)}, u32[]{:S(2)}) collective-permute-start(bf16[240,384]{1,0:T(8,128)(2,1)S(1)} %get-tuple-element.201), channel_id=1, source_target_pairs={{0,24},{1,25},{2,26},{3,27},{4,28},{5,29},{6,30},{7,31},{8,0},{9,1... | collective-permute-start | bytes 552968 | tf_op jit(solution)/shard_map/ppermute | solution.py:134
  250.1 4.6 %collective-permute-done.33 = bf16[4,144,384]{2,1,0:T(8,128)(2,1)S(1)} collective-permute-done((bf16[4,144,384]{2,1,0:T(8,128)(2,1)S(1)}, bf16[4,144,384]{2,1,0:T(8,128)(2,1)S(1)}, u32[]{:S(2)}, u32[]{:S(2)}) %collective-permute-start.33) | collective-permute-done | bytes 442400 | tf_op jit(solution)/shard_map/ppermute | solution.py:134
  254.9 10.0 %shard_map.149 = bf16[1024,768]{1,0:T(8,128)(2,1)} custom-call(s32[32,3]{1,0:T(8,128)S(1)} %copy.71.refs_0_, bf16[1536,1024]{1,0:T(8,128)(2,1)S(1)} %copy-done.41, bf16[1536,1024]{1,0:T(8,128)(2,1)S(1)} %copy-done.45, f32[1024,768]{1,0:T(8,128)S(1)} %copy-done.31, f32[8,768]{1,0:T(8,128)S(1)} %copy-done.39, ...), custom_call_target="tpu_custom_call" | custom-call | flops 54999998464 | bytes 165000000 | tf_op jit(solution)/shard_map/pallas_call | solution.py:217
  271.2 2.9 %collective-permute-start.48 = (bf16[16,384]{1,0:T(8,128)(2,1)S(1)}, bf16[16,384]{1,0:T(8,128)(2,1)S(1)}, u32[]{:S(2)}, u32[]{:S(2)}) collective-permute-start(bf16[16,384]{1,0:T(8,128)(2,1)S(1)} %get-tuple-element.241), channel_id=1, source_target_pairs={{0,24},{1,25},{2,26},{3,27},{4,28},{5,29},{6,30},{7,31},{8,0},{9,1... | collective-permute-start | bytes 36872 | tf_op jit(solution)/shard_map/ppermute | solution.py:134
  275.9 3.7 %collective-permute-start.35 = (bf16[144,384]{1,0:T(8,128)(2,1)S(1)}, bf16[144,384]{1,0:T(8,128)(2,1)S(1)}, u32[]{:S(2)}, u32[]{:S(2)}) collective-permute-start(bf16[144,384]{1,0:T(8,128)(2,1)S(1)} %get-tuple-element.210.refs_13_), channel_id=1, source_target_pairs={{0,24},{1,25},{2,26},{3,27},{4,28},{5,29},{6,30},{7,31},{8,0},{9,1... | collective-permute-start | bytes 331784 | tf_op jit(solution)/shard_map/ppermute | solution.py:134
  (265 shorter events, 71.7 us)
Async XLA Ops:
  4.5 15.8 %collective-permute-start.2 = (bf16[208,384]{1,0:T(8,128)(2,1)S(1)}, bf16[208,384]{1,0:T(8,128)(2,1)S(1)}, u32[]{:S(2)}, u32[]{:S(2)}) collective-permute-start(bf16[208,384]{1,0:T(8,128)(2,1)S(1)} %fusion.24), channel_id=1, source_target_pairs={{0,16},{1,17},{2,18},{3,19},{4,20},{5,21},{6,22},{7,23},{8,24},{9,... | collective-permute-start | bytes 479240 | tf_op jit(solution)/shard_map/ppermute | solution.py:134
  8.5 11.8 %collective-permute-start.1 = (bf16[208,384]{1,0:T(8,128)(2,1)S(1)}, bf16[208,384]{1,0:T(8,128)(2,1)S(1)}, u32[]{:S(2)}, u32[]{:S(2)}) collective-permute-start(bf16[208,384]{1,0:T(8,128)(2,1)S(1)} %fusion.24), channel_id=1, source_target_pairs={{0,8},{1,9},{2,10},{3,11},{4,12},{5,13},{6,14},{7,15},{8,16},{9,17... | collective-permute-start | bytes 479240 | tf_op jit(solution)/shard_map/ppermute | solution.py:134
  10.1 11.3 %collective-permute-start.3 = (bf16[208,384]{1,0:T(8,128)(2,1)S(1)}, bf16[208,384]{1,0:T(8,128)(2,1)S(1)}, u32[]{:S(2)}, u32[]{:S(2)}) collective-permute-start(bf16[208,384]{1,0:T(8,128)(2,1)S(1)} %fusion.24), channel_id=1, source_target_pairs={{0,24},{1,25},{2,26},{3,27},{4,28},{5,29},{6,30},{7,31},{8,0},{9,1... | collective-permute-start | bytes 479240 | tf_op jit(solution)/shard_map/ppermute | solution.py:134
  32.1 22.6 %collective-permute-start.6 = (bf16[2,4,208,384]{3,2,1,0:T(8,128)(2,1)S(1)}, bf16[2,4,208,384]{3,2,1,0:T(8,128)(2,1)S(1)}, u32[]{:S(2)}, u32[]{:S(2)}) collective-permute-start(bf16[2,4,208,384]{3,2,1,0:T(8,128)(2,1)S(1)} %pad_maximum_fusion.refs_1_.refs_4_.refs_5_.refs_6_), channel_id=1, source_target_pairs={{0,2},{1,5},{2,0},{3,7},{4,6},{5,1},{6,4},{7,3},{8,10},{9,13},{10,... | collective-permute-start | bytes 3833864 | tf_op jit(solution)/shard_map/ppermute | solution.py:134
  37.7 16.0 %collective-permute-start.8 = (bf16[192,384]{1,0:T(8,128)(2,1)S(1)}, bf16[192,384]{1,0:T(8,128)(2,1)S(1)}, u32[]{:S(2)}, u32[]{:S(2)}) collective-permute-start(bf16[192,384]{1,0:T(8,128)(2,1)S(1)} %pad_maximum_fusion.11), channel_id=1, source_target_pairs={{0,16},{1,17},{2,18},{3,19},{4,20},{5,21},{6,22},{7,23},{8,24},{9,... | collective-permute-start | bytes 442376 | tf_op jit(solution)/shard_map/ppermute | solution.py:134
  40.2 13.6 %collective-permute-start.7 = (bf16[192,384]{1,0:T(8,128)(2,1)S(1)}, bf16[192,384]{1,0:T(8,128)(2,1)S(1)}, u32[]{:S(2)}, u32[]{:S(2)}) collective-permute-start(bf16[192,384]{1,0:T(8,128)(2,1)S(1)} %pad_maximum_fusion.11), channel_id=1, source_target_pairs={{0,8},{1,9},{2,10},{3,11},{4,12},{5,13},{6,14},{7,15},{8,16},{9,17... | collective-permute-start | bytes 442376 | tf_op jit(solution)/shard_map/ppermute | solution.py:134
  42.1 24.6 %collective-permute-start.10 = (bf16[2,4,208,384]{3,2,1,0:T(8,128)(2,1)S(1)}, bf16[2,4,208,384]{3,2,1,0:T(8,128)(2,1)}, u32[]{:S(2)}, u32[]{:S(2)}) collective-permute-start(bf16[2,4,208,384]{3,2,1,0:T(8,128)(2,1)S(1)} %pad_maximum_fusion.refs_1_.refs_4_.refs_5_.refs_6_), channel_id=1, source_target_pairs={{0,1},{1,0},{2,3},{3,2},{4,5},{5,4},{6,7},{7,6},{8,9},{9,8},{10,11... | collective-permute-start | bytes 3833864 | tf_op jit(solution)/shard_map/ppermute | solution.py:134
  54.7 12.0 %collective-permute-start.11 = (bf16[2,4,208,384]{3,2,1,0:T(8,128)(2,1)S(1)}, bf16[2,4,208,384]{3,2,1,0:T(8,128)(2,1)}, u32[]{:S(2)}, u32[]{:S(2)}) collective-permute-start(bf16[2,4,208,384]{3,2,1,0:T(8,128)(2,1)S(1)} %collective-permute-done.6.refs_2_.refs_5_.refs_6_.refs_7_), channel_id=1, source_target_pairs={{0,1},{1,0},{2,3},{3,2},{4,5},{5,4},{6,7},{7,6},{8,9},{9,8},{10,11... | collective-permute-start | bytes 3833864 | tf_op jit(solution)/shard_map/ppermute | solution.py:134
  66.0 39.9 %collective-permute-start.17 = (bf16[2,4,192,384]{3,2,1,0:T(8,128)(2,1)S(1)}, bf16[2,4,192,384]{3,2,1,0:T(8,128)(2,1)S(1)}, u32[]{:S(2)}, u32[]{:S(2)}) collective-permute-start(bf16[2,4,192,384]{3,2,1,0:T(8,128)(2,1)S(1)} %pad_maximum_fusion.1.refs_4_.refs_6_.refs_5_), channel_id=1, source_target_pairs={{0,1},{1,0},{2,3},{3,2},{4,5},{5,4},{6,7},{7,6},{8,9},{9,8},{10,11... | collective-permute-start | bytes 3538952 | tf_op jit(solution)/shard_map/ppermute | solution.py:134
  66.1 21.8 %collective-permute-start.16 = (bf16[2,4,192,384]{3,2,1,0:T(8,128)(2,1)S(1)}, bf16[2,4,192,384]{3,2,1,0:T(8,128)(2,1)S(1)}, u32[]{:S(2)}, u32[]{:S(2)}) collective-permute-start(bf16[2,4,192,384]{3,2,1,0:T(8,128)(2,1)S(1)} %pad_maximum_fusion.1.refs_4_.refs_6_.refs_5_), channel_id=1, source_target_pairs={{0,2},{1,5},{2,0},{3,7},{4,6},{5,1},{6,4},{7,3},{8,10},{9,13},{10,... | collective-permute-start | bytes 3538952 | tf_op jit(solution)/shard_map/ppermute | solution.py:134
  79.5 14.8 %collective-permute-start.15 = (bf16[192,384]{1,0:T(8,128)(2,1)S(1)}, bf16[192,384]{1,0:T(8,128)(2,1)S(1)}, u32[]{:S(2)}, u32[]{:S(2)}) collective-permute-start(bf16[192,384]{1,0:T(8,128)(2,1)S(1)} %pad_maximum_fusion.12), channel_id=1, source_target_pairs={{0,24},{1,25},{2,26},{3,27},{4,28},{5,29},{6,30},{7,31},{8,0},{9,1... | collective-permute-start | bytes 442376 | tf_op jit(solution)/shard_map/ppermute | solution.py:134
  79.6 14.8 %collective-permute-start.14 = (bf16[192,384]{1,0:T(8,128)(2,1)S(1)}, bf16[192,384]{1,0:T(8,128)(2,1)S(1)}, u32[]{:S(2)}, u32[]{:S(2)}) collective-permute-start(bf16[192,384]{1,0:T(8,128)(2,1)S(1)} %pad_maximum_fusion.12), channel_id=1, source_target_pairs={{0,16},{1,17},{2,18},{3,19},{4,20},{5,21},{6,22},{7,23},{8,24},{9,... | collective-permute-start | bytes 442376 | tf_op jit(solution)/shard_map/ppermute | solution.py:134
  79.8 14.5 %collective-permute-start.13 = (bf16[192,384]{1,0:T(8,128)(2,1)S(1)}, bf16[192,384]{1,0:T(8,128)(2,1)S(1)}, u32[]{:S(2)}, u32[]{:S(2)}) collective-permute-start(bf16[192,384]{1,0:T(8,128)(2,1)S(1)} %pad_maximum_fusion.12), channel_id=1, source_target_pairs={{0,8},{1,9},{2,10},{3,11},{4,12},{5,13},{6,14},{7,15},{8,16},{9,17... | collective-permute-start | bytes 442376 | tf_op jit(solution)/shard_map/ppermute | solution.py:134
  88.0 18.0 %collective-permute-start.18 = (bf16[2,4,192,384]{3,2,1,0:T(8,128)(2,1)S(1)}, bf16[2,4,192,384]{3,2,1,0:T(8,128)(2,1)S(1)}, u32[]{:S(2)}, u32[]{:S(2)}) collective-permute-start(bf16[2,4,192,384]{3,2,1,0:T(8,128)(2,1)S(1)} %collective-permute-done.16.refs_5_.refs_7_.refs_6_), channel_id=1, source_target_pairs={{0,1},{1,0},{2,3},{3,2},{4,5},{5,4},{6,7},{7,6},{8,9},{9,8},{10,11... | collective-permute-start | bytes 3538952 | tf_op jit(solution)/shard_map/ppermute | solution.py:134
  104.5 24.2 %collective-permute-start.21 = (bf16[2,4,192,384]{3,2,1,0:T(8,128)(2,1)S(1)}, bf16[2,4,192,384]{3,2,1,0:T(8,128)(2,1)S(1)}, u32[]{:S(2)}, u32[]{:S(2)}) collective-permute-start(bf16[2,4,192,384]{3,2,1,0:T(8,128)(2,1)S(1)} %pad_maximum_fusion.2.refs_8_.refs_4_.refs_10_.refs_9_), channel_id=1, source_target_pairs={{0,1},{1,0},{2,3},{3,2},{4,5},{5,4},{6,7},{7,6},{8,9},{9,8},{10,11... | collective-permute-start | bytes 3538952 | tf_op jit(solution)/shard_map/ppermute | solution.py:134
  104.6 23.6 %collective-permute-start.20 = (bf16[2,4,192,384]{3,2,1,0:T(8,128)(2,1)S(1)}, bf16[2,4,192,384]{3,2,1,0:T(8,128)(2,1)S(1)}, u32[]{:S(2)}, u32[]{:S(2)}) collective-permute-start(bf16[2,4,192,384]{3,2,1,0:T(8,128)(2,1)S(1)} %pad_maximum_fusion.2.refs_8_.refs_4_.refs_10_.refs_9_), channel_id=1, source_target_pairs={{0,2},{1,5},{2,0},{3,7},{4,6},{5,1},{6,4},{7,3},{8,10},{9,13},{10,... | collective-permute-start | bytes 3538952 | tf_op jit(solution)/shard_map/ppermute | solution.py:134
  128.4 24.2 %collective-permute-start.23 = (bf16[4,4,192,384]{3,2,1,0:T(8,128)(2,1)}, bf16[4,4,192,384]{3,2,1,0:T(8,128)(2,1)S(1)}, u32[]{:S(2)}, u32[]{:S(2)}) collective-permute-start(bf16[4,4,192,384]{3,2,1,0:T(8,128)(2,1)} %get-tuple-element.111), channel_id=1, source_target_pairs={{0,1},{1,0},{2,3},{3,2},{4,5},{5,4},{6,7},{7,6},{8,9},{9,8},{10,11... | collective-permute-start | bytes 7077896 | tf_op jit(solution)/shard_map/ppermute | solution.py:134
  154.2 21.2 %collective-permute-start.24 = (bf16[2,4,192,384]{3,2,1,0:T(8,128)(2,1)S(1)}, bf16[2,4,192,384]{3,2,1,0:T(8,128)(2,1)S(1)}, u32[]{:S(2)}, u32[]{:S(2)}) collective-permute-start(bf16[2,4,192,384]{3,2,1,0:T(8,128)(2,1)S(1)} %get-tuple-element.190.refs_14_), channel_id=1, source_target_pairs={{0,2},{1,5},{2,0},{3,7},{4,6},{5,1},{6,4},{7,3},{8,10},{9,13},{10,... | collective-permute-start | bytes 3538952 | tf_op jit(solution)/shard_map/ppermute | solution.py:134
  175.2 21.6 %collective-permute-start.26 = (bf16[4,4,240,384]{3,2,1,0:T(8,128)(2,1)}, bf16[4,4,240,384]{3,2,1,0:T(8,128)(2,1)S(1)}, u32[]{:S(2)}, u32[]{:S(2)}) collective-permute-start(bf16[4,4,240,384]{3,2,1,0:T(8,128)(2,1)} %get-tuple-element.126), channel_id=1, source_target_pairs={{0,1},{1,0},{2,3},{3,2},{4,5},{5,4},{6,7},{7,6},{8,9},{9,8},{10,11... | collective-permute-start | bytes 8847368 | tf_op jit(solution)/shard_map/ppermute | solution.py:134
  175.7 14.7 %collective-permute-start.25 = (bf16[4,192,384]{2,1,0:T(8,128)(2,1)S(1)}, bf16[4,192,384]{2,1,0:T(8,128)(2,1)S(1)}, u32[]{:S(2)}, u32[]{:S(2)}) collective-permute-start(bf16[4,192,384]{2,1,0:T(8,128)(2,1)S(1)} %get-tuple-element.196.refs_7_), channel_id=1, source_target_pairs={{0,4},{1,3},{2,6},{3,1},{4,0},{5,7},{6,2},{7,5},{8,12},{9,11},{10,... | collective-permute-start | bytes 1769480 | tf_op jit(solution)/shard_map/ppermute | solution.py:134
  191.2 26.1 %collective-permute-start.29 = (bf16[192,384]{1,0:T(8,128)(2,1)S(1)}, bf16[192,384]{1,0:T(8,128)(2,1)S(1)}, u32[]{:S(2)}, u32[]{:S(2)}) collective-permute-start(bf16[192,384]{1,0:T(8,128)(2,1)S(1)} %get-tuple-element.204.refs_9_), channel_id=1, source_target_pairs={{0,8},{1,9},{2,10},{3,11},{4,12},{5,13},{6,14},{7,15},{8,16},{9,17... | collective-permute-start | bytes 442376 | tf_op jit(solution)/shard_map/ppermute | solution.py:134
  192.4 24.9 %collective-permute-start.28 = (bf16[192,384]{1,0:T(8,128)(2,1)S(1)}, bf16[192,384]{1,0:T(8,128)(2,1)S(1)}, u32[]{:S(2)}, u32[]{:S(2)}) collective-permute-start(bf16[192,384]{1,0:T(8,128)(2,1)S(1)} %get-tuple-element.205.refs_8_), channel_id=1, source_target_pairs={{0,16},{1,17},{2,18},{3,19},{4,20},{5,21},{6,22},{7,23},{8,24},{9,... | collective-permute-start | bytes 442376 | tf_op jit(solution)/shard_map/ppermute | solution.py:134
  193.9 23.4 %collective-permute-start.27 = (bf16[192,384]{1,0:T(8,128)(2,1)S(1)}, bf16[192,384]{1,0:T(8,128)(2,1)S(1)}, u32[]{:S(2)}, u32[]{:S(2)}) collective-permute-start(bf16[192,384]{1,0:T(8,128)(2,1)S(1)} %get-tuple-element.206.refs_7_), channel_id=1, source_target_pairs={{0,24},{1,25},{2,26},{3,27},{4,28},{5,29},{6,30},{7,31},{8,0},{9,1... | collective-permute-start | bytes 442376 | tf_op jit(solution)/shard_map/ppermute | solution.py:134
  197.5 19.4 %collective-permute-start.30 = (bf16[2,4,240,384]{3,2,1,0:T(8,128)(2,1)S(1)}, bf16[2,4,240,384]{3,2,1,0:T(8,128)(2,1)S(1)}, u32[]{:S(2)}, u32[]{:S(2)}) collective-permute-start(bf16[2,4,240,384]{3,2,1,0:T(8,128)(2,1)S(1)} %get-tuple-element.188.refs_10_), channel_id=1, source_target_pairs={{0,2},{1,5},{2,0},{3,7},{4,6},{5,1},{6,4},{7,3},{8,10},{9,13},{10,... | collective-permute-start | bytes 4423688 | tf_op jit(solution)/shard_map/ppermute | solution.py:134
  224.6 16.1 %collective-permute-start.39 = (bf16[4,240,384]{2,1,0:T(8,128)(2,1)S(1)}, bf16[4,240,384]{2,1,0:T(8,128)(2,1)S(1)}, u32[]{:S(2)}, u32[]{:S(2)}) collective-permute-start(bf16[4,240,384]{2,1,0:T(8,128)(2,1)S(1)} %get-tuple-element.194.refs_7_.refs_11_), channel_id=1, source_target_pairs={{0,4},{1,3},{2,6},{3,1},{4,0},{5,7},{6,2},{7,5},{8,12},{9,11},{10,... | collective-permute-start | bytes 2211848 | tf_op jit(solution)/shard_map/ppermute | solution.py:134
  228.7 16.4 %collective-permute-start.32 = (bf16[2,4,144,384]{3,2,1,0:T(8,128)(2,1)S(1)}, bf16[2,4,144,384]{3,2,1,0:T(8,128)(2,1)S(1)}, u32[]{:S(2)}, u32[]{:S(2)}) collective-permute-start(bf16[2,4,144,384]{3,2,1,0:T(8,128)(2,1)S(1)} %get-tuple-element.191.refs_10_), channel_id=1, source_target_pairs={{0,2},{1,5},{2,0},{3,7},{4,6},{5,1},{6,4},{7,3},{8,10},{9,13},{10,... | collective-permute-start | bytes 2654216 | tf_op jit(solution)/shard_map/ppermute | solution.py:134
  240.8 24.1 %collective-permute-start.42 = (bf16[240,384]{1,0:T(8,128)(2,1)S(1)}, bf16[240,384]{1,0:T(8,128)(2,1)S(1)}, u32[]{:S(2)}, u32[]{:S(2)}) collective-permute-start(bf16[240,384]{1,0:T(8,128)(2,1)S(1)} %get-tuple-element.199), channel_id=1, source_target_pairs={{0,8},{1,9},{2,10},{3,11},{4,12},{5,13},{6,14},{7,15},{8,16},{9,17... | collective-permute-start | bytes 552968 | tf_op jit(solution)/shard_map/ppermute | solution.py:134
  240.9 24.0 %collective-permute-start.41 = (bf16[240,384]{1,0:T(8,128)(2,1)S(1)}, bf16[240,384]{1,0:T(8,128)(2,1)S(1)}, u32[]{:S(2)}, u32[]{:S(2)}) collective-permute-start(bf16[240,384]{1,0:T(8,128)(2,1)S(1)} %get-tuple-element.200), channel_id=1, source_target_pairs={{0,16},{1,17},{2,18},{3,19},{4,20},{5,21},{6,22},{7,23},{8,24},{9,... | collective-permute-start | bytes 552968 | tf_op jit(solution)/shard_map/ppermute | solution.py:134
  241.5 23.5 %collective-permute-start.40 = (bf16[240,384]{1,0:T(8,128)(2,1)S(1)}, bf16[240,384]{1,0:T(8,128)(2,1)S(1)}, u32[]{:S(2)}, u32[]{:S(2)}) collective-permute-start(bf16[240,384]{1,0:T(8,128)(2,1)S(1)} %get-tuple-element.201), channel_id=1, source_target_pairs={{0,24},{1,25},{2,26},{3,27},{4,28},{5,29},{6,30},{7,31},{8,0},{9,1... | collective-permute-start | bytes 552968 | tf_op jit(solution)/shard_map/ppermute | solution.py:134
  248.7 18.3 %collective-permute-start.46 = (bf16[2,4,16,384]{3,2,1,0:T(8,128)(2,1)S(1)}, bf16[2,4,16,384]{3,2,1,0:T(8,128)(2,1)S(1)}, u32[]{:S(2)}, u32[]{:S(2)}) collective-permute-start(bf16[2,4,16,384]{3,2,1,0:T(8,128)(2,1)S(1)} %get-tuple-element.218.refs_16_), channel_id=1, source_target_pairs={{0,2},{1,5},{2,0},{3,7},{4,6},{5,1},{6,4},{7,3},{8,10},{9,13},{10,... | collective-permute-start | bytes 294920 | tf_op jit(solution)/shard_map/ppermute | solution.py:134
  265.1 15.8 %collective-permute-start.37 = (bf16[144,384]{1,0:T(8,128)(2,1)S(1)}, bf16[144,384]{1,0:T(8,128)(2,1)S(1)}, u32[]{:S(2)}, u32[]{:S(2)}) collective-permute-start(bf16[144,384]{1,0:T(8,128)(2,1)S(1)} %get-tuple-element.208.refs_15_), channel_id=1, source_target_pairs={{0,8},{1,9},{2,10},{3,11},{4,12},{5,13},{6,14},{7,15},{8,16},{9,17... | collective-permute-start | bytes 331784 | tf_op jit(solution)/shard_map/ppermute | solution.py:134
  265.4 15.4 %collective-permute-start.36 = (bf16[144,384]{1,0:T(8,128)(2,1)S(1)}, bf16[144,384]{1,0:T(8,128)(2,1)S(1)}, u32[]{:S(2)}, u32[]{:S(2)}) collective-permute-start(bf16[144,384]{1,0:T(8,128)(2,1)S(1)} %get-tuple-element.209.refs_14_), channel_id=1, source_target_pairs={{0,16},{1,17},{2,18},{3,19},{4,20},{5,21},{6,22},{7,23},{8,24},{9,... | collective-permute-start | bytes 331784 | tf_op jit(solution)/shard_map/ppermute | solution.py:134
  (73 other events, 654.2 us)
